TPU v7x, 128 devices: a whole 4x4x4 slice. The times are simulated.
128 devices in a mesh: ctx: 32 (over y, z, core), head: 4 (over x).
Axes of the slice: x: 4, y: 4, z: 4, core: 2. Of those that a mesh axis runs over, the one named last changes fastest.
Arguments:
- token_ids: int32 [4096], P('ctx'), may hold values from 0 to 16383
- targets: int32 [4096], P(('ctx', 'head')), may hold values from 0 to 16383
- embed: bfloat16 [16384, 4096], P('head', 'ctx'), may hold values from -6 to 6
- w_zx: bfloat16 [4096, 2, 4096], P(None, None, 'head'), may hold values from -0.09375 to 0.09375
- w_bc: bfloat16 [4096, 2, 512], P(None, None, 'head'), may hold values from -0.09375 to 0.09375
- w_dt: bfloat16 [4096, 64], P(None, 'head'), may hold values from -0.21875 to 0.21875
- conv_x: float32 [4, 4096], P(None, 'head'), may hold values from -3 to 3
- conv_bc: float32 [4, 2, 512], P(None, None, 'head'), may hold values from -3 to 3
- dt_bias: float32 [64], P('head'), may hold values from -7 to 0.2
- a_log: float32 [64], P('head')
- d_skip: float32 [64], P('head'), may hold values from 0.3 to 4
- norm_gain: float32 [4096], P('head'), may hold values from 0.1 to 1.9
- pre_gain: float32 [4096], replicated, may hold values from 0.1 to 1.9
- final_gain: float32 [4096], replicated, may hold values from 0.1 to 1.9
- w_out: bfloat16 [4096, 4096], P('head', 'ctx'), may hold values from -0.09375 to 0.09375
- lm_head: bfloat16 [4096, 16384], P('head', 'ctx'), as said below
Outputs:
- scores: float32 [4096], P(('ctx', 'head'))
Inputs may be any that keep to these rules, and one draw needn't show every extreme that they name: `lm_head`: vocabulary projection, every entry within 552 / sqrt(4096) in magnitude.
All inputs are finite; a program needn't handle non-finite values.
Results may differ from a plain program's by a relative error of at most 0.038.
Values may be sent and summed in bfloat16 or wider, within the bound.
No kernel may reach another device: no remote copies, remote signals or barrier semaphores. Data moves between devices by JAX's collectives and lax.ppermute only.
A program may use at most 128 MiB of HBM per device.

v0:
```python
import jax
import jax.numpy as jnp
from jax import lax
from jax.sharding import PartitionSpec as P

HEAD_DIM = 64
STATE = 128


exact_prec = lax.Precision.HIGHEST


def passed_along(value, axis, by):
    length = lax.axis_size(axis)
    pairs = [(i, i + by) for i in range(length) if 0 <= i + by < length]
    return lax.ppermute(value, axis, pairs)


def entering(part, axis, combine, identity):
    place = lax.axis_index(axis)
    gathered = jax.tree.map(lambda a: lax.all_gather(a, axis), part)
    state = jax.tree.map(lambda a, e: jnp.zeros_like(a) + jnp.asarray(e, a.dtype), part, identity)

    def one(hop, state):
        return combine(
            state, jax.tree.map(lambda a: lax.dynamic_index_in_dim(a, hop, 0, False), gathered)
        )

    return lax.fori_loop(0, place, one, state)


def combined_all(value, axis, combine):
    everything = jax.tree.map(lambda part: lax.all_gather(part, axis), value)
    leading = jax.tree.map(lambda part: part[0], everything)

    def hop(k, so_far):
        return combine(so_far, jax.tree.map(lambda part: part[k], everything))

    return lax.fori_loop(1, lax.axis_size(axis), hop, leading)


def rms_scale(values, gain):
    return values * lax.rsqrt(jnp.mean(values * values, axis=-1, keepdims=True) + 1e-05) * gain


def chain_states(earlier, following):
    decay_one, state_one = earlier
    decay_two, state_two = following
    return (decay_one * decay_two, decay_two[:, None, None] * state_one + state_two)


def join_stats(left_set, right_set):
    peak_left, sum_left, first_left, second_left, target_left = left_set
    peak_right, sum_right, first_right, second_right, target_right = right_set
    row_peak = jnp.maximum(peak_left, peak_right)
    shift_left = peak_left - row_peak
    shift_right = peak_right - row_peak
    weight_left = jnp.exp(shift_left)
    weight_right = jnp.exp(shift_right)
    exp_sum = weight_left * sum_left + weight_right * sum_right
    first_moment = weight_left * (first_left + shift_left * sum_left) + weight_right * (
        first_right + shift_right * sum_right
    )
    second_moment = weight_left * (
        second_left + 2.0 * shift_left * first_left + shift_left * shift_left * sum_left
    ) + weight_right * (
        second_right + 2.0 * shift_right * first_right + shift_right * shift_right * sum_right
    )
    return (row_peak, exp_sum, first_moment, second_moment, target_left + target_right)


def on_device(
    token_ids,
    targets,
    embed,
    w_zx,
    w_bc,
    w_dt,
    conv_x,
    conv_bc,
    dt_bias,
    a_log,
    d_skip,
    norm_gain,
    pre_gain,
    final_gain,
    w_out,
    lm_head,
):
    ctx_count = lax.axis_size("ctx")
    head_count = lax.axis_size("head")
    tok_rows = token_ids.shape[0]
    quarter = tok_rows // head_count
    model_width = pre_gain.shape[0]
    head_pos = lax.axis_index("head")
    ctx_pos = lax.axis_index("ctx")
    all_ids, group_targets = (
        lax.all_gather(token_ids, "ctx", axis=0, tiled=True),
        lax.all_gather(targets, "ctx", axis=0, tiled=True),
    )
    emb_table, vocab_cols = (
        lax.all_gather(embed, "head", axis=0, tiled=True),
        lax.all_gather(lm_head, "head", axis=0, tiled=True),
    )
    looked = jnp.take(emb_table, all_ids, axis=0)
    slice_cols = looked.shape[1]
    by_span = looked.reshape(ctx_count, tok_rows, slice_cols)
    arrived = lax.all_to_all(by_span, "ctx", split_axis=0, concat_axis=2, tiled=True).reshape(
        tok_rows, model_width
    )
    normed_in = rms_scale(arrived.astype(jnp.float32), pre_gain).astype(jnp.bfloat16)
    channels = w_zx.shape[2]
    group_cols = w_bc.shape[2]
    proj_zx = jnp.dot(
        normed_in, w_zx.reshape(model_width, 2 * channels), preferred_element_type=jnp.float32
    )
    proj_bc = jnp.dot(
        normed_in, w_bc.reshape(model_width, 2 * group_cols), preferred_element_type=jnp.float32
    )
    step_raw = jnp.dot(normed_in, w_dt, preferred_element_type=jnp.float32)
    gate_z = proj_zx[:, :channels]
    mixed_in = jnp.concatenate([proj_zx[:, channels:], proj_bc], axis=1)
    conv_taps = conv_x.shape[0]
    kernel = jnp.concatenate([conv_x, conv_bc.reshape(conv_taps, 2 * group_cols)], axis=1)
    rim_rows = passed_along(mixed_in[tok_rows - conv_taps + 1 :], "ctx", 1)
    extended = jnp.concatenate([rim_rows, mixed_in], axis=0)
    convolved = jnp.zeros_like(mixed_in)
    for offset in range(conv_taps):
        convolved = convolved + kernel[offset] * extended[offset : offset + tok_rows]
    activated = jax.nn.silu(convolved)
    head_local = step_raw.shape[1]
    group_local = group_cols // STATE
    per_group = head_local // group_local
    x_heads = activated[:, :channels].reshape(tok_rows, head_local, HEAD_DIM)
    b_groups = activated[:, channels : channels + group_cols].reshape(tok_rows, group_local, STATE)
    c_groups = activated[:, channels + group_cols :].reshape(tok_rows, group_local, STATE)
    step_size = jax.nn.softplus(step_raw + dt_bias)
    log_rate = -jnp.exp(a_log) * step_size
    log_decay = jnp.cumsum(log_rate, axis=0)
    decay_gap = log_decay.T[:, :, None] - log_decay.T[:, None, :]
    positions = jnp.arange(tok_rows)
    causal = positions[:, None] >= positions[None, :]
    decay_mask = jnp.exp(jnp.where(causal[None], decay_gap, -jnp.inf))
    group_scores = jnp.einsum("tgn,sgn->gts", c_groups, b_groups, precision=exact_prec)
    mixing = jnp.repeat(group_scores, per_group, axis=0) * decay_mask * step_size.T[:, None, :]
    y_local = jnp.einsum("hts,shp->thp", mixing, x_heads, precision=exact_prec)
    b_heads = jnp.repeat(b_groups, per_group, axis=1)
    c_heads = jnp.repeat(c_groups, per_group, axis=1)
    tail_decay = jnp.exp(log_decay[-1][None, :] - log_decay) * step_size
    end_state = jnp.einsum("sh,shp,shn->hpn", tail_decay, x_heads, b_heads, precision=exact_prec)
    end_decay = jnp.exp(log_decay[-1])
    state_in = entering(
        (end_decay, end_state),
        "ctx",
        chain_states,
        (jnp.ones_like(end_decay), jnp.zeros_like(end_state)),
    )[1]
    y_carry = (
        jnp.einsum("thn,hpn->thp", c_heads, state_in, precision=exact_prec)
        * jnp.exp(log_decay)[:, :, None]
    )
    mixer_out = y_local + y_carry + d_skip[None, :, None] * x_heads
    gated_raw = mixer_out.reshape(tok_rows, channels) * jax.nn.silu(gate_z)
    grouped = gated_raw.reshape(tok_rows, group_local, channels // group_local)
    grouped = grouped * lax.rsqrt(jnp.mean(grouped * grouped, axis=-1, keepdims=True) + 1e-05)
    gated_out = (grouped.reshape(tok_rows, channels) * norm_gain).astype(jnp.bfloat16)
    vocab_width = vocab_cols.shape[1]
    vocab_ids = ctx_pos * vocab_width + jnp.arange(vocab_width, dtype=jnp.int32)
    partial_out = jnp.dot(
        gated_out,
        lax.all_gather(w_out, "ctx", axis=1, tiled=True),
        preferred_element_type=jnp.float32,
    )
    own_emb = lax.dynamic_slice_in_dim(arrived, head_pos * quarter, quarter, 0)
    summed_out = lax.psum_scatter(partial_out, "head", scatter_dimension=0, tiled=True)
    residual = (own_emb.astype(jnp.float32) + summed_out).astype(jnp.bfloat16)
    normed_out = rms_scale(residual.astype(jnp.float32), final_gain).astype(jnp.bfloat16)
    logits = jnp.dot(
        lax.all_gather(normed_out, "ctx", axis=0, tiled=True),
        vocab_cols,
        preferred_element_type=jnp.float32,
    )
    row_peak = jnp.max(logits, axis=1)
    shifted = logits - row_peak[:, None]
    weights = jnp.exp(shifted)
    is_target = group_targets[:, None] == vocab_ids[None, :]
    fresh = (
        row_peak,
        jnp.sum(weights, axis=1),
        jnp.sum(weights * shifted, axis=1),
        jnp.sum(weights * shifted * shifted, axis=1),
        jnp.sum(jnp.where(is_target, logits, 0.0), axis=1),
    )
    partials = tuple((new_part for new_part in fresh))
    peak_parts, sum_parts, first_parts, second_parts, target_parts = partials
    merged = combined_all(
        (peak_parts, sum_parts, first_parts, second_parts, target_parts), "ctx", join_stats
    )
    row_base = ctx_pos * quarter
    row_peak, exp_sum, first_moment, second_moment, target_logit = tuple(
        (lax.dynamic_slice_in_dim(member, row_base, quarter, 0) for member in merged)
    )
    mean_shift = first_moment / exp_sum
    spread = second_moment / exp_sum - mean_shift * mean_shift
    return (target_logit - row_peak - mean_shift) * lax.rsqrt(jnp.maximum(spread, 0.25))


def solution(mesh):
    placed = (
        P("ctx"),
        P(("ctx", "head")),
        P("head", "ctx"),
        P(None, None, "head"),
        P(None, None, "head"),
        P(None, "head"),
        P(None, "head"),
        P(None, None, "head"),
        P("head"),
        P("head"),
        P("head"),
        P("head"),
        P(),
        P(),
        P("head", "ctx"),
        P("head", "ctx"),
    )
    return jax.shard_map(
        on_device, mesh=mesh, in_specs=placed, out_specs=P(("ctx", "head")), check_vma=False
    )
```

profile of v0, /device:TPU:0, one launch (start us, length us, event | category | flops | bytes accessed | tf_op | source)
XLA Modules:
  0.0 533.4 jit_solution(11438941202038946032)
XLA Ops:
  6.5 0.7 all-gather.14.cloned.1.call-update
  7.3 23.0 %all-gather.6 = s32[32,1,128]{2,1,0:T(1,128)S(1)} all-gather(s32[1,1,128]{2,1,0:T(1,128)} %bitcast.117), channel_id=1, replica_groups=mesh['ctx'=32,'head'=4] {'ctx'}, dimensions={0}, use_global_device_ids=true | all-gather | bytes 16896 | tf_op jit(solution)/shard_map/all_gather | solution.py:98
  30.3 29.5 %all-gather.14.cloned.1.call-done = bf16[16384,128]{1,0:T(8,128)(2,1)} async-done(((bf16[4096,128]{1,0:T(8,128)(2,1)}), bf16[16384,128]{1,0:T(8,128)(2,1)}) %all-gather.14.cloned.1.call-update) | async-done | bytes 4194320 | tf_op jit(solution)/shard_map/all_gather | solution.py:102
  59.8 13.8 %gather_fusion = bf16[4096,128]{1,0:T(8,128)(2,1)S(1)} fusion(bf16[16384,128]{1,0:T(8,128)(2,1)} %all-gather.14.cloned.1.call-done, s32[4096]{0:T(1024)S(1)} %fusion.41), kind=kCustom, calls=%fused_computation | custom fusion | bytes 2113536 | tf_op jit(solution)/shard_map/jit(_take)/gather | solution.py:105
  73.5 1.5 broadcast_select_fusion
  75.0 7.3 %all-to-all-start = ((bf16[32,128,128]{2,1,0:T(8,128)(2,1)}), bf16[32,128,128]{2,1,0:T(8,128)(2,1)S(1)}, u32[]{:S(2)}, u32[]{:S(2)}) async-start(bf16[32,128,128]{2,1,0:T(8,128)(2,1)} %broadcast_select_fusion), calls=%async_computation | async-start | bytes 2097152 | tf_op jit(solution)/shard_map/all_to_all | solution.py:108
  82.3 0.0 all-gather.22.cloned.1.call-start
  82.4 17.1 %copy.55 = bf16[512,8,2,1024]{3,1,2,0:T(8,128)(2,1)} copy(bf16[512,8,2,1024]{3,2,1,0:T(2,128)(2,1)} %bitcast.93) | data formatting | bytes 33554432
  99.5 0.1 slice_reduce_fusion.3
  99.6 0.7 copy.44
  100.3 0.6 fusion.2
  100.8 0.5 copy.53
  101.4 0.5 compare_select_fusion.1
  101.9 0.1 fusion.46
  102.0 0.1 copy.47
  102.1 0.2 reduce_window_sum.11
  102.3 0.1 copy.50
  102.3 0.7 fusion.4
  103.1 8.3 %fusion.53 = f32[128,2048]{1,0:T(8,128)S(1)} fusion(bf16[128,4096]{0,1:T(8,128)(2,1)S(1)} %bitcast.94, bf16[4096,2048]{1,0:T(8,128)(2,1)} %bitcast.91), kind=kOutput, calls=%fused_computation.110 | convolution fusion | flops 2147483648 | bytes 18874368 | tf_op jit(solution)/shard_map/dot_general | solution.py:114
  111.5 0.5 fusion.6
  112.0 2.2 collective-permute-start
  114.1 0.1 exponential_multiply_fusion.1
  114.2 0.8 collective-permute-done
  115.0 0.1 maximum_maximum_fusion
  115.0 0.4 divide_multiply_fusion
  115.5 0.2 copy.46
  115.7 1.7 fusion.27
  117.4 0.0 all-gather.22.cloned.1.call-update
  117.4 0.0 all-gather.16.cloned.1.call-start
  117.5 0.7 all-gather.16.cloned.1.call-update
  118.2 0.0 reduce-scatter.2.cloned.1.call-start
  118.3 0.1 copy.48
  118.3 0.1 copy.51
  118.4 25.3 %all-gather.7 = f32[32,1,16]{2,1,0:T(1,128)S(1)} all-gather(f32[1,1,16]{2,1,0:T(1,128)S(1)} %get-tuple-element.376), channel_id=1, replica_groups=mesh['ctx'=32,'head'=4] {'ctx'}, dimensions={0}, use_global_device_ids=true | all-gather | bytes 2112 | tf_op jit(solution)/shard_map/all_gather | solution.py:21
  143.7 0.3 fusion.48
  144.0 2.2 convolution_bitcast_fusion.1
  146.2 46.6 %all-gather.22.cloned.1.call-done = f32[512,64,128]{2,1,0:T(8,128)} async-done(((f32[16,64,128]{2,1,0:T(8,128)}), f32[512,64,128]{2,1,0:T(8,128)}) %all-gather.22.cloned.1.call-update) | async-done | bytes 16777232 | tf_op jit(solution)/shard_map/all_gather | solution.py:21
  192.8 0.2 while.35
  193.0 0.4 copy-done.9
  193.5 2.1 fusion.11
  195.6 0.2 copy.52
  195.8 0.2 multiply_reduce_fusion
  196.1 58.0 %all-gather.16.cloned.1.call-done = bf16[1024,4096]{1,0:T(8,128)(2,1)} async-done(((bf16[1024,128]{1,0:T(8,128)(2,1)}), bf16[1024,4096]{1,0:T(8,128)(2,1)}) %all-gather.16.cloned.1.call-update) | async-done | bytes 8388624 | tf_op jit(solution)/shard_map/all_gather | solution.py:171
  254.1 6.1 %fusion.36 = f32[128,4096]{1,0:T(8,128)} fusion(bf16[1024,4096]{1,0:T(8,128)(2,1)} %all-gather.16.cloned.1.call-done, f32[1024]{0:T(1024)S(1)} %copy-done.4, f32[128]{0:T(128)S(1)} %add_rsqrt_fusion.1, f32[128,1024]{1,0:T(8,128)S(1)} %copy.52, f32[128,2048]{1,0:T(8,128)S(1)} %fusion.53), kind=kOutput, calls=%fused_computation.71 | convolution fusion | flops 1074790400 | bytes 11538944 | tf_op jit(solution)/shard_map/dot_general | solution.py:169
  260.2 0.0 all-gather.20.cloned.1.call-start
  260.3 0.5 all-gather.20.cloned.1.call-update
  260.8 0.0 all-gather.18.cloned.1.call-start
  260.9 28.8 %reduce-scatter.2.cloned.1.call-done = f32[32,4096]{1,0:T(8,128)} async-done(((f32[128,4096]{1,0:T(8,128)}), f32[32,4096]{1,0:T(8,128)}) %reduce-scatter.2.cloned.1.call-update) | async-done | bytes 524304 | tf_op jit(solution)/shard_map/reduce_scatter | solution.py:175
  289.6 1.3 fusion.23
  290.9 0.8 fusion.25
  291.8 0.7 dynamic-slice
  293.2 0.2 dynamic-update-slice
  293.5 16.8 %all-reduce = s32[1024]{0:T(1024)S(1)} all-reduce(s32[1024]{0:T(1024)S(1)} %dynamic-update-slice), channel_id=1, replica_groups=mesh['ctx'=32,'head'=4] {'ctx'}, use_global_device_ids=true, to_apply=%add | all-reduce | flops 1024 | bytes 8192
  310.3 29.0 %all-gather.20.cloned.1.call-done = bf16[4096,512]{1,0:T(8,128)(2,1)} async-done(((bf16[1024,512]{1,0:T(8,128)(2,1)}), bf16[4096,512]{1,0:T(8,128)(2,1)}) %all-gather.20.cloned.1.call-update) | async-done | bytes 4194320 | tf_op jit(solution)/shard_map/all_gather | solution.py:103
  339.2 55.8 %all-gather.18.cloned.1.call-done = bf16[1024,4096]{1,0:T(8,128)(2,1)} async-done(((bf16[32,4096]{1,0:T(8,128)(2,1)}), bf16[1024,4096]{1,0:T(8,128)(2,1)}) %all-gather.18.cloned.1.call-update) | async-done | bytes 8388624 | tf_op jit(solution)/shard_map/all_gather | solution.py:179
  395.0 8.3 %fusion.52 = (f32[1024]{0:T(1024)S(1)}, f32[1024,512]{0,1:T(8,128)S(1)}) fusion(bf16[1024,4096]{1,0:T(8,128)(2,1)} %all-gather.18.cloned.1.call-done, bf16[4096,512]{1,0:T(8,128)(2,1)} %all-gather.20.cloned.1.call-done), kind=kOutput, calls=%fused_computation.109 | convolution fusion | flops 4295490560 | bytes 14684160 | tf_op jit(solution)/shard_map/dot_general | solution.py:178
  403.3 0.8 fusion.5
  404.1 24.3 %all-gather.2 = f32[32768]{0:T(1024)S(1)} all-gather(f32[1024]{0:T(1024)S(1)} %get-tuple-element.325), channel_id=4, replica_groups=mesh['ctx'=32,'head'=4] {'ctx'}, dimensions={0}, use_global_device_ids=true | all-gather | bytes 135168 | tf_op jit(solution)/shard_map/all_gather | solution.py:33
  428.5 22.4 %all-gather.3 = f32[32768]{0:T(1024)S(1)} all-gather(f32[1024]{0:T(1024)S(1)} %get-tuple-element.324), channel_id=5, replica_groups=mesh['ctx'=32,'head'=4] {'ctx'}, dimensions={0}, use_global_device_ids=true | all-gather | bytes 135168 | tf_op jit(solution)/shard_map/all_gather | solution.py:33
  450.9 23.9 %all-gather.4 = f32[32768]{0:T(1024)S(1)} all-gather(f32[1024]{0:T(1024)S(1)} %get-tuple-element.323), channel_id=6, replica_groups=mesh['ctx'=32,'head'=4] {'ctx'}, dimensions={0}, use_global_device_ids=true | all-gather | bytes 135168 | tf_op jit(solution)/shard_map/all_gather | solution.py:33
  474.9 22.4 %all-gather.5 = f32[32768]{0:T(1024)S(1)} all-gather(f32[1024]{0:T(1024)S(1)} %get-tuple-element.326), channel_id=7, replica_groups=mesh['ctx'=32,'head'=4] {'ctx'}, dimensions={0}, use_global_device_ids=true | all-gather | bytes 135168 | tf_op jit(solution)/shard_map/all_gather | solution.py:33
  497.3 23.9 %all-gather.1 = f32[32768]{0:T(1024)S(1)} all-gather(f32[1024]{0:T(1024)S(1)} %get-tuple-element.379), channel_id=3, replica_groups=mesh['ctx'=32,'head'=4] {'ctx'}, dimensions={0}, use_global_device_ids=true | all-gather | bytes 135168 | tf_op jit(solution)/shard_map/all_gather | solution.py:33
  521.3 4.7 while.36
  526.0 0.6 rsqrt_multiply_fusion
  (276 shorter events, 3.0 us)
Async XLA Ops:
  6.5 94.8 %copy-start = (bf16[4096,16]{0,1:T(8,128)(2,1)S(1)}, bf16[4096,16]{0,1:T(8,128)(2,1)}, u32[]{:S(2)}) copy-start(bf16[4096,16]{0,1:T(8,128)(2,1)} %param.25) | copy-start | bytes 393220
  6.5 53.2 %all-gather.14.cloned.1.call-start = ((), (), s32[]{:S(2)}) async-start(), calls=%async_computation.2 | async-start | bytes 5242880 | tf_op jit(solution)/shard_map/all_gather | solution.py:102
  75.0 24.6 %all-to-all-start = ((bf16[32,128,128]{2,1,0:T(8,128)(2,1)}), bf16[32,128,128]{2,1,0:T(8,128)(2,1)S(1)}, u32[]{:S(2)}, u32[]{:S(2)}) async-start(bf16[32,128,128]{2,1,0:T(8,128)(2,1)} %broadcast_select_fusion), calls=%async_computation | async-start | bytes 2097152 | tf_op jit(solution)/shard_map/all_to_all | solution.py:108
  82.3 110.5 %all-gather.22.cloned.1.call-start = ((), (), s32[]{:S(2)}) async-start(), calls=%async_computation.7 | async-start | bytes 17301504 | tf_op jit(solution)/shard_map/all_gather | solution.py:21
  82.3 17.1 %copy-start.7 = (f32[4,1024]{1,0:T(4,128)S(1)}, f32[4,1024]{1,0:T(4,128)}, u32[]{:S(2)}) copy-start(f32[4,1024]{1,0:T(4,128)} %param.26) | copy-start | bytes 49156
  82.3 17.1 %copy-start.8 = (f32[4,2,128]{2,1,0:T(2,128)S(1)}, f32[4,2,128]{2,1,0:T(2,128)}, u32[]{:S(2)}) copy-start(f32[4,2,128]{2,1,0:T(2,128)} %param.27) | copy-start | bytes 12292
  82.4 17.2 %copy-start.10 = (f32[16]{0:T(128)S(1)}, f32[16]{0:T(128)}, u32[]{:S(2)}) copy-start(f32[16]{0:T(128)} %param.29) | copy-start | bytes 196
  100.3 1.1 copy-start.5
  100.3 1.1 copy-start.11
  101.4 1.6 copy-start.3
  103.0 8.4 %copy-start.2 = (bf16[4096,2,128]{2,1,0:T(2,128)(2,1)S(1)}, bf16[4096,2,128]{2,1,0:T(2,128)(2,1)}, u32[]{:S(2)}) copy-start(bf16[4096,2,128]{2,1,0:T(2,128)(2,1)} %param.24) | copy-start | bytes 6291460
  112.0 3.0 collective-permute-start
  117.4 136.7 %all-gather.16.cloned.1.call-start = ((), (), s32[]{:S(2)}) async-start(), calls=%async_computation.3 | async-start | bytes 8650752 | tf_op jit(solution)/shard_map/all_gather | solution.py:171
  118.2 171.5 %reduce-scatter.2.cloned.1.call-start = ((), (), s32[]{:S(2)}) async-start(), calls=%async_computation.4 | async-start | bytes 2621440 | tf_op jit(solution)/shard_map/reduce_scatter | solution.py:175
  192.8 0.7 copy-start.9
  193.5 60.6 %copy-start.4 = (f32[1024]{0:T(1024)S(1)}, f32[1024]{0:T(1024)}, u32[]{:S(2)}) copy-start(f32[1024]{0:T(1024)} %param.31) | copy-start | bytes 12292
  260.2 30.7 %copy-start.6 = (f32[4096]{0:T(1024)S(1)}, f32[4096]{0:T(1024)}, u32[]{:S(2)}) copy-start(f32[4096]{0:T(1024)} %param.33) | copy-start | bytes 49156
  260.2 31.6 %copy-start.13 = (u32[128]{0:T(128)S(1)}, u32[128]{0:T(128)}, u32[]{:S(2)}) copy-start(u32[128]{0:T(128)} %constant.127) | copy-start | bytes 1540
  260.2 33.0 %copy-start.12 = (s32[32]{0:T(128)S(1)}, s32[32]{0:T(128)}, u32[]{:S(2)}) copy-start(s32[32]{0:T(128)} %param.21) | copy-start | bytes 388
  260.2 79.0 %all-gather.20.cloned.1.call-start = ((), (), s32[]{:S(2)}) async-start(), calls=%async_computation.6 | async-start | bytes 5242880 | tf_op jit(solution)/shard_map/all_gather | solution.py:103
  260.8 134.2 %all-gather.18.cloned.1.call-start = ((), (), s32[]{:S(2)}) async-start(), calls=%async_computation.5 | async-start | bytes 8650752 | tf_op jit(solution)/shard_map/all_gather | solution.py:179
  403.3 123.3 %copy-start.1 = (bf16[4096,16]{0,1:T(8,128)(2,1)S(1)}, bf16[4096,16]{0,1:T(8,128)(2,1)}, u32[]{:S(2)}) copy-start(bf16[4096,16]{0,1:T(8,128)(2,1)} %param.25) | copy-start | bytes 393220
Sparse Core Ops, SparseCore 0:
  9.0 50.6 all-gather.13
  117.5 75.1 all-gather.21
  195.0 59.0 all-gather.15
  260.4 29.2 reduce-scatter.1
  291.2 47.9 all-gather.19
  341.6 53.3 all-gather.17
where the time goes:
time: 537 us; the launch traced here: 533 us
  waiting for transfers between devices  250 us (47%)
  blocking collectives  182 us (34%)
  local copies, waits for them, and re-layouts  36 us (7%)
  matrix products  30 us (6%)
  between operations  14.6 us (3%)
  starting transfers between devices  9.65 us (2%)
  other arithmetic  8.32 us (2%)
    all_gather x5, blocking collectives, combined_all(): everything = jax.tree.map(lambda part: lax.all_gather(part, axis), value)  117 us
    all_gather x1, waiting for transfers between devices, on_device(): lax.all_gather(w_out, 'ctx', axis=1, tiled=True)  58 us
    all_gather x1, waiting for transfers between devices, on_device(): lax.all_gather(normed_out, 'ctx', axis=0, tiled=True)  55.8 us
    all_gather x1, waiting for transfers between devices, entering(): gathered = jax.tree.map(lambda a: lax.all_gather(a, axis), part)  46.6 us
    all_gather x1, waiting for transfers between devices, on_device(): lax.all_gather(embed, 'head', axis=0, tiled=True)  29.5 us
    all_gather x1, waiting for transfers between devices, on_device(): lax.all_gather(lm_head, 'head', axis=0, tiled=True)  29 us
    reduce_scatter x1, waiting for transfers between devices, on_device(): lax.psum_scatter(partial_out, 'head', scatter_dimension=0, tiled=True)  28.8 us
    all_gather x1, blocking collectives, entering(): gathered = jax.tree.map(lambda a: lax.all_gather(a, axis), part)  25.3 us
  transfers between devices with their start and end apart: 8, of which 7 were waited for; matrix products, arithmetic and copies ran while one was open for 5% of the time, Pallas kernels for 0%

commit v1 on v0

v1 whole, which is shorter than its diff:
```python
import jax
import jax.numpy as jnp
from jax import lax
from jax.experimental import pallas as pl
from jax.experimental.pallas import tpu as pltpu
from jax.sharding import PartitionSpec as P

HEAD_DIM = 64
STATE = 128


exact_prec = lax.Precision.HIGHEST


def shift_head(by):
    return "head", [(i, (i + by) % 4) for i in range(4)]


def shift_mixed(first):
    def shift(by):
        pairs = []
        for i in range(32):
            y, z, core = i // 8, (i // 2) % 4, i % 2
            if (core == 0) == first:
                z = (z + by) % 4
            else:
                y = (y + by) % 4
            pairs.append((i, y * 8 + z * 2 + core))
        return "ctx", pairs

    return shift


def swap_core(value):
    return lax.ppermute(value, "ctx", [(i, i ^ 1) for i in range(32)])


def moved(value, shift, by):
    axis, pairs = shift(by)
    return lax.ppermute(value, axis, pairs)


def passed_along(value, axis, by):
    length = lax.axis_size(axis)
    pairs = [(i, i + by) for i in range(length) if 0 <= i + by < length]
    return lax.ppermute(value, axis, pairs)


def ring_gather(value, shift):
    half = value.shape[0] // 2
    left = moved(value, shift, 1)
    right = moved(value, shift, -1)
    far_low = moved(left[:half], shift, 1)
    far_high = moved(right[half:], shift, -1)
    return value, right, jnp.concatenate([far_low, far_high]), left


def ring_reduce(parts, shift):
    own, ahead, far, behind = parts
    half = own.shape[0] // 2
    from_left = moved(far[:half], shift, 1)
    from_right = moved(far[half:], shift, -1)
    ahead = jnp.concatenate([ahead[:half] + from_left, ahead[half:]])
    behind = jnp.concatenate([behind[:half], behind[half:] + from_right])
    left = moved(ahead, shift, 1)
    right = moved(behind, shift, -1)
    f32 = jnp.float32
    return own.astype(f32) + left.astype(f32) + right.astype(f32)


def look_up(ids, table):
    count, (table_rows, cols) = ids.shape[0], table.shape
    depth, block = 512, 1024
    parts = table_rows // depth
    bf16, f32 = jnp.bfloat16, jnp.float32

    def kernel(ids_ref, table_ref, out_ref):
        lane = lax.broadcasted_iota(jnp.int32, (128, 128), 1)
        for r in range(block // 128):
            column = jnp.broadcast_to(ids_ref[0, r : r + 1, :], (128, 128)).T
            low = jnp.bitwise_and(column, depth - 1)
            rest = jnp.right_shift(column, depth.bit_length() - 1)
            picks = [(low == lane + 128 * c).astype(f32).astype(bf16) for c in range(depth // 128)]
            found = jnp.dot(
                jnp.concatenate(picks, axis=1), table_ref[...], preferred_element_type=f32
            )
            chosen = jnp.zeros((128, cols), f32)
            for g in range(parts):
                chosen = jnp.where(rest == g, found[:, g * cols : (g + 1) * cols], chosen)
            out_ref[r * 128 : (r + 1) * 128, :] = chosen.astype(bf16)

    side_by_side = table.reshape(parts, depth, cols).transpose(1, 0, 2).reshape(depth, parts * cols)
    return pl.pallas_call(
        kernel,
        grid=(count // block,),
        in_specs=[
            pl.BlockSpec((1, block // 128, 128), lambda i: (i, 0, 0)),
            pl.BlockSpec((depth, parts * cols), lambda i: (0, 0)),
        ],
        out_specs=pl.BlockSpec((block, cols), lambda i: (i, 0)),
        out_shape=jax.ShapeDtypeStruct((count, cols), bf16),
        compiler_params=pltpu.CompilerParams(vmem_limit_bytes=24 << 20),
        cost_estimate=pl.CostEstimate(
            flops=2 * count * table_rows * cols, bytes_accessed=4 << 20, transcendentals=0
        ),
    )(ids.reshape(count // block, block // 128, 128), side_by_side)


def project(rows, w_zx, w_bc, w_dt):
    count, width = rows.shape
    channels, group_cols, heads = w_zx.shape[2], w_bc.shape[2], w_dt.shape[1]
    depth = 1024
    f32 = jnp.float32

    def kernel(rows_ref, zx_ref, bc_ref, dt_ref, z_out, x_out, bc_out, dt_out):
        @pl.when(pl.program_id(0) == 0)
        def _():
            for out in (z_out, x_out, bc_out, dt_out):
                out[...] = jnp.zeros_like(out)

        part = rows_ref[...]
        zx = zx_ref[...].reshape(depth, 2 * channels)
        z_out[...] += jnp.dot(part, zx[:, :channels], preferred_element_type=f32)
        x_out[...] += jnp.dot(part, zx[:, channels:], preferred_element_type=f32)
        bc = bc_ref[...].reshape(depth, 2 * group_cols)
        bc_out[...] += jnp.dot(part, bc, preferred_element_type=f32)
        dt_out[...] += jnp.dot(part, dt_ref[...], preferred_element_type=f32)

    widths = (channels, channels, 2 * group_cols, heads)
    return pl.pallas_call(
        kernel,
        grid=(width // depth,),
        in_specs=[
            pl.BlockSpec((count, depth), lambda i: (0, i)),
            pl.BlockSpec((depth, 2, channels), lambda i: (i, 0, 0)),
            pl.BlockSpec((depth, 2, group_cols), lambda i: (i, 0, 0)),
            pl.BlockSpec((depth, heads), lambda i: (i, 0)),
        ],
        out_specs=[pl.BlockSpec((count, n), lambda i: (0, 0)) for n in widths],
        out_shape=[jax.ShapeDtypeStruct((count, n), f32) for n in widths],
        compiler_params=pltpu.CompilerParams(vmem_limit_bytes=40 << 20),
        cost_estimate=pl.CostEstimate(
            flops=2 * count * width * sum(widths),
            bytes_accessed=2 * width * sum(widths),
            transcendentals=0,
        ),
    )(rows, w_zx, w_bc, w_dt)


def rms_scale(values, gain):
    return values * lax.rsqrt(jnp.mean(values * values, axis=-1, keepdims=True) + 1e-05) * gain


def join_stats(left_set, right_set):
    peak_left, sum_left, first_left, second_left, target_left = left_set
    peak_right, sum_right, first_right, second_right, target_right = right_set
    row_peak = jnp.maximum(peak_left, peak_right)
    shift_left = peak_left - row_peak
    shift_right = peak_right - row_peak
    weight_left = jnp.exp(shift_left)
    weight_right = jnp.exp(shift_right)
    exp_sum = weight_left * sum_left + weight_right * sum_right
    first_moment = weight_left * (first_left + shift_left * sum_left) + weight_right * (
        first_right + shift_right * sum_right
    )
    second_moment = weight_left * (
        second_left + 2.0 * shift_left * first_left + shift_left * shift_left * sum_left
    ) + weight_right * (
        second_right + 2.0 * shift_right * first_right + shift_right * shift_right * sum_right
    )
    return (row_peak, exp_sum, first_moment, second_moment, target_left + target_right)


def vocab_stats(rows, row_targets, tables):
    logits = jnp.concatenate(
        [jnp.dot(rows, table, preferred_element_type=jnp.float32) for table, _ in tables], axis=1
    )
    vocab_ids = jnp.concatenate([ids for _, ids in tables])
    row_peak = jnp.max(logits, axis=1)
    shifted = logits - row_peak[:, None]
    weights = jnp.exp(shifted)
    is_target = row_targets[:, None] == vocab_ids[None, :]
    return jnp.stack(
        [
            row_peak,
            jnp.sum(weights, axis=1),
            jnp.sum(weights * shifted, axis=1),
            jnp.sum(weights * shifted * shifted, axis=1),
            jnp.sum(jnp.where(is_target, logits, 0.0), axis=1),
        ]
    )


def on_device(
    token_ids,
    targets,
    embed,
    w_zx,
    w_bc,
    w_dt,
    conv_x,
    conv_bc,
    dt_bias,
    a_log,
    d_skip,
    norm_gain,
    pre_gain,
    final_gain,
    w_out,
    lm_head,
):
    bf16, f32 = jnp.bfloat16, jnp.float32
    ctx_count = lax.axis_size("ctx")
    head_count = lax.axis_size("head")
    tok_rows = token_ids.shape[0]
    quarter = tok_rows // head_count
    model_width = pre_gain.shape[0]
    head_pos = lax.axis_index("head")
    ctx_pos = lax.axis_index("ctx")
    w_out_full = lax.all_gather(w_out, "ctx", axis=1, tiled=True)

    packed = jnp.concatenate([token_ids, targets])
    packed = jnp.broadcast_to(packed[None], (ctx_count, tok_rows + quarter))
    packed = lax.all_to_all(packed, "ctx", 0, 0, tiled=True)
    all_ids = packed[:, :tok_rows].reshape(ctx_count, head_count, quarter)
    group_targets = packed[:, tok_rows:]

    table_rows, slice_cols = embed.shape
    by_owner = jnp.roll(all_ids, -head_pos, axis=1).transpose(1, 0, 2)
    local_ids = by_owner.reshape(-1) - head_pos * table_rows
    looked = look_up(local_ids, embed)
    looked = looked.reshape(head_count, ctx_count * quarter, slice_cols)
    mine = ring_reduce([looked[k] for k in range(4)], shift_head).astype(bf16)
    mine = mine.reshape(ctx_count, quarter, slice_cols)
    own_emb = lax.all_to_all(mine, "ctx", split_axis=0, concat_axis=2, tiled=True)
    own_emb = own_emb.reshape(quarter, model_width)
    normed_own = rms_scale(own_emb.astype(f32), pre_gain).astype(bf16)
    normed_in = jnp.zeros((tok_rows, model_width), bf16)
    for ahead, block in enumerate(ring_gather(normed_own, shift_head)):
        row = ((head_pos + ahead) % head_count) * quarter
        normed_in = lax.dynamic_update_slice_in_dim(normed_in, block, row, 0)

    normed_in, lm_head = lax.optimization_barrier((normed_in, lm_head))
    vocab_own = lax.all_gather(lm_head, "head", axis=0, tiled=True)
    vocab_other = swap_core(vocab_own)

    channels = w_zx.shape[2]
    group_cols = w_bc.shape[2]
    gate_z, proj_x, proj_bc, step_raw = project(normed_in, w_zx, w_bc, w_dt)
    mixed_in = jnp.concatenate([proj_x, proj_bc], axis=1)
    conv_taps = conv_x.shape[0]
    rim_rows = passed_along(mixed_in[tok_rows - conv_taps + 1 :], "ctx", 1)
    kernel = jnp.concatenate([conv_x, conv_bc.reshape(conv_taps, 2 * group_cols)], axis=1)
    extended = jnp.concatenate([rim_rows, mixed_in], axis=0)
    convolved = jnp.zeros_like(mixed_in)
    for offset in range(conv_taps):
        convolved = convolved + kernel[offset] * extended[offset : offset + tok_rows]
    activated = jax.nn.silu(convolved)
    heads = step_raw.shape[1]
    x_heads = activated[:, :channels].reshape(tok_rows, heads, HEAD_DIM)
    b_act = activated[:, channels : channels + group_cols]
    c_act = activated[:, channels + group_cols :]
    step_size = jax.nn.softplus(step_raw + dt_bias)
    log_rate = -jnp.exp(a_log) * step_size
    positions = jnp.arange(tok_rows)
    causal = positions[:, None] >= positions[None, :]
    log_decay = jnp.dot(causal.astype(f32), log_rate, precision=exact_prec)
    log_total = log_decay[-1]

    tail_decay = jnp.exp(log_total[None, :] - log_decay) * step_size
    end_state = jnp.einsum("sh,shp,sn->hpn", tail_decay, x_heads, b_act, precision=exact_prec)
    part_rows = heads * HEAD_DIM // ctx_count
    slices = end_state.astype(bf16).reshape(ctx_count, part_rows, STATE)
    first = log_total.astype(bf16)
    second = (log_total - first.astype(f32)).astype(bf16)
    third = (log_total - first.astype(f32) - second.astype(f32)).astype(bf16)
    totals = jnp.repeat(jnp.stack([first, second, third], axis=1), ctx_count // heads, axis=0)
    totals = jnp.broadcast_to(totals[:, :, None], (ctx_count, 3, STATE))
    totals = jnp.concatenate([totals, jnp.zeros((ctx_count, 13, STATE), bf16)], axis=1)
    message = jnp.concatenate([slices, totals], axis=1)
    arrived = lax.all_to_all(message, "ctx", 0, 0, tiled=True)
    block_logs = jnp.sum(arrived[:, part_rows : part_rows + 3, 0].astype(f32), axis=1)
    blocks = jnp.arange(ctx_count)
    earlier = blocks[:, None] > blocks[None, :]
    upto = jnp.sum(jnp.where(blocks[:, None] >= blocks[None, :], block_logs[None, :], 0.0), axis=1)
    gap = (upto - block_logs)[:, None] - upto[None, :]
    weigh = jnp.exp(jnp.where(earlier, gap, -jnp.inf))
    parts = arrived[:, :part_rows].astype(f32).reshape(ctx_count, part_rows * STATE)
    entering = jnp.dot(weigh, parts, precision=exact_prec).astype(bf16)
    entering = entering.reshape(ctx_count, part_rows, STATE)
    state_in = lax.all_to_all(entering, "ctx", 0, 0, tiled=True)
    state_in = state_in.reshape(heads, HEAD_DIM, STATE).astype(f32)

    decay_gap = log_decay.T[:, :, None] - log_decay.T[:, None, :]
    decay_mask = jnp.exp(jnp.where(causal[None], decay_gap, -jnp.inf))
    scores = jnp.einsum("tn,sn->ts", c_act, b_act, precision=exact_prec)
    mixing = scores[None] * decay_mask * step_size.T[:, None, :]
    y_local = jnp.einsum("hts,shp->thp", mixing, x_heads, precision=exact_prec)
    y_carry = (
        jnp.einsum("tn,hpn->thp", c_act, state_in, precision=exact_prec)
        * jnp.exp(log_decay)[:, :, None]
    )
    mixer_out = y_local + y_carry + d_skip[None, :, None] * x_heads
    gated_raw = mixer_out.reshape(tok_rows, channels) * jax.nn.silu(gate_z)
    gated_out = rms_scale(gated_raw, norm_gain).astype(bf16)

    partial_out = jnp.dot(gated_out, w_out_full, preferred_element_type=f32).astype(bf16)
    partial_out = partial_out.reshape(head_count, quarter, model_width)
    by_owner_out = jnp.roll(partial_out, -head_pos, axis=0)
    summed_out = ring_reduce([by_owner_out[k] for k in range(4)], shift_head)
    residual = (own_emb.astype(f32) + summed_out).astype(bf16)
    normed_out = rms_scale(residual.astype(f32), final_gain).astype(bf16)

    along_first, along_second = shift_mixed(True), shift_mixed(False)
    first_rows = jnp.stack(ring_gather(normed_out, along_first))
    all_rows = ring_gather(first_rows, along_second)
    y_pos, z_pos, core = ctx_pos // 8, (ctx_pos // 2) % 4, ctx_pos % 2
    by_chip = lax.dynamic_index_in_dim(group_targets.reshape(4, 4, 2, quarter), core, 2, False)
    by_chip = jnp.roll(by_chip, (-y_pos, -z_pos), (0, 1))
    by_chip = jnp.where(core == 0, by_chip, by_chip.transpose(1, 0, 2))
    vocab_width = vocab_own.shape[1]
    columns = jnp.arange(vocab_width, dtype=jnp.int32)
    tables = [
        (vocab_own, ctx_pos * vocab_width + columns),
        (vocab_other, (ctx_pos ^ 1) * vocab_width + columns),
    ]
    all_stats = [None] * 4
    for group in ((0,), (1, 3), (2,)):
        rows = jnp.concatenate([all_rows[k].reshape(-1, model_width) for k in group])
        wanted = jnp.concatenate([by_chip[k].reshape(-1) for k in group])
        stats = vocab_stats(rows, wanted, tables).reshape(5, len(group), 4, quarter)
        for place, k in enumerate(group):
            all_stats[k] = stats[:, place]
    merged = tuple(all_stats[0])
    for ahead in range(1, 4):
        merged = join_stats(merged, tuple(moved(all_stats[ahead], along_second, ahead)))
    both = jnp.stack(merged)
    merged = tuple(both[:, 0])
    for ahead in range(1, 4):
        merged = join_stats(merged, tuple(moved(both[:, ahead], along_first, ahead)))
    row_peak, exp_sum, first_moment, second_moment, target_logit = merged
    mean_shift = first_moment / exp_sum
    spread = second_moment / exp_sum - mean_shift * mean_shift
    return (target_logit - row_peak - mean_shift) * lax.rsqrt(jnp.maximum(spread, 0.25))


def solution(mesh):
    placed = (
        P("ctx"),
        P(("ctx", "head")),
        P("head", "ctx"),
        P(None, None, "head"),
        P(None, None, "head"),
        P(None, "head"),
        P(None, "head"),
        P(None, None, "head"),
        P("head"),
        P("head"),
        P("head"),
        P("head"),
        P(),
        P(),
        P("head", "ctx"),
        P("head", "ctx"),
    )
    return jax.shard_map(
        on_device, mesh=mesh, in_specs=placed, out_specs=P(("ctx", "head")), check_vma=False
    )
```

time: 537 us -> 246 us (0.46)
  blocking collectives: 182 us -> 0 us
  waiting for transfers between devices: 250 us -> 103 us
  starting transfers between devices: 9.65 us -> 67.3 us
  local copies, waits for them, and re-layouts: 36 us -> 11.7 us
  Pallas kernels: 0 us -> 14.8 us
    all_gather x5 -> x2, waiting for transfers between devices: 219 us -> 10.5 us  [the longest x1 10.5 us: on_device(): vocab_own = lax.all_gather(lm_head, 'head', axis=0, tiled=True)]
    all_gather x7 -> x0, blocking collectives: 165 us -> none  [the longest x5 117 us: combined_all(): everything = jax.tree.map(lambda part: lax.all_gather(part, axis), value)]
    ppermute x0 -> x27, waiting for transfers between devices: none -> 56.6 us  [the longest x26 56.6 us: moved(): return lax.ppermute(value, axis, pairs)]
    ppermute x0 -> x27, starting transfers between devices: none -> 41.9 us  [the longest x26 41.9 us: moved(): return lax.ppermute(value, axis, pairs)]
    all_to_all x1 -> x4, waiting for transfers between devices: 0.01 us -> 33.8 us  [the longest x1 10.8 us: on_device(): lax.all_to_all(mine, 'ctx', split_axis=0, concat_axis=2, tiled=True)]
    reduce_scatter x1 -> x0, waiting for transfers between devices: 28.8 us -> none  [on_device(): lax.psum_scatter(partial_out, 'head', scatter_dimension=0, tiled=True)]
    unnamed x1 -> x0, blocking collectives: 16.8 us -> none
    all_to_all x1 -> x4, starting transfers between devices: 7.27 us -> 24 us  [the longest x1 8.41 us: on_device(): packed = lax.all_to_all(packed, 'ctx', 0, 0, tiled=True)]
  transfers between devices with their start and end apart: 8 -> 34, of which waited for: 7 -> 21; matrix products, arithmetic and copies ran while one was open for 5% -> 18% of each run, Pallas kernels for 0% -> 6%
where the time goes in v1:
time: 246 us; the launch traced here: 245 us
  waiting for transfers between devices  103 us (42%)
  starting transfers between devices  67.3 us (27%)
  matrix products  25.9 us (11%)
  Pallas kernels  14.8 us (6%)
  between operations  14.3 us (6%)
  local copies, waits for them, and re-layouts  11.7 us (5%)
  other arithmetic  8.65 us (4%)
    ppermute x26, waiting for transfers between devices, moved(): return lax.ppermute(value, axis, pairs)  56.6 us
    ppermute x26, starting transfers between devices, moved(): return lax.ppermute(value, axis, pairs)  41.9 us
    dot_general x6, matrix products, vocab_stats(): jnp.dot(rows, table, preferred_element_type=jnp.float32)  17 us
    all_to_all x1, waiting for transfers between devices, on_device(): lax.all_to_all(mine, 'ctx', split_axis=0, concat_axis=2, tiled=True)  10.8 us
    all_gather x1, waiting for transfers between devices, on_device(): vocab_own = lax.all_gather(lm_head, 'head', axis=0, tiled=True)  10.5 us
    pallas_call x1, Pallas kernels, project(): pl.pallas_call(kernel, grid=(width // depth,), in_specs=[pl.BlockSpec((co...  9.48 us
    all_to_all x1, waiting for transfers between devices, on_device(): arrived = lax.all_to_all(message, 'ctx', 0, 0, tiled=True)  9.18 us
    all_to_all x1, waiting for transfers between devices, on_device(): state_in = lax.all_to_all(entering, 'ctx', 0, 0, tiled=True)  8.58 us
  transfers between devices with their start and end apart: 34, of which 21 were waited for; matrix products, arithmetic and copies ran while one was open for 18% of the time, Pallas kernels for 6%

profile of v1, /device:TPU:0, one launch (start us, length us, event | category | flops | bytes accessed | tf_op | source)
XLA Modules:
  0.0 245.3 jit_solution(3979250594259713060)
XLA Ops:
  6.5 0.7 all-gather.3.cloned.1.call-update
  7.3 0.7 pad_add_fusion.1
  7.9 0.6 broadcast_in_dim.47
  8.6 8.4 %all-to-all-start = ((s32[32,1,160]{2,1,0:T(1,128)}), s32[32,1,160]{2,1,0:T(1,128)S(1)}, u32[]{:S(2)}, u32[]{:S(2)}) async-start(s32[32,1,160]{2,1,0:T(1,128)} %broadcast_in_dim.47), calls=%async_computation | async-start | bytes 65536 | tf_op jit(solution)/shard_map/all_to_all | solution.py:224
  17.0 1.9 copy.75
  19.2 5.2 %all-to-all-done = s32[32,1,160]{2,1,0:T(1,128)S(1)} async-done(((s32[32,1,160]{2,1,0:T(1,128)}), s32[32,1,160]{2,1,0:T(1,128)S(1)}, u32[]{:S(2)}, u32[]{:S(2)}) %all-to-all-start) | async-done | bytes 20512 | tf_op jit(solution)/shard_map/all_to_all | solution.py:224
  24.7 5.3 %shard_map.154 = bf16[4096,128]{1,0:T(8,128)(2,1)S(1)} custom-call(s32[4,8,128]{2,1,0:T(8,128)S(1)} %sub.197.ids_ref, bf16[512,1024]{1,0:T(8,128)(2,1)S(1)} %bitcast.345), custom_call_target="tpu_custom_call" | custom-call | flops 4294967296 | bytes 4194304 | tf_op jit(solution)/shard_map/pallas_call | solution.py:93
  30.1 1.6 collective-permute-start
  31.7 5.2 %collective-permute-done = bf16[512,128]{1,0:T(8,128)(2,1)S(1)} collective-permute-done((bf16[512,128]{1,0:T(8,128)(2,1)S(1)}, bf16[512,128]{1,0:T(8,128)(2,1)S(1)}, u32[]{:S(2)}, u32[]{:S(2)}) %collective-permute-start) | collective-permute-done | bytes 131104 | tf_op jit(solution)/shard_map/ppermute | solution.py:40
  36.9 1.6 collective-permute-start.2
  39.1 2.8 %collective-permute-done.2 = bf16[512,128]{1,0:T(8,128)(2,1)S(1)} collective-permute-done((bf16[512,128]{1,0:T(8,128)(2,1)S(1)}, bf16[512,128]{1,0:T(8,128)(2,1)S(1)}, u32[]{:S(2)}, u32[]{:S(2)}) %collective-permute-start.2) | collective-permute-done | bytes 131104 | tf_op jit(solution)/shard_map/ppermute | solution.py:40
  42.0 2.8 %collective-permute-start.3 = (bf16[1024,128]{1,0:T(8,128)(2,1)S(1)}, bf16[1024,128]{1,0:T(8,128)(2,1)S(1)}, u32[]{:S(2)}, u32[]{:S(2)}) collective-permute-start(bf16[1024,128]{1,0:T(8,128)(2,1)S(1)} %pad_maximum_fusion.10), channel_id=1, source_target_pairs={{0,3},{1,0},{2,1},{3,2},{4,7},{5,4},{6,5},{7,6},{8,11},{9,8},{10,9... | collective-permute-start | bytes 786440 | tf_op jit(solution)/shard_map/ppermute | solution.py:40
  44.9 2.2 collective-permute-done.1
  47.1 1.7 collective-permute-done.3
  48.8 0.8 add_convert_fusion
  49.6 3.9 %all-to-all-start.1 = ((bf16[32,32,128]{2,1,0:T(8,128)(2,1)}), bf16[32,32,128]{2,1,0:T(8,128)(2,1)S(1)}, u32[]{:S(2)}, u32[]{:S(2)}) async-start(bf16[32,32,128]{2,1,0:T(8,128)(2,1)} %bitcast.6), calls=%async_computation.1 | async-start | bytes 524288 | tf_op jit(solution)/shard_map/all_to_all | solution.py:235
  53.5 10.8 %all-to-all-done.1 = bf16[32,32,128]{2,1,0:T(8,128)(2,1)S(1)} async-done(((bf16[32,32,128]{2,1,0:T(8,128)(2,1)}), bf16[32,32,128]{2,1,0:T(8,128)(2,1)S(1)}, u32[]{:S(2)}, u32[]{:S(2)}) %all-to-all-start.1) | async-done | bytes 262176 | tf_op jit(solution)/shard_map/all_to_all | solution.py:235
  65.5 3.2 %collective-permute-start.4 = (bf16[32,4096]{1,0:T(8,128)(2,1)S(1)}, bf16[32,4096]{1,0:T(8,128)(2,1)S(1)}, u32[]{:S(2)}, u32[]{:S(2)}) collective-permute-start(bf16[32,4096]{1,0:T(8,128)(2,1)S(1)} %get-tuple-element.46), channel_id=1, source_target_pairs={{0,3},{1,0},{2,1},{3,2},{4,7},{5,4},{6,5},{7,6},{8,11},{9,8},{10,9... | collective-permute-start | bytes 786440 | tf_op jit(solution)/shard_map/ppermute | solution.py:40
  69.4 9.5 %collective-permute-done.5 = bf16[32,4096]{1,0:T(8,128)(2,1)S(1)} collective-permute-done((bf16[32,4096]{1,0:T(8,128)(2,1)S(1)}, bf16[32,4096]{1,0:T(8,128)(2,1)S(1)}, u32[]{:S(2)}, u32[]{:S(2)}) %collective-permute-start.5) | collective-permute-done | bytes 262176 | tf_op jit(solution)/shard_map/ppermute | solution.py:40
  79.1 3.3 %collective-permute-start.7 = (bf16[16,4096]{1,0:T(8,128)(2,1)S(1)}, bf16[16,4096]{1,0:T(8,128)(2,1)S(1)}, u32[]{:S(2)}, u32[]{:S(2)}) collective-permute-start(bf16[16,4096]{1,0:T(8,128)(2,1)S(1)} %slice.262), channel_id=1, source_target_pairs={{0,3},{1,0},{2,1},{3,2},{4,7},{5,4},{6,5},{7,6},{8,11},{9,8},{10,9... | collective-permute-start | bytes 393224 | tf_op jit(solution)/shard_map/ppermute | solution.py:40
  82.4 3.2 %collective-permute-done.6 = bf16[16,4096]{1,0:T(8,128)(2,1)S(1)} collective-permute-done((bf16[16,4096]{1,0:T(8,128)(2,1)S(1)}, bf16[16,4096]{1,0:T(8,128)(2,1)S(1)}, u32[]{:S(2)}, u32[]{:S(2)}) %collective-permute-start.6) | collective-permute-done | bytes 131104 | tf_op jit(solution)/shard_map/ppermute | solution.py:40
  85.7 1.6 copy-done
  87.3 9.5 %shard_map.155 = (f32[128,1024]{1,0:T(8,128)S(1)}, f32[128,1024]{1,0:T(8,128)S(1)}, f32[128,256]{1,0:T(8,128)S(1)}, f32[128,16]{1,0:T(8,128)S(1)}) custom-call(bf16[128,4096]{1,0:T(8,128)(2,1)S(1)} %constant_dynamic-update-slice_fusion.19.rows_ref, bf16[4096,2,1024]{2,1,0:T(2,128)(2,1)} %zx_ref.1, bf16[4096,2,128]{2,1,0:T(2,128)(2,1)S(1)} %copy-done, ...), custom_call_target="tpu_custom_call" | custom-call | flops 2432696320 | bytes 19005440 | tf_op jit(solution)/shard_map/pallas_call | solution.py:130
  97.2 1.3 collective-permute-start.8
  100.7 0.9 maximum_maximum_fusion
  101.6 7.8 %all-to-all-start.2 = ((bf16[32,48,128]{2,1,0:T(8,128)(2,1)}), bf16[32,48,128]{2,1,0:T(8,128)(2,1)S(1)}, u32[]{:S(2)}, u32[]{:S(2)}) async-start(bf16[32,48,128]{2,1,0:T(8,128)(2,1)} %maximum_maximum_fusion), calls=%async_computation.2 | async-start | bytes 786432 | tf_op jit(solution)/shard_map/all_to_all | solution.py:281
  109.5 0.7 all-gather.5.cloned.1.call-update
  110.2 9.2 %all-to-all-done.2 = bf16[32,48,128]{2,1,0:T(8,128)(2,1)S(1)} async-done(((bf16[32,48,128]{2,1,0:T(8,128)(2,1)}), bf16[32,48,128]{2,1,0:T(8,128)(2,1)S(1)}, u32[]{:S(2)}, u32[]{:S(2)}) %all-to-all-start.2) | async-done | bytes 393248 | tf_op jit(solution)/shard_map/all_to_all | solution.py:281
  120.3 0.8 copy.95
  121.1 3.9 %all-to-all-start.3 = ((bf16[32,32,128]{2,1,0:T(8,128)(2,1)}), bf16[32,32,128]{2,1,0:T(8,128)(2,1)S(1)}, u32[]{:S(2)}, u32[]{:S(2)}) async-start(bf16[32,32,128]{2,1,0:T(8,128)(2,1)} %bitcast.74), calls=%async_computation.3 | async-start | bytes 524288 | tf_op jit(solution)/shard_map/all_to_all | solution.py:291
  125.3 8.6 %all-to-all-done.3 = bf16[32,32,128]{2,1,0:T(8,128)(2,1)S(1)} async-done(((bf16[32,32,128]{2,1,0:T(8,128)(2,1)}), bf16[32,32,128]{2,1,0:T(8,128)(2,1)S(1)}, u32[]{:S(2)}, u32[]{:S(2)}) %all-to-all-start.3) | async-done | bytes 262176 | tf_op jit(solution)/shard_map/all_to_all | solution.py:291
  134.3 2.2 fusion.5
  137.0 4.9 %convolution_convert_fusion = bf16[128,4096]{1,0:T(8,128)(2,1)S(1)} fusion(bf16[1024,4096]{1,0:T(8,128)(2,1)} %all-gather.3.cloned.1.call-done, f32[1024]{0:T(1024)S(1)} %copy-done.11, f32[128]{0:T(128)S(1)} %add_rsqrt_fusion.1, f32[128,1024]{1,0:T(8,128)S(1)} %copy.84, f32[128,1024]{1,0:T(8,128)S(1)} %get-tuple-element.15), kind=kOutput, calls=%fused_computation | convolution fusion | flops 1075314688 | bytes 10490368 | tf_op jit(solution)/shard_map/dot_general | solution.py:307
  142.4 3.3 %collective-permute-start.11 = (bf16[16,4096]{1,0:T(8,128)(2,1)S(1)}, bf16[16,4096]{1,0:T(8,128)(2,1)S(1)}, u32[]{:S(2)}, u32[]{:S(2)}) collective-permute-start(bf16[16,4096]{1,0:T(8,128)(2,1)S(1)} %get-tuple-element.52), channel_id=1, source_target_pairs={{0,3},{1,0},{2,1},{3,2},{4,7},{5,4},{6,5},{7,6},{8,11},{9,8},{10,9... | collective-permute-start | bytes 393224 | tf_op jit(solution)/shard_map/ppermute | solution.py:40
  145.6 6.4 %collective-permute-done.11 = bf16[16,4096]{1,0:T(8,128)(2,1)S(1)} collective-permute-done((bf16[16,4096]{1,0:T(8,128)(2,1)S(1)}, bf16[16,4096]{1,0:T(8,128)(2,1)S(1)}, u32[]{:S(2)}, u32[]{:S(2)}) %collective-permute-start.11) | collective-permute-done | bytes 131104 | tf_op jit(solution)/shard_map/ppermute | solution.py:40
  152.1 3.6 %collective-permute-done.9 = bf16[16,4096]{1,0:T(8,128)(2,1)S(1)} collective-permute-done((bf16[16,4096]{1,0:T(8,128)(2,1)S(1)}, bf16[16,4096]{1,0:T(8,128)(2,1)S(1)}, u32[]{:S(2)}, u32[]{:S(2)}) %collective-permute-start.9) | collective-permute-done | bytes 131104 | tf_op jit(solution)/shard_map/ppermute | solution.py:40
  155.8 3.3 %collective-permute-start.12 = (bf16[32,4096]{1,0:T(8,128)(2,1)S(1)}, bf16[32,4096]{1,0:T(8,128)(2,1)S(1)}, u32[]{:S(2)}, u32[]{:S(2)}) collective-permute-start(bf16[32,4096]{1,0:T(8,128)(2,1)S(1)} %pad_maximum_fusion.12), channel_id=1, source_target_pairs={{0,3},{1,0},{2,1},{3,2},{4,7},{5,4},{6,5},{7,6},{8,11},{9,8},{10,9... | collective-permute-start | bytes 786440 | tf_op jit(solution)/shard_map/ppermute | solution.py:40
  159.2 10.5 %all-gather.5.cloned.1.call-done = bf16[4096,512]{1,0:T(8,128)(2,1)} async-done(((bf16[1024,512]{1,0:T(8,128)(2,1)}), bf16[4096,512]{1,0:T(8,128)(2,1)}) %all-gather.5.cloned.1.call-update) | async-done | bytes 4194320 | tf_op jit(solution)/shard_map/all_gather | solution.py:244
  170.5 2.0 collective-permute-start.14
  172.5 1.5 collective-permute-start.13
  174.0 4.2 %collective-permute-done.14 = bf16[32,4096]{1,0:T(8,128)(2,1)S(1)} collective-permute-done((bf16[32,4096]{1,0:T(8,128)(2,1)S(1)}, bf16[32,4096]{1,0:T(8,128)(2,1)S(1)}, u32[]{:S(2)}, u32[]{:S(2)}) %collective-permute-start.14) | collective-permute-done | bytes 262176 | tf_op jit(solution)/shard_map/ppermute | solution.py:40
  178.3 0.7 collective-permute-start.15
  179.0 2.7 %collective-permute-start.16 = (bf16[16,4096]{1,0:T(8,128)(2,1)S(1)}, bf16[16,4096]{1,0:T(8,128)(2,1)S(1)}, u32[]{:S(2)}, u32[]{:S(2)}) collective-permute-start(bf16[16,4096]{1,0:T(8,128)(2,1)S(1)} %slice.285), channel_id=1, source_target_pairs={{0,24},{4,100},{8,0},{12,108},{16,8},{20,116},{24,16},{28,124},{32... | collective-permute-start | bytes 393224 | tf_op jit(solution)/shard_map/ppermute | solution.py:40
  181.8 2.7 %collective-permute-done.15 = bf16[16,4096]{1,0:T(8,128)(2,1)S(1)} collective-permute-done((bf16[16,4096]{1,0:T(8,128)(2,1)S(1)}, bf16[16,4096]{1,0:T(8,128)(2,1)S(1)}, u32[]{:S(2)}, u32[]{:S(2)}) %collective-permute-start.15) | collective-permute-done | bytes 131104 | tf_op jit(solution)/shard_map/ppermute | solution.py:40
  184.7 1.8 collective-permute-start.19
  186.4 1.6 collective-permute-start.18
  188.3 3.0 %fusion.132 = (f32[128]{0:T(128)S(1)}, f32[128,512]{1,0:T(8,128)S(1)}) fusion(bf16[128,4096]{1,0:T(8,128)(2,1)S(1)} %bitcast.346, bf16[4096,512]{1,0:T(8,128)(2,1)} %all-gather.5.cloned.1.call-done), kind=kOutput, calls=%fused_computation.296 | convolution fusion | flops 536936320 | bytes 5505536 | tf_op jit(solution)/shard_map/dot_general | solution.py:176
  191.3 3.0 %fusion.133 = (f32[128]{0:T(128)S(1)}, f32[128,512]{1,0:T(8,128)S(1)}) fusion(bf16[128,4096]{1,0:T(8,128)(2,1)S(1)} %bitcast.347, bf16[4096,512]{1,0:T(8,128)(2,1)} %collective-permute-done.17), kind=kOutput, calls=%fused_computation.297 | convolution fusion | flops 536936320 | bytes 5505536 | tf_op jit(solution)/shard_map/dot_general | solution.py:176
  194.3 6.5 %collective-permute-done.19 = bf16[4,32,4096]{2,1,0:T(8,128)(2,1)} collective-permute-done((bf16[4,32,4096]{2,1,0:T(8,128)(2,1)S(1)}, bf16[4,32,4096]{2,1,0:T(8,128)(2,1)}, u32[]{:S(2)}, u32[]{:S(2)}) %collective-permute-start.19) | collective-permute-done | bytes 1048608 | tf_op jit(solution)/shard_map/ppermute | solution.py:40
  200.9 1.1 slice.289
  201.9 0.8 collective-permute-start.21
  202.7 1.1 slice.290
  203.8 2.8 %collective-permute-start.22 = (bf16[2,32,4096]{2,1,0:T(8,128)(2,1)S(1)}, bf16[2,32,4096]{2,1,0:T(8,128)(2,1)}, u32[]{:S(2)}, u32[]{:S(2)}) collective-permute-start(bf16[2,32,4096]{2,1,0:T(8,128)(2,1)S(1)} %slice.290), channel_id=1, source_target_pairs={{0,96},{4,28},{8,104},{12,4},{16,112},{20,12},{24,120},{28,20},{32... | collective-permute-start | bytes 1572872 | tf_op jit(solution)/shard_map/ppermute | solution.py:40
  206.6 4.3 %fusion.129 = (f32[256]{0:T(256)S(1)}, f32[256,512]{1,0:T(8,128)S(1)}) fusion(bf16[4096,512]{1,0:T(8,128)(2,1)} %collective-permute-done.17, bf16[128,4096]{1,0:T(8,128)(2,1)} %bitcast.33, bf16[128,4096]{1,0:T(8,128)(2,1)} %bitcast.32), kind=kOutput, calls=%fused_computation.293 | convolution fusion | flops 1078066944 | bytes 6816768 | tf_op jit(solution)/shard_map/dot_general | solution.py:176
  210.9 2.9 %fusion.128 = (f32[256]{0:T(256)S(1)}, f32[256,512]{1,0:T(8,128)S(1)}) fusion(bf16[4096,512]{1,0:T(8,128)(2,1)S(1)} %copy-done.1, bf16[128,4096]{1,0:T(8,128)(2,1)} %bitcast.33, bf16[128,4096]{1,0:T(8,128)(2,1)} %bitcast.32), kind=kOutput, calls=%fused_computation.292 | convolution fusion | flops 1078066944 | bytes 6816768 | tf_op jit(solution)/shard_map/dot_general | solution.py:176
  214.9 3.2 %collective-permute-start.24 = (f32[5,4,32]{2,1,0:T(4,128)S(1)}, f32[5,4,32]{2,1,0:T(4,128)S(1)}, u32[]{:S(2)}, u32[]{:S(2)}) collective-permute-start(f32[5,4,32]{2,1,0:T(4,128)S(1)} %get-tuple-element.60), channel_id=1, source_target_pairs={{0,96},{4,28},{8,104},{12,4},{16,112},{20,12},{24,120},{28,20},{32... | collective-permute-start | bytes 7688 | tf_op jit(solution)/shard_map/ppermute | solution.py:40
  218.1 1.1 pad_maximum_fusion.5
  219.3 3.0 %fusion.131 = (f32[128]{0:T(128)S(1)}, f32[128,512]{1,0:T(8,128)S(1)}) fusion(bf16[128,4096]{1,0:T(8,128)(2,1)S(1)} %bitcast.348, bf16[4096,512]{1,0:T(8,128)(2,1)} %collective-permute-done.17), kind=kOutput, calls=%fused_computation.295 | convolution fusion | flops 536936320 | bytes 5505536 | tf_op jit(solution)/shard_map/dot_general | solution.py:176
  222.3 0.8 fusion.130
  224.6 4.7 %collective-permute-done.23 = f32[5,4,32]{2,1,0:T(4,128)S(1)} collective-permute-done((f32[5,4,32]{2,1,0:T(4,128)S(1)}, f32[5,4,32]{2,1,0:T(4,128)S(1)}, u32[]{:S(2)}, u32[]{:S(2)}) %collective-permute-start.23) | collective-permute-done | bytes 2592 | tf_op jit(solution)/shard_map/ppermute | solution.py:40
  229.5 1.2 collective-permute-start.25
  230.7 3.7 %collective-permute-start.26 = (f32[5,32]{1,0:T(8,128)S(1)}, f32[5,32]{1,0:T(8,128)S(1)}, u32[]{:S(2)}, u32[]{:S(2)}) collective-permute-start(f32[5,32]{1,0:T(8,128)S(1)} %bitcast.371), channel_id=1, source_target_pairs={{0,16},{4,68},{8,24},{12,76},{16,0},{20,84},{24,8},{28,92},{32,48}... | collective-permute-start | bytes 1928 | tf_op jit(solution)/shard_map/ppermute | solution.py:40
  234.6 1.4 collective-permute-done.26
  236.0 2.0 collective-permute-done.27
  (180 shorter events, 13.4 us)
Async XLA Ops:
  6.5 130.5 %all-gather.3.cloned.1.call-start = ((), (), s32[]{:S(2)}) async-start(), calls=%async_computation.4 | async-start | bytes 8650752 | tf_op jit(solution)/shard_map/all_gather | solution.py:220
  8.6 15.9 %all-to-all-start = ((s32[32,1,160]{2,1,0:T(1,128)}), s32[32,1,160]{2,1,0:T(1,128)S(1)}, u32[]{:S(2)}, u32[]{:S(2)}) async-start(s32[32,1,160]{2,1,0:T(1,128)} %broadcast_in_dim.47), calls=%async_computation | async-start | bytes 65536 | tf_op jit(solution)/shard_map/all_to_all | solution.py:224
  30.0 23.4 %copy-start.8 = (f32[4,1024]{1,0:T(4,128)S(1)}, f32[4,1024]{1,0:T(4,128)}, u32[]{:S(2)}) copy-start(f32[4,1024]{1,0:T(4,128)} %param.22) | copy-start | bytes 49156
  30.1 23.4 %copy-start.9 = (f32[4,2,128]{2,1,0:T(2,128)S(1)}, f32[4,2,128]{2,1,0:T(2,128)}, u32[]{:S(2)}) copy-start(f32[4,2,128]{2,1,0:T(2,128)} %param.23) | copy-start | bytes 12292
  30.1 34.9 %copy-start.7 = (f32[4096]{0:T(1024)S(1)}, f32[4096]{0:T(1024)}, u32[]{:S(2)}) copy-start(f32[4096]{0:T(1024)} %param.28) | copy-start | bytes 49156
  30.1 38.7 %copy-start.5 = (bf16[4096,16]{0,1:T(8,128)(2,1)S(1)}, bf16[4096,16]{0,1:T(8,128)(2,1)}, u32[]{:S(2)}) copy-start(bf16[4096,16]{0,1:T(8,128)(2,1)} %param.21) | copy-start | bytes 393220
  30.1 6.8 %collective-permute-start = (bf16[512,128]{1,0:T(8,128)(2,1)S(1)}, bf16[512,128]{1,0:T(8,128)(2,1)S(1)}, u32[]{:S(2)}, u32[]{:S(2)}) collective-permute-start(bf16[512,128]{1,0:T(8,128)(2,1)S(1)} %slice.255), channel_id=1, source_target_pairs={{0,1},{1,2},{2,3},{3,0},{4,5},{5,6},{6,7},{7,4},{8,9},{9,10},{10,1... | collective-permute-start | bytes 393224 | tf_op jit(solution)/shard_map/ppermute | solution.py:40
  36.9 5.0 %collective-permute-start.2 = (bf16[512,128]{1,0:T(8,128)(2,1)S(1)}, bf16[512,128]{1,0:T(8,128)(2,1)S(1)}, u32[]{:S(2)}, u32[]{:S(2)}) collective-permute-start(bf16[512,128]{1,0:T(8,128)(2,1)S(1)} %get-tuple-element.54), channel_id=1, source_target_pairs={{0,3},{1,0},{2,1},{3,2},{4,7},{5,4},{6,5},{7,6},{8,11},{9,8},{10,9... | collective-permute-start | bytes 393224 | tf_op jit(solution)/shard_map/ppermute | solution.py:40
  38.6 30.8 %copy-start.12 = (f32[16]{0:T(128)S(1)}, f32[16]{0:T(128)}, u32[]{:S(2)}) copy-start(f32[16]{0:T(128)} %param.25) | copy-start | bytes 196
  38.6 8.5 %collective-permute-start.1 = (bf16[1024,128]{1,0:T(8,128)(2,1)S(1)}, bf16[1024,128]{1,0:T(8,128)(2,1)S(1)}, u32[]{:S(2)}, u32[]{:S(2)}) collective-permute-start(bf16[1024,128]{1,0:T(8,128)(2,1)S(1)} %pad_maximum_fusion.9), channel_id=1, source_target_pairs={{0,1},{1,2},{2,3},{3,0},{4,5},{5,6},{6,7},{7,4},{8,9},{9,10},{10,1... | collective-permute-start | bytes 786440 | tf_op jit(solution)/shard_map/ppermute | solution.py:40
  42.0 6.7 %collective-permute-start.3 = (bf16[1024,128]{1,0:T(8,128)(2,1)S(1)}, bf16[1024,128]{1,0:T(8,128)(2,1)S(1)}, u32[]{:S(2)}, u32[]{:S(2)}) collective-permute-start(bf16[1024,128]{1,0:T(8,128)(2,1)S(1)} %pad_maximum_fusion.10), channel_id=1, source_target_pairs={{0,3},{1,0},{2,1},{3,2},{4,7},{5,4},{6,5},{7,6},{8,11},{9,8},{10,9... | collective-permute-start | bytes 786440 | tf_op jit(solution)/shard_map/ppermute | solution.py:40
  49.6 14.7 %all-to-all-start.1 = ((bf16[32,32,128]{2,1,0:T(8,128)(2,1)}), bf16[32,32,128]{2,1,0:T(8,128)(2,1)S(1)}, u32[]{:S(2)}, u32[]{:S(2)}) async-start(bf16[32,32,128]{2,1,0:T(8,128)(2,1)} %bitcast.6), calls=%async_computation.1 | async-start | bytes 524288 | tf_op jit(solution)/shard_map/all_to_all | solution.py:235
  64.7 0.8 copy-start.3
  65.5 13.5 %collective-permute-start.4 = (bf16[32,4096]{1,0:T(8,128)(2,1)S(1)}, bf16[32,4096]{1,0:T(8,128)(2,1)S(1)}, u32[]{:S(2)}, u32[]{:S(2)}) collective-permute-start(bf16[32,4096]{1,0:T(8,128)(2,1)S(1)} %get-tuple-element.46), channel_id=1, source_target_pairs={{0,3},{1,0},{2,1},{3,2},{4,7},{5,4},{6,5},{7,6},{8,11},{9,8},{10,9... | collective-permute-start | bytes 786440 | tf_op jit(solution)/shard_map/ppermute | solution.py:40
  68.7 10.2 %collective-permute-start.5 = (bf16[32,4096]{1,0:T(8,128)(2,1)S(1)}, bf16[32,4096]{1,0:T(8,128)(2,1)S(1)}, u32[]{:S(2)}, u32[]{:S(2)}) collective-permute-start(bf16[32,4096]{1,0:T(8,128)(2,1)S(1)} %get-tuple-element.46), channel_id=1, source_target_pairs={{0,1},{1,2},{2,3},{3,0},{4,5},{5,6},{6,7},{7,4},{8,9},{9,10},{10,1... | collective-permute-start | bytes 786440 | tf_op jit(solution)/shard_map/ppermute | solution.py:40
  79.0 6.6 %collective-permute-start.6 = (bf16[16,4096]{1,0:T(8,128)(2,1)S(1)}, bf16[16,4096]{1,0:T(8,128)(2,1)S(1)}, u32[]{:S(2)}, u32[]{:S(2)}) collective-permute-start(bf16[16,4096]{1,0:T(8,128)(2,1)S(1)} %slice.261), channel_id=1, source_target_pairs={{0,1},{1,2},{2,3},{3,0},{4,5},{5,6},{6,7},{7,4},{8,9},{9,10},{10,1... | collective-permute-start | bytes 393224 | tf_op jit(solution)/shard_map/ppermute | solution.py:40
  79.1 6.5 %collective-permute-start.7 = (bf16[16,4096]{1,0:T(8,128)(2,1)S(1)}, bf16[16,4096]{1,0:T(8,128)(2,1)S(1)}, u32[]{:S(2)}, u32[]{:S(2)}) collective-permute-start(bf16[16,4096]{1,0:T(8,128)(2,1)S(1)} %slice.262), channel_id=1, source_target_pairs={{0,3},{1,0},{2,1},{3,2},{4,7},{5,4},{6,5},{7,6},{8,11},{9,8},{10,9... | collective-permute-start | bytes 393224 | tf_op jit(solution)/shard_map/ppermute | solution.py:40
  85.7 1.6 copy-start
  87.3 9.5 %copy-start.10 = (f32[16]{0:T(128)S(1)}, f32[16]{0:T(128)}, u32[]{:S(2)}) copy-start(f32[16]{0:T(128)} %param.24) | copy-start | bytes 196
  97.2 2.1 collective-permute-start.8
  99.7 34.6 %copy-start.13 = (f32[16]{0:T(128)S(1)}, f32[16]{0:T(128)}, u32[]{:S(2)}) copy-start(f32[16]{0:T(128)} %param.26) | copy-start | bytes 196
  101.6 17.8 %all-to-all-start.2 = ((bf16[32,48,128]{2,1,0:T(8,128)(2,1)}), bf16[32,48,128]{2,1,0:T(8,128)(2,1)S(1)}, u32[]{:S(2)}, u32[]{:S(2)}) async-start(bf16[32,48,128]{2,1,0:T(8,128)(2,1)} %maximum_maximum_fusion), calls=%async_computation.2 | async-start | bytes 786432 | tf_op jit(solution)/shard_map/all_to_all | solution.py:281
  109.4 27.6 %copy-start.11 = (f32[1024]{0:T(1024)S(1)}, f32[1024]{0:T(1024)}, u32[]{:S(2)}) copy-start(f32[1024]{0:T(1024)} %param.27) | copy-start | bytes 12292
  109.5 60.2 %all-gather.5.cloned.1.call-start = ((), (), s32[]{:S(2)}) async-start(), calls=%async_computation.5 | async-start | bytes 5242880 | tf_op jit(solution)/shard_map/all_gather | solution.py:244
  121.1 12.8 %all-to-all-start.3 = ((bf16[32,32,128]{2,1,0:T(8,128)(2,1)}), bf16[32,32,128]{2,1,0:T(8,128)(2,1)S(1)}, u32[]{:S(2)}, u32[]{:S(2)}) async-start(bf16[32,32,128]{2,1,0:T(8,128)(2,1)} %bitcast.74), calls=%async_computation.3 | async-start | bytes 524288 | tf_op jit(solution)/shard_map/all_to_all | solution.py:291
  141.9 28.0 %copy-start.4 = (f32[1,32,32,128]{3,2,1,0:T(8,128)S(1)}, f32[1,32,32,128]{3,2,1,0:T(8,128)}, u32[]{:S(2)}) copy-start(f32[1,32,32,128]{3,2,1,0:T(8,128)} %copy-done.3) | copy-start | bytes 1572868
  141.9 28.5 %copy-start.6 = (f32[4096]{0:T(1024)S(1)}, f32[4096]{0:T(1024)}, u32[]{:S(2)}) copy-start(f32[4096]{0:T(1024)} %param.29) | copy-start | bytes 49156
  142.4 9.7 %collective-permute-start.11 = (bf16[16,4096]{1,0:T(8,128)(2,1)S(1)}, bf16[16,4096]{1,0:T(8,128)(2,1)S(1)}, u32[]{:S(2)}, u32[]{:S(2)}) collective-permute-start(bf16[16,4096]{1,0:T(8,128)(2,1)S(1)} %get-tuple-element.52), channel_id=1, source_target_pairs={{0,3},{1,0},{2,1},{3,2},{4,7},{5,4},{6,5},{7,6},{8,11},{9,8},{10,9... | collective-permute-start | bytes 393224 | tf_op jit(solution)/shard_map/ppermute | solution.py:40
  145.6 10.0 %collective-permute-start.9 = (bf16[16,4096]{1,0:T(8,128)(2,1)S(1)}, bf16[16,4096]{1,0:T(8,128)(2,1)S(1)}, u32[]{:S(2)}, u32[]{:S(2)}) collective-permute-start(bf16[16,4096]{1,0:T(8,128)(2,1)S(1)} %get-tuple-element.49), channel_id=1, source_target_pairs={{0,1},{1,2},{2,3},{3,0},{4,5},{5,6},{6,7},{7,4},{8,9},{9,10},{10,1... | collective-permute-start | bytes 393224 | tf_op jit(solution)/shard_map/ppermute | solution.py:40
  155.7 14.1 %collective-permute-start.10 = (bf16[32,4096]{1,0:T(8,128)(2,1)S(1)}, bf16[32,4096]{1,0:T(8,128)(2,1)S(1)}, u32[]{:S(2)}, u32[]{:S(2)}) collective-permute-start(bf16[32,4096]{1,0:T(8,128)(2,1)S(1)} %pad_maximum_fusion.11), channel_id=1, source_target_pairs={{0,1},{1,2},{2,3},{3,0},{4,5},{5,6},{6,7},{7,4},{8,9},{9,10},{10,1... | collective-permute-start | bytes 786440 | tf_op jit(solution)/shard_map/ppermute | solution.py:40
  155.8 14.0 %collective-permute-start.12 = (bf16[32,4096]{1,0:T(8,128)(2,1)S(1)}, bf16[32,4096]{1,0:T(8,128)(2,1)S(1)}, u32[]{:S(2)}, u32[]{:S(2)}) collective-permute-start(bf16[32,4096]{1,0:T(8,128)(2,1)S(1)} %pad_maximum_fusion.12), channel_id=1, source_target_pairs={{0,3},{1,0},{2,1},{3,2},{4,7},{5,4},{6,5},{7,6},{8,11},{9,8},{10,9... | collective-permute-start | bytes 786440 | tf_op jit(solution)/shard_map/ppermute | solution.py:40
  169.7 21.6 %collective-permute-start.17 = (bf16[4096,512]{1,0:T(8,128)(2,1)}, bf16[4096,512]{1,0:T(8,128)(2,1)}, u32[]{:S(2)}, u32[]{:S(2)}) collective-permute-start(bf16[4096,512]{1,0:T(8,128)(2,1)} %all-gather.5.cloned.1.call-done), channel_id=1, source_target_pairs={{0,4},{4,0},{8,12},{12,8},{16,20},{20,16},{24,28},{28,24},{32,36},... | collective-permute-start | bytes 12582920 | tf_op jit(solution)/shard_map/ppermute | solution.py:35
  170.5 7.7 %collective-permute-start.14 = (bf16[32,4096]{1,0:T(8,128)(2,1)S(1)}, bf16[32,4096]{1,0:T(8,128)(2,1)S(1)}, u32[]{:S(2)}, u32[]{:S(2)}) collective-permute-start(bf16[32,4096]{1,0:T(8,128)(2,1)S(1)} %fusion.28), channel_id=1, source_target_pairs={{0,8},{4,36},{8,16},{12,44},{16,24},{20,52},{24,0},{28,60},{32,40}... | collective-permute-start | bytes 786440 | tf_op jit(solution)/shard_map/ppermute | solution.py:40
  172.5 6.5 %collective-permute-start.13 = (bf16[32,4096]{1,0:T(8,128)(2,1)S(1)}, bf16[32,4096]{1,0:T(8,128)(2,1)S(1)}, u32[]{:S(2)}, u32[]{:S(2)}) collective-permute-start(bf16[32,4096]{1,0:T(8,128)(2,1)S(1)} %fusion.28), channel_id=1, source_target_pairs={{0,24},{4,100},{8,0},{12,108},{16,8},{20,116},{24,16},{28,124},{32... | collective-permute-start | bytes 786440 | tf_op jit(solution)/shard_map/ppermute | solution.py:40
  178.3 6.2 %collective-permute-start.15 = (bf16[16,4096]{1,0:T(8,128)(2,1)S(1)}, bf16[16,4096]{1,0:T(8,128)(2,1)S(1)}, u32[]{:S(2)}, u32[]{:S(2)}) collective-permute-start(bf16[16,4096]{1,0:T(8,128)(2,1)S(1)} %slice.284), channel_id=1, source_target_pairs={{0,8},{4,36},{8,16},{12,44},{16,24},{20,52},{24,0},{28,60},{32,40}... | collective-permute-start | bytes 393224 | tf_op jit(solution)/shard_map/ppermute | solution.py:40
  179.0 5.5 %collective-permute-start.16 = (bf16[16,4096]{1,0:T(8,128)(2,1)S(1)}, bf16[16,4096]{1,0:T(8,128)(2,1)S(1)}, u32[]{:S(2)}, u32[]{:S(2)}) collective-permute-start(bf16[16,4096]{1,0:T(8,128)(2,1)S(1)} %slice.285), channel_id=1, source_target_pairs={{0,24},{4,100},{8,0},{12,108},{16,8},{20,116},{24,16},{28,124},{32... | collective-permute-start | bytes 393224 | tf_op jit(solution)/shard_map/ppermute | solution.py:40
  184.7 16.2 %collective-permute-start.19 = (bf16[4,32,4096]{2,1,0:T(8,128)(2,1)S(1)}, bf16[4,32,4096]{2,1,0:T(8,128)(2,1)}, u32[]{:S(2)}, u32[]{:S(2)}) collective-permute-start(bf16[4,32,4096]{2,1,0:T(8,128)(2,1)S(1)} %pad_maximum_fusion.3), channel_id=1, source_target_pairs={{0,32},{4,12},{8,40},{12,20},{16,48},{20,28},{24,56},{28,4},{32,64... | collective-permute-start | bytes 3145736 | tf_op jit(solution)/shard_map/ppermute | solution.py:40
  186.4 16.3 %collective-permute-start.18 = (bf16[4,32,4096]{2,1,0:T(8,128)(2,1)S(1)}, bf16[4,32,4096]{2,1,0:T(8,128)(2,1)}, u32[]{:S(2)}, u32[]{:S(2)}) collective-permute-start(bf16[4,32,4096]{2,1,0:T(8,128)(2,1)S(1)} %pad_maximum_fusion.3), channel_id=1, source_target_pairs={{0,96},{4,28},{8,104},{12,4},{16,112},{20,12},{24,120},{28,20},{32... | collective-permute-start | bytes 3145736 | tf_op jit(solution)/shard_map/ppermute | solution.py:40
  201.9 16.2 %collective-permute-start.21 = (bf16[2,32,4096]{2,1,0:T(8,128)(2,1)S(1)}, bf16[2,32,4096]{2,1,0:T(8,128)(2,1)S(1)}, u32[]{:S(2)}, u32[]{:S(2)}) collective-permute-start(bf16[2,32,4096]{2,1,0:T(8,128)(2,1)S(1)} %slice.289), channel_id=1, source_target_pairs={{0,32},{4,12},{8,40},{12,20},{16,48},{20,28},{24,56},{28,4},{32,64... | collective-permute-start | bytes 1572872 | tf_op jit(solution)/shard_map/ppermute | solution.py:40
  203.8 14.3 %collective-permute-start.22 = (bf16[2,32,4096]{2,1,0:T(8,128)(2,1)S(1)}, bf16[2,32,4096]{2,1,0:T(8,128)(2,1)}, u32[]{:S(2)}, u32[]{:S(2)}) collective-permute-start(bf16[2,32,4096]{2,1,0:T(8,128)(2,1)S(1)} %slice.290), channel_id=1, source_target_pairs={{0,96},{4,28},{8,104},{12,4},{16,112},{20,12},{24,120},{28,20},{32... | collective-permute-start | bytes 1572872 | tf_op jit(solution)/shard_map/ppermute | solution.py:40
  206.6 4.3 %copy-start.1 = (bf16[4096,512]{1,0:T(8,128)(2,1)S(1)}, bf16[4096,512]{1,0:T(8,128)(2,1)}, u32[]{:S(2)}) copy-start(bf16[4096,512]{1,0:T(8,128)(2,1)} %all-gather.5.cloned.1.call-done) | copy-start | bytes 12582916
  214.7 7.6 %copy-start.2 = (bf16[4096,512]{1,0:T(8,128)(2,1)S(1)}, bf16[4096,512]{1,0:T(8,128)(2,1)}, u32[]{:S(2)}) copy-start(bf16[4096,512]{1,0:T(8,128)(2,1)} %all-gather.5.cloned.1.call-done) | copy-start | bytes 12582916
  214.8 9.8 %collective-permute-start.20 = (f32[5,4,32]{2,1,0:T(4,128)S(1)}, f32[5,4,32]{2,1,0:T(4,128)S(1)}, u32[]{:S(2)}, u32[]{:S(2)}) collective-permute-start(f32[5,4,32]{2,1,0:T(4,128)S(1)} %get-tuple-element.59), channel_id=1, source_target_pairs={{0,32},{4,12},{8,40},{12,20},{16,48},{20,28},{24,56},{28,4},{32,64... | collective-permute-start | bytes 7688 | tf_op jit(solution)/shard_map/ppermute | solution.py:40
  214.9 9.7 %collective-permute-start.24 = (f32[5,4,32]{2,1,0:T(4,128)S(1)}, f32[5,4,32]{2,1,0:T(4,128)S(1)}, u32[]{:S(2)}, u32[]{:S(2)}) collective-permute-start(f32[5,4,32]{2,1,0:T(4,128)S(1)} %get-tuple-element.60), channel_id=1, source_target_pairs={{0,96},{4,28},{8,104},{12,4},{16,112},{20,12},{24,120},{28,20},{32... | collective-permute-start | bytes 7688 | tf_op jit(solution)/shard_map/ppermute | solution.py:40
  224.1 5.3 %collective-permute-start.23 = (f32[5,4,32]{2,1,0:T(4,128)S(1)}, f32[5,4,32]{2,1,0:T(4,128)S(1)}, u32[]{:S(2)}, u32[]{:S(2)}) collective-permute-start(f32[5,4,32]{2,1,0:T(4,128)S(1)} %constant_dynamic-update-slice_fusion.9), channel_id=1, source_target_pairs={{0,64},{4,20},{8,72},{12,28},{16,80},{20,4},{24,88},{28,12},{32,96... | collective-permute-start | bytes 7688 | tf_op jit(solution)/shard_map/ppermute | solution.py:40
  229.5 5.1 %collective-permute-start.25 = (f32[5,32]{1,0:T(8,128)S(1)}, f32[5,32]{1,0:T(8,128)S(1)}, u32[]{:S(2)}, u32[]{:S(2)}) collective-permute-start(f32[5,32]{1,0:T(8,128)S(1)} %bitcast.370), channel_id=1, source_target_pairs={{0,8},{4,36},{8,16},{12,44},{16,24},{20,52},{24,0},{28,60},{32,40}... | collective-permute-start | bytes 1928 | tf_op jit(solution)/shard_map/ppermute | solution.py:40
  230.7 5.3 %collective-permute-start.26 = (f32[5,32]{1,0:T(8,128)S(1)}, f32[5,32]{1,0:T(8,128)S(1)}, u32[]{:S(2)}, u32[]{:S(2)}) collective-permute-start(f32[5,32]{1,0:T(8,128)S(1)} %bitcast.371), channel_id=1, source_target_pairs={{0,16},{4,68},{8,24},{12,76},{16,0},{20,84},{24,8},{28,92},{32,48}... | collective-permute-start | bytes 1928 | tf_op jit(solution)/shard_map/ppermute | solution.py:40
  234.4 3.6 %collective-permute-start.27 = (f32[5,32]{1,0:T(8,128)S(1)}, f32[5,32]{1,0:T(8,128)S(1)}, u32[]{:S(2)}, u32[]{:S(2)}) collective-permute-start(f32[5,32]{1,0:T(8,128)S(1)} %bitcast.372), channel_id=1, source_target_pairs={{0,24},{4,100},{8,0},{12,108},{16,8},{20,116},{24,16},{28,124},{32... | collective-permute-start | bytes 1928 | tf_op jit(solution)/shard_map/ppermute | solution.py:40
Sparse Core Ops, SparseCore 0:
  9.5 64.9 all-gather.2
  112.0 57.6 all-gather.4

commit v2 on v1

--- a/solution.py
+++ b/solution.py
@@ -171,24 +171,66 @@
     return (row_peak, exp_sum, first_moment, second_moment, target_left + target_right)
 
 
-def vocab_stats(rows, row_targets, tables):
-    logits = jnp.concatenate(
-        [jnp.dot(rows, table, preferred_element_type=jnp.float32) for table, _ in tables], axis=1
-    )
-    vocab_ids = jnp.concatenate([ids for _, ids in tables])
-    row_peak = jnp.max(logits, axis=1)
-    shifted = logits - row_peak[:, None]
-    weights = jnp.exp(shifted)
-    is_target = row_targets[:, None] == vocab_ids[None, :]
-    return jnp.stack(
-        [
-            row_peak,
-            jnp.sum(weights, axis=1),
-            jnp.sum(weights * shifted, axis=1),
-            jnp.sum(weights * shifted * shifted, axis=1),
-            jnp.sum(jnp.where(is_target, logits, 0.0), axis=1),
-        ]
-    )
+def vocab_stats(pieces, wanted, tables):
+    count = sum(piece.shape[0] for piece in pieces)
+    width, columns = tables[0].shape
+    tile = 256
+    f32 = jnp.float32
+
+    def kernel(*refs):
+        piece_refs = refs[: len(pieces)]
+        wanted_ref, *table_refs, out_ref, rows_ref, logits_ref = refs[len(pieces) :]
+        start = 0
+        for ref in piece_refs:
+            rows_ref[start : start + ref.shape[0], :] = ref[...]
+            start += ref.shape[0]
+        rows = rows_ref[...]
+        for place, table_ref in enumerate(table_refs):
+            for j in range(columns // tile):
+                at = place * columns + j * tile
+                logits_ref[:, at : at + tile] = jnp.dot(
+                    rows, table_ref[:, j * tile : (j + 1) * tile], preferred_element_type=f32
+                )
+        lane = lax.broadcasted_iota(jnp.int32, (128, 128), 1)
+        column = lax.broadcasted_iota(jnp.int32, (128, columns), 1)
+        for r in range(count // 128):
+            logits = logits_ref[r * 128 : (r + 1) * 128, :]
+            peak = jnp.max(logits, axis=1, keepdims=True)
+            shifted = logits - peak
+            weights = jnp.exp(shifted)
+            first = weights * shifted
+            target = jnp.zeros((128, 1), f32)
+            for place in range(len(table_refs)):
+                aim = jnp.broadcast_to(wanted_ref[place, r : r + 1, :], (128, 128)).T[:, :1]
+                part = logits[:, place * columns : (place + 1) * columns]
+                target += jnp.sum(jnp.where(column == aim, part, 0.0), axis=1, keepdims=True)
+            stats = (
+                peak,
+                jnp.sum(weights, axis=1, keepdims=True),
+                jnp.sum(first, axis=1, keepdims=True),
+                jnp.sum(first * shifted, axis=1, keepdims=True),
+                target,
+            )
+            table = jnp.zeros((128, 128), f32)
+            for k, stat in enumerate(stats):
+                table = jnp.where(lane == k, stat, table)
+            out_ref[:, r * 128 : (r + 1) * 128] = table.T[:8]
+
+    whole = pl.BlockSpec(memory_space=pltpu.VMEM)
+    every = len(tables) * columns
+    return pl.pallas_call(
+        kernel,
+        in_specs=[whole] * (len(pieces) + 1 + len(tables)),
+        out_specs=whole,
+        out_shape=jax.ShapeDtypeStruct((8, count), f32),
+        scratch_shapes=[pltpu.VMEM((count, width), jnp.bfloat16), pltpu.VMEM((count, every), f32)],
+        compiler_params=pltpu.CompilerParams(vmem_limit_bytes=24 << 20),
+        cost_estimate=pl.CostEstimate(
+            flops=2 * count * width * every,
+            bytes_accessed=2 * count * width,
+            transcendentals=count * every,
+        ),
+    )(*pieces, wanted, *tables)
 
 
 def on_device(
@@ -241,7 +283,10 @@
         normed_in = lax.dynamic_update_slice_in_dim(normed_in, block, row, 0)
 
     normed_in, lm_head = lax.optimization_barrier((normed_in, lm_head))
-    vocab_own = lax.all_gather(lm_head, "head", axis=0, tiled=True)
+    vocab_own = jnp.zeros((model_width, lm_head.shape[1]), bf16)
+    for ahead, block in enumerate(ring_gather(lm_head, shift_head)):
+        row = ((head_pos + ahead) % head_count) * lm_head.shape[0]
+        vocab_own = lax.dynamic_update_slice_in_dim(vocab_own, block, row, 0)
     vocab_other = swap_core(vocab_own)
 
     channels = w_zx.shape[2]
@@ -279,6 +324,13 @@
     totals = jnp.concatenate([totals, jnp.zeros((ctx_count, 13, STATE), bf16)], axis=1)
     message = jnp.concatenate([slices, totals], axis=1)
     arrived = lax.all_to_all(message, "ctx", 0, 0, tiled=True)
+    decay_gap = log_decay.T[:, :, None] - log_decay.T[:, None, :]
+    decay_mask = jnp.exp(jnp.where(causal[None], decay_gap, -jnp.inf))
+    scores = jnp.einsum("tn,sn->ts", c_act, b_act, precision=exact_prec)
+    mixing = scores[None] * decay_mask * step_size.T[:, None, :]
+    y_local = jnp.einsum("hts,shp->thp", mixing, x_heads, precision=exact_prec)
+    y_local = y_local + d_skip[None, :, None] * x_heads
+    arrived, y_local = lax.optimization_barrier((arrived, y_local))
     block_logs = jnp.sum(arrived[:, part_rows : part_rows + 3, 0].astype(f32), axis=1)
     blocks = jnp.arange(ctx_count)
     earlier = blocks[:, None] > blocks[None, :]
@@ -291,16 +343,11 @@
     state_in = lax.all_to_all(entering, "ctx", 0, 0, tiled=True)
     state_in = state_in.reshape(heads, HEAD_DIM, STATE).astype(f32)
 
-    decay_gap = log_decay.T[:, :, None] - log_decay.T[:, None, :]
-    decay_mask = jnp.exp(jnp.where(causal[None], decay_gap, -jnp.inf))
-    scores = jnp.einsum("tn,sn->ts", c_act, b_act, precision=exact_prec)
-    mixing = scores[None] * decay_mask * step_size.T[:, None, :]
-    y_local = jnp.einsum("hts,shp->thp", mixing, x_heads, precision=exact_prec)
     y_carry = (
         jnp.einsum("tn,hpn->thp", c_act, state_in, precision=exact_prec)
         * jnp.exp(log_decay)[:, :, None]
     )
-    mixer_out = y_local + y_carry + d_skip[None, :, None] * x_heads
+    mixer_out = y_local + y_carry
     gated_raw = mixer_out.reshape(tok_rows, channels) * jax.nn.silu(gate_z)
     gated_out = rms_scale(gated_raw, norm_gain).astype(bf16)
 
@@ -312,32 +359,40 @@
     normed_out = rms_scale(residual.astype(f32), final_gain).astype(bf16)
 
     along_first, along_second = shift_mixed(True), shift_mixed(False)
-    first_rows = jnp.stack(ring_gather(normed_out, along_first))
-    all_rows = ring_gather(first_rows, along_second)
+    from_left = moved(normed_out, along_first, 1)
+    from_right = moved(normed_out, along_first, -1)
+    from_far = moved(normed_out, along_first, 2)
+    near = jnp.concatenate([normed_out, from_left])
+    rest = jnp.concatenate([from_right, from_far])
+    near_left = moved(near, along_second, 1)
+    near_right = moved(near, along_second, -1)
+    rest_left = moved(rest, along_second, 1)
+    rest_right = moved(rest, along_second, -1)
+    near_far = moved(near_left, along_second, 1)
+    rest_far = moved(rest_right, along_second, -1)
+    pieces = ((near, rest), (near_right, rest_right), (near_far, rest_far), (near_left, rest_left))
+    order = (0, 3, 1, 2)
     y_pos, z_pos, core = ctx_pos // 8, (ctx_pos // 2) % 4, ctx_pos % 2
     by_chip = lax.dynamic_index_in_dim(group_targets.reshape(4, 4, 2, quarter), core, 2, False)
     by_chip = jnp.roll(by_chip, (-y_pos, -z_pos), (0, 1))
     by_chip = jnp.where(core == 0, by_chip, by_chip.transpose(1, 0, 2))
+    by_chip = jnp.stack([by_chip[:, k] for k in order], axis=1).reshape(4, 1, 4 * quarter)
     vocab_width = vocab_own.shape[1]
-    columns = jnp.arange(vocab_width, dtype=jnp.int32)
-    tables = [
-        (vocab_own, ctx_pos * vocab_width + columns),
-        (vocab_other, (ctx_pos ^ 1) * vocab_width + columns),
-    ]
-    all_stats = [None] * 4
-    for group in ((0,), (1, 3), (2,)):
-        rows = jnp.concatenate([all_rows[k].reshape(-1, model_width) for k in group])
-        wanted = jnp.concatenate([by_chip[k].reshape(-1) for k in group])
-        stats = vocab_stats(rows, wanted, tables).reshape(5, len(group), 4, quarter)
-        for place, k in enumerate(group):
-            all_stats[k] = stats[:, place]
-    merged = tuple(all_stats[0])
-    for ahead in range(1, 4):
-        merged = join_stats(merged, tuple(moved(all_stats[ahead], along_second, ahead)))
-    both = jnp.stack(merged)
+    by_chip = jnp.stack([by_chip - ctx_pos * vocab_width, by_chip - (ctx_pos ^ 1) * vocab_width])
+    tables = (vocab_own, vocab_other)
+    rows = 4 * quarter
+    stats = [vocab_stats(pieces[0], by_chip[:, 0], tables)]
+    sides = vocab_stats(pieces[1] + pieces[3], jnp.concatenate([by_chip[:, 1], by_chip[:, 3]], axis=1), tables)
+    stats.append(moved(sides[:, :rows], along_second, 1))
+    stats.append(moved(vocab_stats(pieces[2], by_chip[:, 2], tables), along_second, 2))
+    stats.append(moved(sides[:, rows:], along_second, -1))
+    merged = tuple(stats[0][:5])
+    for other in (stats[1], stats[3], stats[2]):
+        merged = join_stats(merged, tuple(other[:5]))
+    both = jnp.stack(merged).reshape(5, 4, quarter)
     merged = tuple(both[:, 0])
-    for ahead in range(1, 4):
-        merged = join_stats(merged, tuple(moved(both[:, ahead], along_first, ahead)))
+    for place in range(1, 4):
+        merged = join_stats(merged, tuple(moved(both[:, place], along_first, order[place])))
     row_peak, exp_sum, first_moment, second_moment, target_logit = merged
     mean_shift = first_moment / exp_sum
     spread = second_moment / exp_sum - mean_shift * mean_shift

time: 246 us -> 245 us (level)
  matrix products: 25.9 us -> 9.5 us
  Pallas kernels: 14.8 us -> 31.1 us
  waiting for transfers between devices: 103 us -> 88.1 us
  local copies, waits for them, and re-layouts: 11.7 us -> 19.7 us
  starting transfers between devices: 67.3 us -> 72.5 us
    dot_general x6 -> x0, matrix products: 17 us -> none  [vocab_stats(): jnp.dot(rows, table, preferred_element_type=jnp.float32)]
    pallas_call x0 -> x3, Pallas kernels: none -> 16.3 us  [vocab_stats(): pl.pallas_call(kernel, in_specs=[whole] * (len(pieces) + 1 + len(tables))...]
    all_gather x1 -> x0, waiting for transfers between devices: 10.5 us -> none  [on_device(): vocab_own = lax.all_gather(lm_head, 'head', axis=0, tiled=True)]
    dynamic_update_slice x0 -> x3, local copies, waits for them, and re-layouts: none -> 5.7 us  [on_device(): vocab_own = lax.dynamic_update_slice_in_dim(vocab_own, block, row, 0)]
    ppermute x26 -> x31, starting transfers between devices: 41.9 us -> 47.3 us  [moved(): return lax.ppermute(value, axis, pairs)]
    all_to_all x1, waiting for transfers between devices: 8.58 us -> 5.52 us  [on_device(): state_in = lax.all_to_all(entering, 'ctx', 0, 0, tiled=True)]
    ppermute x26 -> x31, waiting for transfers between devices: 56.6 us -> 59.4 us  [moved(): return lax.ppermute(value, axis, pairs)]
  transfers between devices with their start and end apart: 34 -> 38, of which waited for: 21 -> 23; matrix products, arithmetic and copies ran while one was open for 18% -> 12% of each run, Pallas kernels for 6% -> 13%
where the time goes in v2:
time: 245 us; the launch traced here: 244 us
  waiting for transfers between devices  88.1 us (36%)
  starting transfers between devices  72.5 us (30%)
  Pallas kernels  31.1 us (13%)
  local copies, waits for them, and re-layouts  19.7 us (8%)
  between operations  14.2 us (6%)
  matrix products  9.5 us (4%)
  other arithmetic  8.51 us (3%)
    ppermute x31, waiting for transfers between devices, moved(): return lax.ppermute(value, axis, pairs)  59.4 us
    ppermute x31, starting transfers between devices, moved(): return lax.ppermute(value, axis, pairs)  47.3 us
    pallas_call x3, Pallas kernels, vocab_stats(): pl.pallas_call(kernel, in_specs=[whole] * (len(pieces) + 1 + len(tables))...  16.3 us
    all_to_all x1, waiting for transfers between devices, on_device(): lax.all_to_all(mine, 'ctx', split_axis=0, concat_axis=2, tiled=True)  9.85 us
    pallas_call x1, Pallas kernels, project(): pl.pallas_call(kernel, grid=(width // depth,), in_specs=[pl.BlockSpec((co...  9.47 us
    all_to_all x1, starting transfers between devices, on_device(): packed = lax.all_to_all(packed, 'ctx', 0, 0, tiled=True)  8.41 us
    all_to_all x1, starting transfers between devices, on_device(): arrived = lax.all_to_all(message, 'ctx', 0, 0, tiled=True)  7.49 us
    all_to_all x1, waiting for transfers between devices, on_device(): arrived = lax.all_to_all(message, 'ctx', 0, 0, tiled=True)  7.43 us
  transfers between devices with their start and end apart: 38, of which 23 were waited for; matrix products, arithmetic and copies ran while one was open for 12% of the time, Pallas kernels for 13%

profile of v2, /device:TPU:0, one launch (start us, length us, event | category | flops | bytes accessed | tf_op | source)
XLA Modules:
  0.0 243.6 jit_solution(18024831043636959627)
XLA Ops:
  8.6 8.4 %all-to-all-start = ((s32[32,1,160]{2,1,0:T(1,128)}), s32[32,1,160]{2,1,0:T(1,128)S(1)}, u32[]{:S(2)}, u32[]{:S(2)}) async-start(s32[32,1,160]{2,1,0:T(1,128)} %broadcast_in_dim.37), calls=%async_computation | async-start | bytes 65536 | tf_op jit(solution)/shard_map/all_to_all | solution.py:266
  17.0 1.9 copy.84
  19.2 5.2 %all-to-all-done = s32[32,1,160]{2,1,0:T(1,128)S(1)} async-done(((s32[32,1,160]{2,1,0:T(1,128)}), s32[32,1,160]{2,1,0:T(1,128)S(1)}, u32[]{:S(2)}, u32[]{:S(2)}) %all-to-all-start) | async-done | bytes 20512 | tf_op jit(solution)/shard_map/all_to_all | solution.py:266
  25.3 5.3 %shard_map.154 = bf16[4096,128]{1,0:T(8,128)(2,1)S(1)} custom-call(s32[4,8,128]{2,1,0:T(8,128)S(1)} %sub.205.ids_ref, bf16[512,1024]{1,0:T(8,128)(2,1)S(1)} %bitcast.327), custom_call_target="tpu_custom_call" | custom-call | flops 4294967296 | bytes 4194304 | tf_op jit(solution)/shard_map/pallas_call | solution.py:93
  30.7 1.6 collective-permute-start
  32.3 5.2 %collective-permute-done = bf16[512,128]{1,0:T(8,128)(2,1)S(1)} collective-permute-done((bf16[512,128]{1,0:T(8,128)(2,1)S(1)}, bf16[512,128]{1,0:T(8,128)(2,1)S(1)}, u32[]{:S(2)}, u32[]{:S(2)}) %collective-permute-start) | collective-permute-done | bytes 131104 | tf_op jit(solution)/shard_map/ppermute | solution.py:40
  37.6 1.6 collective-permute-start.2
  39.7 2.9 %collective-permute-done.2 = bf16[512,128]{1,0:T(8,128)(2,1)S(1)} collective-permute-done((bf16[512,128]{1,0:T(8,128)(2,1)S(1)}, bf16[512,128]{1,0:T(8,128)(2,1)S(1)}, u32[]{:S(2)}, u32[]{:S(2)}) %collective-permute-start.2) | collective-permute-done | bytes 131104 | tf_op jit(solution)/shard_map/ppermute | solution.py:40
  42.6 2.8 %collective-permute-start.3 = (bf16[1024,128]{1,0:T(8,128)(2,1)S(1)}, bf16[1024,128]{1,0:T(8,128)(2,1)S(1)}, u32[]{:S(2)}, u32[]{:S(2)}) collective-permute-start(bf16[1024,128]{1,0:T(8,128)(2,1)S(1)} %pad_maximum_fusion.3), channel_id=1, source_target_pairs={{0,3},{1,0},{2,1},{3,2},{4,7},{5,4},{6,5},{7,6},{8,11},{9,8},{10,9... | collective-permute-start | bytes 786440 | tf_op jit(solution)/shard_map/ppermute | solution.py:40
  45.5 2.3 collective-permute-done.1
  47.8 1.6 collective-permute-done.3
  49.4 0.8 add_convert_fusion
  50.3 3.9 %all-to-all-start.1 = ((bf16[32,32,128]{2,1,0:T(8,128)(2,1)}), bf16[32,32,128]{2,1,0:T(8,128)(2,1)S(1)}, u32[]{:S(2)}, u32[]{:S(2)}) async-start(bf16[32,32,128]{2,1,0:T(8,128)(2,1)} %bitcast.3), calls=%async_computation.1 | async-start | bytes 524288 | tf_op jit(solution)/shard_map/all_to_all | solution.py:277
  54.8 9.8 %all-to-all-done.1 = bf16[32,32,128]{2,1,0:T(8,128)(2,1)S(1)} async-done(((bf16[32,32,128]{2,1,0:T(8,128)(2,1)}), bf16[32,32,128]{2,1,0:T(8,128)(2,1)S(1)}, u32[]{:S(2)}, u32[]{:S(2)}) %all-to-all-start.1) | async-done | bytes 262176 | tf_op jit(solution)/shard_map/all_to_all | solution.py:277
  65.7 3.2 %collective-permute-start.4 = (bf16[32,4096]{1,0:T(8,128)(2,1)S(1)}, bf16[32,4096]{1,0:T(8,128)(2,1)S(1)}, u32[]{:S(2)}, u32[]{:S(2)}) collective-permute-start(bf16[32,4096]{1,0:T(8,128)(2,1)S(1)} %get-tuple-element.36), channel_id=1, source_target_pairs={{0,3},{1,0},{2,1},{3,2},{4,7},{5,4},{6,5},{7,6},{8,11},{9,8},{10,9... | collective-permute-start | bytes 786440 | tf_op jit(solution)/shard_map/ppermute | solution.py:40
  70.7 4.7 %collective-permute-done.4 = bf16[32,4096]{1,0:T(8,128)(2,1)S(1)} collective-permute-done((bf16[32,4096]{1,0:T(8,128)(2,1)S(1)}, bf16[32,4096]{1,0:T(8,128)(2,1)S(1)}, u32[]{:S(2)}, u32[]{:S(2)}) %collective-permute-start.4) | collective-permute-done | bytes 262176 | tf_op jit(solution)/shard_map/ppermute | solution.py:40
  75.5 3.8 %collective-permute-start.7 = (bf16[16,4096]{1,0:T(8,128)(2,1)S(1)}, bf16[16,4096]{1,0:T(8,128)(2,1)S(1)}, u32[]{:S(2)}, u32[]{:S(2)}) collective-permute-start(bf16[16,4096]{1,0:T(8,128)(2,1)S(1)} %slice.284), channel_id=1, source_target_pairs={{0,3},{1,0},{2,1},{3,2},{4,7},{5,4},{6,5},{7,6},{8,11},{9,8},{10,9... | collective-permute-start | bytes 393224 | tf_op jit(solution)/shard_map/ppermute | solution.py:40
  79.4 2.8 %collective-permute-done.7 = bf16[16,4096]{1,0:T(8,128)(2,1)S(1)} collective-permute-done((bf16[16,4096]{1,0:T(8,128)(2,1)S(1)}, bf16[16,4096]{1,0:T(8,128)(2,1)S(1)}, u32[]{:S(2)}, u32[]{:S(2)}) %collective-permute-start.7) | collective-permute-done | bytes 131104 | tf_op jit(solution)/shard_map/ppermute | solution.py:40
  82.2 3.5 %collective-permute-done.6 = bf16[16,4096]{1,0:T(8,128)(2,1)S(1)} collective-permute-done((bf16[16,4096]{1,0:T(8,128)(2,1)S(1)}, bf16[16,4096]{1,0:T(8,128)(2,1)S(1)}, u32[]{:S(2)}, u32[]{:S(2)}) %collective-permute-start.6) | collective-permute-done | bytes 131104 | tf_op jit(solution)/shard_map/ppermute | solution.py:40
  86.0 1.8 collective-permute-start.17
  87.9 1.6 copy-done
  89.5 9.5 %shard_map.155 = (f32[128,1024]{1,0:T(8,128)S(1)}, f32[128,1024]{1,0:T(8,128)S(1)}, f32[128,256]{1,0:T(8,128)S(1)}, f32[128,16]{1,0:T(8,128)S(1)}) custom-call(bf16[128,4096]{1,0:T(8,128)(2,1)S(1)} %constant_dynamic-update-slice_fusion.14.rows_ref, bf16[4096,2,1024]{2,1,0:T(2,128)(2,1)} %zx_ref.1, bf16[4096,2,128]{2,1,0:T(2,128)(2,1)S(1)} %copy-done, ...), custom_call_target="tpu_custom_call" | custom-call | flops 2432696320 | bytes 19005440 | tf_op jit(solution)/shard_map/pallas_call | solution.py:130
  99.0 1.5 collective-permute-start.8
  100.5 0.8 fusion.105
  103.4 1.0 maximum_maximum_fusion
  104.3 7.5 %all-to-all-start.2 = ((bf16[32,48,128]{2,1,0:T(8,128)(2,1)}), bf16[32,48,128]{2,1,0:T(8,128)(2,1)S(1)}, u32[]{:S(2)}, u32[]{:S(2)}) async-start(bf16[32,48,128]{2,1,0:T(8,128)(2,1)} %maximum_maximum_fusion), calls=%async_computation.2 | async-start | bytes 786432 | tf_op jit(solution)/shard_map/all_to_all | solution.py:326
  112.1 2.2 fusion
  114.3 7.4 %all-to-all-done.2 = bf16[32,48,128]{2,1,0:T(8,128)(2,1)S(1)} async-done(((bf16[32,48,128]{2,1,0:T(8,128)(2,1)}), bf16[32,48,128]{2,1,0:T(8,128)(2,1)S(1)}, u32[]{:S(2)}, u32[]{:S(2)}) %all-to-all-start.2) | async-done | bytes 393248 | tf_op jit(solution)/shard_map/all_to_all | solution.py:326
  122.7 0.8 copy.107
  123.4 3.9 %all-to-all-start.3 = ((bf16[32,32,128]{2,1,0:T(8,128)(2,1)}), bf16[32,32,128]{2,1,0:T(8,128)(2,1)S(1)}, u32[]{:S(2)}, u32[]{:S(2)}) async-start(bf16[32,32,128]{2,1,0:T(8,128)(2,1)} %bitcast.70), calls=%async_computation.3 | async-start | bytes 524288 | tf_op jit(solution)/shard_map/all_to_all | solution.py:343
  127.4 2.3 broadcast_in_dim.53
  129.7 1.1 constant_dynamic-update-slice_fusion.13
  130.8 5.5 %all-to-all-done.3 = bf16[32,32,128]{2,1,0:T(8,128)(2,1)S(1)} async-done(((bf16[32,32,128]{2,1,0:T(8,128)(2,1)}), bf16[32,32,128]{2,1,0:T(8,128)(2,1)S(1)}, u32[]{:S(2)}, u32[]{:S(2)}) %all-to-all-start.3) | async-done | bytes 262176 | tf_op jit(solution)/shard_map/all_to_all | solution.py:343
  136.9 1.1 slice.312
  138.0 1.5 collective-permute-start.19
  139.5 1.1 slice.311
  141.5 2.3 constant_dynamic-update-slice_fusion.12
  143.8 8.4 %collective-permute-done.19 = bf16[512,512]{1,0:T(8,128)(2,1)S(1)} collective-permute-done((bf16[512,512]{1,0:T(8,128)(2,1)S(1)}, bf16[512,512]{1,0:T(8,128)(2,1)S(1)}, u32[]{:S(2)}, u32[]{:S(2)}) %collective-permute-start.19) | collective-permute-done | bytes 524320 | tf_op jit(solution)/shard_map/ppermute | solution.py:40
  152.2 3.5 %collective-permute-done.18 = bf16[512,512]{1,0:T(8,128)(2,1)S(1)} collective-permute-done((bf16[512,512]{1,0:T(8,128)(2,1)S(1)}, bf16[512,512]{1,0:T(8,128)(2,1)S(1)}, u32[]{:S(2)}, u32[]{:S(2)}) %collective-permute-start.18) | collective-permute-done | bytes 524320 | tf_op jit(solution)/shard_map/ppermute | solution.py:40
  155.7 1.1 maximum_dynamic-update-slice_fusion
  156.8 4.8 %convolution_convert_fusion = bf16[128,4096]{1,0:T(8,128)(2,1)S(1)} fusion(bf16[1024,4096]{1,0:T(8,128)(2,1)} %all-gather.2.cloned.1.call-done, f32[1024]{0:T(1024)S(1)} %copy-done.14, f32[128]{0:T(128)S(1)} %add_rsqrt_fusion.1, f32[128,1024]{1,0:T(8,128)S(1)} %copy.93, f32[128,1024]{1,0:T(8,128)S(1)} %get-tuple-element.19), kind=kOutput, calls=%fused_computation | convolution fusion | flops 1075314688 | bytes 10490368 | tf_op jit(solution)/shard_map/dot_general | solution.py:354
  162.1 3.2 %collective-permute-start.11 = (bf16[16,4096]{1,0:T(8,128)(2,1)S(1)}, bf16[16,4096]{1,0:T(8,128)(2,1)S(1)}, u32[]{:S(2)}, u32[]{:S(2)}) collective-permute-start(bf16[16,4096]{1,0:T(8,128)(2,1)S(1)} %get-tuple-element.42), channel_id=1, source_target_pairs={{0,3},{1,0},{2,1},{3,2},{4,7},{5,4},{6,5},{7,6},{8,11},{9,8},{10,9... | collective-permute-start | bytes 393224 | tf_op jit(solution)/shard_map/ppermute | solution.py:40
  165.3 2.3 constant_dynamic-update-slice_fusion.11.refs_3_.refs_5_
  168.3 3.3 %collective-permute-start.12 = (bf16[32,4096]{1,0:T(8,128)(2,1)S(1)}, bf16[32,4096]{1,0:T(8,128)(2,1)S(1)}, u32[]{:S(2)}, u32[]{:S(2)}) collective-permute-start(bf16[32,4096]{1,0:T(8,128)(2,1)S(1)} %pad_maximum_fusion.5), channel_id=1, source_target_pairs={{0,3},{1,0},{2,1},{3,2},{4,7},{5,4},{6,5},{7,6},{8,11},{9,8},{10,9... | collective-permute-start | bytes 786440 | tf_op jit(solution)/shard_map/ppermute | solution.py:40
  171.9 4.6 %collective-permute-done.12 = bf16[32,4096]{1,0:T(8,128)(2,1)S(1)} collective-permute-done((bf16[32,4096]{1,0:T(8,128)(2,1)S(1)}, bf16[32,4096]{1,0:T(8,128)(2,1)S(1)}, u32[]{:S(2)}, u32[]{:S(2)}) %collective-permute-start.12) | collective-permute-done | bytes 262176 | tf_op jit(solution)/shard_map/ppermute | solution.py:40
  176.5 2.8 %collective-permute-done.10 = bf16[32,4096]{1,0:T(8,128)(2,1)S(1)} collective-permute-done((bf16[32,4096]{1,0:T(8,128)(2,1)S(1)}, bf16[32,4096]{1,0:T(8,128)(2,1)S(1)}, u32[]{:S(2)}, u32[]{:S(2)}) %collective-permute-start.10) | collective-permute-done | bytes 262176 | tf_op jit(solution)/shard_map/ppermute | solution.py:40
  180.5 2.8 %collective-permute-start.14 = (bf16[32,4096]{1,0:T(8,128)(2,1)S(1)}, bf16[32,4096]{1,0:T(8,128)(2,1)S(1)}, u32[]{:S(2)}, u32[]{:S(2)}) collective-permute-start(bf16[32,4096]{1,0:T(8,128)(2,1)S(1)} %fusion.19), channel_id=1, source_target_pairs={{0,24},{4,100},{8,0},{12,108},{16,8},{20,116},{24,16},{28,124},{32... | collective-permute-start | bytes 786440 | tf_op jit(solution)/shard_map/ppermute | solution.py:40
  183.4 5.0 %collective-permute-done.13 = bf16[32,4096]{1,0:T(8,128)(2,1)S(1)} collective-permute-done((bf16[32,4096]{1,0:T(8,128)(2,1)S(1)}, bf16[32,4096]{1,0:T(8,128)(2,1)S(1)}, u32[]{:S(2)}, u32[]{:S(2)}) %collective-permute-start.13) | collective-permute-done | bytes 262176 | tf_op jit(solution)/shard_map/ppermute | solution.py:40
  188.4 2.6 %collective-permute-start.23 = (bf16[64,4096]{1,0:T(8,128)(2,1)S(1)}, bf16[64,4096]{1,0:T(8,128)(2,1)S(1)}, u32[]{:S(2)}, u32[]{:S(2)}) collective-permute-start(bf16[64,4096]{1,0:T(8,128)(2,1)S(1)} %pad_maximum_fusion.1.refs_0_), channel_id=1, source_target_pairs={{0,32},{4,12},{8,40},{12,20},{16,48},{20,28},{24,56},{28,4},{32,64... | collective-permute-start | bytes 1572872 | tf_op jit(solution)/shard_map/ppermute | solution.py:40
  191.1 3.0 %collective-permute-done.15 = bf16[32,4096]{1,0:T(8,128)(2,1)S(1)} collective-permute-done((bf16[32,4096]{1,0:T(8,128)(2,1)S(1)}, bf16[32,4096]{1,0:T(8,128)(2,1)S(1)}, u32[]{:S(2)}, u32[]{:S(2)}) %collective-permute-start.15) | collective-permute-done | bytes 262176 | tf_op jit(solution)/shard_map/ppermute | solution.py:40
  194.1 1.7 collective-permute-start.22
  196.2 1.8 collective-permute-start.24
  198.9 1.4 collective-permute-start.27
  200.3 3.1 %collective-permute-done.22.refs_1_ = bf16[64,4096]{1,0:T(8,128)(2,1)S(1)} collective-permute-done((bf16[64,4096]{1,0:T(8,128)(2,1)S(1)}, bf16[64,4096]{1,0:T(8,128)(2,1)S(1)}, u32[]{:S(2)}, u32[]{:S(2)}) %collective-permute-start.22) | collective-permute-done | bytes 524320 | tf_op jit(solution)/shard_map/ppermute | solution.py:40
  203.4 2.8 %collective-permute-start.28 = (bf16[64,4096]{1,0:T(8,128)(2,1)S(1)}, bf16[64,4096]{1,0:T(8,128)(2,1)S(1)}, u32[]{:S(2)}, u32[]{:S(2)}) collective-permute-start(bf16[64,4096]{1,0:T(8,128)(2,1)S(1)} %collective-permute-done.22.refs_1_), channel_id=1, source_target_pairs={{0,96},{4,28},{8,104},{12,4},{16,112},{20,12},{24,120},{28,20},{32... | collective-permute-start | bytes 1572872 | tf_op jit(solution)/shard_map/ppermute | solution.py:40
  206.2 2.8 %collective-permute-done.21.refs_0_ = bf16[64,4096]{1,0:T(8,128)(2,1)S(1)} collective-permute-done((bf16[64,4096]{1,0:T(8,128)(2,1)S(1)}, bf16[64,4096]{1,0:T(8,128)(2,1)S(1)}, u32[]{:S(2)}, u32[]{:S(2)}) %collective-permute-start.21) | collective-permute-done | bytes 524320 | tf_op jit(solution)/shard_map/ppermute | solution.py:40
  209.0 6.3 %shard_map.157 = f32[8,256]{1,0:T(8,128)S(1)} custom-call(bf16[64,4096]{1,0:T(8,128)(2,1)S(1)} %collective-permute-done.21.refs_0_, bf16[64,4096]{1,0:T(8,128)(2,1)S(1)} %collective-permute-done.22.refs_1_, bf16[64,4096]{1,0:T(8,128)(2,1)S(1)} %collective-permute-done.23.refs_2_, bf16[64,4096]{1,0:T(8,128)(2,1)S(1)} %collective-permute-done.24.refs_3_, ...), custom_call_target="tpu_custom_call" | custom-call | flops 2147483648 | bytes 2097152 | tf_op jit(solution)/shard_map/pallas_call | solution.py:221
  215.3 2.8 %collective-permute-start.26 = (f32[8,128]{1,0:T(8,128)S(1)}, f32[8,128]{1,0:T(8,128)S(1)}, u32[]{:S(2)}, u32[]{:S(2)}) collective-permute-start(f32[8,128]{1,0:T(8,128)S(1)} %get-tuple-element.54), channel_id=1, source_target_pairs={{0,96},{4,28},{8,104},{12,4},{16,112},{20,12},{24,120},{28,20},{32... | collective-permute-start | bytes 12296 | tf_op jit(solution)/shard_map/ppermute | solution.py:40
  218.1 5.0 %shard_map.158 = f32[8,128]{1,0:T(8,128)S(1)} custom-call(bf16[64,4096]{1,0:T(8,128)(2,1)S(1)} %collective-permute-done.27.refs_0_, bf16[64,4096]{1,0:T(8,128)(2,1)S(1)} %collective-permute-done.28.refs_1_, s32[2,1,128]{2,1,0:T(1,128)S(1)} %bitcast.329, bf16[4096,512]{1,0:T(8,128)(2,1)} %constant_dynamic-update-slice_fusion.11.refs_3_.refs_5_, ...), custom_call_target="tpu_custom_call" | custom-call | flops 1073741824 | bytes 1048576 | tf_op jit(solution)/shard_map/pallas_call | solution.py:221
  223.2 1.6 collective-permute-start.29
  224.7 5.0 %shard_map.156 = f32[8,128]{1,0:T(8,128)S(1)} custom-call(bf16[64,4096]{1,0:T(8,128)(2,1)S(1)} %pad_maximum_fusion.1.refs_0_, bf16[64,4096]{1,0:T(8,128)(2,1)S(1)} %constant_dynamic-update-slice_fusion.4.refs_1_, s32[2,1,128]{2,1,0:T(1,128)S(1)} %bitcast.328, bf16[4096,512]{1,0:T(8,128)(2,1)} %constant_dynamic-update-slice_fusion.11.refs_3_.refs_5_, ...), custom_call_target="tpu_custom_call" | custom-call | flops 1073741824 | bytes 1048576 | tf_op jit(solution)/shard_map/pallas_call | solution.py:221
  230.3 1.1 collective-permute-start.32
  231.4 3.2 %collective-permute-start.30 = (f32[5,32]{1,0:T(8,128)S(1)}, f32[5,32]{1,0:T(8,128)S(1)}, u32[]{:S(2)}, u32[]{:S(2)}) collective-permute-start(f32[5,32]{1,0:T(8,128)S(1)} %bitcast.350), channel_id=1, source_target_pairs={{0,24},{4,100},{8,0},{12,108},{16,8},{20,116},{24,16},{28,124},{32... | collective-permute-start | bytes 1928 | tf_op jit(solution)/shard_map/ppermute | solution.py:40
  234.7 0.8 collective-permute-done.32
  (167 shorter events, 18.1 us)
Async XLA Ops:
  6.5 150.2 %all-gather.2.cloned.1.call-start = ((), (), s32[]{:S(2)}) async-start(), calls=%async_computation.4 | async-start | bytes 8650752 | tf_op jit(solution)/shard_map/all_gather | solution.py:262
  8.6 15.9 %all-to-all-start = ((s32[32,1,160]{2,1,0:T(1,128)}), s32[32,1,160]{2,1,0:T(1,128)S(1)}, u32[]{:S(2)}, u32[]{:S(2)}) async-start(s32[32,1,160]{2,1,0:T(1,128)} %broadcast_in_dim.37), calls=%async_computation | async-start | bytes 65536 | tf_op jit(solution)/shard_map/all_to_all | solution.py:266
  24.4 0.6 copy-start.3
  25.3 20.2 %copy-start.9 = (f32[4,1024]{1,0:T(4,128)S(1)}, f32[4,1024]{1,0:T(4,128)}, u32[]{:S(2)}) copy-start(f32[4,1024]{1,0:T(4,128)} %param.22) | copy-start | bytes 49156
  30.7 23.5 %copy-start.12 = (f32[4,2,128]{2,1,0:T(2,128)S(1)}, f32[4,2,128]{2,1,0:T(2,128)}, u32[]{:S(2)}) copy-start(f32[4,2,128]{2,1,0:T(2,128)} %param.23) | copy-start | bytes 12292
  30.7 34.6 %copy-start.7 = (f32[4096]{0:T(1024)S(1)}, f32[4096]{0:T(1024)}, u32[]{:S(2)}) copy-start(f32[4096]{0:T(1024)} %param.28) | copy-start | bytes 49156
  30.7 38.8 %copy-start.2 = (bf16[4096,16]{0,1:T(8,128)(2,1)S(1)}, bf16[4096,16]{0,1:T(8,128)(2,1)}, u32[]{:S(2)}) copy-start(bf16[4096,16]{0,1:T(8,128)(2,1)} %param.21) | copy-start | bytes 393220
  30.7 6.8 %collective-permute-start = (bf16[512,128]{1,0:T(8,128)(2,1)S(1)}, bf16[512,128]{1,0:T(8,128)(2,1)S(1)}, u32[]{:S(2)}, u32[]{:S(2)}) collective-permute-start(bf16[512,128]{1,0:T(8,128)(2,1)S(1)} %slice.278), channel_id=1, source_target_pairs={{0,1},{1,2},{2,3},{3,0},{4,5},{5,6},{6,7},{7,4},{8,9},{9,10},{10,1... | collective-permute-start | bytes 393224 | tf_op jit(solution)/shard_map/ppermute | solution.py:40
  37.6 5.0 %collective-permute-start.2 = (bf16[512,128]{1,0:T(8,128)(2,1)S(1)}, bf16[512,128]{1,0:T(8,128)(2,1)S(1)}, u32[]{:S(2)}, u32[]{:S(2)}) collective-permute-start(bf16[512,128]{1,0:T(8,128)(2,1)S(1)} %get-tuple-element.44), channel_id=1, source_target_pairs={{0,3},{1,0},{2,1},{3,2},{4,7},{5,4},{6,5},{7,6},{8,11},{9,8},{10,9... | collective-permute-start | bytes 393224 | tf_op jit(solution)/shard_map/ppermute | solution.py:40
  39.2 8.6 %collective-permute-start.1 = (bf16[1024,128]{1,0:T(8,128)(2,1)S(1)}, bf16[1024,128]{1,0:T(8,128)(2,1)S(1)}, u32[]{:S(2)}, u32[]{:S(2)}) collective-permute-start(bf16[1024,128]{1,0:T(8,128)(2,1)S(1)} %pad_maximum_fusion.2), channel_id=1, source_target_pairs={{0,1},{1,2},{2,3},{3,0},{4,5},{5,6},{6,7},{7,4},{8,9},{9,10},{10,1... | collective-permute-start | bytes 786440 | tf_op jit(solution)/shard_map/ppermute | solution.py:40
  42.6 6.8 %collective-permute-start.3 = (bf16[1024,128]{1,0:T(8,128)(2,1)S(1)}, bf16[1024,128]{1,0:T(8,128)(2,1)S(1)}, u32[]{:S(2)}, u32[]{:S(2)}) collective-permute-start(bf16[1024,128]{1,0:T(8,128)(2,1)S(1)} %pad_maximum_fusion.3), channel_id=1, source_target_pairs={{0,3},{1,0},{2,1},{3,2},{4,7},{5,4},{6,5},{7,6},{8,11},{9,8},{10,9... | collective-permute-start | bytes 786440 | tf_op jit(solution)/shard_map/ppermute | solution.py:40
  50.3 14.4 %all-to-all-start.1 = ((bf16[32,32,128]{2,1,0:T(8,128)(2,1)}), bf16[32,32,128]{2,1,0:T(8,128)(2,1)S(1)}, u32[]{:S(2)}, u32[]{:S(2)}) async-start(bf16[32,32,128]{2,1,0:T(8,128)(2,1)} %bitcast.3), calls=%async_computation.1 | async-start | bytes 524288 | tf_op jit(solution)/shard_map/all_to_all | solution.py:277
  65.7 9.8 %collective-permute-start.4 = (bf16[32,4096]{1,0:T(8,128)(2,1)S(1)}, bf16[32,4096]{1,0:T(8,128)(2,1)S(1)}, u32[]{:S(2)}, u32[]{:S(2)}) collective-permute-start(bf16[32,4096]{1,0:T(8,128)(2,1)S(1)} %get-tuple-element.36), channel_id=1, source_target_pairs={{0,3},{1,0},{2,1},{3,2},{4,7},{5,4},{6,5},{7,6},{8,11},{9,8},{10,9... | collective-permute-start | bytes 786440 | tf_op jit(solution)/shard_map/ppermute | solution.py:40
  68.9 10.4 %collective-permute-start.5 = (bf16[32,4096]{1,0:T(8,128)(2,1)S(1)}, bf16[32,4096]{1,0:T(8,128)(2,1)S(1)}, u32[]{:S(2)}, u32[]{:S(2)}) collective-permute-start(bf16[32,4096]{1,0:T(8,128)(2,1)S(1)} %get-tuple-element.36), channel_id=1, source_target_pairs={{0,1},{1,2},{2,3},{3,0},{4,5},{5,6},{6,7},{7,4},{8,9},{9,10},{10,1... | collective-permute-start | bytes 786440 | tf_op jit(solution)/shard_map/ppermute | solution.py:40
  75.5 6.7 %collective-permute-start.7 = (bf16[16,4096]{1,0:T(8,128)(2,1)S(1)}, bf16[16,4096]{1,0:T(8,128)(2,1)S(1)}, u32[]{:S(2)}, u32[]{:S(2)}) collective-permute-start(bf16[16,4096]{1,0:T(8,128)(2,1)S(1)} %slice.284), channel_id=1, source_target_pairs={{0,3},{1,0},{2,1},{3,2},{4,7},{5,4},{6,5},{7,6},{8,11},{9,8},{10,9... | collective-permute-start | bytes 393224 | tf_op jit(solution)/shard_map/ppermute | solution.py:40
  79.3 6.4 %collective-permute-start.6 = (bf16[16,4096]{1,0:T(8,128)(2,1)S(1)}, bf16[16,4096]{1,0:T(8,128)(2,1)S(1)}, u32[]{:S(2)}, u32[]{:S(2)}) collective-permute-start(bf16[16,4096]{1,0:T(8,128)(2,1)S(1)} %slice.283), channel_id=1, source_target_pairs={{0,1},{1,2},{2,3},{3,0},{4,5},{5,6},{6,7},{7,4},{8,9},{9,10},{10,1... | collective-permute-start | bytes 393224 | tf_op jit(solution)/shard_map/ppermute | solution.py:40
  85.7 14.8 %copy-start.13 = (f32[16]{0:T(128)S(1)}, f32[16]{0:T(128)}, u32[]{:S(2)}) copy-start(f32[16]{0:T(128)} %param.24) | copy-start | bytes 196
  85.7 16.3 %copy-start.5 = (f32[1280]{0:T(1024)S(1)}, f32[1280]{0:T(1024)}, u32[]{:S(2)}) copy-start(f32[1280]{0:T(1024)} %get-tuple-element.23) | copy-start | bytes 15364
  85.7 16.3 %copy-start.6 = (f32[1280]{0:T(1024)S(1)}, f32[1280]{0:T(1024)}, u32[]{:S(2)}) copy-start(f32[1280]{0:T(1024)} %get-tuple-element.24) | copy-start | bytes 15364
  85.8 51.1 %collective-permute-start.16 = (bf16[1024,512]{1,0:T(8,128)(2,1)}, bf16[1024,512]{1,0:T(8,128)(2,1)}, u32[]{:S(2)}, u32[]{:S(2)}) collective-permute-start(bf16[1024,512]{1,0:T(8,128)(2,1)} %param.31), channel_id=1, source_target_pairs={{0,3},{1,0},{2,1},{3,2},{4,7},{5,4},{6,5},{7,6},{8,11},{9,8},{10,9... | collective-permute-start | bytes 3145736 | tf_op jit(solution)/shard_map/ppermute | solution.py:40
  86.0 53.4 %collective-permute-start.17 = (bf16[1024,512]{1,0:T(8,128)(2,1)}, bf16[1024,512]{1,0:T(8,128)(2,1)}, u32[]{:S(2)}, u32[]{:S(2)}) collective-permute-start(bf16[1024,512]{1,0:T(8,128)(2,1)} %param.31), channel_id=1, source_target_pairs={{0,1},{1,2},{2,3},{3,0},{4,5},{5,6},{6,7},{7,4},{8,9},{9,10},{10,1... | collective-permute-start | bytes 3145736 | tf_op jit(solution)/shard_map/ppermute | solution.py:40
  87.9 1.6 copy-start
  98.9 13.2 %copy-start.10 = (pred[128,128]{1,0:T(8,128)(4,1)S(1)}, pred[128,128]{1,0:T(8,128)(4,1)}, u32[]{:S(2)}) copy-start(pred[128,128]{1,0:T(8,128)(4,1)} %iota_compare_fusion) | copy-start | bytes 49156
  99.0 13.1 %copy-start.15 = (f32[16]{0:T(128)S(1)}, f32[16]{0:T(128)}, u32[]{:S(2)}) copy-start(f32[16]{0:T(128)} %param.26) | copy-start | bytes 196
  99.0 2.9 %collective-permute-start.8 = (f32[3,1280]{1,0:T(4,128)S(1)}, f32[3,1280]{1,0:T(4,128)S(1)}, u32[]{:S(2)}, u32[]{:S(2)}) collective-permute-start(f32[3,1280]{1,0:T(4,128)S(1)} %slice.287), channel_id=1, source_target_pairs={{0,4},{4,8},{8,12},{12,16},{16,20},{20,24},{24,28},{28,32},{32,36}... | collective-permute-start | bytes 46088 | tf_op jit(solution)/shard_map/ppermute | solution.py:46
  104.3 17.4 %all-to-all-start.2 = ((bf16[32,48,128]{2,1,0:T(8,128)(2,1)}), bf16[32,48,128]{2,1,0:T(8,128)(2,1)S(1)}, u32[]{:S(2)}, u32[]{:S(2)}) async-start(bf16[32,48,128]{2,1,0:T(8,128)(2,1)} %maximum_maximum_fusion), calls=%async_computation.2 | async-start | bytes 786432 | tf_op jit(solution)/shard_map/all_to_all | solution.py:326
  114.3 22.0 %copy-start.11 = (f32[128,16]{0,1:T(8,128)S(1)}, f32[128,16]{0,1:T(8,128)}, u32[]{:S(2)}) copy-start(f32[128,16]{0,1:T(8,128)} %get-tuple-element.65) | copy-start | bytes 24580
  122.1 7.5 %copy-start.1 = (bf16[1024,512]{1,0:T(8,128)(2,1)S(1)}, bf16[1024,512]{1,0:T(8,128)(2,1)}, u32[]{:S(2)}) copy-start(bf16[1024,512]{1,0:T(8,128)(2,1)} %param.31) | copy-start | bytes 3145732
  123.4 12.8 %all-to-all-start.3 = ((bf16[32,32,128]{2,1,0:T(8,128)(2,1)}), bf16[32,32,128]{2,1,0:T(8,128)(2,1)S(1)}, u32[]{:S(2)}, u32[]{:S(2)}) async-start(bf16[32,32,128]{2,1,0:T(8,128)(2,1)} %bitcast.70), calls=%async_computation.3 | async-start | bytes 524288 | tf_op jit(solution)/shard_map/all_to_all | solution.py:343
  136.7 20.1 %copy-start.14 = (f32[1024]{0:T(1024)S(1)}, f32[1024]{0:T(1024)}, u32[]{:S(2)}) copy-start(f32[1024]{0:T(1024)} %param.27) | copy-start | bytes 12292
  138.0 14.2 %collective-permute-start.19 = (bf16[512,512]{1,0:T(8,128)(2,1)S(1)}, bf16[512,512]{1,0:T(8,128)(2,1)S(1)}, u32[]{:S(2)}, u32[]{:S(2)}) collective-permute-start(bf16[512,512]{1,0:T(8,128)(2,1)S(1)} %slice.312), channel_id=1, source_target_pairs={{0,3},{1,0},{2,1},{3,2},{4,7},{5,4},{6,5},{7,6},{8,11},{9,8},{10,9... | collective-permute-start | bytes 1572872 | tf_op jit(solution)/shard_map/ppermute | solution.py:40
  140.5 15.2 %collective-permute-start.18 = (bf16[512,512]{1,0:T(8,128)(2,1)S(1)}, bf16[512,512]{1,0:T(8,128)(2,1)S(1)}, u32[]{:S(2)}, u32[]{:S(2)}) collective-permute-start(bf16[512,512]{1,0:T(8,128)(2,1)S(1)} %slice.311), channel_id=1, source_target_pairs={{0,1},{1,2},{2,3},{3,0},{4,5},{5,6},{6,7},{7,4},{8,9},{9,10},{10,1... | collective-permute-start | bytes 1572872 | tf_op jit(solution)/shard_map/ppermute | solution.py:40
  161.6 10.3 %copy-start.4 = (s32[32,1,160]{2,0,1:T(8,128)S(1)}, s32[32,1,160]{2,0,1:T(8,128)}, u32[]{:S(2)}) copy-start(s32[32,1,160]{2,0,1:T(8,128)} %copy-done.3) | copy-start | bytes 61444
  161.6 18.2 %copy-start.8 = (f32[4096]{0:T(1024)S(1)}, f32[4096]{0:T(1024)}, u32[]{:S(2)}) copy-start(f32[4096]{0:T(1024)} %param.29) | copy-start | bytes 49156
  162.0 6.2 %collective-permute-start.9 = (bf16[16,4096]{1,0:T(8,128)(2,1)S(1)}, bf16[16,4096]{1,0:T(8,128)(2,1)S(1)}, u32[]{:S(2)}, u32[]{:S(2)}) collective-permute-start(bf16[16,4096]{1,0:T(8,128)(2,1)S(1)} %get-tuple-element.39), channel_id=1, source_target_pairs={{0,1},{1,2},{2,3},{3,0},{4,5},{5,6},{6,7},{7,4},{8,9},{9,10},{10,1... | collective-permute-start | bytes 393224 | tf_op jit(solution)/shard_map/ppermute | solution.py:40
  162.1 6.2 %collective-permute-start.11 = (bf16[16,4096]{1,0:T(8,128)(2,1)S(1)}, bf16[16,4096]{1,0:T(8,128)(2,1)S(1)}, u32[]{:S(2)}, u32[]{:S(2)}) collective-permute-start(bf16[16,4096]{1,0:T(8,128)(2,1)S(1)} %get-tuple-element.42), channel_id=1, source_target_pairs={{0,3},{1,0},{2,1},{3,2},{4,7},{5,4},{6,5},{7,6},{8,11},{9,8},{10,9... | collective-permute-start | bytes 393224 | tf_op jit(solution)/shard_map/ppermute | solution.py:40
  167.6 38.6 %collective-permute-start.20 = (bf16[4096,512]{1,0:T(8,128)(2,1)}, bf16[4096,512]{1,0:T(8,128)(2,1)}, u32[]{:S(2)}, u32[]{:S(2)}) collective-permute-start(bf16[4096,512]{1,0:T(8,128)(2,1)} %constant_dynamic-update-slice_fusion.11.refs_3_.refs_5_), channel_id=1, source_target_pairs={{0,4},{4,0},{8,12},{12,8},{16,20},{20,16},{24,28},{28,24},{32,36},... | collective-permute-start | bytes 12582920 | tf_op jit(solution)/shard_map/ppermute | solution.py:35
  168.3 8.2 %collective-permute-start.12 = (bf16[32,4096]{1,0:T(8,128)(2,1)S(1)}, bf16[32,4096]{1,0:T(8,128)(2,1)S(1)}, u32[]{:S(2)}, u32[]{:S(2)}) collective-permute-start(bf16[32,4096]{1,0:T(8,128)(2,1)S(1)} %pad_maximum_fusion.5), channel_id=1, source_target_pairs={{0,3},{1,0},{2,1},{3,2},{4,7},{5,4},{6,5},{7,6},{8,11},{9,8},{10,9... | collective-permute-start | bytes 786440 | tf_op jit(solution)/shard_map/ppermute | solution.py:40
  171.7 7.7 %collective-permute-start.10 = (bf16[32,4096]{1,0:T(8,128)(2,1)S(1)}, bf16[32,4096]{1,0:T(8,128)(2,1)S(1)}, u32[]{:S(2)}, u32[]{:S(2)}) collective-permute-start(bf16[32,4096]{1,0:T(8,128)(2,1)S(1)} %pad_maximum_fusion.4), channel_id=1, source_target_pairs={{0,1},{1,2},{2,3},{3,0},{4,5},{5,6},{6,7},{7,4},{8,9},{9,10},{10,1... | collective-permute-start | bytes 786440 | tf_op jit(solution)/shard_map/ppermute | solution.py:40
  179.9 8.5 %collective-permute-start.13 = (bf16[32,4096]{1,0:T(8,128)(2,1)S(1)}, bf16[32,4096]{1,0:T(8,128)(2,1)S(1)}, u32[]{:S(2)}, u32[]{:S(2)}) collective-permute-start(bf16[32,4096]{1,0:T(8,128)(2,1)S(1)} %fusion.19), channel_id=1, source_target_pairs={{0,8},{4,36},{8,16},{12,44},{16,24},{20,52},{24,0},{28,60},{32,40}... | collective-permute-start | bytes 786440 | tf_op jit(solution)/shard_map/ppermute | solution.py:40
  180.5 10.6 %collective-permute-start.14 = (bf16[32,4096]{1,0:T(8,128)(2,1)S(1)}, bf16[32,4096]{1,0:T(8,128)(2,1)S(1)}, u32[]{:S(2)}, u32[]{:S(2)}) collective-permute-start(bf16[32,4096]{1,0:T(8,128)(2,1)S(1)} %fusion.19), channel_id=1, source_target_pairs={{0,24},{4,100},{8,0},{12,108},{16,8},{20,116},{24,16},{28,124},{32... | collective-permute-start | bytes 786440 | tf_op jit(solution)/shard_map/ppermute | solution.py:40
  183.4 10.8 %collective-permute-start.15 = (bf16[32,4096]{1,0:T(8,128)(2,1)S(1)}, bf16[32,4096]{1,0:T(8,128)(2,1)S(1)}, u32[]{:S(2)}, u32[]{:S(2)}) collective-permute-start(bf16[32,4096]{1,0:T(8,128)(2,1)S(1)} %fusion.19), channel_id=1, source_target_pairs={{0,16},{4,68},{8,24},{12,76},{16,0},{20,84},{24,8},{28,92},{32,48}... | collective-permute-start | bytes 786440 | tf_op jit(solution)/shard_map/ppermute | solution.py:40
  188.4 10.5 %collective-permute-start.23 = (bf16[64,4096]{1,0:T(8,128)(2,1)S(1)}, bf16[64,4096]{1,0:T(8,128)(2,1)S(1)}, u32[]{:S(2)}, u32[]{:S(2)}) collective-permute-start(bf16[64,4096]{1,0:T(8,128)(2,1)S(1)} %pad_maximum_fusion.1.refs_0_), channel_id=1, source_target_pairs={{0,32},{4,12},{8,40},{12,20},{16,48},{20,28},{24,56},{28,4},{32,64... | collective-permute-start | bytes 1572872 | tf_op jit(solution)/shard_map/ppermute | solution.py:40
  194.1 9.2 %collective-permute-start.22 = (bf16[64,4096]{1,0:T(8,128)(2,1)S(1)}, bf16[64,4096]{1,0:T(8,128)(2,1)S(1)}, u32[]{:S(2)}, u32[]{:S(2)}) collective-permute-start(bf16[64,4096]{1,0:T(8,128)(2,1)S(1)} %constant_dynamic-update-slice_fusion.4.refs_1_), channel_id=1, source_target_pairs={{0,96},{4,28},{8,104},{12,4},{16,112},{20,12},{24,120},{28,20},{32... | collective-permute-start | bytes 1572872 | tf_op jit(solution)/shard_map/ppermute | solution.py:40
  195.9 13.2 %collective-permute-start.21 = (bf16[64,4096]{1,0:T(8,128)(2,1)S(1)}, bf16[64,4096]{1,0:T(8,128)(2,1)S(1)}, u32[]{:S(2)}, u32[]{:S(2)}) collective-permute-start(bf16[64,4096]{1,0:T(8,128)(2,1)S(1)} %pad_maximum_fusion.1.refs_0_), channel_id=1, source_target_pairs={{0,96},{4,28},{8,104},{12,4},{16,112},{20,12},{24,120},{28,20},{32... | collective-permute-start | bytes 1572872 | tf_op jit(solution)/shard_map/ppermute | solution.py:40
  196.2 12.9 %collective-permute-start.24 = (bf16[64,4096]{1,0:T(8,128)(2,1)S(1)}, bf16[64,4096]{1,0:T(8,128)(2,1)S(1)}, u32[]{:S(2)}, u32[]{:S(2)}) collective-permute-start(bf16[64,4096]{1,0:T(8,128)(2,1)S(1)} %constant_dynamic-update-slice_fusion.4.refs_1_), channel_id=1, source_target_pairs={{0,32},{4,12},{8,40},{12,20},{16,48},{20,28},{24,56},{28,4},{32,64... | collective-permute-start | bytes 1572872 | tf_op jit(solution)/shard_map/ppermute | solution.py:40
  198.9 19.2 %collective-permute-start.27 = (bf16[64,4096]{1,0:T(8,128)(2,1)S(1)}, bf16[64,4096]{1,0:T(8,128)(2,1)S(1)}, u32[]{:S(2)}, u32[]{:S(2)}) collective-permute-start(bf16[64,4096]{1,0:T(8,128)(2,1)S(1)} %collective-permute-done.23.refs_2_), channel_id=1, source_target_pairs={{0,32},{4,12},{8,40},{12,20},{16,48},{20,28},{24,56},{28,4},{32,64... | collective-permute-start | bytes 1572872 | tf_op jit(solution)/shard_map/ppermute | solution.py:40
  203.4 14.7 %collective-permute-start.28 = (bf16[64,4096]{1,0:T(8,128)(2,1)S(1)}, bf16[64,4096]{1,0:T(8,128)(2,1)S(1)}, u32[]{:S(2)}, u32[]{:S(2)}) collective-permute-start(bf16[64,4096]{1,0:T(8,128)(2,1)S(1)} %collective-permute-done.22.refs_1_), channel_id=1, source_target_pairs={{0,96},{4,28},{8,104},{12,4},{16,112},{20,12},{24,120},{28,20},{32... | collective-permute-start | bytes 1572872 | tf_op jit(solution)/shard_map/ppermute | solution.py:40
  215.3 14.5 %collective-permute-start.26 = (f32[8,128]{1,0:T(8,128)S(1)}, f32[8,128]{1,0:T(8,128)S(1)}, u32[]{:S(2)}, u32[]{:S(2)}) collective-permute-start(f32[8,128]{1,0:T(8,128)S(1)} %get-tuple-element.54), channel_id=1, source_target_pairs={{0,96},{4,28},{8,104},{12,4},{16,112},{20,12},{24,120},{28,20},{32... | collective-permute-start | bytes 12296 | tf_op jit(solution)/shard_map/ppermute | solution.py:40
  218.1 11.6 %collective-permute-start.25 = (f32[8,128]{1,0:T(8,128)S(1)}, f32[8,128]{1,0:T(8,128)S(1)}, u32[]{:S(2)}, u32[]{:S(2)}) collective-permute-start(f32[8,128]{1,0:T(8,128)S(1)} %get-tuple-element.53), channel_id=1, source_target_pairs={{0,32},{4,12},{8,40},{12,20},{16,48},{20,28},{24,56},{28,4},{32,64... | collective-permute-start | bytes 12296 | tf_op jit(solution)/shard_map/ppermute | solution.py:40
  223.2 6.6 %collective-permute-start.29 = (f32[8,128]{1,0:T(8,128)S(1)}, f32[8,128]{1,0:T(8,128)S(1)}, u32[]{:S(2)}, u32[]{:S(2)}) collective-permute-start(f32[8,128]{1,0:T(8,128)S(1)} %shard_map.158), channel_id=1, source_target_pairs={{0,64},{4,20},{8,72},{12,28},{16,80},{20,4},{24,88},{28,12},{32,96... | collective-permute-start | bytes 12296 | tf_op jit(solution)/shard_map/ppermute | solution.py:40
  230.3 5.2 %collective-permute-start.32 = (f32[5,32]{1,0:T(8,128)S(1)}, f32[5,32]{1,0:T(8,128)S(1)}, u32[]{:S(2)}, u32[]{:S(2)}) collective-permute-start(f32[5,32]{1,0:T(8,128)S(1)} %bitcast.348), channel_id=1, source_target_pairs={{0,16},{4,68},{8,24},{12,76},{16,0},{20,84},{24,8},{28,92},{32,48}... | collective-permute-start | bytes 1928 | tf_op jit(solution)/shard_map/ppermute | solution.py:40
  231.4 4.8 %collective-permute-start.31 = (f32[5,32]{1,0:T(8,128)S(1)}, f32[5,32]{1,0:T(8,128)S(1)}, u32[]{:S(2)}, u32[]{:S(2)}) collective-permute-start(f32[5,32]{1,0:T(8,128)S(1)} %bitcast.349), channel_id=1, source_target_pairs={{0,8},{4,36},{8,16},{12,44},{16,24},{20,52},{24,0},{28,60},{32,40}... | collective-permute-start | bytes 1928 | tf_op jit(solution)/shard_map/ppermute | solution.py:40
  231.4 4.8 %collective-permute-start.30 = (f32[5,32]{1,0:T(8,128)S(1)}, f32[5,32]{1,0:T(8,128)S(1)}, u32[]{:S(2)}, u32[]{:S(2)}) collective-permute-start(f32[5,32]{1,0:T(8,128)S(1)} %bitcast.350), channel_id=1, source_target_pairs={{0,24},{4,100},{8,0},{12,108},{16,8},{20,116},{24,16},{28,124},{32... | collective-permute-start | bytes 1928 | tf_op jit(solution)/shard_map/ppermute | solution.py:40
Sparse Core Ops, SparseCore 0:
  9.5 64.9 all-gather.1

commit v3 on v2

--- a/solution.py
+++ b/solution.py
@@ -50,9 +50,10 @@
     half = value.shape[0] // 2
     left = moved(value, shift, 1)
     right = moved(value, shift, -1)
+    left, right = lax.optimization_barrier((left, right))
     far_low = moved(left[:half], shift, 1)
     far_high = moved(right[half:], shift, -1)
-    return value, right, jnp.concatenate([far_low, far_high]), left
+    return value, right, far_low, far_high, left
 
 
 def ring_reduce(parts, shift):
@@ -60,6 +61,7 @@
     half = own.shape[0] // 2
     from_left = moved(far[:half], shift, 1)
     from_right = moved(far[half:], shift, -1)
+    from_left, from_right = lax.optimization_barrier((from_left, from_right))
     ahead = jnp.concatenate([ahead[:half] + from_left, ahead[half:]])
     behind = jnp.concatenate([behind[:half], behind[half:] + from_right])
     left = moved(ahead, shift, 1)
@@ -68,42 +70,168 @@
     return own.astype(f32) + left.astype(f32) + right.astype(f32)
 
 
-def look_up(ids, table):
-    count, (table_rows, cols) = ids.shape[0], table.shape
-    depth, block = 512, 1024
-    parts = table_rows // depth
+def in_vmem():
+    return pl.BlockSpec(memory_space=pltpu.VMEM)
+
+
+def spot(index):
+    group = jnp.bitwise_and(jnp.right_shift(index, 5), 3)
+    return group * 128 + jnp.right_shift(index, 7) * 32 + jnp.bitwise_and(index, 31)
+
+
+def pack_columns(table):
+    rows = table.shape[0] // 4
     bf16, f32 = jnp.bfloat16, jnp.float32
 
-    def kernel(ids_ref, table_ref, out_ref):
-        lane = lax.broadcasted_iota(jnp.int32, (128, 128), 1)
-        for r in range(block // 128):
-            column = jnp.broadcast_to(ids_ref[0, r : r + 1, :], (128, 128)).T
-            low = jnp.bitwise_and(column, depth - 1)
-            rest = jnp.right_shift(column, depth.bit_length() - 1)
-            picks = [(low == lane + 128 * c).astype(f32).astype(bf16) for c in range(depth // 128)]
-            found = jnp.dot(
-                jnp.concatenate(picks, axis=1), table_ref[...], preferred_element_type=f32
-            )
-            chosen = jnp.zeros((128, cols), f32)
-            for g in range(parts):
-                chosen = jnp.where(rest == g, found[:, g * cols : (g + 1) * cols], chosen)
-            out_ref[r * 128 : (r + 1) * 128, :] = chosen.astype(bf16)
-
-    side_by_side = table.reshape(parts, depth, cols).transpose(1, 0, 2).reshape(depth, parts * cols)
+    def kernel(table_ref, out_ref):
+        row = lax.broadcasted_iota(jnp.int32, (512, 512), 0)
+        col = lax.broadcasted_iota(jnp.int32, (512, 512), 1)
+        swap = (col == spot(row)).astype(f32).astype(bf16)
+        for at in range(0, rows, 256):
+            wide = [table_ref[g * rows + at : g * rows + at + 256, :] for g in range(4)]
+            wide = jnp.concatenate(wide, axis=1)
+            swapped = jnp.dot(wide, swap, preferred_element_type=f32).astype(bf16)
+            for h in range(4):
+                out_ref[h, at : at + 256, :] = swapped[:, h * 128 : (h + 1) * 128]
+
     return pl.pallas_call(
         kernel,
-        grid=(count // block,),
+        in_specs=[in_vmem()],
+        out_specs=in_vmem(),
+        out_shape=jax.ShapeDtypeStruct((4, rows, 128), bf16),
+        compiler_params=pltpu.CompilerParams(vmem_limit_bytes=16 << 20),
+        cost_estimate=pl.CostEstimate(
+            flops=2 * rows * 512 * 512, bytes_accessed=8 * rows * 128 * 2, transcendentals=0
+        ),
+    )(table)
+
+
+def look_up(ids, table):
+    steps = ids.shape[0]
+    bf16, f32 = jnp.bfloat16, jnp.float32
+
+    def kernel(ids_ref, table_ref, out_ref, side_ref):
+        @pl.when(pl.program_id(0) == 0)
+        def _():
+            for q in range(8):
+                rows = pl.ds((q % 2) * 512, 512)
+                side_ref[:, q * 128 : (q + 1) * 128] = table_ref[q // 2, rows, :]
+
+        lane = lax.broadcasted_iota(jnp.int32, (128, 128), 1)
+        row = lax.broadcasted_iota(jnp.int32, (128, 128), 0)
+        lane_group = jnp.right_shift(lane, 5)
+        same = jnp.bitwise_and(row, 31) == jnp.bitwise_and(lane, 31)
+        total = jnp.zeros((128, 128), f32)
+        for g in range(4):
+            column = jnp.broadcast_to(ids_ref[0, g : g + 1, :], (128, 128)).T
+            low = jnp.bitwise_and(column, 511)
+            picks = [(low == lane + 128 * c).astype(f32).astype(bf16) for c in range(4)]
+            picks = jnp.concatenate(picks, axis=1)
+            found = jnp.dot(picks, side_ref[...], preferred_element_type=f32)
+            rest = jnp.right_shift(column, 9)
+            here = jnp.bitwise_and(jnp.right_shift(rest, 1), 3) == lane_group
+            block = jnp.where(here, jnp.bitwise_and(rest, 25), -1)
+            chosen = jnp.zeros((128, 128), f32)
+            for q in range(8):
+                wanted = (q // 2) * 8 + q % 2
+                chosen = jnp.where(block == wanted, found[:, q * 128 : (q + 1) * 128], chosen)
+            fold = jnp.logical_and(same, lane_group == g).astype(f32).astype(bf16)
+            total = total + jnp.dot(chosen.astype(bf16), fold, preferred_element_type=f32)
+        out_ref[...] = total.astype(bf16)
+
+    return pl.pallas_call(
+        kernel,
+        grid=(steps,),
         in_specs=[
-            pl.BlockSpec((1, block // 128, 128), lambda i: (i, 0, 0)),
-            pl.BlockSpec((depth, parts * cols), lambda i: (0, 0)),
+            pl.BlockSpec((1, 4, 128), lambda i: (i, 0, 0)),
+            pl.BlockSpec((4, 1024, 128), lambda i: (0, 0, 0)),
         ],
-        out_specs=pl.BlockSpec((block, cols), lambda i: (i, 0)),
-        out_shape=jax.ShapeDtypeStruct((count, cols), bf16),
-        compiler_params=pltpu.CompilerParams(vmem_limit_bytes=24 << 20),
+        out_specs=pl.BlockSpec((128, 128), lambda i: (i, 0)),
+        out_shape=jax.ShapeDtypeStruct((steps * 128, 128), bf16),
+        scratch_shapes=[pltpu.VMEM((512, 1024), bf16)],
+        compiler_params=pltpu.CompilerParams(vmem_limit_bytes=16 << 20),
         cost_estimate=pl.CostEstimate(
-            flops=2 * count * table_rows * cols, bytes_accessed=4 << 20, transcendentals=0
+            flops=2 * steps * 512 * 512 * 1024, bytes_accessed=2 << 20, transcendentals=0
         ),
-    )(ids.reshape(count // block, block // 128, 128), side_by_side)
+    )(ids, table)
+
+
+def assemble(pieces, head, gain):
+    own, right, far_low, far_high, left = pieces
+    blocks, quarter = own.shape[:2]
+    rows, width = blocks * quarter, blocks * 128
+    bf16, f32 = jnp.bfloat16, jnp.float32
+
+    def kernel(head_ref, own_ref, right_ref, low_ref, high_ref, left_ref, gain_ref, normed_ref, quarter_ref, emb_ref):
+        head = head_ref[0]
+        row = lax.broadcasted_iota(jnp.int32, (512, 512), 0)
+        col = lax.broadcasted_iota(jnp.int32, (512, 512), 1)
+        source = jnp.bitwise_and(jnp.right_shift(row, 7) + head, 3)
+        goal = spot(source * 128 + jnp.bitwise_and(row, 127))
+        swap = (col == goal).astype(f32).astype(bf16)
+        for at in range(0, rows, 256):
+            if at < rows // 2:
+                far = low_ref[at : at + 256, :]
+            else:
+                far = high_ref[at - rows // 2 : at - rows // 2 + 256, :]
+            here = pl.ds(at, 256)
+            wide = jnp.concatenate([own_ref[here, :], right_ref[here, :], far, left_ref[here, :]], axis=1)
+            swapped = jnp.dot(wide, swap, preferred_element_type=f32).astype(bf16)
+            for c in range(256 // quarter):
+                column = (at // quarter + c) * 128
+                for q in range(4):
+                    emb_ref[q * quarter : (q + 1) * quarter, column : column + 128] = swapped[
+                        c * quarter : (c + 1) * quarter, q * 128 : (q + 1) * 128
+                    ]
+        quarter_ref[...] = emb_ref[pl.ds(pl.multiple_of(head * quarter, quarter), quarter), :]
+        for q in range(4):
+            values = emb_ref[q * quarter : (q + 1) * quarter, :].astype(f32)
+            scale = lax.rsqrt(jnp.mean(values * values, axis=1, keepdims=True) + 1e-05)
+            normed_ref[q * quarter : (q + 1) * quarter, :] = (values * scale * gain_ref[...]).astype(bf16)
+
+    flat = [piece.reshape(-1, 128) for piece in (own, right, far_low, far_high, left)]
+    return pl.pallas_call(
+        kernel,
+        in_specs=[pl.BlockSpec(memory_space=pltpu.SMEM)] + [in_vmem()] * 6,
+        out_specs=[in_vmem()] * 2,
+        out_shape=[
+            jax.ShapeDtypeStruct((4 * quarter, width), bf16),
+            jax.ShapeDtypeStruct((quarter, width), bf16),
+        ],
+        scratch_shapes=[pltpu.VMEM((4 * quarter, width), bf16)],
+        compiler_params=pltpu.CompilerParams(vmem_limit_bytes=16 << 20),
+        cost_estimate=pl.CostEstimate(
+            flops=2 * rows * 512 * 512, bytes_accessed=4 << 20, transcendentals=0
+        ),
+    )(head, *flat, gain.reshape(1, width))
+
+
+def project_out(gated, weights, head):
+    count, depth = gated.shape
+    width, tile = weights.shape[1], 1024
+    quarter = count // 4
+
+    def kernel(head_ref, gated_ref, weights_ref, out_ref):
+        product = jnp.dot(gated_ref[...], weights_ref[...], preferred_element_type=jnp.float32)
+        for q in range(4):
+            ahead = jnp.bitwise_and(q - head_ref[0], 3)
+            out_ref[ahead] = product[q * quarter : (q + 1) * quarter, :].astype(jnp.bfloat16)
+
+    return pl.pallas_call(
+        kernel,
+        grid=(width // tile,),
+        in_specs=[
+            pl.BlockSpec(memory_space=pltpu.SMEM),
+            pl.BlockSpec((count, depth), lambda i: (0, 0)),
+            pl.BlockSpec((depth, tile), lambda i: (0, i)),
+        ],
+        out_specs=pl.BlockSpec((4, quarter, tile), lambda i: (0, 0, i)),
+        out_shape=jax.ShapeDtypeStruct((4, quarter, width), jnp.bfloat16),
+        compiler_params=pltpu.CompilerParams(vmem_limit_bytes=12 << 20),
+        cost_estimate=pl.CostEstimate(
+            flops=2 * count * depth * width, bytes_accessed=2 * depth * width, transcendentals=0
+        ),
+    )(head, gated, weights)
 
 
 def project(rows, w_zx, w_bc, w_dt):
@@ -138,7 +266,7 @@
         ],
         out_specs=[pl.BlockSpec((count, n), lambda i: (0, 0)) for n in widths],
         out_shape=[jax.ShapeDtypeStruct((count, n), f32) for n in widths],
-        compiler_params=pltpu.CompilerParams(vmem_limit_bytes=40 << 20),
+        compiler_params=pltpu.CompilerParams(vmem_limit_bytes=20 << 20),
         cost_estimate=pl.CostEstimate(
             flops=2 * count * width * sum(widths),
             bytes_accessed=2 * width * sum(widths),
@@ -175,59 +303,77 @@
     count = sum(piece.shape[0] for piece in pieces)
     width, columns = tables[0].shape
     tile = 256
+    tiles = columns // tile
     f32 = jnp.float32
 
     def kernel(*refs):
         piece_refs = refs[: len(pieces)]
-        wanted_ref, *table_refs, out_ref, rows_ref, logits_ref = refs[len(pieces) :]
-        start = 0
-        for ref in piece_refs:
-            rows_ref[start : start + ref.shape[0], :] = ref[...]
-            start += ref.shape[0]
-        rows = rows_ref[...]
-        for place, table_ref in enumerate(table_refs):
-            for j in range(columns // tile):
-                at = place * columns + j * tile
-                logits_ref[:, at : at + tile] = jnp.dot(
-                    rows, table_ref[:, j * tile : (j + 1) * tile], preferred_element_type=f32
+        wanted_ref, first_ref, second_ref, out_ref, rows_ref, logits_ref = refs[len(pieces) :]
+        step = pl.program_id(0)
+
+        @pl.when(step == 0)
+        def _():
+            start = 0
+            for ref in piece_refs:
+                rows_ref[start : start + ref.shape[0], :] = ref[...]
+                start += ref.shape[0]
+
+        @pl.when(step < tiles)
+        def _():
+            logits_ref[step] = jnp.dot(rows_ref[...], first_ref[...], preferred_element_type=f32)
+
+        @pl.when(step >= tiles)
+        def _():
+            logits_ref[step] = jnp.dot(rows_ref[...], second_ref[...], preferred_element_type=f32)
+
+        @pl.when(step == 2 * tiles - 1)
+        def _():
+            lane = lax.broadcasted_iota(jnp.int32, (128, 128), 1)
+            column = lax.broadcasted_iota(jnp.int32, (128, columns), 1)
+            for r in range(count // 128):
+                logits = [logits_ref[j, r * 128 : (r + 1) * 128, :] for j in range(2 * tiles)]
+                logits = jnp.concatenate(logits, axis=1)
+                peak = jnp.max(logits, axis=1, keepdims=True)
+                shifted = logits - peak
+                weights = jnp.exp(shifted)
+                first = weights * shifted
+                target = jnp.zeros((128, 1), f32)
+                for place in range(2):
+                    aim = jnp.broadcast_to(wanted_ref[place, r : r + 1, :], (128, 128)).T[:, :1]
+                    part = logits[:, place * columns : (place + 1) * columns]
+                    target += jnp.sum(jnp.where(column == aim, part, 0.0), axis=1, keepdims=True)
+                stats = (
+                    peak,
+                    jnp.sum(weights, axis=1, keepdims=True),
+                    jnp.sum(first, axis=1, keepdims=True),
+                    jnp.sum(first * shifted, axis=1, keepdims=True),
+                    target,
                 )
-        lane = lax.broadcasted_iota(jnp.int32, (128, 128), 1)
-        column = lax.broadcasted_iota(jnp.int32, (128, columns), 1)
-        for r in range(count // 128):
-            logits = logits_ref[r * 128 : (r + 1) * 128, :]
-            peak = jnp.max(logits, axis=1, keepdims=True)
-            shifted = logits - peak
-            weights = jnp.exp(shifted)
-            first = weights * shifted
-            target = jnp.zeros((128, 1), f32)
-            for place in range(len(table_refs)):
-                aim = jnp.broadcast_to(wanted_ref[place, r : r + 1, :], (128, 128)).T[:, :1]
-                part = logits[:, place * columns : (place + 1) * columns]
-                target += jnp.sum(jnp.where(column == aim, part, 0.0), axis=1, keepdims=True)
-            stats = (
-                peak,
-                jnp.sum(weights, axis=1, keepdims=True),
-                jnp.sum(first, axis=1, keepdims=True),
-                jnp.sum(first * shifted, axis=1, keepdims=True),
-                target,
-            )
-            table = jnp.zeros((128, 128), f32)
-            for k, stat in enumerate(stats):
-                table = jnp.where(lane == k, stat, table)
-            out_ref[:, r * 128 : (r + 1) * 128] = table.T[:8]
-
-    whole = pl.BlockSpec(memory_space=pltpu.VMEM)
-    every = len(tables) * columns
+                table = jnp.zeros((128, 128), f32)
+                for k, stat in enumerate(stats):
+                    table = jnp.where(lane == k, stat, table)
+                out_ref[:, r * 128 : (r + 1) * 128] = table.T[:8]
+
+    every = 2 * columns
     return pl.pallas_call(
         kernel,
-        in_specs=[whole] * (len(pieces) + 1 + len(tables)),
-        out_specs=whole,
+        grid=(2 * tiles,),
+        in_specs=[pl.BlockSpec(piece.shape, lambda i: (0, 0)) for piece in pieces]
+        + [
+            pl.BlockSpec(wanted.shape, lambda i: (0, 0, 0)),
+            pl.BlockSpec((width, tile), lambda i: (0, jnp.minimum(i, tiles - 1))),
+            pl.BlockSpec((width, tile), lambda i: (0, jnp.maximum(i - tiles, 0))),
+        ],
+        out_specs=pl.BlockSpec((8, count), lambda i: (0, 0)),
         out_shape=jax.ShapeDtypeStruct((8, count), f32),
-        scratch_shapes=[pltpu.VMEM((count, width), jnp.bfloat16), pltpu.VMEM((count, every), f32)],
-        compiler_params=pltpu.CompilerParams(vmem_limit_bytes=24 << 20),
+        scratch_shapes=[
+            pltpu.VMEM((count, width), jnp.bfloat16),
+            pltpu.VMEM((2 * tiles, count, tile), f32),
+        ],
+        compiler_params=pltpu.CompilerParams(vmem_limit_bytes=20 << 20),
         cost_estimate=pl.CostEstimate(
             flops=2 * count * width * every,
-            bytes_accessed=2 * count * width,
+            bytes_accessed=2 * width * every,
             transcendentals=count * every,
         ),
     )(*pieces, wanted, *tables)
@@ -259,35 +405,22 @@
     model_width = pre_gain.shape[0]
     head_pos = lax.axis_index("head")
     ctx_pos = lax.axis_index("ctx")
+    head_at = head_pos[None].astype(jnp.int32)
     w_out_full = lax.all_gather(w_out, "ctx", axis=1, tiled=True)
+    vocab_own = lax.all_gather(lm_head, "head", axis=0, tiled=True)
+    vocab_other = swap_core(vocab_own)
 
     packed = jnp.concatenate([token_ids, targets])
     packed = jnp.broadcast_to(packed[None], (ctx_count, tok_rows + quarter))
     packed = lax.all_to_all(packed, "ctx", 0, 0, tiled=True)
-    all_ids = packed[:, :tok_rows].reshape(ctx_count, head_count, quarter)
+    all_ids = packed[:, :tok_rows].reshape(ctx_count // 4, 4, head_count, quarter)
     group_targets = packed[:, tok_rows:]
 
-    table_rows, slice_cols = embed.shape
-    by_owner = jnp.roll(all_ids, -head_pos, axis=1).transpose(1, 0, 2)
-    local_ids = by_owner.reshape(-1) - head_pos * table_rows
-    looked = look_up(local_ids, embed)
-    looked = looked.reshape(head_count, ctx_count * quarter, slice_cols)
-    mine = ring_reduce([looked[k] for k in range(4)], shift_head).astype(bf16)
-    mine = mine.reshape(ctx_count, quarter, slice_cols)
-    own_emb = lax.all_to_all(mine, "ctx", split_axis=0, concat_axis=2, tiled=True)
-    own_emb = own_emb.reshape(quarter, model_width)
-    normed_own = rms_scale(own_emb.astype(f32), pre_gain).astype(bf16)
-    normed_in = jnp.zeros((tok_rows, model_width), bf16)
-    for ahead, block in enumerate(ring_gather(normed_own, shift_head)):
-        row = ((head_pos + ahead) % head_count) * quarter
-        normed_in = lax.dynamic_update_slice_in_dim(normed_in, block, row, 0)
-
-    normed_in, lm_head = lax.optimization_barrier((normed_in, lm_head))
-    vocab_own = jnp.zeros((model_width, lm_head.shape[1]), bf16)
-    for ahead, block in enumerate(ring_gather(lm_head, shift_head)):
-        row = ((head_pos + ahead) % head_count) * lm_head.shape[0]
-        vocab_own = lax.dynamic_update_slice_in_dim(vocab_own, block, row, 0)
-    vocab_other = swap_core(vocab_own)
+    columns = lax.all_to_all(pack_columns(embed), "head", 0, 0, tiled=True)
+    all_ids = all_ids.transpose(0, 2, 1, 3).reshape(ctx_count // 4, head_count, 4 * quarter)
+    mine = look_up(all_ids, columns).reshape(ctx_count, quarter, 128)
+    mine = lax.all_to_all(mine, "ctx", 0, 0, tiled=True)
+    normed_in, own_emb = assemble(ring_gather(mine, shift_head), head_at, pre_gain)
 
     channels = w_zx.shape[2]
     group_cols = w_bc.shape[2]
@@ -351,10 +484,8 @@
     gated_raw = mixer_out.reshape(tok_rows, channels) * jax.nn.silu(gate_z)
     gated_out = rms_scale(gated_raw, norm_gain).astype(bf16)
 
-    partial_out = jnp.dot(gated_out, w_out_full, preferred_element_type=f32).astype(bf16)
-    partial_out = partial_out.reshape(head_count, quarter, model_width)
-    by_owner_out = jnp.roll(partial_out, -head_pos, axis=0)
-    summed_out = ring_reduce([by_owner_out[k] for k in range(4)], shift_head)
+    partial_out = project_out(gated_out, w_out_full, head_at)
+    summed_out = ring_reduce([partial_out[k] for k in range(4)], shift_head)
     residual = (own_emb.astype(f32) + summed_out).astype(bf16)
     normed_out = rms_scale(residual.astype(f32), final_gain).astype(bf16)
 
@@ -368,23 +499,24 @@
     near_right = moved(near, along_second, -1)
     rest_left = moved(rest, along_second, 1)
     rest_right = moved(rest, along_second, -1)
-    near_far = moved(near_left, along_second, 1)
-    rest_far = moved(rest_right, along_second, -1)
-    pieces = ((near, rest), (near_right, rest_right), (near_far, rest_far), (near_left, rest_left))
-    order = (0, 3, 1, 2)
     y_pos, z_pos, core = ctx_pos // 8, (ctx_pos // 2) % 4, ctx_pos % 2
     by_chip = lax.dynamic_index_in_dim(group_targets.reshape(4, 4, 2, quarter), core, 2, False)
     by_chip = jnp.roll(by_chip, (-y_pos, -z_pos), (0, 1))
     by_chip = jnp.where(core == 0, by_chip, by_chip.transpose(1, 0, 2))
+    order = (0, 3, 1, 2)
     by_chip = jnp.stack([by_chip[:, k] for k in order], axis=1).reshape(4, 1, 4 * quarter)
     vocab_width = vocab_own.shape[1]
     by_chip = jnp.stack([by_chip - ctx_pos * vocab_width, by_chip - (ctx_pos ^ 1) * vocab_width])
     tables = (vocab_own, vocab_other)
     rows = 4 * quarter
-    stats = [vocab_stats(pieces[0], by_chip[:, 0], tables)]
-    sides = vocab_stats(pieces[1] + pieces[3], jnp.concatenate([by_chip[:, 1], by_chip[:, 3]], axis=1), tables)
+    stats = [vocab_stats((near, rest), by_chip[:, 0], tables)]
+    near_left, rest_right, stats[0] = lax.optimization_barrier((near_left, rest_right, stats[0]))
+    near_far = moved(near_left, along_second, 1)
+    rest_far = moved(rest_right, along_second, -1)
+    aims = jnp.concatenate([by_chip[:, 1], by_chip[:, 3]], axis=1)
+    sides = vocab_stats((near_right, rest_right, near_left, rest_left), aims, tables)
     stats.append(moved(sides[:, :rows], along_second, 1))
-    stats.append(moved(vocab_stats(pieces[2], by_chip[:, 2], tables), along_second, 2))
+    stats.append(moved(vocab_stats((near_far, rest_far), by_chip[:, 2], tables), along_second, 2))
     stats.append(moved(sides[:, rows:], along_second, -1))
     merged = tuple(stats[0][:5])
     for other in (stats[1], stats[3], stats[2]):

time: 245 us -> 233 us (0.951)
  waiting for transfers between devices: 88.1 us -> 70.7 us
  starting transfers between devices: 72.5 us -> 59.2 us
  blocking collectives: 0 us -> 12.6 us
  Pallas kernels: 31.1 us -> 40.1 us
  local copies, waits for them, and re-layouts: 19.7 us -> 26.1 us
  matrix products: 9.5 us -> 4.08 us
  other arithmetic: 8.51 us -> 5.23 us
    ppermute x31 -> x23, waiting for transfers between devices: 59.4 us -> 34.4 us  [moved(): return lax.ppermute(value, axis, pairs)]
    unnamed x47 -> x76, local copies, waits for them, and re-layouts: 3.99 us -> 20.1 us
    ppermute x31 -> x23, starting transfers between devices: 47.3 us -> 32.3 us  [moved(): return lax.ppermute(value, axis, pairs)]
    all_to_all x0 -> x1, blocking collectives: none -> 12.6 us  [on_device(): state_in = lax.all_to_all(entering, 'ctx', 0, 0, tiled=True)]
    pallas_call x4 -> x7, Pallas kernels: 21.6 us -> 33.5 us  [the longest x3 17.1 us: vocab_stats(): pl.pallas_call(kernel, grid=(2 * tiles,), in_specs=[pl.BlockSpec(piece.sh...]
    all_to_all x2, waiting for transfers between devices: 15.4 us -> 23.2 us  [the longest x1 14.5 us: on_device(): columns = lax.all_to_all(pack_columns(embed), 'head', 0, 0, tiled=True)]
    dynamic_update_slice x5 -> x0, local copies, waits for them, and re-layouts: 5.75 us -> none  [the longest x3 5.7 us: on_device(): vocab_own = lax.dynamic_update_slice_in_dim(vocab_own, block, row, 0)]
    dot_general x1 -> x0, matrix products: 4.79 us -> none  [on_device(): jnp.dot(gated_out, w_out_full, preferred_element_type=f32).astype(bf16)]
  transfers between devices with their start and end apart: 38 -> 31, of which waited for: 23 -> 15; matrix products, arithmetic and copies ran while one was open for 12% -> 7% of each run, Pallas kernels for 13% -> 17%
where the time goes in v3:
time: 233 us; the launch traced here: 232 us
  waiting for transfers between devices  70.7 us (30%)
  starting transfers between devices  59.2 us (25%)
  Pallas kernels  40.1 us (17%)
  local copies, waits for them, and re-layouts  26.1 us (11%)
  between operations  14.1 us (6%)
  blocking collectives  12.6 us (5%)
  other arithmetic  5.23 us (2%)
  matrix products  4.08 us (2%)
    ppermute x23, waiting for transfers between devices, moved(): return lax.ppermute(value, axis, pairs)  34.4 us
    ppermute x23, starting transfers between devices, moved(): return lax.ppermute(value, axis, pairs)  32.3 us
    unnamed x76, local copies, waits for them, and re-layouts  20.1 us
    pallas_call x3, Pallas kernels, vocab_stats(): pl.pallas_call(kernel, grid=(2 * tiles,), in_specs=[pl.BlockSpec(piece.sh...  17.1 us
    all_to_all x1, waiting for transfers between devices, on_device(): columns = lax.all_to_all(pack_columns(embed), 'head', 0, 0, tiled=True)  14.5 us
    all_to_all x1, blocking collectives, on_device(): state_in = lax.all_to_all(entering, 'ctx', 0, 0, tiled=True)  12.6 us
    pallas_call x1, Pallas kernels, look_up(): pl.pallas_call(kernel, grid=(steps,), in_specs=[pl.BlockSpec((1, 4, 128),...  10 us
    all_to_all x1, waiting for transfers between devices, on_device(): mine = lax.all_to_all(mine, 'ctx', 0, 0, tiled=True)  8.73 us
  transfers between devices with their start and end apart: 31, of which 15 were waited for; matrix products, arithmetic and copies ran while one was open for 7% of the time, Pallas kernels for 17%

profile of v3, /device:TPU:0, one launch (start us, length us, event | category | flops | bytes accessed | tf_op | source)
XLA Modules:
  0.0 232.2 jit_solution(7628051332351573269)
XLA Ops:
  6.5 0.7 all-gather.3.cloned.1.call-update
  7.3 0.7 pad_add_fusion.3
  7.9 0.6 broadcast_in_dim.36
  8.6 8.4 %all-to-all-start = ((s32[32,1,160]{2,1,0:T(1,128)}), s32[32,1,160]{2,1,0:T(1,128)S(1)}, u32[]{:S(2)}, u32[]{:S(2)}) async-start(s32[32,1,160]{2,1,0:T(1,128)} %broadcast_in_dim.36), calls=%async_computation | async-start | bytes 65536 | tf_op jit(solution)/shard_map/all_to_all | solution.py:415
  17.0 1.2 copy-done.4
  18.2 1.8 shard_map.154
  20.0 4.4 %all-to-all-done = s32[32,1,160]{2,1,0:T(1,128)S(1)} async-done(((s32[32,1,160]{2,1,0:T(1,128)}), s32[32,1,160]{2,1,0:T(1,128)S(1)}, u32[]{:S(2)}, u32[]{:S(2)}) %all-to-all-start) | async-done | bytes 20512 | tf_op jit(solution)/shard_map/all_to_all | solution.py:415
  24.4 4.3 %all-to-all-start.1 = ((bf16[4,1024,128]{2,1,0:T(8,128)(2,1)}), bf16[4,1024,128]{2,1,0:T(8,128)(2,1)S(1)}, u32[]{:S(2)}, u32[]{:S(2)}) async-start(bf16[4,1024,128]{2,1,0:T(8,128)(2,1)} %shard_map.154), calls=%async_computation.1 | async-start | bytes 2097152 | tf_op jit(solution)/shard_map/all_to_all | solution.py:419
  29.6 14.5 %all-to-all-done.1.table_ref = bf16[4,1024,128]{2,1,0:T(8,128)(2,1)S(1)} async-done(((bf16[4,1024,128]{2,1,0:T(8,128)(2,1)}), bf16[4,1024,128]{2,1,0:T(8,128)(2,1)S(1)}, u32[]{:S(2)}, u32[]{:S(2)}) %all-to-all-start.1) | async-done | bytes 1048608 | tf_op jit(solution)/shard_map/all_to_all | solution.py:419
  44.1 10.0 %shard_map.155 = bf16[1024,128]{1,0:T(8,128)(2,1)} custom-call(s32[8,4,128]{2,1,0:T(4,128)S(1)} %reshape.205.ids_ref, bf16[4,1024,128]{2,1,0:T(8,128)(2,1)S(1)} %all-to-all-done.1.table_ref), custom_call_target="tpu_custom_call" | custom-call | flops 4294967296 | bytes 2097152 | tf_op jit(solution)/shard_map/pallas_call | solution.py:142
  54.1 4.0 %all-to-all-start.2 = ((bf16[32,32,128]{2,1,0:T(8,128)(2,1)}), bf16[32,32,128]{2,1,0:T(8,128)(2,1)S(1)}, u32[]{:S(2)}, u32[]{:S(2)}) async-start(bf16[32,32,128]{2,1,0:T(8,128)(2,1)} %bitcast.2), calls=%async_computation.2 | async-start | bytes 524288 | tf_op jit(solution)/shard_map/all_to_all | solution.py:422
  58.1 0.7 all-gather.5.cloned.1.call-update
  58.8 8.7 %all-to-all-done.2 = bf16[32,32,128]{2,1,0:T(8,128)(2,1)S(1)} async-done(((bf16[32,32,128]{2,1,0:T(8,128)(2,1)}), bf16[32,32,128]{2,1,0:T(8,128)(2,1)S(1)}, u32[]{:S(2)}, u32[]{:S(2)}) %all-to-all-start.2) | async-done | bytes 262176 | tf_op jit(solution)/shard_map/all_to_all | solution.py:422
  67.6 0.7 collective-permute-start
  68.3 2.5 %collective-permute-start.1 = (bf16[32,32,128]{2,1,0:T(8,128)(2,1)S(1)}, bf16[32,32,128]{2,1,0:T(8,128)(2,1)S(1)}, u32[]{:S(2)}, u32[]{:S(2)}) collective-permute-start(bf16[32,32,128]{2,1,0:T(8,128)(2,1)S(1)} %all-to-all-done.2), channel_id=1, source_target_pairs={{0,3},{1,0},{2,1},{3,2},{4,7},{5,4},{6,5},{7,6},{8,11},{9,8},{10,9... | collective-permute-start | bytes 786440 | tf_op jit(solution)/shard_map/ppermute | solution.py:40
  71.4 5.6 %collective-permute-done = bf16[32,32,128]{2,1,0:T(8,128)(2,1)S(1)} collective-permute-done((bf16[32,32,128]{2,1,0:T(8,128)(2,1)S(1)}, bf16[32,32,128]{2,1,0:T(8,128)(2,1)S(1)}, u32[]{:S(2)}, u32[]{:S(2)}) %collective-permute-start) | collective-permute-done | bytes 262176 | tf_op jit(solution)/shard_map/ppermute | solution.py:40
  77.2 0.7 slice.181
  77.9 0.7 copy-done.9
  78.6 0.7 slice.182
  79.2 0.7 copy-done.11
  79.9 3.4 %collective-permute-start.3 = (bf16[16,32,128]{2,1,0:T(8,128)(2,1)}, bf16[16,32,128]{2,1,0:T(8,128)(2,1)}, u32[]{:S(2)}, u32[]{:S(2)}) collective-permute-start(bf16[16,32,128]{2,1,0:T(8,128)(2,1)} %slice.182), channel_id=1, source_target_pairs={{0,3},{1,0},{2,1},{3,2},{4,7},{5,4},{6,5},{7,6},{8,11},{9,8},{10,9... | collective-permute-start | bytes 393224 | tf_op jit(solution)/shard_map/ppermute | solution.py:40
  83.9 1.4 copy.74.dt_ref
  85.3 0.7 pad.19.clone
  86.0 1.5 slice_reduce_fusion.4
  87.5 1.0 copy-done.8
  88.5 0.9 copy-done.10
  89.4 0.9 copy-done.12
  90.4 2.1 shard_map.156
  92.5 5.9 %copy-done.1 = bf16[4096,2,1024]{2,1,0:T(2,128)(2,1)S(1)} copy-done((bf16[4096,2,1024]{2,1,0:T(2,128)(2,1)S(1)}, bf16[4096,2,1024]{2,1,0:T(2,128)(2,1)}, u32[]{:S(2)}) %copy-start.1) | copy-done | bytes 16777240
  98.5 6.6 %shard_map.157 = (f32[128,1024]{1,0:T(8,128)S(1)}, f32[128,1024]{1,0:T(8,128)S(1)}, f32[128,256]{1,0:T(8,128)S(1)}, f32[128,16]{1,0:T(8,128)S(1)}) custom-call(bf16[128,4096]{1,0:T(8,128)(2,1)S(1)} %get-tuple-element.23.rows_ref, bf16[4096,2,1024]{2,1,0:T(2,128)(2,1)S(1)} %copy-done.1, bf16[4096,2,128]{2,1,0:T(2,128)(2,1)S(1)} %copy-done.3, ...), custom_call_target="tpu_custom_call" | custom-call | flops 2432696320 | bytes 19005440 | tf_op jit(solution)/shard_map/pallas_call | solution.py:258
  105.1 0.8 copy-done.5
  106.0 2.1 collective-permute-start.4
  110.4 0.9 maximum_maximum_fusion
  111.3 8.1 %all-to-all-start.3 = ((bf16[32,48,128]{2,1,0:T(8,128)(2,1)}), bf16[32,48,128]{2,1,0:T(8,128)(2,1)S(1)}, u32[]{:S(2)}, u32[]{:S(2)}) async-start(bf16[32,48,128]{2,1,0:T(8,128)(2,1)} %maximum_maximum_fusion), calls=%async_computation.3 | async-start | bytes 786432 | tf_op jit(solution)/shard_map/all_to_all | solution.py:459
  119.7 2.2 fusion
  121.9 7.3 %all-to-all-done.3 = bf16[32,48,128]{2,1,0:T(8,128)(2,1)S(1)} async-done(((bf16[32,48,128]{2,1,0:T(8,128)(2,1)}), bf16[32,48,128]{2,1,0:T(8,128)(2,1)S(1)}, u32[]{:S(2)}, u32[]{:S(2)}) %all-to-all-start.3) | async-done | bytes 393248 | tf_op jit(solution)/shard_map/all_to_all | solution.py:459
  130.1 12.6 %all_to_all.29 = bf16[32,32,128]{2,1,0:T(8,128)(2,1)S(1)} all-to-all(bf16[32,32,128]{2,1,0:T(8,128)(2,1)S(1)} %bitcast.320), channel_id=1, replica_groups=mesh['ctx'=32,'head'=4] {'ctx'}, dimensions={0} | all-to-all | bytes 524288 | tf_op jit(solution)/shard_map/all_to_all | solution.py:476
  143.8 3.4 %copy-done.2 = bf16[1024,4096]{1,0:T(8,128)(2,1)S(1)} copy-done((bf16[1024,4096]{1,0:T(8,128)(2,1)S(1)}, bf16[1024,4096]{1,0:T(8,128)(2,1)}, u32[]{:S(2)}) %copy-start.2) | copy-done | bytes 8388632
  147.1 2.5 %shard_map.158 = bf16[4,32,4096]{2,1,0:T(8,128)(2,1)S(1)} custom-call(s32[1]{0:T(128)} %bitcast.head_ref, bf16[128,1024]{1,0:T(8,128)(2,1)S(1)} %multiply_convert_fusion.gated_ref, bf16[1024,4096]{1,0:T(8,128)(2,1)S(1)} %copy-done.2), custom_call_target="tpu_custom_call" | custom-call | flops 1073741824 | bytes 8388608 | tf_op jit(solution)/shard_map/pallas_call | solution.py:220
  149.7 0.7 collective-permute-start.5
  150.4 2.6 %collective-permute-start.6 = (bf16[16,4096]{1,0:T(8,128)(2,1)S(1)}, bf16[16,4096]{1,0:T(8,128)(2,1)S(1)}, u32[]{:S(2)}, u32[]{:S(2)}) collective-permute-start(bf16[16,4096]{1,0:T(8,128)(2,1)S(1)} %get-tuple-element.55), channel_id=1, source_target_pairs={{0,3},{1,0},{2,1},{3,2},{4,7},{5,4},{6,5},{7,6},{8,11},{9,8},{10,9... | collective-permute-start | bytes 393224 | tf_op jit(solution)/shard_map/ppermute | solution.py:40
  153.0 3.7 %collective-permute-done.5 = bf16[16,4096]{1,0:T(8,128)(2,1)S(1)} collective-permute-done((bf16[16,4096]{1,0:T(8,128)(2,1)S(1)}, bf16[16,4096]{1,0:T(8,128)(2,1)S(1)}, u32[]{:S(2)}, u32[]{:S(2)}) %collective-permute-start.5) | collective-permute-done | bytes 131104 | tf_op jit(solution)/shard_map/ppermute | solution.py:40
  156.8 1.0 collective-permute-start.7
  157.8 2.4 %collective-permute-start.8 = (bf16[32,4096]{1,0:T(8,128)(2,1)S(1)}, bf16[32,4096]{1,0:T(8,128)(2,1)S(1)}, u32[]{:S(2)}, u32[]{:S(2)}) collective-permute-start(bf16[32,4096]{1,0:T(8,128)(2,1)S(1)} %pad_maximum_fusion.3), channel_id=1, source_target_pairs={{0,3},{1,0},{2,1},{3,2},{4,7},{5,4},{6,5},{7,6},{8,11},{9,8},{10,9... | collective-permute-start | bytes 786440 | tf_op jit(solution)/shard_map/ppermute | solution.py:40
  160.2 5.6 %collective-permute-done.7 = bf16[32,4096]{1,0:T(8,128)(2,1)S(1)} collective-permute-done((bf16[32,4096]{1,0:T(8,128)(2,1)S(1)}, bf16[32,4096]{1,0:T(8,128)(2,1)S(1)}, u32[]{:S(2)}, u32[]{:S(2)}) %collective-permute-start.7) | collective-permute-done | bytes 262176 | tf_op jit(solution)/shard_map/ppermute | solution.py:40
  166.2 1.5 collective-permute-start.11
  167.7 1.5 collective-permute-start.12
  169.3 3.4 %collective-permute-done.11 = bf16[32,4096]{1,0:T(8,128)(2,1)S(1)} collective-permute-done((bf16[32,4096]{1,0:T(8,128)(2,1)S(1)}, bf16[32,4096]{1,0:T(8,128)(2,1)S(1)}, u32[]{:S(2)}, u32[]{:S(2)}) %collective-permute-start.11) | collective-permute-done | bytes 262176 | tf_op jit(solution)/shard_map/ppermute | solution.py:40
  172.7 3.1 %collective-permute-done.12 = bf16[32,4096]{1,0:T(8,128)(2,1)S(1)} collective-permute-done((bf16[32,4096]{1,0:T(8,128)(2,1)S(1)}, bf16[32,4096]{1,0:T(8,128)(2,1)S(1)}, u32[]{:S(2)}, u32[]{:S(2)}) %collective-permute-start.12) | collective-permute-done | bytes 262176 | tf_op jit(solution)/shard_map/ppermute | solution.py:40
  175.8 1.2 collective-permute-start.13
  177.1 0.8 collective-permute-start.16
  177.9 1.0 collective-permute-done.9
  179.3 3.0 %collective-permute-start.15 = (bf16[64,4096]{1,0:T(8,128)(2,1)S(1)}, bf16[64,4096]{1,0:T(8,128)(2,1)S(1)}, u32[]{:S(2)}, u32[]{:S(2)}) collective-permute-start(bf16[64,4096]{1,0:T(8,128)(2,1)S(1)} %pad_maximum_fusion.1.refs_0_), channel_id=1, source_target_pairs={{0,96},{4,28},{8,104},{12,4},{16,112},{20,12},{24,120},{28,20},{32... | collective-permute-start | bytes 1572872 | tf_op jit(solution)/shard_map/ppermute | solution.py:40
  182.5 2.2 copy-done
  184.7 5.3 %shard_map.159 = f32[8,128]{1,0:T(8,128)S(1)} custom-call(bf16[64,4096]{1,0:T(8,128)(2,1)S(1)} %pad_maximum_fusion.1.refs_0_, bf16[64,4096]{1,0:T(8,128)(2,1)S(1)} %constant_dynamic-update-slice_fusion.4.refs_1_, s32[2,1,128]{2,1,0:T(1,128)S(1)} %bitcast.312, bf16[4096,512]{1,0:T(8,128)(2,1)S(1)} %copy-done, ...), custom_call_target="tpu_custom_call" | custom-call | flops 1073741824 | bytes 8388608 | tf_op jit(solution)/shard_map/pallas_call | solution.py:358
  190.0 3.1 %collective-permute-done.10.refs_2_ = bf16[64,4096]{1,0:T(8,128)(2,1)S(1)} collective-permute-done((bf16[64,4096]{1,0:T(8,128)(2,1)S(1)}, bf16[64,4096]{1,0:T(8,128)(2,1)S(1)}, u32[]{:S(2)}, u32[]{:S(2)}) %collective-permute-start.10) | collective-permute-done | bytes 524320 | tf_op jit(solution)/shard_map/ppermute | solution.py:40
  193.1 3.2 %collective-permute-start.20 = (bf16[64,4096]{1,0:T(8,128)(2,1)S(1)}, bf16[64,4096]{1,0:T(8,128)(2,1)S(1)}, u32[]{:S(2)}, u32[]{:S(2)}) collective-permute-start(bf16[64,4096]{1,0:T(8,128)(2,1)S(1)} %collective-permute-done.13.refs_1_), channel_id=1, source_target_pairs={{0,96},{4,28},{8,104},{12,4},{16,112},{20,12},{24,120},{28,20},{32... | collective-permute-start | bytes 1572872 | tf_op jit(solution)/shard_map/ppermute | solution.py:40
  196.3 6.6 %shard_map.160 = f32[8,256]{1,0:T(8,128)S(1)} custom-call(bf16[64,4096]{1,0:T(8,128)(2,1)S(1)} %collective-permute-done.15.refs_0_, bf16[64,4096]{1,0:T(8,128)(2,1)S(1)} %collective-permute-done.13.refs_1_, bf16[64,4096]{1,0:T(8,128)(2,1)S(1)} %collective-permute-done.10.refs_2_, bf16[64,4096]{1,0:T(8,128)(2,1)S(1)} %collective-permute-done.16.refs_3_, ...), custom_call_target="tpu_custom_call" | custom-call | flops 2147483648 | bytes 8388608 | tf_op jit(solution)/shard_map/pallas_call | solution.py:358
  203.0 3.2 %collective-permute-start.18 = (f32[8,128]{1,0:T(8,128)S(1)}, f32[8,128]{1,0:T(8,128)S(1)}, u32[]{:S(2)}, u32[]{:S(2)}) collective-permute-start(f32[8,128]{1,0:T(8,128)S(1)} %get-tuple-element.64), channel_id=1, source_target_pairs={{0,96},{4,28},{8,104},{12,4},{16,112},{20,12},{24,120},{28,20},{32... | collective-permute-start | bytes 12296 | tf_op jit(solution)/shard_map/ppermute | solution.py:40
  206.3 5.3 %shard_map.161 = f32[8,128]{1,0:T(8,128)S(1)} custom-call(bf16[64,4096]{1,0:T(8,128)(2,1)S(1)} %collective-permute-done.19.refs_0_, bf16[64,4096]{1,0:T(8,128)(2,1)S(1)} %collective-permute-done.20.refs_1_, s32[2,1,128]{2,1,0:T(1,128)S(1)} %bitcast.311, bf16[4096,512]{1,0:T(8,128)(2,1)S(1)} %copy-done, bf16[4096,512]{1,0:T(8,128)(2,1)} %collective-permute-done.14.refs_4_.refs_6_), custom_call_target="tpu_custom_call" | custom-call | flops 1073741824 | bytes 8388608 | tf_op jit(solution)/shard_map/pallas_call | solution.py:358
  211.6 5.1 %collective-permute-done.21 = f32[8,128]{1,0:T(8,128)S(1)} collective-permute-done((f32[8,128]{1,0:T(8,128)S(1)}, f32[8,128]{1,0:T(8,128)S(1)}, u32[]{:S(2)}, u32[]{:S(2)}) %collective-permute-start.21) | collective-permute-done | bytes 4128 | tf_op jit(solution)/shard_map/ppermute | solution.py:40
  217.3 2.4 %collective-permute-start.22 = (f32[5,32]{1,0:T(8,128)S(1)}, f32[5,32]{1,0:T(8,128)S(1)}, u32[]{:S(2)}, u32[]{:S(2)}) collective-permute-start(f32[5,32]{1,0:T(8,128)S(1)} %bitcast.330), channel_id=1, source_target_pairs={{0,24},{4,100},{8,0},{12,108},{16,8},{20,116},{24,16},{28,124},{32... | collective-permute-start | bytes 1928 | tf_op jit(solution)/shard_map/ppermute | solution.py:40
  219.7 1.6 collective-permute-start.24
  221.2 3.3 %collective-permute-done.23 = f32[5,32]{1,0:T(8,128)S(1)} collective-permute-done((f32[5,32]{1,0:T(8,128)S(1)}, f32[5,32]{1,0:T(8,128)S(1)}, u32[]{:S(2)}, u32[]{:S(2)}) %collective-permute-start.23) | collective-permute-done | bytes 672 | tf_op jit(solution)/shard_map/ppermute | solution.py:40
  (162 shorter events, 9.4 us)
Async XLA Ops:
  6.5 137.2 %all-gather.3.cloned.1.call-start = ((), (), s32[]{:S(2)}) async-start(), calls=%async_computation.5 | async-start | bytes 8650752 | tf_op jit(solution)/shard_map/all_gather | solution.py:409
  8.6 15.8 %all-to-all-start = ((s32[32,1,160]{2,1,0:T(1,128)}), s32[32,1,160]{2,1,0:T(1,128)S(1)}, u32[]{:S(2)}, u32[]{:S(2)}) async-start(s32[32,1,160]{2,1,0:T(1,128)} %broadcast_in_dim.36), calls=%async_computation | async-start | bytes 65536 | tf_op jit(solution)/shard_map/all_to_all | solution.py:415
  17.0 1.2 copy-start.4
  24.4 19.7 %all-to-all-start.1 = ((bf16[4,1024,128]{2,1,0:T(8,128)(2,1)}), bf16[4,1024,128]{2,1,0:T(8,128)(2,1)S(1)}, u32[]{:S(2)}, u32[]{:S(2)}) async-start(bf16[4,1024,128]{2,1,0:T(8,128)(2,1)} %shard_map.154), calls=%async_computation.1 | async-start | bytes 2097152 | tf_op jit(solution)/shard_map/all_to_all | solution.py:419
  28.7 0.6 copy-start.14
  29.5 29.3 %copy-start.22 = (f32[4,1024]{1,0:T(4,128)S(1)}, f32[4,1024]{1,0:T(4,128)}, u32[]{:S(2)}) copy-start(f32[4,1024]{1,0:T(4,128)} %param.22) | copy-start | bytes 49156
  29.5 41.3 %copy-start.25 = (f32[4,2,128]{2,1,0:T(2,128)S(1)}, f32[4,2,128]{2,1,0:T(2,128)}, u32[]{:S(2)}) copy-start(f32[4,2,128]{2,1,0:T(2,128)} %param.23) | copy-start | bytes 12292
  29.5 41.3 %copy-start.28 = (f32[16]{0:T(128)S(1)}, f32[16]{0:T(128)}, u32[]{:S(2)}) copy-start(f32[16]{0:T(128)} %param.25) | copy-start | bytes 196
  29.6 58.0 %copy-start.13 = (f32[4096]{0:T(1024)S(1)}, f32[4096]{0:T(1024)}, u32[]{:S(2)}) copy-start(f32[4096]{0:T(1024)} %param.28) | copy-start | bytes 49156
  54.1 38.5 %copy-start.3 = (bf16[4096,2,128]{2,1,0:T(2,128)(2,1)S(1)}, bf16[4096,2,128]{2,1,0:T(2,128)(2,1)}, u32[]{:S(2)}) copy-start(bf16[4096,2,128]{2,1,0:T(2,128)(2,1)} %bc_ref.1) | copy-start | bytes 6291460
  54.1 13.5 %all-to-all-start.2 = ((bf16[32,32,128]{2,1,0:T(8,128)(2,1)}), bf16[32,32,128]{2,1,0:T(8,128)(2,1)S(1)}, u32[]{:S(2)}, u32[]{:S(2)}) async-start(bf16[32,32,128]{2,1,0:T(8,128)(2,1)} %bitcast.2), calls=%async_computation.2 | async-start | bytes 524288 | tf_op jit(solution)/shard_map/all_to_all | solution.py:422
  58.1 94.9 %all-gather.5.cloned.1.call-start = ((), (), s32[]{:S(2)}) async-start(), calls=%async_computation.6 | async-start | bytes 5242880 | tf_op jit(solution)/shard_map/all_gather | solution.py:410
  67.6 19.9 %copy-start.7 = (bf16[32,32,128]{2,1,0:T(8,128)(2,1)}, bf16[32,32,128]{2,1,0:T(8,128)(2,1)S(1)}, u32[]{:S(2)}) copy-start(bf16[32,32,128]{2,1,0:T(8,128)(2,1)S(1)} %all-to-all-done.2) | copy-start | bytes 786436
  67.6 9.4 %collective-permute-start = (bf16[32,32,128]{2,1,0:T(8,128)(2,1)S(1)}, bf16[32,32,128]{2,1,0:T(8,128)(2,1)S(1)}, u32[]{:S(2)}, u32[]{:S(2)}) collective-permute-start(bf16[32,32,128]{2,1,0:T(8,128)(2,1)S(1)} %all-to-all-done.2), channel_id=1, source_target_pairs={{0,1},{1,2},{2,3},{3,0},{4,5},{5,6},{6,7},{7,4},{8,9},{9,10},{10,1... | collective-permute-start | bytes 786440 | tf_op jit(solution)/shard_map/ppermute | solution.py:40
  68.3 8.9 %collective-permute-start.1 = (bf16[32,32,128]{2,1,0:T(8,128)(2,1)S(1)}, bf16[32,32,128]{2,1,0:T(8,128)(2,1)S(1)}, u32[]{:S(2)}, u32[]{:S(2)}) collective-permute-start(bf16[32,32,128]{2,1,0:T(8,128)(2,1)S(1)} %all-to-all-done.2), channel_id=1, source_target_pairs={{0,3},{1,0},{2,1},{3,2},{4,7},{5,4},{6,5},{7,6},{8,11},{9,8},{10,9... | collective-permute-start | bytes 786440 | tf_op jit(solution)/shard_map/ppermute | solution.py:40
  70.8 6.4 %copy-start.16 = (f32[4,1280]{1,0:T(4,128)}, f32[4,1280]{1,0:T(4,128)S(1)}, u32[]{:S(2)}) copy-start(f32[4,1280]{1,0:T(4,128)S(1)} %constant_dynamic-update-slice_fusion) | copy-start | bytes 61444
  77.8 0.7 copy-start.9
  78.6 9.0 %collective-permute-start.2 = (bf16[16,32,128]{2,1,0:T(8,128)(2,1)}, bf16[16,32,128]{2,1,0:T(8,128)(2,1)S(1)}, u32[]{:S(2)}, u32[]{:S(2)}) collective-permute-start(bf16[16,32,128]{2,1,0:T(8,128)(2,1)} %slice.181), channel_id=1, source_target_pairs={{0,1},{1,2},{2,3},{3,0},{4,5},{5,6},{6,7},{7,4},{8,9},{9,10},{10,1... | collective-permute-start | bytes 393224 | tf_op jit(solution)/shard_map/ppermute | solution.py:40
  79.2 0.7 copy-start.11
  79.9 7.6 %collective-permute-start.3 = (bf16[16,32,128]{2,1,0:T(8,128)(2,1)}, bf16[16,32,128]{2,1,0:T(8,128)(2,1)}, u32[]{:S(2)}, u32[]{:S(2)}) collective-permute-start(bf16[16,32,128]{2,1,0:T(8,128)(2,1)} %slice.182), channel_id=1, source_target_pairs={{0,3},{1,0},{2,1},{3,2},{4,7},{5,4},{6,5},{7,6},{8,11},{9,8},{10,9... | collective-permute-start | bytes 393224 | tf_op jit(solution)/shard_map/ppermute | solution.py:40
  87.5 1.0 copy-start.8
  88.5 0.9 copy-start.10
  89.4 0.9 copy-start.12
  92.5 5.9 %copy-start.1 = (bf16[4096,2,1024]{2,1,0:T(2,128)(2,1)S(1)}, bf16[4096,2,1024]{2,1,0:T(2,128)(2,1)}, u32[]{:S(2)}) copy-start(bf16[4096,2,1024]{2,1,0:T(2,128)(2,1)} %zx_ref.1) | copy-start | bytes 50331652
  98.5 9.6 %copy-start.26 = (f32[16]{0:T(128)S(1)}, f32[16]{0:T(128)}, u32[]{:S(2)}) copy-start(f32[16]{0:T(128)} %param.24) | copy-start | bytes 196
  98.5 9.7 %copy-start.30 = (f32[16]{0:T(128)S(1)}, f32[16]{0:T(128)}, u32[]{:S(2)}) copy-start(f32[16]{0:T(128)} %exponential_negate_fusion) | copy-start | bytes 196
  98.5 10.5 %copy-start.17 = (f32[1280]{0:T(1024)S(1)}, f32[1280]{0:T(1024)}, u32[]{:S(2)}) copy-start(f32[1280]{0:T(1024)} %get-tuple-element.35) | copy-start | bytes 15364
  98.5 10.5 %copy-start.18 = (f32[1280]{0:T(1024)S(1)}, f32[1280]{0:T(1024)}, u32[]{:S(2)}) copy-start(f32[1280]{0:T(1024)} %get-tuple-element.36) | copy-start | bytes 15364
  98.5 10.5 %copy-start.19 = (f32[1280]{0:T(1024)S(1)}, f32[1280]{0:T(1024)}, u32[]{:S(2)}) copy-start(f32[1280]{0:T(1024)} %get-tuple-element.37) | copy-start | bytes 15364
  98.5 10.5 %copy-start.20 = (f32[1280]{0:T(1024)S(1)}, f32[1280]{0:T(1024)}, u32[]{:S(2)}) copy-start(f32[1280]{0:T(1024)} %get-tuple-element.38) | copy-start | bytes 15364
  105.1 0.8 copy-start.5
  105.9 4.5 %copy-start.27 = (bf16[48]{0:T(256)(128)(2,1)S(1)}, bf16[48]{0:T(256)(128)(2,1)}, u32[]{:S(2)}) copy-start(bf16[48]{0:T(256)(128)(2,1)} %pad.19.clone) | copy-start | bytes 292
  105.9 13.7 %copy-start.23 = (pred[128,128]{1,0:T(8,128)(4,1)S(1)}, pred[128,128]{1,0:T(8,128)(4,1)}, u32[]{:S(2)}) copy-start(pred[128,128]{1,0:T(8,128)(4,1)} %iota_compare_fusion) | copy-start | bytes 49156
  105.9 13.7 %copy-start.29 = (f32[16]{0:T(128)S(1)}, f32[16]{0:T(128)}, u32[]{:S(2)}) copy-start(f32[16]{0:T(128)} %param.26) | copy-start | bytes 196
  106.0 3.0 %collective-permute-start.4 = (f32[3,1280]{1,0:T(4,128)S(1)}, f32[3,1280]{1,0:T(4,128)S(1)}, u32[]{:S(2)}, u32[]{:S(2)}) collective-permute-start(f32[3,1280]{1,0:T(4,128)S(1)} %slice.226), channel_id=1, source_target_pairs={{0,4},{4,8},{8,12},{12,16},{16,20},{20,24},{24,28},{28,32},{32,36}... | collective-permute-start | bytes 46088 | tf_op jit(solution)/shard_map/ppermute | solution.py:46
  110.3 33.1 %copy-start.6 = (f32[128,1024]{1,0:T(8,128)S(1)}, f32[128,1024]{1,0:T(8,128)}, u32[]{:S(2)}) copy-start(f32[128,1024]{1,0:T(8,128)} %copy-done.5) | copy-start | bytes 1572868
  111.3 17.8 %all-to-all-start.3 = ((bf16[32,48,128]{2,1,0:T(8,128)(2,1)}), bf16[32,48,128]{2,1,0:T(8,128)(2,1)S(1)}, u32[]{:S(2)}, u32[]{:S(2)}) async-start(bf16[32,48,128]{2,1,0:T(8,128)(2,1)} %maximum_maximum_fusion), calls=%async_computation.3 | async-start | bytes 786432 | tf_op jit(solution)/shard_map/all_to_all | solution.py:459
  119.4 24.2 %copy-start.24 = (f32[1024]{0:T(1024)S(1)}, f32[1024]{0:T(1024)}, u32[]{:S(2)}) copy-start(f32[1024]{0:T(1024)} %param.27) | copy-start | bytes 12292
  143.8 3.4 %copy-start.2 = (bf16[1024,4096]{1,0:T(8,128)(2,1)S(1)}, bf16[1024,4096]{1,0:T(8,128)(2,1)}, u32[]{:S(2)}) copy-start(bf16[1024,4096]{1,0:T(8,128)(2,1)} %all-gather.3.cloned.1.call-done.weights_ref) | copy-start | bytes 25165828
  147.1 13.0 %copy-start.15 = (s32[32,1,160]{2,0,1:T(8,128)S(1)}, s32[32,1,160]{2,0,1:T(8,128)}, u32[]{:S(2)}) copy-start(s32[32,1,160]{2,0,1:T(8,128)} %copy-done.14) | copy-start | bytes 61444
  149.6 16.4 %copy-start.21 = (f32[4096]{0:T(1024)S(1)}, f32[4096]{0:T(1024)}, u32[]{:S(2)}) copy-start(f32[4096]{0:T(1024)} %param.29) | copy-start | bytes 49156
  149.7 7.0 %collective-permute-start.5 = (bf16[16,4096]{1,0:T(8,128)(2,1)S(1)}, bf16[16,4096]{1,0:T(8,128)(2,1)S(1)}, u32[]{:S(2)}, u32[]{:S(2)}) collective-permute-start(bf16[16,4096]{1,0:T(8,128)(2,1)S(1)} %get-tuple-element.56), channel_id=1, source_target_pairs={{0,1},{1,2},{2,3},{3,0},{4,5},{5,6},{6,7},{7,4},{8,9},{9,10},{10,1... | collective-permute-start | bytes 393224 | tf_op jit(solution)/shard_map/ppermute | solution.py:40
  150.4 6.3 %collective-permute-start.6 = (bf16[16,4096]{1,0:T(8,128)(2,1)S(1)}, bf16[16,4096]{1,0:T(8,128)(2,1)S(1)}, u32[]{:S(2)}, u32[]{:S(2)}) collective-permute-start(bf16[16,4096]{1,0:T(8,128)(2,1)S(1)} %get-tuple-element.55), channel_id=1, source_target_pairs={{0,3},{1,0},{2,1},{3,2},{4,7},{5,4},{6,5},{7,6},{8,11},{9,8},{10,9... | collective-permute-start | bytes 393224 | tf_op jit(solution)/shard_map/ppermute | solution.py:40
  153.0 29.5 %collective-permute-start.14 = (bf16[4096,512]{1,0:T(8,128)(2,1)}, bf16[4096,512]{1,0:T(8,128)(2,1)}, u32[]{:S(2)}, u32[]{:S(2)}) collective-permute-start(bf16[4096,512]{1,0:T(8,128)(2,1)} %all-gather.5.cloned.1.call-done.refs_3_.refs_5_), channel_id=1, source_target_pairs={{0,4},{4,0},{8,12},{12,8},{16,20},{20,16},{24,28},{28,24},{32,36},... | collective-permute-start | bytes 12582920 | tf_op jit(solution)/shard_map/ppermute | solution.py:35
  156.8 9.0 %collective-permute-start.7 = (bf16[32,4096]{1,0:T(8,128)(2,1)S(1)}, bf16[32,4096]{1,0:T(8,128)(2,1)S(1)}, u32[]{:S(2)}, u32[]{:S(2)}) collective-permute-start(bf16[32,4096]{1,0:T(8,128)(2,1)S(1)} %pad_maximum_fusion.2), channel_id=1, source_target_pairs={{0,1},{1,2},{2,3},{3,0},{4,5},{5,6},{6,7},{7,4},{8,9},{9,10},{10,1... | collective-permute-start | bytes 786440 | tf_op jit(solution)/shard_map/ppermute | solution.py:40
  157.8 8.0 %collective-permute-start.8 = (bf16[32,4096]{1,0:T(8,128)(2,1)S(1)}, bf16[32,4096]{1,0:T(8,128)(2,1)S(1)}, u32[]{:S(2)}, u32[]{:S(2)}) collective-permute-start(bf16[32,4096]{1,0:T(8,128)(2,1)S(1)} %pad_maximum_fusion.3), channel_id=1, source_target_pairs={{0,3},{1,0},{2,1},{3,2},{4,7},{5,4},{6,5},{7,6},{8,11},{9,8},{10,9... | collective-permute-start | bytes 786440 | tf_op jit(solution)/shard_map/ppermute | solution.py:40
  166.2 6.4 %collective-permute-start.11 = (bf16[32,4096]{1,0:T(8,128)(2,1)S(1)}, bf16[32,4096]{1,0:T(8,128)(2,1)S(1)}, u32[]{:S(2)}, u32[]{:S(2)}) collective-permute-start(bf16[32,4096]{1,0:T(8,128)(2,1)S(1)} %fusion.18), channel_id=1, source_target_pairs={{0,24},{4,100},{8,0},{12,108},{16,8},{20,116},{24,16},{28,124},{32... | collective-permute-start | bytes 786440 | tf_op jit(solution)/shard_map/ppermute | solution.py:40
  167.7 8.1 %collective-permute-start.12 = (bf16[32,4096]{1,0:T(8,128)(2,1)S(1)}, bf16[32,4096]{1,0:T(8,128)(2,1)S(1)}, u32[]{:S(2)}, u32[]{:S(2)}) collective-permute-start(bf16[32,4096]{1,0:T(8,128)(2,1)S(1)} %fusion.18), channel_id=1, source_target_pairs={{0,16},{4,68},{8,24},{12,76},{16,0},{20,84},{24,8},{28,92},{32,48}... | collective-permute-start | bytes 786440 | tf_op jit(solution)/shard_map/ppermute | solution.py:40
  169.3 9.7 %collective-permute-start.9 = (bf16[32,4096]{1,0:T(8,128)(2,1)S(1)}, bf16[32,4096]{1,0:T(8,128)(2,1)S(1)}, u32[]{:S(2)}, u32[]{:S(2)}) collective-permute-start(bf16[32,4096]{1,0:T(8,128)(2,1)S(1)} %fusion.18), channel_id=1, source_target_pairs={{0,8},{4,36},{8,16},{12,44},{16,24},{20,52},{24,0},{28,60},{32,40}... | collective-permute-start | bytes 786440 | tf_op jit(solution)/shard_map/ppermute | solution.py:40
  175.8 14.2 %collective-permute-start.13 = (bf16[64,4096]{1,0:T(8,128)(2,1)S(1)}, bf16[64,4096]{1,0:T(8,128)(2,1)S(1)}, u32[]{:S(2)}, u32[]{:S(2)}) collective-permute-start(bf16[64,4096]{1,0:T(8,128)(2,1)S(1)} %constant_dynamic-update-slice_fusion.4.refs_1_), channel_id=1, source_target_pairs={{0,96},{4,28},{8,104},{12,4},{16,112},{20,12},{24,120},{28,20},{32... | collective-permute-start | bytes 1572872 | tf_op jit(solution)/shard_map/ppermute | solution.py:40
  177.1 19.3 %collective-permute-start.16 = (bf16[64,4096]{1,0:T(8,128)(2,1)S(1)}, bf16[64,4096]{1,0:T(8,128)(2,1)S(1)}, u32[]{:S(2)}, u32[]{:S(2)}) collective-permute-start(bf16[64,4096]{1,0:T(8,128)(2,1)S(1)} %constant_dynamic-update-slice_fusion.4.refs_1_), channel_id=1, source_target_pairs={{0,32},{4,12},{8,40},{12,20},{16,48},{20,28},{24,56},{28,4},{32,64... | collective-permute-start | bytes 1572872 | tf_op jit(solution)/shard_map/ppermute | solution.py:40
  179.0 14.1 %collective-permute-start.10 = (bf16[64,4096]{1,0:T(8,128)(2,1)S(1)}, bf16[64,4096]{1,0:T(8,128)(2,1)S(1)}, u32[]{:S(2)}, u32[]{:S(2)}) collective-permute-start(bf16[64,4096]{1,0:T(8,128)(2,1)S(1)} %pad_maximum_fusion.1.refs_0_), channel_id=1, source_target_pairs={{0,32},{4,12},{8,40},{12,20},{16,48},{20,28},{24,56},{28,4},{32,64... | collective-permute-start | bytes 1572872 | tf_op jit(solution)/shard_map/ppermute | solution.py:40
  179.3 17.1 %collective-permute-start.15 = (bf16[64,4096]{1,0:T(8,128)(2,1)S(1)}, bf16[64,4096]{1,0:T(8,128)(2,1)S(1)}, u32[]{:S(2)}, u32[]{:S(2)}) collective-permute-start(bf16[64,4096]{1,0:T(8,128)(2,1)S(1)} %pad_maximum_fusion.1.refs_0_), channel_id=1, source_target_pairs={{0,96},{4,28},{8,104},{12,4},{16,112},{20,12},{24,120},{28,20},{32... | collective-permute-start | bytes 1572872 | tf_op jit(solution)/shard_map/ppermute | solution.py:40
  182.5 2.2 copy-start
  193.1 13.2 %collective-permute-start.19 = (bf16[64,4096]{1,0:T(8,128)(2,1)S(1)}, bf16[64,4096]{1,0:T(8,128)(2,1)S(1)}, u32[]{:S(2)}, u32[]{:S(2)}) collective-permute-start(bf16[64,4096]{1,0:T(8,128)(2,1)S(1)} %collective-permute-done.10.refs_2_), channel_id=1, source_target_pairs={{0,32},{4,12},{8,40},{12,20},{16,48},{20,28},{24,56},{28,4},{32,64... | collective-permute-start | bytes 1572872 | tf_op jit(solution)/shard_map/ppermute | solution.py:40
  193.1 13.2 %collective-permute-start.20 = (bf16[64,4096]{1,0:T(8,128)(2,1)S(1)}, bf16[64,4096]{1,0:T(8,128)(2,1)S(1)}, u32[]{:S(2)}, u32[]{:S(2)}) collective-permute-start(bf16[64,4096]{1,0:T(8,128)(2,1)S(1)} %collective-permute-done.13.refs_1_), channel_id=1, source_target_pairs={{0,96},{4,28},{8,104},{12,4},{16,112},{20,12},{24,120},{28,20},{32... | collective-permute-start | bytes 1572872 | tf_op jit(solution)/shard_map/ppermute | solution.py:40
  202.9 8.7 %collective-permute-start.17 = (f32[8,128]{1,0:T(8,128)S(1)}, f32[8,128]{1,0:T(8,128)S(1)}, u32[]{:S(2)}, u32[]{:S(2)}) collective-permute-start(f32[8,128]{1,0:T(8,128)S(1)} %get-tuple-element.63), channel_id=1, source_target_pairs={{0,32},{4,12},{8,40},{12,20},{16,48},{20,28},{24,56},{28,4},{32,64... | collective-permute-start | bytes 12296 | tf_op jit(solution)/shard_map/ppermute | solution.py:40
  203.0 8.6 %collective-permute-start.18 = (f32[8,128]{1,0:T(8,128)S(1)}, f32[8,128]{1,0:T(8,128)S(1)}, u32[]{:S(2)}, u32[]{:S(2)}) collective-permute-start(f32[8,128]{1,0:T(8,128)S(1)} %get-tuple-element.64), channel_id=1, source_target_pairs={{0,96},{4,28},{8,104},{12,4},{16,112},{20,12},{24,120},{28,20},{32... | collective-permute-start | bytes 12296 | tf_op jit(solution)/shard_map/ppermute | solution.py:40
  211.5 5.2 %collective-permute-start.21 = (f32[8,128]{1,0:T(8,128)S(1)}, f32[8,128]{1,0:T(8,128)S(1)}, u32[]{:S(2)}, u32[]{:S(2)}) collective-permute-start(f32[8,128]{1,0:T(8,128)S(1)} %shard_map.161), channel_id=1, source_target_pairs={{0,64},{4,20},{8,72},{12,28},{16,80},{20,4},{24,88},{28,12},{32,96... | collective-permute-start | bytes 12296 | tf_op jit(solution)/shard_map/ppermute | solution.py:40
  217.3 4.0 %collective-permute-start.22 = (f32[5,32]{1,0:T(8,128)S(1)}, f32[5,32]{1,0:T(8,128)S(1)}, u32[]{:S(2)}, u32[]{:S(2)}) collective-permute-start(f32[5,32]{1,0:T(8,128)S(1)} %bitcast.330), channel_id=1, source_target_pairs={{0,24},{4,100},{8,0},{12,108},{16,8},{20,116},{24,16},{28,124},{32... | collective-permute-start | bytes 1928 | tf_op jit(solution)/shard_map/ppermute | solution.py:40
  219.7 4.8 %collective-permute-start.23 = (f32[5,32]{1,0:T(8,128)S(1)}, f32[5,32]{1,0:T(8,128)S(1)}, u32[]{:S(2)}, u32[]{:S(2)}) collective-permute-start(f32[5,32]{1,0:T(8,128)S(1)} %bitcast.331), channel_id=1, source_target_pairs={{0,8},{4,36},{8,16},{12,44},{16,24},{20,52},{24,0},{28,60},{32,40}... | collective-permute-start | bytes 1928 | tf_op jit(solution)/shard_map/ppermute | solution.py:40
  219.7 5.1 %collective-permute-start.24 = (f32[5,32]{1,0:T(8,128)S(1)}, f32[5,32]{1,0:T(8,128)S(1)}, u32[]{:S(2)}, u32[]{:S(2)}) collective-permute-start(f32[5,32]{1,0:T(8,128)S(1)} %bitcast.332), channel_id=1, source_target_pairs={{0,16},{4,68},{8,24},{12,76},{16,0},{20,84},{24,8},{28,92},{32,48}... | collective-permute-start | bytes 1928 | tf_op jit(solution)/shard_map/ppermute | solution.py:40
Sparse Core Ops, SparseCore 0:
  9.5 63.4 all-gather.2
  74.7 49.1 all-gather.4

commit v4 on v3

--- a/solution.py
+++ b/solution.py
@@ -47,27 +47,15 @@
 
 
 def ring_gather(value, shift):
-    half = value.shape[0] // 2
-    left = moved(value, shift, 1)
-    right = moved(value, shift, -1)
-    left, right = lax.optimization_barrier((left, right))
-    far_low = moved(left[:half], shift, 1)
-    far_high = moved(right[half:], shift, -1)
-    return value, right, far_low, far_high, left
+    return (value, *(moved(value, shift, -ahead) for ahead in (1, 2, 3)))
 
 
 def ring_reduce(parts, shift):
-    own, ahead, far, behind = parts
-    half = own.shape[0] // 2
-    from_left = moved(far[:half], shift, 1)
-    from_right = moved(far[half:], shift, -1)
-    from_left, from_right = lax.optimization_barrier((from_left, from_right))
-    ahead = jnp.concatenate([ahead[:half] + from_left, ahead[half:]])
-    behind = jnp.concatenate([behind[:half], behind[half:] + from_right])
-    left = moved(ahead, shift, 1)
-    right = moved(behind, shift, -1)
-    f32 = jnp.float32
-    return own.astype(f32) + left.astype(f32) + right.astype(f32)
+    arrived = [moved(parts[ahead], shift, ahead) for ahead in (1, 2, 3)]
+    total = parts[0].astype(jnp.float32)
+    for part in arrived:
+        total = total + part.astype(jnp.float32)
+    return total
 
 
 def in_vmem():
@@ -79,131 +67,171 @@
     return group * 128 + jnp.right_shift(index, 7) * 32 + jnp.bitwise_and(index, 31)
 
 
-def pack_columns(table):
+def swap_matrix(head):
+    row = lax.broadcasted_iota(jnp.int32, (512, 512), 0)
+    col = lax.broadcasted_iota(jnp.int32, (512, 512), 1)
+    source = jnp.bitwise_and(jnp.right_shift(row, 7) + head, 3)
+    goal = spot(source * 128 + jnp.bitwise_and(row, 127))
+    return (col == goal).astype(jnp.float32).astype(jnp.bfloat16)
+
+
+def pack_columns(table, head):
     rows = table.shape[0] // 4
     bf16, f32 = jnp.bfloat16, jnp.float32
 
-    def kernel(table_ref, out_ref):
+    def kernel(head_ref, table_ref, *out_refs):
         row = lax.broadcasted_iota(jnp.int32, (512, 512), 0)
         col = lax.broadcasted_iota(jnp.int32, (512, 512), 1)
-        swap = (col == spot(row)).astype(f32).astype(bf16)
+        owner = jnp.bitwise_and(jnp.right_shift(row, 5), 3)
+        ahead = jnp.bitwise_and(owner - head_ref[0], 3)
+        goal = ahead * 128 + jnp.right_shift(row, 7) * 32 + jnp.bitwise_and(row, 31)
+        swap = (col == goal).astype(f32).astype(bf16)
         for at in range(0, rows, 256):
             wide = [table_ref[g * rows + at : g * rows + at + 256, :] for g in range(4)]
             wide = jnp.concatenate(wide, axis=1)
             swapped = jnp.dot(wide, swap, preferred_element_type=f32).astype(bf16)
-            for h in range(4):
-                out_ref[h, at : at + 256, :] = swapped[:, h * 128 : (h + 1) * 128]
+            for k, out_ref in enumerate(out_refs):
+                out_ref[at : at + 256, :] = swapped[:, k * 128 : (k + 1) * 128]
 
     return pl.pallas_call(
         kernel,
-        in_specs=[in_vmem()],
-        out_specs=in_vmem(),
-        out_shape=jax.ShapeDtypeStruct((4, rows, 128), bf16),
+        in_specs=[pl.BlockSpec(memory_space=pltpu.SMEM), in_vmem()],
+        out_specs=[in_vmem()] * 4,
+        out_shape=[jax.ShapeDtypeStruct((rows, 128), bf16)] * 4,
         compiler_params=pltpu.CompilerParams(vmem_limit_bytes=16 << 20),
         cost_estimate=pl.CostEstimate(
             flops=2 * rows * 512 * 512, bytes_accessed=8 * rows * 128 * 2, transcendentals=0
         ),
-    )(table)
-
-
-def look_up(ids, table):
-    steps = ids.shape[0]
+    )(head, table)
+
+
+def look_up(ids, tables):
+    steps, sets = ids.shape[0], ids.shape[1] // 4
     bf16, f32 = jnp.bfloat16, jnp.float32
 
-    def kernel(ids_ref, table_ref, out_ref, side_ref):
+    def kernel(ids_ref, *refs):
+        table_refs, (out_ref, side_ref) = refs[:4], refs[4:]
+
         @pl.when(pl.program_id(0) == 0)
         def _():
             for q in range(8):
                 rows = pl.ds((q % 2) * 512, 512)
-                side_ref[:, q * 128 : (q + 1) * 128] = table_ref[q // 2, rows, :]
+                side_ref[:, q * 128 : (q + 1) * 128] = table_refs[q // 2][rows, :]
 
         lane = lax.broadcasted_iota(jnp.int32, (128, 128), 1)
-        row = lax.broadcasted_iota(jnp.int32, (128, 128), 0)
         lane_group = jnp.right_shift(lane, 5)
-        same = jnp.bitwise_and(row, 31) == jnp.bitwise_and(lane, 31)
-        total = jnp.zeros((128, 128), f32)
-        for g in range(4):
-            column = jnp.broadcast_to(ids_ref[0, g : g + 1, :], (128, 128)).T
-            low = jnp.bitwise_and(column, 511)
-            picks = [(low == lane + 128 * c).astype(f32).astype(bf16) for c in range(4)]
-            picks = jnp.concatenate(picks, axis=1)
-            found = jnp.dot(picks, side_ref[...], preferred_element_type=f32)
-            rest = jnp.right_shift(column, 9)
-            here = jnp.bitwise_and(jnp.right_shift(rest, 1), 3) == lane_group
-            block = jnp.where(here, jnp.bitwise_and(rest, 25), -1)
-            chosen = jnp.zeros((128, 128), f32)
-            for q in range(8):
-                wanted = (q // 2) * 8 + q % 2
-                chosen = jnp.where(block == wanted, found[:, q * 128 : (q + 1) * 128], chosen)
-            fold = jnp.logical_and(same, lane_group == g).astype(f32).astype(bf16)
-            total = total + jnp.dot(chosen.astype(bf16), fold, preferred_element_type=f32)
-        out_ref[...] = total.astype(bf16)
+        row = lax.broadcasted_iota(jnp.int32, (512, 128), 0)
+        spread = lax.broadcasted_iota(jnp.int32, (512, 128), 1)
+        goal = jnp.right_shift(row, 7) * 32 + jnp.bitwise_and(row, 31)
+        fold = (spread == goal).astype(f32).astype(bf16)
+        for t in range(sets):
+            picked = []
+            for g in range(4):
+                column = jnp.broadcast_to(ids_ref[0, 4 * t + g : 4 * t + g + 1, :], (128, 128)).T
+                low = jnp.bitwise_and(column, 511)
+                picks = [(low == lane + 128 * c).astype(f32).astype(bf16) for c in range(4)]
+                picks = jnp.concatenate(picks, axis=1)
+                found = jnp.dot(picks, side_ref[...], preferred_element_type=f32)
+                rest = jnp.right_shift(column, 9)
+                here = jnp.bitwise_and(jnp.right_shift(rest, 1), 3) == lane_group
+                block = jnp.where(here, jnp.bitwise_and(rest, 25), -1)
+                chosen = jnp.zeros((128, 128), f32)
+                for q in range(8):
+                    wanted = (q // 2) * 8 + q % 2
+                    chosen = jnp.where(block == wanted, found[:, q * 128 : (q + 1) * 128], chosen)
+                picked.append(chosen.astype(bf16))
+            folded = jnp.dot(jnp.concatenate(picked, axis=1), fold, preferred_element_type=f32)
+            out_ref[t * 128 : (t + 1) * 128, :] = folded.astype(bf16)
 
     return pl.pallas_call(
         kernel,
         grid=(steps,),
-        in_specs=[
-            pl.BlockSpec((1, 4, 128), lambda i: (i, 0, 0)),
-            pl.BlockSpec((4, 1024, 128), lambda i: (0, 0, 0)),
-        ],
-        out_specs=pl.BlockSpec((128, 128), lambda i: (i, 0)),
-        out_shape=jax.ShapeDtypeStruct((steps * 128, 128), bf16),
+        in_specs=[pl.BlockSpec((1, 4 * sets, 128), lambda i: (i, 0, 0))]
+        + [pl.BlockSpec((1024, 128), lambda i: (0, 0))] * 4,
+        out_specs=pl.BlockSpec((sets * 128, 128), lambda i: (i, 0)),
+        out_shape=jax.ShapeDtypeStruct((steps * sets * 128, 128), bf16),
         scratch_shapes=[pltpu.VMEM((512, 1024), bf16)],
         compiler_params=pltpu.CompilerParams(vmem_limit_bytes=16 << 20),
         cost_estimate=pl.CostEstimate(
-            flops=2 * steps * 512 * 512 * 1024, bytes_accessed=2 << 20, transcendentals=0
+            flops=2 * steps * sets * 512 * 512 * 1024, bytes_accessed=2 << 20, transcendentals=0
         ),
-    )(ids, table)
-
-
-def assemble(pieces, head, gain):
-    own, right, far_low, far_high, left = pieces
-    blocks, quarter = own.shape[:2]
+    )(ids, *tables)
+
+
+def embed_and_project(pieces, head, gain, w_zx, w_bc, w_dt):
+    blocks, quarter = pieces[0].shape[:2]
     rows, width = blocks * quarter, blocks * 128
+    count = 4 * quarter
+    channels, group_cols, heads = w_zx.shape[2], w_bc.shape[2], w_dt.shape[1]
+    depth = 1024
     bf16, f32 = jnp.bfloat16, jnp.float32
 
-    def kernel(head_ref, own_ref, right_ref, low_ref, high_ref, left_ref, gain_ref, normed_ref, quarter_ref, emb_ref):
-        head = head_ref[0]
-        row = lax.broadcasted_iota(jnp.int32, (512, 512), 0)
-        col = lax.broadcasted_iota(jnp.int32, (512, 512), 1)
-        source = jnp.bitwise_and(jnp.right_shift(row, 7) + head, 3)
-        goal = spot(source * 128 + jnp.bitwise_and(row, 127))
-        swap = (col == goal).astype(f32).astype(bf16)
-        for at in range(0, rows, 256):
-            if at < rows // 2:
-                far = low_ref[at : at + 256, :]
-            else:
-                far = high_ref[at - rows // 2 : at - rows // 2 + 256, :]
-            here = pl.ds(at, 256)
-            wide = jnp.concatenate([own_ref[here, :], right_ref[here, :], far, left_ref[here, :]], axis=1)
-            swapped = jnp.dot(wide, swap, preferred_element_type=f32).astype(bf16)
-            for c in range(256 // quarter):
-                column = (at // quarter + c) * 128
-                for q in range(4):
-                    emb_ref[q * quarter : (q + 1) * quarter, column : column + 128] = swapped[
-                        c * quarter : (c + 1) * quarter, q * 128 : (q + 1) * 128
-                    ]
-        quarter_ref[...] = emb_ref[pl.ds(pl.multiple_of(head * quarter, quarter), quarter), :]
-        for q in range(4):
-            values = emb_ref[q * quarter : (q + 1) * quarter, :].astype(f32)
-            scale = lax.rsqrt(jnp.mean(values * values, axis=1, keepdims=True) + 1e-05)
-            normed_ref[q * quarter : (q + 1) * quarter, :] = (values * scale * gain_ref[...]).astype(bf16)
-
-    flat = [piece.reshape(-1, 128) for piece in (own, right, far_low, far_high, left)]
+    def kernel(*refs):
+        head_ref, piece_refs, gain_ref = refs[0], refs[1:5], refs[5]
+        zx_ref, bc_ref, dt_ref, z_out, x_out, bc_out, dt_out, quarter_ref, emb_ref, normed_ref = refs[6:]
+        step = pl.program_id(0)
+
+        @pl.when(step == 0)
+        def _():
+            head = head_ref[0]
+            swap = swap_matrix(head)
+            for at in range(0, rows, 256):
+                wide = jnp.concatenate([ref[at : at + 256, :] for ref in piece_refs], axis=1)
+                swapped = jnp.dot(wide, swap, preferred_element_type=f32).astype(bf16)
+                for c in range(256 // quarter):
+                    column = (at // quarter + c) * 128
+                    for q in range(4):
+                        emb_ref[q * quarter : (q + 1) * quarter, column : column + 128] = swapped[
+                            c * quarter : (c + 1) * quarter, q * 128 : (q + 1) * 128
+                        ]
+            mine = pl.ds(pl.multiple_of(head * quarter, quarter), quarter)
+            quarter_ref[...] = emb_ref[mine, :]
+            for q in range(4):
+                at = slice(q * quarter, (q + 1) * quarter)
+                values = emb_ref[at, :].astype(f32)
+                scale = lax.rsqrt(jnp.mean(values * values, axis=1, keepdims=True) + 1e-05)
+                values = (values * scale * gain_ref[...]).astype(bf16)
+                for k in range(width // depth):
+                    normed_ref[k, at, :] = values[:, k * depth : (k + 1) * depth]
+            for out in (z_out, x_out, bc_out, dt_out):
+                out[...] = jnp.zeros_like(out)
+
+        part = normed_ref[step]
+        zx = zx_ref[...].reshape(depth, 2 * channels)
+        z_out[...] += jnp.dot(part, zx[:, :channels], preferred_element_type=f32)
+        x_out[...] += jnp.dot(part, zx[:, channels:], preferred_element_type=f32)
+        bc = bc_ref[...].reshape(depth, 2 * group_cols)
+        bc_out[...] += jnp.dot(part, bc, preferred_element_type=f32)
+        dt_out[...] += jnp.dot(part, dt_ref[...], preferred_element_type=f32)
+
+    flat = [piece.reshape(-1, 128) for piece in pieces]
+    widths = (channels, channels, 2 * group_cols, heads)
     return pl.pallas_call(
         kernel,
-        in_specs=[pl.BlockSpec(memory_space=pltpu.SMEM)] + [in_vmem()] * 6,
-        out_specs=[in_vmem()] * 2,
-        out_shape=[
-            jax.ShapeDtypeStruct((4 * quarter, width), bf16),
-            jax.ShapeDtypeStruct((quarter, width), bf16),
+        grid=(width // depth,),
+        in_specs=[pl.BlockSpec(memory_space=pltpu.SMEM)]
+        + [pl.BlockSpec(piece.shape, lambda i: (0, 0)) for piece in flat]
+        + [
+            pl.BlockSpec((1, width), lambda i: (0, 0)),
+            pl.BlockSpec((depth, 2, channels), lambda i: (i, 0, 0)),
+            pl.BlockSpec((depth, 2, group_cols), lambda i: (i, 0, 0)),
+            pl.BlockSpec((depth, heads), lambda i: (i, 0)),
         ],
-        scratch_shapes=[pltpu.VMEM((4 * quarter, width), bf16)],
-        compiler_params=pltpu.CompilerParams(vmem_limit_bytes=16 << 20),
+        out_specs=[pl.BlockSpec((count, n), lambda i: (0, 0)) for n in widths]
+        + [pl.BlockSpec((quarter, width), lambda i: (0, 0))],
+        out_shape=[jax.ShapeDtypeStruct((count, n), f32) for n in widths]
+        + [jax.ShapeDtypeStruct((quarter, width), bf16)],
+        scratch_shapes=[
+            pltpu.VMEM((count, width), bf16),
+            pltpu.VMEM((width // depth, count, depth), bf16),
+        ],
+        compiler_params=pltpu.CompilerParams(vmem_limit_bytes=48 << 20),
         cost_estimate=pl.CostEstimate(
-            flops=2 * rows * 512 * 512, bytes_accessed=4 << 20, transcendentals=0
+            flops=2 * count * width * sum(widths),
+            bytes_accessed=2 * width * sum(widths),
+            transcendentals=0,
         ),
-    )(head, *flat, gain.reshape(1, width))
+    )(head, *flat, gain.reshape(1, width), w_zx, w_bc, w_dt)
 
 
 def project_out(gated, weights, head):
@@ -227,52 +255,11 @@
         ],
         out_specs=pl.BlockSpec((4, quarter, tile), lambda i: (0, 0, i)),
         out_shape=jax.ShapeDtypeStruct((4, quarter, width), jnp.bfloat16),
-        compiler_params=pltpu.CompilerParams(vmem_limit_bytes=12 << 20),
+        compiler_params=pltpu.CompilerParams(vmem_limit_bytes=48 << 20),
         cost_estimate=pl.CostEstimate(
             flops=2 * count * depth * width, bytes_accessed=2 * depth * width, transcendentals=0
         ),
     )(head, gated, weights)
-
-
-def project(rows, w_zx, w_bc, w_dt):
-    count, width = rows.shape
-    channels, group_cols, heads = w_zx.shape[2], w_bc.shape[2], w_dt.shape[1]
-    depth = 1024
-    f32 = jnp.float32
-
-    def kernel(rows_ref, zx_ref, bc_ref, dt_ref, z_out, x_out, bc_out, dt_out):
-        @pl.when(pl.program_id(0) == 0)
-        def _():
-            for out in (z_out, x_out, bc_out, dt_out):
-                out[...] = jnp.zeros_like(out)
-
-        part = rows_ref[...]
-        zx = zx_ref[...].reshape(depth, 2 * channels)
-        z_out[...] += jnp.dot(part, zx[:, :channels], preferred_element_type=f32)
-        x_out[...] += jnp.dot(part, zx[:, channels:], preferred_element_type=f32)
-        bc = bc_ref[...].reshape(depth, 2 * group_cols)
-        bc_out[...] += jnp.dot(part, bc, preferred_element_type=f32)
-        dt_out[...] += jnp.dot(part, dt_ref[...], preferred_element_type=f32)
-
-    widths = (channels, channels, 2 * group_cols, heads)
-    return pl.pallas_call(
-        kernel,
-        grid=(width // depth,),
-        in_specs=[
-            pl.BlockSpec((count, depth), lambda i: (0, i)),
-            pl.BlockSpec((depth, 2, channels), lambda i: (i, 0, 0)),
-            pl.BlockSpec((depth, 2, group_cols), lambda i: (i, 0, 0)),
-            pl.BlockSpec((depth, heads), lambda i: (i, 0)),
-        ],
-        out_specs=[pl.BlockSpec((count, n), lambda i: (0, 0)) for n in widths],
-        out_shape=[jax.ShapeDtypeStruct((count, n), f32) for n in widths],
-        compiler_params=pltpu.CompilerParams(vmem_limit_bytes=20 << 20),
-        cost_estimate=pl.CostEstimate(
-            flops=2 * count * width * sum(widths),
-            bytes_accessed=2 * width * sum(widths),
-            transcendentals=0,
-        ),
-    )(rows, w_zx, w_bc, w_dt)
 
 
 def rms_scale(values, gain):
@@ -370,7 +357,7 @@
             pltpu.VMEM((count, width), jnp.bfloat16),
             pltpu.VMEM((2 * tiles, count, tile), f32),
         ],
-        compiler_params=pltpu.CompilerParams(vmem_limit_bytes=20 << 20),
+        compiler_params=pltpu.CompilerParams(vmem_limit_bytes=48 << 20),
         cost_estimate=pl.CostEstimate(
             flops=2 * count * width * every,
             bytes_accessed=2 * width * every,
@@ -410,21 +397,30 @@
     vocab_own = lax.all_gather(lm_head, "head", axis=0, tiled=True)
     vocab_other = swap_core(vocab_own)
 
+    leaving = pack_columns(embed, head_at)
+    columns = [
+        leaving[0],
+        moved(leaving[3], shift_head, -1),
+        moved(leaving[2], shift_head, 2),
+        moved(leaving[1], shift_head, 1),
+    ]
     packed = jnp.concatenate([token_ids, targets])
     packed = jnp.broadcast_to(packed[None], (ctx_count, tok_rows + quarter))
+    packed, leaving = lax.optimization_barrier((packed, leaving))
     packed = lax.all_to_all(packed, "ctx", 0, 0, tiled=True)
-    all_ids = packed[:, :tok_rows].reshape(ctx_count // 4, 4, head_count, quarter)
     group_targets = packed[:, tok_rows:]
-
-    columns = lax.all_to_all(pack_columns(embed), "head", 0, 0, tiled=True)
-    all_ids = all_ids.transpose(0, 2, 1, 3).reshape(ctx_count // 4, head_count, 4 * quarter)
-    mine = look_up(all_ids, columns).reshape(ctx_count, quarter, 128)
+    all_ids = packed[:, :tok_rows] - head_pos * embed.shape[0]
+    all_ids = jnp.bitwise_and(all_ids, head_count * embed.shape[0] - 1)
+    all_ids = all_ids.reshape(ctx_count // 4, 4, head_count, quarter).transpose(0, 2, 1, 3)
+    mine = look_up(all_ids.reshape(2, ctx_count // 2, 4 * quarter), columns)
+    mine = mine.reshape(ctx_count, quarter, 128)
     mine = lax.all_to_all(mine, "ctx", 0, 0, tiled=True)
-    normed_in, own_emb = assemble(ring_gather(mine, shift_head), head_at, pre_gain)
 
     channels = w_zx.shape[2]
     group_cols = w_bc.shape[2]
-    gate_z, proj_x, proj_bc, step_raw = project(normed_in, w_zx, w_bc, w_dt)
+    gate_z, proj_x, proj_bc, step_raw, own_emb = embed_and_project(
+        ring_gather(mine, shift_head), head_at, pre_gain, w_zx, w_bc, w_dt
+    )
     mixed_in = jnp.concatenate([proj_x, proj_bc], axis=1)
     conv_taps = conv_x.shape[0]
     rim_rows = passed_along(mixed_in[tok_rows - conv_taps + 1 :], "ctx", 1)
@@ -490,36 +486,49 @@
     normed_out = rms_scale(residual.astype(f32), final_gain).astype(bf16)
 
     along_first, along_second = shift_mixed(True), shift_mixed(False)
-    from_left = moved(normed_out, along_first, 1)
-    from_right = moved(normed_out, along_first, -1)
-    from_far = moved(normed_out, along_first, 2)
-    near = jnp.concatenate([normed_out, from_left])
-    rest = jnp.concatenate([from_right, from_far])
+    own, right, far, left = ring_gather(normed_out, along_first)
+    near = jnp.concatenate([own, left])
+    rest = jnp.concatenate([right, far])
+    near_right = moved(near, along_second, -1)
     near_left = moved(near, along_second, 1)
-    near_right = moved(near, along_second, -1)
+    near_far = moved(near, along_second, 2)
+    rest_right = moved(rest, along_second, -1)
     rest_left = moved(rest, along_second, 1)
-    rest_right = moved(rest, along_second, -1)
+    rest_far = moved(rest, along_second, 2)
     y_pos, z_pos, core = ctx_pos // 8, (ctx_pos // 2) % 4, ctx_pos % 2
     by_chip = lax.dynamic_index_in_dim(group_targets.reshape(4, 4, 2, quarter), core, 2, False)
     by_chip = jnp.roll(by_chip, (-y_pos, -z_pos), (0, 1))
     by_chip = jnp.where(core == 0, by_chip, by_chip.transpose(1, 0, 2))
     order = (0, 3, 1, 2)
-    by_chip = jnp.stack([by_chip[:, k] for k in order], axis=1).reshape(4, 1, 4 * quarter)
+    by_chip = jnp.stack([by_chip[:, k] for k in order], axis=1).reshape(4, 4 * quarter)
     vocab_width = vocab_own.shape[1]
     by_chip = jnp.stack([by_chip - ctx_pos * vocab_width, by_chip - (ctx_pos ^ 1) * vocab_width])
     tables = (vocab_own, vocab_other)
-    rows = 4 * quarter
-    stats = [vocab_stats((near, rest), by_chip[:, 0], tables)]
-    near_left, rest_right, stats[0] = lax.optimization_barrier((near_left, rest_right, stats[0]))
-    near_far = moved(near_left, along_second, 1)
-    rest_far = moved(rest_right, along_second, -1)
-    aims = jnp.concatenate([by_chip[:, 1], by_chip[:, 3]], axis=1)
-    sides = vocab_stats((near_right, rest_right, near_left, rest_left), aims, tables)
-    stats.append(moved(sides[:, :rows], along_second, 1))
-    stats.append(moved(vocab_stats((near_far, rest_far), by_chip[:, 2], tables), along_second, 2))
-    stats.append(moved(sides[:, rows:], along_second, -1))
+    pair = 2 * quarter
+
+    def aims(places):
+        picked = [by_chip[:, k, part * pair : (part + 1) * pair] for k, part in places]
+        return jnp.concatenate(picked, axis=1).reshape(2, -1, 128)
+
+    stats_own = vocab_stats((near, rest), aims(((0, 0), (0, 1))), tables)
+    near_right, near_left, stats_own = lax.optimization_barrier((near_right, near_left, stats_own))
+    stats_near = vocab_stats((near_right, near_left), aims(((1, 0), (3, 0))), tables)
+    near_far, rest_right, rest_left, rest_far, stats_near = lax.optimization_barrier(
+        (near_far, rest_right, rest_left, rest_far, stats_near)
+    )
+    stats_rest = vocab_stats(
+        (near_far, rest_right, rest_left, rest_far), aims(((2, 0), (1, 1), (3, 1), (2, 1))), tables
+    )
+    found = (
+        (stats_near[:, :pair], stats_rest[:, pair : 2 * pair]),
+        (stats_rest[:, :pair], stats_rest[:, 3 * pair :]),
+        (stats_near[:, pair:], stats_rest[:, 2 * pair : 3 * pair]),
+    )
+    stats = [stats_own]
+    for k in range(1, 4):
+        stats.append(moved(jnp.concatenate(found[k - 1], axis=1), along_second, k))
     merged = tuple(stats[0][:5])
-    for other in (stats[1], stats[3], stats[2]):
+    for other in stats[1:]:
         merged = join_stats(merged, tuple(other[:5]))
     both = jnp.stack(merged).reshape(5, 4, quarter)
     merged = tuple(both[:, 0])

time: 233 us -> 233 us (level)
  starting transfers between devices: 59.2 us -> 74.3 us
  blocking collectives: 12.6 us -> 0 us
  local copies, waits for them, and re-layouts: 26.1 us -> 16.8 us
  waiting for transfers between devices: 70.7 us -> 73.4 us
    all_to_all x1 -> x0, blocking collectives: 12.6 us -> none  [on_device(): state_in = lax.all_to_all(entering, 'ctx', 0, 0, tiled=True)]
    ppermute x23 -> x24, starting transfers between devices: 32.3 us -> 41.8 us  [moved(): return lax.ppermute(value, axis, pairs)]
    unnamed x76 -> x58, local copies, waits for them, and re-layouts: 20.1 us -> 12.9 us
    all_to_all x1, waiting for transfers between devices: 14.5 us -> 10.6 us  [on_device(): state_in = lax.all_to_all(entering, 'ctx', 0, 0, tiled=True)]
    all_to_all x1, starting transfers between devices: 4 us -> 7.81 us  [on_device(): mine = lax.all_to_all(mine, 'ctx', 0, 0, tiled=True)]
    all_to_all x1, waiting for transfers between devices: 7.25 us -> 10.2 us  [on_device(): arrived = lax.all_to_all(message, 'ctx', 0, 0, tiled=True)]
    pallas_call x1, Pallas kernels: 2.5 us -> 4.94 us  [project_out(): pl.pallas_call(kernel, grid=(width // tile,), in_specs=[pl.BlockSpec(memo...]
    pallas_call x4 -> x3, Pallas kernels: 20.5 us -> 19.4 us  [the longest x1 11 us: embed_and_project(): pl.pallas_call(kernel, grid=(width // depth,), in_specs=[pl.BlockSpec(mem...]
  transfers between devices with their start and end apart: 31 -> 32, of which waited for: 15 -> 18; matrix products, arithmetic and copies ran while one was open for 7% -> 7% of each run, Pallas kernels for 17% -> 15%
where the time goes in v4:
time: 233 us; the launch traced here: 232 us
  starting transfers between devices  74.3 us (32%)
  waiting for transfers between devices  73.4 us (32%)
  Pallas kernels  42.2 us (18%)
  local copies, waits for them, and re-layouts  16.8 us (7%)
  between operations  14.1 us (6%)
  other arithmetic  6.79 us (3%)
  matrix products  4.08 us (2%)
    ppermute x24, starting transfers between devices, moved(): return lax.ppermute(value, axis, pairs)  41.8 us
    ppermute x24, waiting for transfers between devices, moved(): return lax.ppermute(value, axis, pairs)  34.1 us
    pallas_call x3, Pallas kernels, vocab_stats(): pl.pallas_call(kernel, grid=(2 * tiles,), in_specs=[pl.BlockSpec(piece.sh...  17.9 us
    unnamed x58, local copies, waits for them, and re-layouts  12.9 us
    pallas_call x1, Pallas kernels, embed_and_project(): pl.pallas_call(kernel, grid=(width // depth,), in_specs=[pl.BlockSpec(mem...  11 us
    all_to_all x1, waiting for transfers between devices, on_device(): state_in = lax.all_to_all(entering, 'ctx', 0, 0, tiled=True)  10.6 us
    all_to_all x1, waiting for transfers between devices, on_device(): arrived = lax.all_to_all(message, 'ctx', 0, 0, tiled=True)  10.2 us
    all_to_all x1, starting transfers between devices, on_device(): packed = lax.all_to_all(packed, 'ctx', 0, 0, tiled=True)  8.33 us
  transfers between devices with their start and end apart: 32, of which 18 were waited for; matrix products, arithmetic and copies ran while one was open for 7% of the time, Pallas kernels for 15%

profile of v4, /device:TPU:0, one launch (start us, length us, event | category | flops | bytes accessed | tf_op | source)
XLA Modules:
  0.0 231.6 jit_solution(8625007036253349904)
XLA Ops:
  6.5 0.7 all-gather.5.cloned.1.call-update
  7.3 0.7 all-gather.3.cloned.1.call-update
  8.0 1.2 copy-done.9
  9.2 1.5 shard_map.154
  10.8 0.7 copy-done.10
  11.5 2.8 %collective-permute-start = (bf16[1024,128]{1,0:T(8,128)(2,1)}, bf16[1024,128]{1,0:T(8,128)(2,1)S(1)}, u32[]{:S(2)}, u32[]{:S(2)}) collective-permute-start(bf16[1024,128]{1,0:T(8,128)(2,1)} %get-tuple-element.28), channel_id=1, source_target_pairs={{0,3},{1,0},{2,1},{3,2},{4,7},{5,4},{6,5},{7,6},{8,11},{9,8},{10,9... | collective-permute-start | bytes 786440 | tf_op jit(solution)/shard_map/ppermute | solution.py:40
  14.3 0.8 collective-permute-start.1
  15.1 0.9 collective-permute-start.2
  16.0 0.7 pad_add_fusion.3
  17.3 8.3 %all-to-all-start = ((s32[32,1,160]{2,1,0:T(1,128)}), s32[32,1,160]{2,1,0:T(1,128)S(1)}, u32[]{:S(2)}, u32[]{:S(2)}) async-start(s32[32,1,160]{2,1,0:T(1,128)} %all_to_all.17), calls=%async_computation | async-start | bytes 65536 | tf_op jit(solution)/shard_map/all_to_all | solution.py:410
  25.7 0.7 constant_dynamic-update-slice_fusion.1
  26.4 6.7 %all-to-all-done = s32[32,1,160]{2,1,0:T(1,128)S(1)} async-done(((s32[32,1,160]{2,1,0:T(1,128)}), s32[32,1,160]{2,1,0:T(1,128)S(1)}, u32[]{:S(2)}, u32[]{:S(2)}) %all-to-all-start) | async-done | bytes 20512 | tf_op jit(solution)/shard_map/all_to_all | solution.py:410
  34.0 1.1 copy-done.11
  35.1 6.9 %shard_map.155 = bf16[1024,128]{1,0:T(8,128)(2,1)} custom-call(s32[2,16,128]{2,1,0:T(8,128)S(1)} %reshape.196.ids_ref, bf16[1024,128]{1,0:T(8,128)(2,1)S(1)} %copy-done.11, bf16[1024,128]{1,0:T(8,128)(2,1)S(1)} %collective-permute-done.refs_1_, bf16[1024,128]{1,0:T(8,128)(2,1)S(1)} %collective-permute-done.1.refs_2_, ...), custom_call_target="tpu_custom_call" | custom-call | flops 4294967296 | bytes 2097152 | tf_op jit(solution)/shard_map/pallas_call | solution.py:146
  42.0 7.8 %all-to-all-start.1 = ((bf16[32,32,128]{2,1,0:T(8,128)(2,1)}), bf16[32,32,128]{2,1,0:T(8,128)(2,1)S(1)}, u32[]{:S(2)}, u32[]{:S(2)}) async-start(bf16[32,32,128]{2,1,0:T(8,128)(2,1)} %bitcast.2), calls=%async_computation.1 | async-start | bytes 524288 | tf_op jit(solution)/shard_map/all_to_all | solution.py:417
  50.5 8.3 %all-to-all-done.1 = bf16[32,32,128]{2,1,0:T(8,128)(2,1)S(1)} async-done(((bf16[32,32,128]{2,1,0:T(8,128)(2,1)}), bf16[32,32,128]{2,1,0:T(8,128)(2,1)S(1)}, u32[]{:S(2)}, u32[]{:S(2)}) %all-to-all-start.1) | async-done | bytes 262176 | tf_op jit(solution)/shard_map/all_to_all | solution.py:417
  58.8 2.1 collective-permute-start.3
  60.9 1.1 collective-permute-start.4
  62.6 1.4 copy.70.refs_8_
  64.6 8.0 %collective-permute-done.3 = bf16[32,32,128]{2,1,0:T(8,128)(2,1)} collective-permute-done((bf16[32,32,128]{2,1,0:T(8,128)(2,1)S(1)}, bf16[32,32,128]{2,1,0:T(8,128)(2,1)}, u32[]{:S(2)}, u32[]{:S(2)}) %collective-permute-start.3) | collective-permute-done | bytes 262176 | tf_op jit(solution)/shard_map/ppermute | solution.py:40
  72.6 3.8 %collective-permute-done.5 = bf16[32,32,128]{2,1,0:T(8,128)(2,1)} collective-permute-done((bf16[32,32,128]{2,1,0:T(8,128)(2,1)S(1)}, bf16[32,32,128]{2,1,0:T(8,128)(2,1)}, u32[]{:S(2)}, u32[]{:S(2)}) %collective-permute-start.5) | collective-permute-done | bytes 262176 | tf_op jit(solution)/shard_map/ppermute | solution.py:40
  76.4 11.0 %shard_map.156 = (f32[128,1024]{1,0:T(8,128)S(1)}, f32[128,1024]{1,0:T(8,128)S(1)}, f32[128,256]{1,0:T(8,128)S(1)}, f32[128,16]{1,0:T(8,128)S(1)}, bf16[32,4096]{1,0:T(8,128)(2,1)S(1)}) custom-call(s32[1]{0:T(128)} %bitcast.head_ref.refs_0_, bf16[1024,128]{1,0:T(8,128)(2,1)S(1)} %bitcast.309, bf16[1024,128]{1,0:T(8,128)(2,1)} %bitcast.4.refs_2_, ...), custom_call_target="tpu_custom_call" | custom-call | flops 2432696320 | bytes 19005440 | tf_op jit(solution)/shard_map/pallas_call | solution.py:209
  87.4 0.8 copy-done.2
  88.2 0.8 copy-done.4
  89.0 0.7 copy-done.5
  90.7 1.1 constant_dynamic-update-slice_fusion.3
  91.8 2.1 collective-permute-start.6
  94.1 0.9 fusion.101
  95.3 1.2 divide_multiply_fusion
  97.4 0.9 maximum_maximum_fusion
  98.3 7.8 %all-to-all-start.2 = ((bf16[32,48,128]{2,1,0:T(8,128)(2,1)}), bf16[32,48,128]{2,1,0:T(8,128)(2,1)S(1)}, u32[]{:S(2)}, u32[]{:S(2)}) async-start(bf16[32,48,128]{2,1,0:T(8,128)(2,1)} %maximum_maximum_fusion), calls=%async_computation.2 | async-start | bytes 786432 | tf_op jit(solution)/shard_map/all_to_all | solution.py:455
  106.4 2.2 fusion
  108.7 10.2 %all-to-all-done.2 = bf16[32,48,128]{2,1,0:T(8,128)(2,1)S(1)} async-done(((bf16[32,48,128]{2,1,0:T(8,128)(2,1)}), bf16[32,48,128]{2,1,0:T(8,128)(2,1)S(1)}, u32[]{:S(2)}, u32[]{:S(2)}) %all-to-all-start.2) | async-done | bytes 393248 | tf_op jit(solution)/shard_map/all_to_all | solution.py:455
  119.8 0.7 copy.89
  120.5 5.3 %all-to-all-start.3 = ((bf16[32,32,128]{2,1,0:T(8,128)(2,1)}), bf16[32,32,128]{2,1,0:T(8,128)(2,1)S(1)}, u32[]{:S(2)}, u32[]{:S(2)}) async-start(bf16[32,32,128]{2,1,0:T(8,128)(2,1)} %bitcast.68), calls=%async_computation.3 | async-start | bytes 524288 | tf_op jit(solution)/shard_map/all_to_all | solution.py:472
  126.0 10.6 %all-to-all-done.3 = bf16[32,32,128]{2,1,0:T(8,128)(2,1)S(1)} async-done(((bf16[32,32,128]{2,1,0:T(8,128)(2,1)}), bf16[32,32,128]{2,1,0:T(8,128)(2,1)S(1)}, u32[]{:S(2)}, u32[]{:S(2)}) %all-to-all-start.3) | async-done | bytes 262176 | tf_op jit(solution)/shard_map/all_to_all | solution.py:472
  137.6 1.1 collective-permute-start.15
  138.6 2.1 all-gather.3.cloned.1.call-done.weights_ref
  140.8 4.9 %shard_map.157 = bf16[4,32,4096]{2,1,0:T(8,128)(2,1)S(1)} custom-call(s32[1]{0:T(128)} %bitcast.head_ref.refs_0_, bf16[128,1024]{1,0:T(8,128)(2,1)S(1)} %multiply_convert_fusion.gated_ref, bf16[1024,4096]{1,0:T(8,128)(2,1)} %all-gather.3.cloned.1.call-done.weights_ref), custom_call_target="tpu_custom_call" | custom-call | flops 1073741824 | bytes 8388608 | tf_op jit(solution)/shard_map/pallas_call | solution.py:248
  145.8 1.5 collective-permute-start.7
  147.2 2.6 %collective-permute-start.8 = (bf16[32,4096]{1,0:T(8,128)(2,1)S(1)}, bf16[32,4096]{1,0:T(8,128)(2,1)S(1)}, u32[]{:S(2)}, u32[]{:S(2)}) collective-permute-start(bf16[32,4096]{1,0:T(8,128)(2,1)S(1)} %get-tuple-element.63), channel_id=1, source_target_pairs={{0,2},{1,3},{2,0},{3,1},{4,6},{5,7},{6,4},{7,5},{8,10},{9,11},{10,... | collective-permute-start | bytes 786440 | tf_op jit(solution)/shard_map/ppermute | solution.py:40
  149.8 2.5 %collective-permute-start.9 = (bf16[32,4096]{1,0:T(8,128)(2,1)S(1)}, bf16[32,4096]{1,0:T(8,128)(2,1)S(1)}, u32[]{:S(2)}, u32[]{:S(2)}) collective-permute-start(bf16[32,4096]{1,0:T(8,128)(2,1)S(1)} %get-tuple-element.62), channel_id=1, source_target_pairs={{0,3},{1,0},{2,1},{3,2},{4,7},{5,4},{6,5},{7,6},{8,11},{9,8},{10,9... | collective-permute-start | bytes 786440 | tf_op jit(solution)/shard_map/ppermute | solution.py:40
  152.3 3.2 %collective-permute-done.7 = bf16[32,4096]{1,0:T(8,128)(2,1)S(1)} collective-permute-done((bf16[32,4096]{1,0:T(8,128)(2,1)S(1)}, bf16[32,4096]{1,0:T(8,128)(2,1)S(1)}, u32[]{:S(2)}, u32[]{:S(2)}) %collective-permute-start.7) | collective-permute-done | bytes 262176 | tf_op jit(solution)/shard_map/ppermute | solution.py:40
  155.5 6.5 %collective-permute-done.8 = bf16[32,4096]{1,0:T(8,128)(2,1)S(1)} collective-permute-done((bf16[32,4096]{1,0:T(8,128)(2,1)S(1)}, bf16[32,4096]{1,0:T(8,128)(2,1)S(1)}, u32[]{:S(2)}, u32[]{:S(2)}) %collective-permute-start.8) | collective-permute-done | bytes 262176 | tf_op jit(solution)/shard_map/ppermute | solution.py:40
  162.5 3.6 %collective-permute-start.10 = (bf16[32,4096]{1,0:T(8,128)(2,1)S(1)}, bf16[32,4096]{1,0:T(8,128)(2,1)S(1)}, u32[]{:S(2)}, u32[]{:S(2)}) collective-permute-start(bf16[32,4096]{1,0:T(8,128)(2,1)S(1)} %fusion.18), channel_id=1, source_target_pairs={{0,8},{4,36},{8,16},{12,44},{16,24},{20,52},{24,0},{28,60},{32,40}... | collective-permute-start | bytes 786440 | tf_op jit(solution)/shard_map/ppermute | solution.py:40
  166.3 0.8 collective-permute-start.13
  167.1 3.0 %collective-permute-start.14 = (bf16[32,4096]{1,0:T(8,128)(2,1)S(1)}, bf16[32,4096]{1,0:T(8,128)(2,1)S(1)}, u32[]{:S(2)}, u32[]{:S(2)}) collective-permute-start(bf16[32,4096]{1,0:T(8,128)(2,1)S(1)} %fusion.18), channel_id=1, source_target_pairs={{0,16},{4,68},{8,24},{12,76},{16,0},{20,84},{24,8},{28,92},{32,48}... | collective-permute-start | bytes 786440 | tf_op jit(solution)/shard_map/ppermute | solution.py:40
  170.1 1.0 collective-permute-done.10
  171.2 3.8 %collective-permute-start.11 = (bf16[64,4096]{1,0:T(8,128)(2,1)S(1)}, bf16[64,4096]{1,0:T(8,128)(2,1)S(1)}, u32[]{:S(2)}, u32[]{:S(2)}) collective-permute-start(bf16[64,4096]{1,0:T(8,128)(2,1)S(1)} %pad_maximum_fusion.1.refs_0_), channel_id=1, source_target_pairs={{0,96},{4,28},{8,104},{12,4},{16,112},{20,12},{24,120},{28,20},{32... | collective-permute-start | bytes 1572872 | tf_op jit(solution)/shard_map/ppermute | solution.py:40
  175.5 5.1 %collective-permute-start.17 = (bf16[64,4096]{1,0:T(8,128)(2,1)S(1)}, bf16[64,4096]{1,0:T(8,128)(2,1)S(1)}, u32[]{:S(2)}, u32[]{:S(2)}) collective-permute-start(bf16[64,4096]{1,0:T(8,128)(2,1)S(1)} %constant_dynamic-update-slice_fusion.4.refs_1_), channel_id=1, source_target_pairs={{0,96},{4,28},{8,104},{12,4},{16,112},{20,12},{24,120},{28,20},{32... | collective-permute-start | bytes 1572872 | tf_op jit(solution)/shard_map/ppermute | solution.py:40
  180.6 1.5 collective-permute-start.19
  182.1 2.0 collective-permute-start.16
  184.3 2.2 copy-done
  186.5 5.3 %shard_map.158 = f32[8,128]{1,0:T(8,128)S(1)} custom-call(bf16[64,4096]{1,0:T(8,128)(2,1)S(1)} %pad_maximum_fusion.1.refs_0_, bf16[64,4096]{1,0:T(8,128)(2,1)S(1)} %constant_dynamic-update-slice_fusion.4.refs_1_, s32[2,1,128]{2,1,0:T(1,128)S(1)} %bitcast.312, bf16[4096,512]{1,0:T(8,128)(2,1)S(1)} %copy-done, ...), custom_call_target="tpu_custom_call" | custom-call | flops 1073741824 | bytes 8388608 | tf_op jit(solution)/shard_map/pallas_call | solution.py:345
  191.8 5.3 %shard_map.159 = f32[8,128]{1,0:T(8,128)S(1)} custom-call(bf16[64,4096]{1,0:T(8,128)(2,1)S(1)} %collective-permute-done.11.refs_0_, bf16[64,4096]{1,0:T(8,128)(2,1)S(1)} %collective-permute-done.12.refs_1_, s32[2,1,128]{2,1,0:T(1,128)S(1)} %bitcast.311, bf16[4096,512]{1,0:T(8,128)(2,1)S(1)} %copy-done, bf16[4096,512]{1,0:T(8,128)(2,1)} %collective-permute-done.15.refs_4_.refs_6_), custom_call_target="tpu_custom_call" | custom-call | flops 1073741824 | bytes 8388608 | tf_op jit(solution)/shard_map/pallas_call | solution.py:345
  197.1 1.4 collective-permute-done.17.refs_1_
  198.5 3.7 %collective-permute-done.18.refs_2_ = bf16[64,4096]{1,0:T(8,128)(2,1)S(1)} collective-permute-done((bf16[64,4096]{1,0:T(8,128)(2,1)S(1)}, bf16[64,4096]{1,0:T(8,128)(2,1)S(1)}, u32[]{:S(2)}, u32[]{:S(2)}) %collective-permute-start.18) | collective-permute-done | bytes 524320 | tf_op jit(solution)/shard_map/ppermute | solution.py:40
  202.2 7.3 %shard_map.160 = f32[8,256]{1,0:T(8,128)S(1)} custom-call(bf16[64,4096]{1,0:T(8,128)(2,1)} %collective-permute-done.16.refs_0_, bf16[64,4096]{1,0:T(8,128)(2,1)S(1)} %collective-permute-done.17.refs_1_, bf16[64,4096]{1,0:T(8,128)(2,1)S(1)} %collective-permute-done.18.refs_2_, bf16[64,4096]{1,0:T(8,128)(2,1)} %collective-permute-done.19.refs_3_, ...), custom_call_target="tpu_custom_call" | custom-call | flops 2147483648 | bytes 8388608 | tf_op jit(solution)/shard_map/pallas_call | solution.py:345
  209.8 1.5 collective-permute-start.21
  211.3 1.8 collective-permute-start.22
  213.1 1.4 collective-permute-done.20
  216.1 3.0 %collective-permute-start.23 = (f32[5,32]{1,0:T(8,128)S(1)}, f32[5,32]{1,0:T(8,128)S(1)}, u32[]{:S(2)}, u32[]{:S(2)}) collective-permute-start(f32[5,32]{1,0:T(8,128)S(1)} %bitcast.329), channel_id=1, source_target_pairs={{0,24},{4,100},{8,0},{12,108},{16,8},{20,116},{24,16},{28,124},{32... | collective-permute-start | bytes 1928 | tf_op jit(solution)/shard_map/ppermute | solution.py:40
  219.1 1.6 collective-permute-start.25
  220.7 3.3 %collective-permute-done.24 = f32[5,32]{1,0:T(8,128)S(1)} collective-permute-done((f32[5,32]{1,0:T(8,128)S(1)}, f32[5,32]{1,0:T(8,128)S(1)}, u32[]{:S(2)}, u32[]{:S(2)}) %collective-permute-start.24) | collective-permute-done | bytes 672 | tf_op jit(solution)/shard_map/ppermute | solution.py:40
  (145 shorter events, 12.3 us)
Async XLA Ops:
  6.5 131.0 %all-gather.5.cloned.1.call-start = ((), (), s32[]{:S(2)}) async-start(), calls=%async_computation.5 | async-start | bytes 5242880 | tf_op jit(solution)/shard_map/all_gather | solution.py:397
  7.3 133.5 %all-gather.3.cloned.1.call-start = ((), (), s32[]{:S(2)}) async-start(), calls=%async_computation.4 | async-start | bytes 8650752 | tf_op jit(solution)/shard_map/all_gather | solution.py:396
  8.0 1.2 copy-start.9
  10.8 0.7 copy-start.10
  11.5 22.5 %collective-permute-start = (bf16[1024,128]{1,0:T(8,128)(2,1)}, bf16[1024,128]{1,0:T(8,128)(2,1)S(1)}, u32[]{:S(2)}, u32[]{:S(2)}) collective-permute-start(bf16[1024,128]{1,0:T(8,128)(2,1)} %get-tuple-element.28), channel_id=1, source_target_pairs={{0,3},{1,0},{2,1},{3,2},{4,7},{5,4},{6,5},{7,6},{8,11},{9,8},{10,9... | collective-permute-start | bytes 786440 | tf_op jit(solution)/shard_map/ppermute | solution.py:40
  14.3 19.7 %collective-permute-start.1 = (bf16[1024,128]{1,0:T(8,128)(2,1)S(1)}, bf16[1024,128]{1,0:T(8,128)(2,1)S(1)}, u32[]{:S(2)}, u32[]{:S(2)}) collective-permute-start(bf16[1024,128]{1,0:T(8,128)(2,1)S(1)} %get-tuple-element.27), channel_id=1, source_target_pairs={{0,2},{1,3},{2,0},{3,1},{4,6},{5,7},{6,4},{7,5},{8,10},{9,11},{10,... | collective-permute-start | bytes 786440 | tf_op jit(solution)/shard_map/ppermute | solution.py:40
  15.1 18.9 %collective-permute-start.2 = (bf16[1024,128]{1,0:T(8,128)(2,1)S(1)}, bf16[1024,128]{1,0:T(8,128)(2,1)S(1)}, u32[]{:S(2)}, u32[]{:S(2)}) collective-permute-start(bf16[1024,128]{1,0:T(8,128)(2,1)S(1)} %get-tuple-element.26), channel_id=1, source_target_pairs={{0,1},{1,2},{2,3},{3,0},{4,5},{5,6},{6,7},{7,4},{8,9},{9,10},{10,1... | collective-permute-start | bytes 786440 | tf_op jit(solution)/shard_map/ppermute | solution.py:40
  17.3 15.8 %all-to-all-start = ((s32[32,1,160]{2,1,0:T(1,128)}), s32[32,1,160]{2,1,0:T(1,128)S(1)}, u32[]{:S(2)}, u32[]{:S(2)}) async-start(s32[32,1,160]{2,1,0:T(1,128)} %all_to_all.17), calls=%async_computation | async-start | bytes 65536 | tf_op jit(solution)/shard_map/all_to_all | solution.py:410
  33.1 0.6 copy-start.12
  33.8 16.0 %copy-start.17 = (f32[4,2,128]{2,1,0:T(2,128)S(1)}, f32[4,2,128]{2,1,0:T(2,128)}, u32[]{:S(2)}) copy-start(f32[4,2,128]{2,1,0:T(2,128)} %param.23) | copy-start | bytes 12292
  33.9 30.8 %copy-start.20 = (f32[16]{0:T(128)S(1)}, f32[16]{0:T(128)}, u32[]{:S(2)}) copy-start(f32[16]{0:T(128)} %param.25) | copy-start | bytes 196
  34.0 42.4 %copy-start.1 = (bf16[4096,2,128]{2,1,0:T(2,128)(2,1)S(1)}, bf16[4096,2,128]{2,1,0:T(2,128)(2,1)}, u32[]{:S(2)}) copy-start(bf16[4096,2,128]{2,1,0:T(2,128)(2,1)} %refs_7_.1) | copy-start | bytes 6291460
  34.0 42.4 %copy-start.8 = (f32[4096]{0:T(1024)S(1)}, f32[4096]{0:T(1024)}, u32[]{:S(2)}) copy-start(f32[4096]{0:T(1024)} %param.28) | copy-start | bytes 49156
  34.0 1.1 copy-start.11
  42.0 16.8 %all-to-all-start.1 = ((bf16[32,32,128]{2,1,0:T(8,128)(2,1)}), bf16[32,32,128]{2,1,0:T(8,128)(2,1)S(1)}, u32[]{:S(2)}, u32[]{:S(2)}) async-start(bf16[32,32,128]{2,1,0:T(8,128)(2,1)} %bitcast.2), calls=%async_computation.1 | async-start | bytes 524288 | tf_op jit(solution)/shard_map/all_to_all | solution.py:417
  58.8 13.8 %collective-permute-start.3 = (bf16[32,32,128]{2,1,0:T(8,128)(2,1)S(1)}, bf16[32,32,128]{2,1,0:T(8,128)(2,1)}, u32[]{:S(2)}, u32[]{:S(2)}) collective-permute-start(bf16[32,32,128]{2,1,0:T(8,128)(2,1)S(1)} %all-to-all-done.1), channel_id=1, source_target_pairs={{0,3},{1,0},{2,1},{3,2},{4,7},{5,4},{6,5},{7,6},{8,11},{9,8},{10,9... | collective-permute-start | bytes 786440 | tf_op jit(solution)/shard_map/ppermute | solution.py:40
  60.9 11.7 %collective-permute-start.4 = (bf16[32,32,128]{2,1,0:T(8,128)(2,1)S(1)}, bf16[32,32,128]{2,1,0:T(8,128)(2,1)}, u32[]{:S(2)}, u32[]{:S(2)}) collective-permute-start(bf16[32,32,128]{2,1,0:T(8,128)(2,1)S(1)} %all-to-all-done.1), channel_id=1, source_target_pairs={{0,2},{1,3},{2,0},{3,1},{4,6},{5,7},{6,4},{7,5},{8,10},{9,11},{10,... | collective-permute-start | bytes 786440 | tf_op jit(solution)/shard_map/ppermute | solution.py:40
  62.0 14.4 %collective-permute-start.5 = (bf16[32,32,128]{2,1,0:T(8,128)(2,1)S(1)}, bf16[32,32,128]{2,1,0:T(8,128)(2,1)}, u32[]{:S(2)}, u32[]{:S(2)}) collective-permute-start(bf16[32,32,128]{2,1,0:T(8,128)(2,1)S(1)} %all-to-all-done.1), channel_id=1, source_target_pairs={{0,1},{1,2},{2,3},{3,0},{4,5},{5,6},{6,7},{7,4},{8,9},{9,10},{10,1... | collective-permute-start | bytes 786440 | tf_op jit(solution)/shard_map/ppermute | solution.py:40
  76.4 13.9 %copy-start.18 = (f32[16]{0:T(128)S(1)}, f32[16]{0:T(128)}, u32[]{:S(2)}) copy-start(f32[16]{0:T(128)} %param.24) | copy-start | bytes 196
  87.4 0.8 copy-start.2
  88.2 0.8 copy-start.4
  89.0 0.7 copy-start.5
  89.7 0.6 copy-start.7
  89.7 7.7 %copy-start.19 = (bf16[48]{0:T(256)(128)(2,1)S(1)}, bf16[48]{0:T(256)(128)(2,1)}, u32[]{:S(2)}) copy-start(bf16[48]{0:T(256)(128)(2,1)} %pad.27.clone) | copy-start | bytes 292
  89.7 16.7 %copy-start.15 = (pred[128,128]{1,0:T(8,128)(4,1)S(1)}, pred[128,128]{1,0:T(8,128)(4,1)}, u32[]{:S(2)}) copy-start(pred[128,128]{1,0:T(8,128)(4,1)} %iota_compare_fusion) | copy-start | bytes 49156
  89.7 16.7 %copy-start.21 = (f32[16]{0:T(128)S(1)}, f32[16]{0:T(128)}, u32[]{:S(2)}) copy-start(f32[16]{0:T(128)} %param.26) | copy-start | bytes 196
  91.8 3.5 %collective-permute-start.6 = (f32[3,1280]{1,0:T(4,128)S(1)}, f32[3,1280]{1,0:T(4,128)S(1)}, u32[]{:S(2)}, u32[]{:S(2)}) collective-permute-start(f32[3,1280]{1,0:T(4,128)S(1)} %slice.205), channel_id=1, source_target_pairs={{0,4},{4,8},{8,12},{12,16},{16,20},{20,24},{24,28},{28,32},{32,36}... | collective-permute-start | bytes 46088 | tf_op jit(solution)/shard_map/ppermute | solution.py:46
  96.5 29.5 %copy-start.13 = (s32[32,1,160]{2,0,1:T(8,128)S(1)}, s32[32,1,160]{2,0,1:T(8,128)}, u32[]{:S(2)}) copy-start(s32[32,1,160]{2,0,1:T(8,128)} %copy-done.12) | copy-start | bytes 61444
  97.4 39.7 %copy-start.3 = (f32[128,1024]{1,0:T(8,128)S(1)}, f32[128,1024]{1,0:T(8,128)}, u32[]{:S(2)}) copy-start(f32[128,1024]{1,0:T(8,128)} %copy-done.2) | copy-start | bytes 1572868
  98.3 20.6 %all-to-all-start.2 = ((bf16[32,48,128]{2,1,0:T(8,128)(2,1)}), bf16[32,48,128]{2,1,0:T(8,128)(2,1)S(1)}, u32[]{:S(2)}, u32[]{:S(2)}) async-start(bf16[32,48,128]{2,1,0:T(8,128)(2,1)} %maximum_maximum_fusion), calls=%async_computation.2 | async-start | bytes 786432 | tf_op jit(solution)/shard_map/all_to_all | solution.py:455
  106.4 31.0 %copy-start.16 = (f32[1024]{0:T(1024)S(1)}, f32[1024]{0:T(1024)}, u32[]{:S(2)}) copy-start(f32[1024]{0:T(1024)} %param.27) | copy-start | bytes 12292
  120.5 16.0 %all-to-all-start.3 = ((bf16[32,32,128]{2,1,0:T(8,128)(2,1)}), bf16[32,32,128]{2,1,0:T(8,128)(2,1)S(1)}, u32[]{:S(2)}, u32[]{:S(2)}) async-start(bf16[32,32,128]{2,1,0:T(8,128)(2,1)} %bitcast.68), calls=%async_computation.3 | async-start | bytes 524288 | tf_op jit(solution)/shard_map/all_to_all | solution.py:472
  137.5 24.5 %copy-start.6 = (bf16[32,4096]{1,0:T(8,128)(2,1)S(1)}, bf16[32,4096]{1,0:T(8,128)(2,1)}, u32[]{:S(2)}) copy-start(bf16[32,4096]{1,0:T(8,128)(2,1)} %copy-done.5) | copy-start | bytes 786436
  137.5 24.8 %copy-start.14 = (f32[4096]{0:T(1024)S(1)}, f32[4096]{0:T(1024)}, u32[]{:S(2)}) copy-start(f32[4096]{0:T(1024)} %param.29) | copy-start | bytes 49156
  137.6 43.0 %collective-permute-start.15 = (bf16[4096,512]{1,0:T(8,128)(2,1)}, bf16[4096,512]{1,0:T(8,128)(2,1)}, u32[]{:S(2)}, u32[]{:S(2)}) collective-permute-start(bf16[4096,512]{1,0:T(8,128)(2,1)} %all-gather.5.cloned.1.call-done.refs_3_.refs_5_), channel_id=1, source_target_pairs={{0,4},{4,0},{8,12},{12,8},{16,20},{20,16},{24,28},{28,24},{32,36},... | collective-permute-start | bytes 12582920 | tf_op jit(solution)/shard_map/ppermute | solution.py:35
  145.8 9.7 %collective-permute-start.7 = (bf16[32,4096]{1,0:T(8,128)(2,1)S(1)}, bf16[32,4096]{1,0:T(8,128)(2,1)S(1)}, u32[]{:S(2)}, u32[]{:S(2)}) collective-permute-start(bf16[32,4096]{1,0:T(8,128)(2,1)S(1)} %get-tuple-element.61), channel_id=1, source_target_pairs={{0,1},{1,2},{2,3},{3,0},{4,5},{5,6},{6,7},{7,4},{8,9},{9,10},{10,1... | collective-permute-start | bytes 786440 | tf_op jit(solution)/shard_map/ppermute | solution.py:40
  147.2 14.8 %collective-permute-start.8 = (bf16[32,4096]{1,0:T(8,128)(2,1)S(1)}, bf16[32,4096]{1,0:T(8,128)(2,1)S(1)}, u32[]{:S(2)}, u32[]{:S(2)}) collective-permute-start(bf16[32,4096]{1,0:T(8,128)(2,1)S(1)} %get-tuple-element.63), channel_id=1, source_target_pairs={{0,2},{1,3},{2,0},{3,1},{4,6},{5,7},{6,4},{7,5},{8,10},{9,11},{10,... | collective-permute-start | bytes 786440 | tf_op jit(solution)/shard_map/ppermute | solution.py:40
  149.8 12.2 %collective-permute-start.9 = (bf16[32,4096]{1,0:T(8,128)(2,1)S(1)}, bf16[32,4096]{1,0:T(8,128)(2,1)S(1)}, u32[]{:S(2)}, u32[]{:S(2)}) collective-permute-start(bf16[32,4096]{1,0:T(8,128)(2,1)S(1)} %get-tuple-element.62), channel_id=1, source_target_pairs={{0,3},{1,0},{2,1},{3,2},{4,7},{5,4},{6,5},{7,6},{8,11},{9,8},{10,9... | collective-permute-start | bytes 786440 | tf_op jit(solution)/shard_map/ppermute | solution.py:40
  162.5 8.7 %collective-permute-start.10 = (bf16[32,4096]{1,0:T(8,128)(2,1)S(1)}, bf16[32,4096]{1,0:T(8,128)(2,1)S(1)}, u32[]{:S(2)}, u32[]{:S(2)}) collective-permute-start(bf16[32,4096]{1,0:T(8,128)(2,1)S(1)} %fusion.18), channel_id=1, source_target_pairs={{0,8},{4,36},{8,16},{12,44},{16,24},{20,52},{24,0},{28,60},{32,40}... | collective-permute-start | bytes 786440 | tf_op jit(solution)/shard_map/ppermute | solution.py:40
  166.3 8.6 %collective-permute-start.13 = (bf16[32,4096]{1,0:T(8,128)(2,1)S(1)}, bf16[32,4096]{1,0:T(8,128)(2,1)S(1)}, u32[]{:S(2)}, u32[]{:S(2)}) collective-permute-start(bf16[32,4096]{1,0:T(8,128)(2,1)S(1)} %fusion.18), channel_id=1, source_target_pairs={{0,24},{4,100},{8,0},{12,108},{16,8},{20,116},{24,16},{28,124},{32... | collective-permute-start | bytes 786440 | tf_op jit(solution)/shard_map/ppermute | solution.py:40
  167.1 8.3 %collective-permute-start.14 = (bf16[32,4096]{1,0:T(8,128)(2,1)S(1)}, bf16[32,4096]{1,0:T(8,128)(2,1)S(1)}, u32[]{:S(2)}, u32[]{:S(2)}) collective-permute-start(bf16[32,4096]{1,0:T(8,128)(2,1)S(1)} %fusion.18), channel_id=1, source_target_pairs={{0,16},{4,68},{8,24},{12,76},{16,0},{20,84},{24,8},{28,92},{32,48}... | collective-permute-start | bytes 786440 | tf_op jit(solution)/shard_map/ppermute | solution.py:40
  171.2 10.9 %collective-permute-start.11 = (bf16[64,4096]{1,0:T(8,128)(2,1)S(1)}, bf16[64,4096]{1,0:T(8,128)(2,1)S(1)}, u32[]{:S(2)}, u32[]{:S(2)}) collective-permute-start(bf16[64,4096]{1,0:T(8,128)(2,1)S(1)} %pad_maximum_fusion.1.refs_0_), channel_id=1, source_target_pairs={{0,96},{4,28},{8,104},{12,4},{16,112},{20,12},{24,120},{28,20},{32... | collective-permute-start | bytes 1572872 | tf_op jit(solution)/shard_map/ppermute | solution.py:40
  175.0 16.8 %collective-permute-start.12 = (bf16[64,4096]{1,0:T(8,128)(2,1)S(1)}, bf16[64,4096]{1,0:T(8,128)(2,1)S(1)}, u32[]{:S(2)}, u32[]{:S(2)}) collective-permute-start(bf16[64,4096]{1,0:T(8,128)(2,1)S(1)} %pad_maximum_fusion.1.refs_0_), channel_id=1, source_target_pairs={{0,32},{4,12},{8,40},{12,20},{16,48},{20,28},{24,56},{28,4},{32,64... | collective-permute-start | bytes 1572872 | tf_op jit(solution)/shard_map/ppermute | solution.py:40
  175.5 23.1 %collective-permute-start.17 = (bf16[64,4096]{1,0:T(8,128)(2,1)S(1)}, bf16[64,4096]{1,0:T(8,128)(2,1)S(1)}, u32[]{:S(2)}, u32[]{:S(2)}) collective-permute-start(bf16[64,4096]{1,0:T(8,128)(2,1)S(1)} %constant_dynamic-update-slice_fusion.4.refs_1_), channel_id=1, source_target_pairs={{0,96},{4,28},{8,104},{12,4},{16,112},{20,12},{24,120},{28,20},{32... | collective-permute-start | bytes 1572872 | tf_op jit(solution)/shard_map/ppermute | solution.py:40
  180.5 21.7 %collective-permute-start.18 = (bf16[64,4096]{1,0:T(8,128)(2,1)S(1)}, bf16[64,4096]{1,0:T(8,128)(2,1)S(1)}, u32[]{:S(2)}, u32[]{:S(2)}) collective-permute-start(bf16[64,4096]{1,0:T(8,128)(2,1)S(1)} %constant_dynamic-update-slice_fusion.4.refs_1_), channel_id=1, source_target_pairs={{0,32},{4,12},{8,40},{12,20},{16,48},{20,28},{24,56},{28,4},{32,64... | collective-permute-start | bytes 1572872 | tf_op jit(solution)/shard_map/ppermute | solution.py:40
  180.6 21.7 %collective-permute-start.19 = (bf16[64,4096]{1,0:T(8,128)(2,1)S(1)}, bf16[64,4096]{1,0:T(8,128)(2,1)}, u32[]{:S(2)}, u32[]{:S(2)}) collective-permute-start(bf16[64,4096]{1,0:T(8,128)(2,1)S(1)} %constant_dynamic-update-slice_fusion.4.refs_1_), channel_id=1, source_target_pairs={{0,64},{4,20},{8,72},{12,28},{16,80},{20,4},{24,88},{28,12},{32,96... | collective-permute-start | bytes 1572872 | tf_op jit(solution)/shard_map/ppermute | solution.py:40
  182.1 20.1 %collective-permute-start.16 = (bf16[64,4096]{1,0:T(8,128)(2,1)S(1)}, bf16[64,4096]{1,0:T(8,128)(2,1)}, u32[]{:S(2)}, u32[]{:S(2)}) collective-permute-start(bf16[64,4096]{1,0:T(8,128)(2,1)S(1)} %pad_maximum_fusion.1.refs_0_), channel_id=1, source_target_pairs={{0,64},{4,20},{8,72},{12,28},{16,80},{20,4},{24,88},{28,12},{32,96... | collective-permute-start | bytes 1572872 | tf_op jit(solution)/shard_map/ppermute | solution.py:40
  184.3 2.2 copy-start
  209.7 4.8 %collective-permute-start.20 = (f32[8,128]{1,0:T(8,128)S(1)}, f32[8,128]{1,0:T(8,128)S(1)}, u32[]{:S(2)}, u32[]{:S(2)}) collective-permute-start(f32[8,128]{1,0:T(8,128)S(1)} %pad_maximum_fusion.2), channel_id=1, source_target_pairs={{0,32},{4,12},{8,40},{12,20},{16,48},{20,28},{24,56},{28,4},{32,64... | collective-permute-start | bytes 12296 | tf_op jit(solution)/shard_map/ppermute | solution.py:40
  209.8 5.1 %collective-permute-start.21 = (f32[8,128]{1,0:T(8,128)S(1)}, f32[8,128]{1,0:T(8,128)S(1)}, u32[]{:S(2)}, u32[]{:S(2)}) collective-permute-start(f32[8,128]{1,0:T(8,128)S(1)} %pad_maximum_fusion.3), channel_id=1, source_target_pairs={{0,64},{4,20},{8,72},{12,28},{16,80},{20,4},{24,88},{28,12},{32,96... | collective-permute-start | bytes 12296 | tf_op jit(solution)/shard_map/ppermute | solution.py:40
  211.3 4.2 %collective-permute-start.22 = (f32[8,128]{1,0:T(8,128)S(1)}, f32[8,128]{1,0:T(8,128)S(1)}, u32[]{:S(2)}, u32[]{:S(2)}) collective-permute-start(f32[8,128]{1,0:T(8,128)S(1)} %pad_maximum_fusion.4), channel_id=1, source_target_pairs={{0,96},{4,28},{8,104},{12,4},{16,112},{20,12},{24,120},{28,20},{32... | collective-permute-start | bytes 12296 | tf_op jit(solution)/shard_map/ppermute | solution.py:40
  216.1 4.6 %collective-permute-start.23 = (f32[5,32]{1,0:T(8,128)S(1)}, f32[5,32]{1,0:T(8,128)S(1)}, u32[]{:S(2)}, u32[]{:S(2)}) collective-permute-start(f32[5,32]{1,0:T(8,128)S(1)} %bitcast.329), channel_id=1, source_target_pairs={{0,24},{4,100},{8,0},{12,108},{16,8},{20,116},{24,16},{28,124},{32... | collective-permute-start | bytes 1928 | tf_op jit(solution)/shard_map/ppermute | solution.py:40
  219.1 4.8 %collective-permute-start.24 = (f32[5,32]{1,0:T(8,128)S(1)}, f32[5,32]{1,0:T(8,128)S(1)}, u32[]{:S(2)}, u32[]{:S(2)}) collective-permute-start(f32[5,32]{1,0:T(8,128)S(1)} %bitcast.330), channel_id=1, source_target_pairs={{0,8},{4,36},{8,16},{12,44},{16,24},{20,52},{24,0},{28,60},{32,40}... | collective-permute-start | bytes 1928 | tf_op jit(solution)/shard_map/ppermute | solution.py:40
  219.1 5.1 %collective-permute-start.25 = (f32[5,32]{1,0:T(8,128)S(1)}, f32[5,32]{1,0:T(8,128)S(1)}, u32[]{:S(2)}, u32[]{:S(2)}) collective-permute-start(f32[5,32]{1,0:T(8,128)S(1)} %bitcast.331), channel_id=1, source_target_pairs={{0,16},{4,68},{8,24},{12,76},{16,0},{20,84},{24,8},{28,92},{32,48}... | collective-permute-start | bytes 1928 | tf_op jit(solution)/shard_map/ppermute | solution.py:40
Sparse Core Ops, SparseCore 0:
  9.0 54.2 all-gather.4
  65.5 75.2 all-gather.2

commit v5 on v4

--- a/solution.py
+++ b/solution.py
@@ -16,19 +16,12 @@
     return "head", [(i, (i + by) % 4) for i in range(4)]
 
 
-def shift_mixed(first):
-    def shift(by):
-        pairs = []
-        for i in range(32):
-            y, z, core = i // 8, (i // 2) % 4, i % 2
-            if (core == 0) == first:
-                z = (z + by) % 4
-            else:
-                y = (y + by) % 4
-            pairs.append((i, y * 8 + z * 2 + core))
-        return "ctx", pairs
-
-    return shift
+def shift_z(by):
+    return "ctx", [(i, (i // 8) * 8 + ((i // 2 + by) % 4) * 2 + i % 2) for i in range(32)]
+
+
+def shift_y(by):
+    return "ctx", [(i, (i + 8 * by) % 32) for i in range(32)]
 
 
 def swap_core(value):
@@ -394,9 +387,6 @@
     ctx_pos = lax.axis_index("ctx")
     head_at = head_pos[None].astype(jnp.int32)
     w_out_full = lax.all_gather(w_out, "ctx", axis=1, tiled=True)
-    vocab_own = lax.all_gather(lm_head, "head", axis=0, tiled=True)
-    vocab_other = swap_core(vocab_own)
-
     leaving = pack_columns(embed, head_at)
     columns = [
         leaving[0],
@@ -408,6 +398,9 @@
     packed = jnp.broadcast_to(packed[None], (ctx_count, tok_rows + quarter))
     packed, leaving = lax.optimization_barrier((packed, leaving))
     packed = lax.all_to_all(packed, "ctx", 0, 0, tiled=True)
+    packed, lm_head = lax.optimization_barrier((packed, lm_head))
+    vocab_own = lax.all_gather(lm_head, "head", axis=0, tiled=True)
+    vocab_other = swap_core(vocab_own)
     group_targets = packed[:, tok_rows:]
     all_ids = packed[:, :tok_rows] - head_pos * embed.shape[0]
     all_ids = jnp.bitwise_and(all_ids, head_count * embed.shape[0] - 1)
@@ -485,55 +478,45 @@
     residual = (own_emb.astype(f32) + summed_out).astype(bf16)
     normed_out = rms_scale(residual.astype(f32), final_gain).astype(bf16)
 
-    along_first, along_second = shift_mixed(True), shift_mixed(False)
-    own, right, far, left = ring_gather(normed_out, along_first)
-    near = jnp.concatenate([own, left])
-    rest = jnp.concatenate([right, far])
-    near_right = moved(near, along_second, -1)
-    near_left = moved(near, along_second, 1)
-    near_far = moved(near, along_second, 2)
-    rest_right = moved(rest, along_second, -1)
-    rest_left = moved(rest, along_second, 1)
-    rest_far = moved(rest, along_second, 2)
+    half = quarter // 2
+    over_z = jnp.concatenate(ring_gather(normed_out[:half], shift_z))
+    over_y = jnp.concatenate(ring_gather(normed_out[half:], shift_y))
+    low = {ahead: moved(over_z, shift_y, -ahead) for ahead in (1, 3, 2)}
+    high = {ahead: moved(over_y, shift_z, -ahead) for ahead in (1, 3, 2)}
+
     y_pos, z_pos, core = ctx_pos // 8, (ctx_pos // 2) % 4, ctx_pos % 2
     by_chip = lax.dynamic_index_in_dim(group_targets.reshape(4, 4, 2, quarter), core, 2, False)
     by_chip = jnp.roll(by_chip, (-y_pos, -z_pos), (0, 1))
-    by_chip = jnp.where(core == 0, by_chip, by_chip.transpose(1, 0, 2))
-    order = (0, 3, 1, 2)
-    by_chip = jnp.stack([by_chip[:, k] for k in order], axis=1).reshape(4, 4 * quarter)
     vocab_width = vocab_own.shape[1]
     by_chip = jnp.stack([by_chip - ctx_pos * vocab_width, by_chip - (ctx_pos ^ 1) * vocab_width])
     tables = (vocab_own, vocab_other)
-    pair = 2 * quarter
+    piece = 4 * half
 
     def aims(places):
-        picked = [by_chip[:, k, part * pair : (part + 1) * pair] for k, part in places]
+        picked = [by_chip[:, k, :, :half].reshape(2, piece) for k in places]
+        picked += [by_chip[:, :, k, half:].reshape(2, piece) for k in places]
         return jnp.concatenate(picked, axis=1).reshape(2, -1, 128)
 
-    stats_own = vocab_stats((near, rest), aims(((0, 0), (0, 1))), tables)
-    near_right, near_left, stats_own = lax.optimization_barrier((near_right, near_left, stats_own))
-    stats_near = vocab_stats((near_right, near_left), aims(((1, 0), (3, 0))), tables)
-    near_far, rest_right, rest_left, rest_far, stats_near = lax.optimization_barrier(
-        (near_far, rest_right, rest_left, rest_far, stats_near)
-    )
-    stats_rest = vocab_stats(
-        (near_far, rest_right, rest_left, rest_far), aims(((2, 0), (1, 1), (3, 1), (2, 1))), tables
-    )
-    found = (
-        (stats_near[:, :pair], stats_rest[:, pair : 2 * pair]),
-        (stats_rest[:, :pair], stats_rest[:, 3 * pair :]),
-        (stats_near[:, pair:], stats_rest[:, 2 * pair : 3 * pair]),
-    )
-    stats = [stats_own]
-    for k in range(1, 4):
-        stats.append(moved(jnp.concatenate(found[k - 1], axis=1), along_second, k))
-    merged = tuple(stats[0][:5])
-    for other in stats[1:]:
-        merged = join_stats(merged, tuple(other[:5]))
+    stats = [None] * 4
+    own = vocab_stats((over_z, over_y), aims((0,)), tables)
+    stats[0] = (own[:, :piece], own[:, piece:])
+    low[1], low[3], high[1], high[3], own = lax.optimization_barrier((low[1], low[3], high[1], high[3], own))
+    near = vocab_stats((low[1], low[3], high[1], high[3]), aims((1, 3)), tables)
+    low[2], high[2], near = lax.optimization_barrier((low[2], high[2], near))
+    near = [near[:, k * piece : (k + 1) * piece] for k in range(4)]
+    stats[1], stats[3] = (near[0], near[2]), (near[1], near[3])
+    far = vocab_stats((low[2], high[2]), aims((2,)), tables)
+    stats[2] = (far[:, :piece], far[:, piece:])
+    low_stats = jnp.stack([pair[0][:5].reshape(5, 4, half) for pair in stats], axis=1)
+    high_stats = jnp.stack([pair[1][:5].reshape(5, 4, half) for pair in stats], axis=2)
+    both = jnp.concatenate([low_stats, high_stats], axis=3).reshape(5, 4, 4 * quarter)
+    merged = tuple(both[:, 0])
+    for ahead in range(1, 4):
+        merged = join_stats(merged, tuple(moved(both[:, ahead], shift_y, ahead)))
     both = jnp.stack(merged).reshape(5, 4, quarter)
     merged = tuple(both[:, 0])
-    for place in range(1, 4):
-        merged = join_stats(merged, tuple(moved(both[:, place], along_first, order[place])))
+    for ahead in range(1, 4):
+        merged = join_stats(merged, tuple(moved(both[:, ahead], shift_z, ahead)))
     row_peak, exp_sum, first_moment, second_moment, target_logit = merged
     mean_shift = first_moment / exp_sum
     spread = second_moment / exp_sum - mean_shift * mean_shift

time: 233 us -> 250 us (1.073)
  waiting for transfers between devices: 73.4 us -> 93.6 us
  starting transfers between devices: 74.3 us -> 55.5 us
  blocking collectives: 0 us -> 15.7 us
    ppermute x24 -> x27, waiting for transfers between devices: 34.1 us -> 65.8 us  [moved(): return lax.ppermute(value, axis, pairs)]
    all_to_all x0 -> x1, blocking collectives: none -> 15.7 us  [on_device(): packed = lax.all_to_all(packed, 'ctx', 0, 0, tiled=True)]
    all_to_all x1 -> x0, starting transfers between devices: 8.33 us -> none  [on_device(): packed = lax.all_to_all(packed, 'ctx', 0, 0, tiled=True)]
    all_to_all x1 -> x0, waiting for transfers between devices: 6.71 us -> none  [on_device(): packed = lax.all_to_all(packed, 'ctx', 0, 0, tiled=True)]
    ppermute x24 -> x27, starting transfers between devices: 41.8 us -> 37.7 us  [moved(): return lax.ppermute(value, axis, pairs)]
    all_to_all x1, starting transfers between devices: 7.81 us -> 3.87 us  [on_device(): mine = lax.all_to_all(mine, 'ctx', 0, 0, tiled=True)]
    unnamed x58 -> x62, local copies, waits for them, and re-layouts: 12.9 us -> 12.2 us
  transfers between devices with their start and end apart: 32 -> 34, of which waited for: 18 -> 23; matrix products, arithmetic and copies ran while one was open for 7% -> 7% of each run, Pallas kernels for 15% -> 14%
where the time goes in v5:
time: 250 us; the launch traced here: 249 us
  waiting for transfers between devices  93.6 us (37%)
  starting transfers between devices  55.5 us (22%)
  Pallas kernels  42.4 us (17%)
  local copies, waits for them, and re-layouts  16.8 us (7%)
  blocking collectives  15.7 us (6%)
  between operations  14.1 us (6%)
  other arithmetic  6.83 us (3%)
  matrix products  4.11 us (2%)
    ppermute x27, waiting for transfers between devices, moved(): return lax.ppermute(value, axis, pairs)  65.8 us
    ppermute x27, starting transfers between devices, moved(): return lax.ppermute(value, axis, pairs)  37.7 us
    pallas_call x3, Pallas kernels, vocab_stats(): pl.pallas_call(kernel, grid=(2 * tiles,), in_specs=[pl.BlockSpec(piece.sh...  17.9 us
    all_to_all x1, blocking collectives, on_device(): packed = lax.all_to_all(packed, 'ctx', 0, 0, tiled=True)  15.7 us
    unnamed x62, local copies, waits for them, and re-layouts  12.2 us
    pallas_call x1, Pallas kernels, embed_and_project(): pl.pallas_call(kernel, grid=(width // depth,), in_specs=[pl.BlockSpec(mem...  10.9 us
    all_to_all x1, waiting for transfers between devices, on_device(): arrived = lax.all_to_all(message, 'ctx', 0, 0, tiled=True)  9.92 us
    all_to_all x1, waiting for transfers between devices, on_device(): state_in = lax.all_to_all(entering, 'ctx', 0, 0, tiled=True)  8.83 us
  transfers between devices with their start and end apart: 34, of which 23 were waited for; matrix products, arithmetic and copies ran while one was open for 7% of the time, Pallas kernels for 14%

profile of v5, /device:TPU:0, one launch (start us, length us, event | category | flops | bytes accessed | tf_op | source)
XLA Modules:
  0.0 249.0 jit_solution(6918258623559071528)
XLA Ops:
  6.5 1.2 copy-done.10
  7.8 0.8 shard_map.154
  8.6 0.7 copy-done.11
  10.0 15.7 %all_to_all.27 = s32[32,1,160]{2,1,0:T(1,128)S(1)} all-to-all(s32[32,1,160]{2,1,0:T(1,128)S(1)} %all_to_all.17), channel_id=1, replica_groups=mesh['ctx'=32,'head'=4] {'ctx'}, dimensions={0} | all-to-all | bytes 40960 | tf_op jit(solution)/shard_map/all_to_all | solution.py:400
  25.7 0.7 all-gather.3.cloned.1.call-update
  26.4 2.8 %collective-permute-start = (bf16[1024,128]{1,0:T(8,128)(2,1)S(1)}, bf16[1024,128]{1,0:T(8,128)(2,1)S(1)}, u32[]{:S(2)}, u32[]{:S(2)}) collective-permute-start(bf16[1024,128]{1,0:T(8,128)(2,1)S(1)} %get-tuple-element.29), channel_id=1, source_target_pairs={{0,3},{1,0},{2,1},{3,2},{4,7},{5,4},{6,5},{7,6},{8,11},{9,8},{10,9... | collective-permute-start | bytes 786440 | tf_op jit(solution)/shard_map/ppermute | solution.py:33
  29.3 0.8 collective-permute-start.1
  30.1 0.9 collective-permute-start.2
  31.0 0.7 constant_dynamic-update-slice_fusion.1
  32.0 9.5 %collective-permute-done.refs_1_ = bf16[1024,128]{1,0:T(8,128)(2,1)S(1)} collective-permute-done((bf16[1024,128]{1,0:T(8,128)(2,1)S(1)}, bf16[1024,128]{1,0:T(8,128)(2,1)S(1)}, u32[]{:S(2)}, u32[]{:S(2)}) %collective-permute-start) | collective-permute-done | bytes 262176 | tf_op jit(solution)/shard_map/ppermute | solution.py:33
  42.1 8.1 %collective-permute-done.2.refs_3_ = bf16[1024,128]{1,0:T(8,128)(2,1)} collective-permute-done((bf16[1024,128]{1,0:T(8,128)(2,1)S(1)}, bf16[1024,128]{1,0:T(8,128)(2,1)}, u32[]{:S(2)}, u32[]{:S(2)}) %collective-permute-start.2) | collective-permute-done | bytes 262176 | tf_op jit(solution)/shard_map/ppermute | solution.py:33
  50.2 0.9 copy-done.12
  51.1 7.9 %shard_map.155 = bf16[1024,128]{1,0:T(8,128)(2,1)} custom-call(s32[2,16,128]{2,1,0:T(8,128)S(1)} %reshape.195.ids_ref, bf16[1024,128]{1,0:T(8,128)(2,1)S(1)} %copy-done.12, bf16[1024,128]{1,0:T(8,128)(2,1)S(1)} %collective-permute-done.refs_1_, bf16[1024,128]{1,0:T(8,128)(2,1)S(1)} %collective-permute-done.1.refs_2_, ...), custom_call_target="tpu_custom_call" | custom-call | flops 4294967296 | bytes 2097152 | tf_op jit(solution)/shard_map/pallas_call | solution.py:139
  59.0 3.9 %all-to-all-start.1 = ((bf16[32,32,128]{2,1,0:T(8,128)(2,1)}), bf16[32,32,128]{2,1,0:T(8,128)(2,1)S(1)}, u32[]{:S(2)}, u32[]{:S(2)}) async-start(bf16[32,32,128]{2,1,0:T(8,128)(2,1)} %bitcast.2), calls=%async_computation.1 | async-start | bytes 524288 | tf_op jit(solution)/shard_map/all_to_all | solution.py:410
  63.5 8.3 %all-to-all-done.1 = bf16[32,32,128]{2,1,0:T(8,128)(2,1)S(1)} async-done(((bf16[32,32,128]{2,1,0:T(8,128)(2,1)}), bf16[32,32,128]{2,1,0:T(8,128)(2,1)S(1)}, u32[]{:S(2)}, u32[]{:S(2)}) %all-to-all-start.1) | async-done | bytes 262176 | tf_op jit(solution)/shard_map/all_to_all | solution.py:410
  71.8 2.7 %collective-permute-start.3 = (bf16[32,32,128]{2,1,0:T(8,128)(2,1)S(1)}, bf16[32,32,128]{2,1,0:T(8,128)(2,1)}, u32[]{:S(2)}, u32[]{:S(2)}) collective-permute-start(bf16[32,32,128]{2,1,0:T(8,128)(2,1)S(1)} %all-to-all-done.1), channel_id=1, source_target_pairs={{0,3},{1,0},{2,1},{3,2},{4,7},{5,4},{6,5},{7,6},{8,11},{9,8},{10,9... | collective-permute-start | bytes 786440 | tf_op jit(solution)/shard_map/ppermute | solution.py:33
  74.5 1.3 collective-permute-start.4
  76.4 1.4 copy.114.refs_8_
  78.4 7.7 %collective-permute-done.3 = bf16[32,32,128]{2,1,0:T(8,128)(2,1)} collective-permute-done((bf16[32,32,128]{2,1,0:T(8,128)(2,1)S(1)}, bf16[32,32,128]{2,1,0:T(8,128)(2,1)}, u32[]{:S(2)}, u32[]{:S(2)}) %collective-permute-start.3) | collective-permute-done | bytes 262176 | tf_op jit(solution)/shard_map/ppermute | solution.py:33
  86.2 3.8 %collective-permute-done.5 = bf16[32,32,128]{2,1,0:T(8,128)(2,1)} collective-permute-done((bf16[32,32,128]{2,1,0:T(8,128)(2,1)S(1)}, bf16[32,32,128]{2,1,0:T(8,128)(2,1)}, u32[]{:S(2)}, u32[]{:S(2)}) %collective-permute-start.5) | collective-permute-done | bytes 262176 | tf_op jit(solution)/shard_map/ppermute | solution.py:33
  90.0 10.9 %shard_map.156 = (f32[128,1024]{1,0:T(8,128)S(1)}, f32[128,1024]{1,0:T(8,128)S(1)}, f32[128,256]{1,0:T(8,128)S(1)}, f32[128,16]{1,0:T(8,128)S(1)}, bf16[32,4096]{1,0:T(8,128)(2,1)S(1)}) custom-call(s32[1]{0:T(128)} %bitcast.head_ref.refs_0_, bf16[1024,128]{1,0:T(8,128)(2,1)S(1)} %bitcast.362, bf16[1024,128]{1,0:T(8,128)(2,1)} %bitcast.4.refs_2_, ...), custom_call_target="tpu_custom_call" | custom-call | flops 2432696320 | bytes 19005440 | tf_op jit(solution)/shard_map/pallas_call | solution.py:202
  100.9 0.9 copy-done.3
  101.7 0.8 copy-done.5
  102.5 0.7 copy-done.6
  104.2 1.1 constant_dynamic-update-slice_fusion.3
  105.3 2.1 collective-permute-start.6
  107.6 0.9 fusion.105
  108.8 1.2 divide_multiply_fusion
  110.9 0.9 maximum_maximum_fusion
  111.8 6.7 %all-to-all-start.2 = ((bf16[32,48,128]{2,1,0:T(8,128)(2,1)}), bf16[32,48,128]{2,1,0:T(8,128)(2,1)S(1)}, u32[]{:S(2)}, u32[]{:S(2)}) async-start(bf16[32,48,128]{2,1,0:T(8,128)(2,1)} %maximum_maximum_fusion), calls=%async_computation.2 | async-start | bytes 786432 | tf_op jit(solution)/shard_map/all_to_all | solution.py:448
  118.8 2.2 fusion
  121.0 9.9 %all-to-all-done.2 = bf16[32,48,128]{2,1,0:T(8,128)(2,1)S(1)} async-done(((bf16[32,48,128]{2,1,0:T(8,128)(2,1)}), bf16[32,48,128]{2,1,0:T(8,128)(2,1)S(1)}, u32[]{:S(2)}, u32[]{:S(2)}) %all-to-all-start.2) | async-done | bytes 393248 | tf_op jit(solution)/shard_map/all_to_all | solution.py:448
  131.9 0.7 copy.143
  132.6 4.7 %all-to-all-start.3 = ((bf16[32,32,128]{2,1,0:T(8,128)(2,1)}), bf16[32,32,128]{2,1,0:T(8,128)(2,1)S(1)}, u32[]{:S(2)}, u32[]{:S(2)}) async-start(bf16[32,32,128]{2,1,0:T(8,128)(2,1)} %bitcast.75), calls=%async_computation.3 | async-start | bytes 524288 | tf_op jit(solution)/shard_map/all_to_all | solution.py:465
  137.4 8.8 %all-to-all-done.3 = bf16[32,32,128]{2,1,0:T(8,128)(2,1)S(1)} async-done(((bf16[32,32,128]{2,1,0:T(8,128)(2,1)}), bf16[32,32,128]{2,1,0:T(8,128)(2,1)S(1)}, u32[]{:S(2)}, u32[]{:S(2)}) %all-to-all-start.3) | async-done | bytes 262176 | tf_op jit(solution)/shard_map/all_to_all | solution.py:465
  147.7 4.9 %shard_map.157 = bf16[4,32,4096]{2,1,0:T(8,128)(2,1)S(1)} custom-call(s32[1]{0:T(128)} %bitcast.head_ref.refs_0_, bf16[128,1024]{1,0:T(8,128)(2,1)S(1)} %multiply_convert_fusion.gated_ref, bf16[1024,4096]{1,0:T(8,128)(2,1)} %all-gather.3.cloned.1.call-done.weights_ref), custom_call_target="tpu_custom_call" | custom-call | flops 1073741824 | bytes 8388608 | tf_op jit(solution)/shard_map/pallas_call | solution.py:241
  153.3 2.4 collective-permute-start.8
  155.7 1.7 collective-permute-start.9
  157.5 10.5 %collective-permute-done.7 = bf16[32,4096]{1,0:T(8,128)(2,1)S(1)} collective-permute-done((bf16[32,4096]{1,0:T(8,128)(2,1)S(1)}, bf16[32,4096]{1,0:T(8,128)(2,1)S(1)}, u32[]{:S(2)}, u32[]{:S(2)}) %collective-permute-start.7) | collective-permute-done | bytes 262176 | tf_op jit(solution)/shard_map/ppermute | solution.py:33
  169.1 1.2 collective-permute-start.13
  170.2 1.6 collective-permute-start.14
  172.8 1.3 collective-permute-start.10
  174.1 0.9 collective-permute-done.13
  175.0 1.5 collective-permute-start.11
  176.5 0.9 collective-permute-done.14
  177.8 1.0 collective-permute-done.15
  178.8 2.0 collective-permute-start.21
  181.5 3.5 %collective-permute-done.12 = bf16[16,4096]{1,0:T(8,128)(2,1)S(1)} collective-permute-done((bf16[16,4096]{1,0:T(8,128)(2,1)S(1)}, bf16[16,4096]{1,0:T(8,128)(2,1)S(1)}, u32[]{:S(2)}, u32[]{:S(2)}) %collective-permute-start.12) | collective-permute-done | bytes 131104 | tf_op jit(solution)/shard_map/ppermute | solution.py:33
  185.0 2.6 %collective-permute-start.19 = (bf16[64,4096]{1,0:T(8,128)(2,1)S(1)}, bf16[64,4096]{1,0:T(8,128)(2,1)S(1)}, u32[]{:S(2)}, u32[]{:S(2)}) collective-permute-start(bf16[64,4096]{1,0:T(8,128)(2,1)S(1)} %pad_maximum_fusion.1.refs_0_), channel_id=1, source_target_pairs={{0,96},{4,100},{8,104},{12,108},{16,112},{20,116},{24,120},{28,124... | collective-permute-start | bytes 1572872 | tf_op jit(solution)/shard_map/ppermute | solution.py:33
  187.8 1.3 collective-permute-start.18
  189.0 4.7 %collective-permute-done.21.refs_2_ = bf16[64,4096]{1,0:T(8,128)(2,1)S(1)} collective-permute-done((bf16[64,4096]{1,0:T(8,128)(2,1)S(1)}, bf16[64,4096]{1,0:T(8,128)(2,1)S(1)}, u32[]{:S(2)}, u32[]{:S(2)}) %collective-permute-start.21) | collective-permute-done | bytes 524320 | tf_op jit(solution)/shard_map/ppermute | solution.py:33
  193.7 1.6 collective-permute-start.17
  195.3 2.2 copy-done
  197.5 5.3 %shard_map.158 = f32[8,128]{1,0:T(8,128)S(1)} custom-call(bf16[64,4096]{1,0:T(8,128)(2,1)S(1)} %pad_maximum_fusion.1.refs_0_, bf16[64,4096]{1,0:T(8,128)(2,1)S(1)} %pad_maximum_fusion.2.refs_1_, s32[2,1,128]{2,1,0:T(1,128)S(1)} %bitcast.365, bf16[4096,512]{1,0:T(8,128)(2,1)S(1)} %copy-done, bf16[4096,512]{1,0:T(8,128)(2,1)} %collective-permute-done.16.refs_4_.refs_6_), custom_call_target="tpu_custom_call" | custom-call | flops 1073741824 | bytes 8388608 | tf_op jit(solution)/shard_map/pallas_call | solution.py:338
  203.0 6.2 %collective-permute-done.20.refs_1_ = bf16[64,4096]{1,0:T(8,128)(2,1)S(1)} collective-permute-done((bf16[64,4096]{1,0:T(8,128)(2,1)S(1)}, bf16[64,4096]{1,0:T(8,128)(2,1)S(1)}, u32[]{:S(2)}, u32[]{:S(2)}) %collective-permute-start.20) | collective-permute-done | bytes 524320 | tf_op jit(solution)/shard_map/ppermute | solution.py:33
  209.2 7.1 %shard_map.159 = f32[8,256]{1,0:T(8,128)S(1)} custom-call(bf16[64,4096]{1,0:T(8,128)(2,1)S(1)} %collective-permute-done.19.refs_0_, bf16[64,4096]{1,0:T(8,128)(2,1)S(1)} %collective-permute-done.20.refs_1_, bf16[64,4096]{1,0:T(8,128)(2,1)S(1)} %collective-permute-done.21.refs_2_, bf16[64,4096]{1,0:T(8,128)(2,1)S(1)} %collective-permute-done.22.refs_3_, ...), custom_call_target="tpu_custom_call" | custom-call | flops 2147483648 | bytes 8388608 | tf_op jit(solution)/shard_map/pallas_call | solution.py:338
  216.3 5.5 %shard_map.160 = f32[8,128]{1,0:T(8,128)S(1)} custom-call(bf16[64,4096]{1,0:T(8,128)(2,1)} %collective-permute-done.17.refs_0_, bf16[64,4096]{1,0:T(8,128)(2,1)} %collective-permute-done.18.refs_1_, s32[2,1,128]{2,1,0:T(1,128)S(1)} %bitcast.364, bf16[4096,512]{1,0:T(8,128)(2,1)S(1)} %copy-done.1, bf16[4096,512]{1,0:T(8,128)(2,1)} %collective-permute-done.16.refs_4_.refs_6_), custom_call_target="tpu_custom_call" | custom-call | flops 1073741824 | bytes 8388608 | tf_op jit(solution)/shard_map/pallas_call | solution.py:338
  222.8 1.7 collective-permute-start.23
  224.5 4.1 %collective-permute-start.24 = (f32[5,128]{1,0:T(8,128)S(1)}, f32[5,128]{1,0:T(8,128)S(1)}, u32[]{:S(2)}, u32[]{:S(2)}) collective-permute-start(f32[5,128]{1,0:T(8,128)S(1)} %bitcast.390), channel_id=1, source_target_pairs={{0,64},{4,68},{8,72},{12,76},{16,80},{20,84},{24,88},{28,92},{32,9... | collective-permute-start | bytes 7688 | tf_op jit(solution)/shard_map/ppermute | solution.py:33
  228.7 1.5 collective-permute-done.24
  230.2 2.0 collective-permute-done.25
  232.9 5.1 %collective-permute-start.27 = (f32[5,32]{1,0:T(8,128)S(1)}, f32[5,32]{1,0:T(8,128)S(1)}, u32[]{:S(2)}, u32[]{:S(2)}) collective-permute-start(f32[5,32]{1,0:T(8,128)S(1)} %bitcast.391), channel_id=1, source_target_pairs={{0,16},{4,20},{8,24},{12,28},{16,0},{20,4},{24,8},{28,12},{32,48},... | collective-permute-start | bytes 1928 | tf_op jit(solution)/shard_map/ppermute | solution.py:33
  238.1 1.5 collective-permute-done.27
  239.6 2.0 collective-permute-done.28
  (168 shorter events, 15.1 us)
Async XLA Ops:
  6.5 140.7 %all-gather.5.cloned.1.call-start = ((), (), s32[]{:S(2)}) async-start(), calls=%async_computation.5 | async-start | bytes 5242880 | tf_op jit(solution)/shard_map/all_gather | solution.py:402
  6.5 1.2 copy-start.10
  8.6 0.7 copy-start.11
  25.7 6.0 %copy-start.13 = (s32[32,1,160]{2,0,1:T(8,128)}, s32[32,1,160]{2,0,1:T(8,128)S(1)}, u32[]{:S(2)}) copy-start(s32[32,1,160]{2,0,1:T(8,128)S(1)} %copy.156) | copy-start | bytes 61444
  25.7 122.0 %all-gather.3.cloned.1.call-start = ((), (), s32[]{:S(2)}) async-start(), calls=%async_computation.4 | async-start | bytes 8650752 | tf_op jit(solution)/shard_map/all_gather | solution.py:389
  26.4 15.0 %collective-permute-start = (bf16[1024,128]{1,0:T(8,128)(2,1)S(1)}, bf16[1024,128]{1,0:T(8,128)(2,1)S(1)}, u32[]{:S(2)}, u32[]{:S(2)}) collective-permute-start(bf16[1024,128]{1,0:T(8,128)(2,1)S(1)} %get-tuple-element.29), channel_id=1, source_target_pairs={{0,3},{1,0},{2,1},{3,2},{4,7},{5,4},{6,5},{7,6},{8,11},{9,8},{10,9... | collective-permute-start | bytes 786440 | tf_op jit(solution)/shard_map/ppermute | solution.py:33
  29.3 12.8 %collective-permute-start.1 = (bf16[1024,128]{1,0:T(8,128)(2,1)S(1)}, bf16[1024,128]{1,0:T(8,128)(2,1)S(1)}, u32[]{:S(2)}, u32[]{:S(2)}) collective-permute-start(bf16[1024,128]{1,0:T(8,128)(2,1)S(1)} %get-tuple-element.28), channel_id=1, source_target_pairs={{0,2},{1,3},{2,0},{3,1},{4,6},{5,7},{6,4},{7,5},{8,10},{9,11},{10,... | collective-permute-start | bytes 786440 | tf_op jit(solution)/shard_map/ppermute | solution.py:33
  30.1 20.1 %collective-permute-start.2 = (bf16[1024,128]{1,0:T(8,128)(2,1)S(1)}, bf16[1024,128]{1,0:T(8,128)(2,1)}, u32[]{:S(2)}, u32[]{:S(2)}) collective-permute-start(bf16[1024,128]{1,0:T(8,128)(2,1)S(1)} %get-tuple-element.27), channel_id=1, source_target_pairs={{0,1},{1,2},{2,3},{3,0},{4,5},{5,6},{6,7},{7,4},{8,9},{9,10},{10,1... | collective-permute-start | bytes 786440 | tf_op jit(solution)/shard_map/ppermute | solution.py:33
  31.8 31.0 %copy-start.18 = (f32[4,2,128]{2,1,0:T(2,128)S(1)}, f32[4,2,128]{2,1,0:T(2,128)}, u32[]{:S(2)}) copy-start(f32[4,2,128]{2,1,0:T(2,128)} %param.23) | copy-start | bytes 12292
  31.8 46.6 %copy-start.21 = (f32[16]{0:T(128)S(1)}, f32[16]{0:T(128)}, u32[]{:S(2)}) copy-start(f32[16]{0:T(128)} %param.25) | copy-start | bytes 196
  31.9 58.0 %copy-start.2 = (bf16[4096,2,128]{2,1,0:T(2,128)(2,1)S(1)}, bf16[4096,2,128]{2,1,0:T(2,128)(2,1)}, u32[]{:S(2)}) copy-start(bf16[4096,2,128]{2,1,0:T(2,128)(2,1)} %refs_7_.1) | copy-start | bytes 6291460
  31.9 58.0 %copy-start.9 = (f32[4096]{0:T(1024)S(1)}, f32[4096]{0:T(1024)}, u32[]{:S(2)}) copy-start(f32[4096]{0:T(1024)} %param.28) | copy-start | bytes 49156
  50.2 1.0 copy-start.12
  59.0 12.8 %all-to-all-start.1 = ((bf16[32,32,128]{2,1,0:T(8,128)(2,1)}), bf16[32,32,128]{2,1,0:T(8,128)(2,1)S(1)}, u32[]{:S(2)}, u32[]{:S(2)}) async-start(bf16[32,32,128]{2,1,0:T(8,128)(2,1)} %bitcast.2), calls=%async_computation.1 | async-start | bytes 524288 | tf_op jit(solution)/shard_map/all_to_all | solution.py:410
  71.8 14.4 %collective-permute-start.3 = (bf16[32,32,128]{2,1,0:T(8,128)(2,1)S(1)}, bf16[32,32,128]{2,1,0:T(8,128)(2,1)}, u32[]{:S(2)}, u32[]{:S(2)}) collective-permute-start(bf16[32,32,128]{2,1,0:T(8,128)(2,1)S(1)} %all-to-all-done.1), channel_id=1, source_target_pairs={{0,3},{1,0},{2,1},{3,2},{4,7},{5,4},{6,5},{7,6},{8,11},{9,8},{10,9... | collective-permute-start | bytes 786440 | tf_op jit(solution)/shard_map/ppermute | solution.py:33
  74.5 11.7 %collective-permute-start.4 = (bf16[32,32,128]{2,1,0:T(8,128)(2,1)S(1)}, bf16[32,32,128]{2,1,0:T(8,128)(2,1)}, u32[]{:S(2)}, u32[]{:S(2)}) collective-permute-start(bf16[32,32,128]{2,1,0:T(8,128)(2,1)S(1)} %all-to-all-done.1), channel_id=1, source_target_pairs={{0,2},{1,3},{2,0},{3,1},{4,6},{5,7},{6,4},{7,5},{8,10},{9,11},{10,... | collective-permute-start | bytes 786440 | tf_op jit(solution)/shard_map/ppermute | solution.py:33
  75.7 14.2 %collective-permute-start.5 = (bf16[32,32,128]{2,1,0:T(8,128)(2,1)S(1)}, bf16[32,32,128]{2,1,0:T(8,128)(2,1)}, u32[]{:S(2)}, u32[]{:S(2)}) collective-permute-start(bf16[32,32,128]{2,1,0:T(8,128)(2,1)S(1)} %all-to-all-done.1), channel_id=1, source_target_pairs={{0,1},{1,2},{2,3},{3,0},{4,5},{5,6},{6,7},{7,4},{8,9},{9,10},{10,1... | collective-permute-start | bytes 786440 | tf_op jit(solution)/shard_map/ppermute | solution.py:33
  89.9 13.9 %copy-start.19 = (f32[16]{0:T(128)S(1)}, f32[16]{0:T(128)}, u32[]{:S(2)}) copy-start(f32[16]{0:T(128)} %param.24) | copy-start | bytes 196
  100.9 0.9 copy-start.3
  101.7 0.8 copy-start.5
  102.5 0.7 copy-start.6
  103.2 0.6 copy-start.8
  103.2 7.7 %copy-start.20 = (bf16[48]{0:T(256)(128)(2,1)S(1)}, bf16[48]{0:T(256)(128)(2,1)}, u32[]{:S(2)}) copy-start(bf16[48]{0:T(256)(128)(2,1)} %pad.32.clone) | copy-start | bytes 292
  103.2 15.6 %copy-start.16 = (pred[128,128]{1,0:T(8,128)(4,1)S(1)}, pred[128,128]{1,0:T(8,128)(4,1)}, u32[]{:S(2)}) copy-start(pred[128,128]{1,0:T(8,128)(4,1)} %iota_compare_fusion) | copy-start | bytes 49156
  103.2 15.6 %copy-start.22 = (f32[16]{0:T(128)S(1)}, f32[16]{0:T(128)}, u32[]{:S(2)}) copy-start(f32[16]{0:T(128)} %param.26) | copy-start | bytes 196
  105.3 3.4 %collective-permute-start.6 = (f32[3,1280]{1,0:T(4,128)S(1)}, f32[3,1280]{1,0:T(4,128)S(1)}, u32[]{:S(2)}, u32[]{:S(2)}) collective-permute-start(f32[3,1280]{1,0:T(4,128)S(1)} %slice.221), channel_id=1, source_target_pairs={{0,4},{4,8},{8,12},{12,16},{16,20},{20,24},{24,28},{28,32},{32,36}... | collective-permute-start | bytes 46088 | tf_op jit(solution)/shard_map/ppermute | solution.py:39
  110.0 27.4 %copy-start.14 = (s32[32,1,160]{2,0,1:T(8,128)S(1)}, s32[32,1,160]{2,0,1:T(8,128)}, u32[]{:S(2)}) copy-start(s32[32,1,160]{2,0,1:T(8,128)} %copy-done.13) | copy-start | bytes 61444
  110.8 36.0 %copy-start.4 = (f32[128,1024]{1,0:T(8,128)S(1)}, f32[128,1024]{1,0:T(8,128)}, u32[]{:S(2)}) copy-start(f32[128,1024]{1,0:T(8,128)} %copy-done.3) | copy-start | bytes 1572868
  111.8 19.2 %all-to-all-start.2 = ((bf16[32,48,128]{2,1,0:T(8,128)(2,1)}), bf16[32,48,128]{2,1,0:T(8,128)(2,1)S(1)}, u32[]{:S(2)}, u32[]{:S(2)}) async-start(bf16[32,48,128]{2,1,0:T(8,128)(2,1)} %maximum_maximum_fusion), calls=%async_computation.2 | async-start | bytes 786432 | tf_op jit(solution)/shard_map/all_to_all | solution.py:448
  118.5 28.6 %copy-start.17 = (f32[1024]{0:T(1024)S(1)}, f32[1024]{0:T(1024)}, u32[]{:S(2)}) copy-start(f32[1024]{0:T(1024)} %param.27) | copy-start | bytes 12292
  132.6 13.6 %all-to-all-start.3 = ((bf16[32,32,128]{2,1,0:T(8,128)(2,1)}), bf16[32,32,128]{2,1,0:T(8,128)(2,1)S(1)}, u32[]{:S(2)}, u32[]{:S(2)}) async-start(bf16[32,32,128]{2,1,0:T(8,128)(2,1)} %bitcast.75), calls=%async_computation.3 | async-start | bytes 524288 | tf_op jit(solution)/shard_map/all_to_all | solution.py:465
  147.2 21.4 %copy-start.7 = (bf16[32,4096]{1,0:T(8,128)(2,1)S(1)}, bf16[32,4096]{1,0:T(8,128)(2,1)}, u32[]{:S(2)}) copy-start(bf16[32,4096]{1,0:T(8,128)(2,1)} %copy-done.6) | copy-start | bytes 786436
  147.2 21.7 %copy-start.15 = (f32[4096]{0:T(1024)S(1)}, f32[4096]{0:T(1024)}, u32[]{:S(2)}) copy-start(f32[4096]{0:T(1024)} %param.29) | copy-start | bytes 49156
  147.3 40.5 %collective-permute-start.16 = (bf16[4096,512]{1,0:T(8,128)(2,1)}, bf16[4096,512]{1,0:T(8,128)(2,1)}, u32[]{:S(2)}, u32[]{:S(2)}) collective-permute-start(bf16[4096,512]{1,0:T(8,128)(2,1)} %all-gather.5.cloned.1.call-done.refs_3_.refs_5_), channel_id=1, source_target_pairs={{0,4},{4,0},{8,12},{12,8},{16,20},{20,16},{24,28},{28,24},{32,36},... | collective-permute-start | bytes 12582920 | tf_op jit(solution)/shard_map/ppermute | solution.py:28
  152.7 15.3 %collective-permute-start.7 = (bf16[32,4096]{1,0:T(8,128)(2,1)S(1)}, bf16[32,4096]{1,0:T(8,128)(2,1)S(1)}, u32[]{:S(2)}, u32[]{:S(2)}) collective-permute-start(bf16[32,4096]{1,0:T(8,128)(2,1)S(1)} %get-tuple-element.67), channel_id=1, source_target_pairs={{0,1},{1,2},{2,3},{3,0},{4,5},{5,6},{6,7},{7,4},{8,9},{9,10},{10,1... | collective-permute-start | bytes 786440 | tf_op jit(solution)/shard_map/ppermute | solution.py:33
  153.3 14.7 %collective-permute-start.8 = (bf16[32,4096]{1,0:T(8,128)(2,1)S(1)}, bf16[32,4096]{1,0:T(8,128)(2,1)S(1)}, u32[]{:S(2)}, u32[]{:S(2)}) collective-permute-start(bf16[32,4096]{1,0:T(8,128)(2,1)S(1)} %get-tuple-element.69), channel_id=1, source_target_pairs={{0,2},{1,3},{2,0},{3,1},{4,6},{5,7},{6,4},{7,5},{8,10},{9,11},{10,... | collective-permute-start | bytes 786440 | tf_op jit(solution)/shard_map/ppermute | solution.py:33
  155.7 12.9 %collective-permute-start.9 = (bf16[32,4096]{1,0:T(8,128)(2,1)S(1)}, bf16[32,4096]{1,0:T(8,128)(2,1)S(1)}, u32[]{:S(2)}, u32[]{:S(2)}) collective-permute-start(bf16[32,4096]{1,0:T(8,128)(2,1)S(1)} %get-tuple-element.68), channel_id=1, source_target_pairs={{0,3},{1,0},{2,1},{3,2},{4,7},{5,4},{6,5},{7,6},{8,11},{9,8},{10,9... | collective-permute-start | bytes 786440 | tf_op jit(solution)/shard_map/ppermute | solution.py:33
  169.1 5.9 %collective-permute-start.13 = (bf16[16,4096]{1,0:T(8,128)(2,1)S(1)}, bf16[16,4096]{1,0:T(8,128)(2,1)S(1)}, u32[]{:S(2)}, u32[]{:S(2)}) collective-permute-start(bf16[16,4096]{1,0:T(8,128)(2,1)S(1)} %get-tuple-element.70), channel_id=1, source_target_pairs={{0,96},{4,100},{8,104},{12,108},{16,112},{20,116},{24,120},{28,124... | collective-permute-start | bytes 393224 | tf_op jit(solution)/shard_map/ppermute | solution.py:33
  170.2 7.2 %collective-permute-start.14 = (bf16[16,4096]{1,0:T(8,128)(2,1)S(1)}, bf16[16,4096]{1,0:T(8,128)(2,1)S(1)}, u32[]{:S(2)}, u32[]{:S(2)}) collective-permute-start(bf16[16,4096]{1,0:T(8,128)(2,1)S(1)} %get-tuple-element.70), channel_id=1, source_target_pairs={{0,64},{4,68},{8,72},{12,76},{16,80},{20,84},{24,88},{28,92},{32,9... | collective-permute-start | bytes 393224 | tf_op jit(solution)/shard_map/ppermute | solution.py:33
  171.8 7.0 %collective-permute-start.15 = (bf16[16,4096]{1,0:T(8,128)(2,1)S(1)}, bf16[16,4096]{1,0:T(8,128)(2,1)S(1)}, u32[]{:S(2)}, u32[]{:S(2)}) collective-permute-start(bf16[16,4096]{1,0:T(8,128)(2,1)S(1)} %get-tuple-element.70), channel_id=1, source_target_pairs={{0,32},{4,36},{8,40},{12,44},{16,48},{20,52},{24,56},{28,60},{32,6... | collective-permute-start | bytes 393224 | tf_op jit(solution)/shard_map/ppermute | solution.py:33
  172.8 8.0 %collective-permute-start.10 = (bf16[16,4096]{1,0:T(8,128)(2,1)S(1)}, bf16[16,4096]{1,0:T(8,128)(2,1)S(1)}, u32[]{:S(2)}, u32[]{:S(2)}) collective-permute-start(bf16[16,4096]{1,0:T(8,128)(2,1)S(1)} %get-tuple-element.71), channel_id=1, source_target_pairs={{0,24},{4,28},{8,0},{12,4},{16,8},{20,12},{24,16},{28,20},{32,56},... | collective-permute-start | bytes 393224 | tf_op jit(solution)/shard_map/ppermute | solution.py:33
  175.0 6.5 %collective-permute-start.11 = (bf16[16,4096]{1,0:T(8,128)(2,1)S(1)}, bf16[16,4096]{1,0:T(8,128)(2,1)S(1)}, u32[]{:S(2)}, u32[]{:S(2)}) collective-permute-start(bf16[16,4096]{1,0:T(8,128)(2,1)S(1)} %get-tuple-element.71), channel_id=1, source_target_pairs={{0,16},{4,20},{8,24},{12,28},{16,0},{20,4},{24,8},{28,12},{32,48},... | collective-permute-start | bytes 393224 | tf_op jit(solution)/shard_map/ppermute | solution.py:33
  177.4 7.6 %collective-permute-start.12 = (bf16[16,4096]{1,0:T(8,128)(2,1)S(1)}, bf16[16,4096]{1,0:T(8,128)(2,1)S(1)}, u32[]{:S(2)}, u32[]{:S(2)}) collective-permute-start(bf16[16,4096]{1,0:T(8,128)(2,1)S(1)} %get-tuple-element.71), channel_id=1, source_target_pairs={{0,8},{4,12},{8,16},{12,20},{16,24},{20,28},{24,0},{28,4},{32,40},... | collective-permute-start | bytes 393224 | tf_op jit(solution)/shard_map/ppermute | solution.py:33
  178.8 14.9 %collective-permute-start.21 = (bf16[64,4096]{1,0:T(8,128)(2,1)S(1)}, bf16[64,4096]{1,0:T(8,128)(2,1)S(1)}, u32[]{:S(2)}, u32[]{:S(2)}) collective-permute-start(bf16[64,4096]{1,0:T(8,128)(2,1)S(1)} %pad_maximum_fusion.2.refs_1_), channel_id=1, source_target_pairs={{0,24},{4,28},{8,0},{12,4},{16,8},{20,12},{24,16},{28,20},{32,56},... | collective-permute-start | bytes 1572872 | tf_op jit(solution)/shard_map/ppermute | solution.py:33
  180.8 22.2 %collective-permute-start.22 = (bf16[64,4096]{1,0:T(8,128)(2,1)S(1)}, bf16[64,4096]{1,0:T(8,128)(2,1)S(1)}, u32[]{:S(2)}, u32[]{:S(2)}) collective-permute-start(bf16[64,4096]{1,0:T(8,128)(2,1)S(1)} %pad_maximum_fusion.2.refs_1_), channel_id=1, source_target_pairs={{0,8},{4,12},{8,16},{12,20},{16,24},{20,28},{24,0},{28,4},{32,40},... | collective-permute-start | bytes 1572872 | tf_op jit(solution)/shard_map/ppermute | solution.py:33
  185.0 18.0 %collective-permute-start.19 = (bf16[64,4096]{1,0:T(8,128)(2,1)S(1)}, bf16[64,4096]{1,0:T(8,128)(2,1)S(1)}, u32[]{:S(2)}, u32[]{:S(2)}) collective-permute-start(bf16[64,4096]{1,0:T(8,128)(2,1)S(1)} %pad_maximum_fusion.1.refs_0_), channel_id=1, source_target_pairs={{0,96},{4,100},{8,104},{12,108},{16,112},{20,116},{24,120},{28,124... | collective-permute-start | bytes 1572872 | tf_op jit(solution)/shard_map/ppermute | solution.py:33
  187.6 21.6 %collective-permute-start.20 = (bf16[64,4096]{1,0:T(8,128)(2,1)S(1)}, bf16[64,4096]{1,0:T(8,128)(2,1)S(1)}, u32[]{:S(2)}, u32[]{:S(2)}) collective-permute-start(bf16[64,4096]{1,0:T(8,128)(2,1)S(1)} %pad_maximum_fusion.1.refs_0_), channel_id=1, source_target_pairs={{0,32},{4,36},{8,40},{12,44},{16,48},{20,52},{24,56},{28,60},{32,6... | collective-permute-start | bytes 1572872 | tf_op jit(solution)/shard_map/ppermute | solution.py:33
  187.8 28.5 %collective-permute-start.18 = (bf16[64,4096]{1,0:T(8,128)(2,1)S(1)}, bf16[64,4096]{1,0:T(8,128)(2,1)}, u32[]{:S(2)}, u32[]{:S(2)}) collective-permute-start(bf16[64,4096]{1,0:T(8,128)(2,1)S(1)} %pad_maximum_fusion.2.refs_1_), channel_id=1, source_target_pairs={{0,16},{4,20},{8,24},{12,28},{16,0},{20,4},{24,8},{28,12},{32,48},... | collective-permute-start | bytes 1572872 | tf_op jit(solution)/shard_map/ppermute | solution.py:33
  193.7 22.6 %collective-permute-start.17 = (bf16[64,4096]{1,0:T(8,128)(2,1)S(1)}, bf16[64,4096]{1,0:T(8,128)(2,1)}, u32[]{:S(2)}, u32[]{:S(2)}) collective-permute-start(bf16[64,4096]{1,0:T(8,128)(2,1)S(1)} %pad_maximum_fusion.1.refs_0_), channel_id=1, source_target_pairs={{0,64},{4,68},{8,72},{12,76},{16,80},{20,84},{24,88},{28,92},{32,9... | collective-permute-start | bytes 1572872 | tf_op jit(solution)/shard_map/ppermute | solution.py:33
  195.3 2.2 copy-start
  203.0 13.4 %copy-start.1 = (bf16[4096,512]{1,0:T(8,128)(2,1)S(1)}, bf16[4096,512]{1,0:T(8,128)(2,1)}, u32[]{:S(2)}) copy-start(bf16[4096,512]{1,0:T(8,128)(2,1)} %all-gather.5.cloned.1.call-done.refs_3_.refs_5_) | copy-start | bytes 12582916
  222.8 6.0 %collective-permute-start.23 = (f32[5,128]{1,0:T(8,128)S(1)}, f32[5,128]{1,0:T(8,128)S(1)}, u32[]{:S(2)}, u32[]{:S(2)}) collective-permute-start(f32[5,128]{1,0:T(8,128)S(1)} %bitcast.388), channel_id=1, source_target_pairs={{0,32},{4,36},{8,40},{12,44},{16,48},{20,52},{24,56},{28,60},{32,6... | collective-permute-start | bytes 7688 | tf_op jit(solution)/shard_map/ppermute | solution.py:33
  224.5 5.8 %collective-permute-start.24 = (f32[5,128]{1,0:T(8,128)S(1)}, f32[5,128]{1,0:T(8,128)S(1)}, u32[]{:S(2)}, u32[]{:S(2)}) collective-permute-start(f32[5,128]{1,0:T(8,128)S(1)} %bitcast.390), channel_id=1, source_target_pairs={{0,64},{4,68},{8,72},{12,76},{16,80},{20,84},{24,88},{28,92},{32,9... | collective-permute-start | bytes 7688 | tf_op jit(solution)/shard_map/ppermute | solution.py:33
  228.6 3.6 %collective-permute-start.25 = (f32[5,128]{1,0:T(8,128)S(1)}, f32[5,128]{1,0:T(8,128)S(1)}, u32[]{:S(2)}, u32[]{:S(2)}) collective-permute-start(f32[5,128]{1,0:T(8,128)S(1)} %bitcast.392), channel_id=1, source_target_pairs={{0,96},{4,100},{8,104},{12,108},{16,112},{20,116},{24,120},{28,124... | collective-permute-start | bytes 7688 | tf_op jit(solution)/shard_map/ppermute | solution.py:33
  232.8 5.3 %collective-permute-start.26 = (f32[5,32]{1,0:T(8,128)S(1)}, f32[5,32]{1,0:T(8,128)S(1)}, u32[]{:S(2)}, u32[]{:S(2)}) collective-permute-start(f32[5,32]{1,0:T(8,128)S(1)} %bitcast.389), channel_id=1, source_target_pairs={{0,8},{4,12},{8,16},{12,20},{16,24},{20,28},{24,0},{28,4},{32,40},... | collective-permute-start | bytes 1928 | tf_op jit(solution)/shard_map/ppermute | solution.py:33
  232.9 6.7 %collective-permute-start.27 = (f32[5,32]{1,0:T(8,128)S(1)}, f32[5,32]{1,0:T(8,128)S(1)}, u32[]{:S(2)}, u32[]{:S(2)}) collective-permute-start(f32[5,32]{1,0:T(8,128)S(1)} %bitcast.391), channel_id=1, source_target_pairs={{0,16},{4,20},{8,24},{12,28},{16,0},{20,4},{24,8},{28,12},{32,48},... | collective-permute-start | bytes 1928 | tf_op jit(solution)/shard_map/ppermute | solution.py:33
  238.0 3.6 %collective-permute-start.28 = (f32[5,32]{1,0:T(8,128)S(1)}, f32[5,32]{1,0:T(8,128)S(1)}, u32[]{:S(2)}, u32[]{:S(2)}) collective-permute-start(f32[5,32]{1,0:T(8,128)S(1)} %bitcast.393), channel_id=1, source_target_pairs={{0,24},{4,28},{8,0},{12,4},{16,8},{20,12},{24,16},{28,20},{32,56},... | collective-permute-start | bytes 1928 | tf_op jit(solution)/shard_map/ppermute | solution.py:33
Sparse Core Ops, SparseCore 0:
  25.8 52.6 all-gather.4
  80.7 58.2 all-gather.2

commit v6 on v4

--- a/solution.py
+++ b/solution.py
@@ -357,7 +357,7 @@
             pltpu.VMEM((count, width), jnp.bfloat16),
             pltpu.VMEM((2 * tiles, count, tile), f32),
         ],
-        compiler_params=pltpu.CompilerParams(vmem_limit_bytes=48 << 20),
+        compiler_params=pltpu.CompilerParams(vmem_limit_bytes=50 << 20),
         cost_estimate=pl.CostEstimate(
             flops=2 * count * width * every,
             bytes_accessed=2 * width * every,
@@ -394,9 +394,6 @@
     ctx_pos = lax.axis_index("ctx")
     head_at = head_pos[None].astype(jnp.int32)
     w_out_full = lax.all_gather(w_out, "ctx", axis=1, tiled=True)
-    vocab_own = lax.all_gather(lm_head, "head", axis=0, tiled=True)
-    vocab_other = swap_core(vocab_own)
-
     leaving = pack_columns(embed, head_at)
     columns = [
         leaving[0],
@@ -415,6 +412,8 @@
     mine = look_up(all_ids.reshape(2, ctx_count // 2, 4 * quarter), columns)
     mine = mine.reshape(ctx_count, quarter, 128)
     mine = lax.all_to_all(mine, "ctx", 0, 0, tiled=True)
+    mine, lm_head = lax.optimization_barrier((mine, lm_head))
+    vocab_own = lax.all_gather(lm_head, "head", axis=0, tiled=True)
 
     channels = w_zx.shape[2]
     group_cols = w_bc.shape[2]
@@ -459,7 +458,7 @@
     mixing = scores[None] * decay_mask * step_size.T[:, None, :]
     y_local = jnp.einsum("hts,shp->thp", mixing, x_heads, precision=exact_prec)
     y_local = y_local + d_skip[None, :, None] * x_heads
-    arrived, y_local = lax.optimization_barrier((arrived, y_local))
+    arrived, y_local, w_out_full = lax.optimization_barrier((arrived, y_local, w_out_full))
     block_logs = jnp.sum(arrived[:, part_rows : part_rows + 3, 0].astype(f32), axis=1)
     blocks = jnp.arange(ctx_count)
     earlier = blocks[:, None] > blocks[None, :]
@@ -483,50 +482,42 @@
     partial_out = project_out(gated_out, w_out_full, head_at)
     summed_out = ring_reduce([partial_out[k] for k in range(4)], shift_head)
     residual = (own_emb.astype(f32) + summed_out).astype(bf16)
+    residual, vocab_own = lax.optimization_barrier((residual, vocab_own))
+    vocab_other = swap_core(vocab_own)
     normed_out = rms_scale(residual.astype(f32), final_gain).astype(bf16)
 
     along_first, along_second = shift_mixed(True), shift_mixed(False)
-    own, right, far, left = ring_gather(normed_out, along_first)
-    near = jnp.concatenate([own, left])
-    rest = jnp.concatenate([right, far])
+    from_left = moved(normed_out, along_first, 1)
+    from_right = moved(normed_out, along_first, -1)
+    from_far = moved(normed_out, along_first, 2)
+    near = jnp.concatenate([normed_out, from_left])
+    rest = jnp.concatenate([from_right, from_far])
+    near_left = moved(near, along_second, 1)
     near_right = moved(near, along_second, -1)
-    near_left = moved(near, along_second, 1)
-    near_far = moved(near, along_second, 2)
+    rest_left = moved(rest, along_second, 1)
     rest_right = moved(rest, along_second, -1)
-    rest_left = moved(rest, along_second, 1)
-    rest_far = moved(rest, along_second, 2)
     y_pos, z_pos, core = ctx_pos // 8, (ctx_pos // 2) % 4, ctx_pos % 2
     by_chip = lax.dynamic_index_in_dim(group_targets.reshape(4, 4, 2, quarter), core, 2, False)
     by_chip = jnp.roll(by_chip, (-y_pos, -z_pos), (0, 1))
     by_chip = jnp.where(core == 0, by_chip, by_chip.transpose(1, 0, 2))
     order = (0, 3, 1, 2)
-    by_chip = jnp.stack([by_chip[:, k] for k in order], axis=1).reshape(4, 4 * quarter)
+    by_chip = jnp.stack([by_chip[:, k] for k in order], axis=1).reshape(4, 1, 4 * quarter)
     vocab_width = vocab_own.shape[1]
     by_chip = jnp.stack([by_chip - ctx_pos * vocab_width, by_chip - (ctx_pos ^ 1) * vocab_width])
     tables = (vocab_own, vocab_other)
-    pair = 2 * quarter
-
-    def aims(places):
-        picked = [by_chip[:, k, part * pair : (part + 1) * pair] for k, part in places]
-        return jnp.concatenate(picked, axis=1).reshape(2, -1, 128)
-
-    stats_own = vocab_stats((near, rest), aims(((0, 0), (0, 1))), tables)
-    near_right, near_left, stats_own = lax.optimization_barrier((near_right, near_left, stats_own))
-    stats_near = vocab_stats((near_right, near_left), aims(((1, 0), (3, 0))), tables)
-    near_far, rest_right, rest_left, rest_far, stats_near = lax.optimization_barrier(
-        (near_far, rest_right, rest_left, rest_far, stats_near)
-    )
-    stats_rest = vocab_stats(
-        (near_far, rest_right, rest_left, rest_far), aims(((2, 0), (1, 1), (3, 1), (2, 1))), tables
-    )
-    found = (
-        (stats_near[:, :pair], stats_rest[:, pair : 2 * pair]),
-        (stats_rest[:, :pair], stats_rest[:, 3 * pair :]),
-        (stats_near[:, pair:], stats_rest[:, 2 * pair : 3 * pair]),
-    )
-    stats = [stats_own]
-    for k in range(1, 4):
-        stats.append(moved(jnp.concatenate(found[k - 1], axis=1), along_second, k))
+    rows = 4 * quarter
+    near, near_left, rest_right = lax.optimization_barrier((near, near_left, rest_right))
+    near_far = moved(near_left, along_second, 1)
+    rest_far = moved(rest_right, along_second, -1)
+    aims = jnp.concatenate([by_chip[:, k] for k in (0, 1, 3)], axis=1)
+    first = (near, rest, near_right, rest_right, near_left, rest_left)
+    first = vocab_stats(first, aims, tables)
+    near_far, rest_far, first = lax.optimization_barrier((near_far, rest_far, first))
+    last = vocab_stats((near_far, rest_far), by_chip[:, 2], tables)
+    stats = [first[:, :rows]]
+    stats.append(moved(first[:, rows : 2 * rows], along_second, 1))
+    stats.append(moved(first[:, 2 * rows :], along_second, 3))
+    stats.append(moved(last, along_second, 2))
     merged = tuple(stats[0][:5])
     for other in stats[1:]:
         merged = join_stats(merged, tuple(other[:5]))

time: 233 us -> 214 us (0.918)
  starting transfers between devices: 74.3 us -> 52.5 us
  blocking collectives: 0 us -> 12.6 us
  local copies, waits for them, and re-layouts: 16.8 us -> 11.1 us
  Pallas kernels: 42.2 us -> 38 us
    ppermute x24, waiting for transfers between devices: 34.1 us -> 48.5 us  [moved(): return lax.ppermute(value, axis, pairs)]
    all_to_all x0 -> x1, blocking collectives: none -> 12.6 us  [on_device(): state_in = lax.all_to_all(entering, 'ctx', 0, 0, tiled=True)]
    ppermute x24, starting transfers between devices: 41.8 us -> 30.8 us  [moved(): return lax.ppermute(value, axis, pairs)]
    all_to_all x1 -> x0, waiting for transfers between devices: 10.6 us -> none  [on_device(): state_in = lax.all_to_all(entering, 'ctx', 0, 0, tiled=True)]
    unnamed x58 -> x54, local copies, waits for them, and re-layouts: 12.9 us -> 7.29 us
    all_to_all x1 -> x0, starting transfers between devices: 5.28 us -> none  [on_device(): state_in = lax.all_to_all(entering, 'ctx', 0, 0, tiled=True)]
    all_to_all x1, starting transfers between devices: 7.81 us -> 4 us  [on_device(): mine = lax.all_to_all(mine, 'ctx', 0, 0, tiled=True)]
    pallas_call x3 -> x2, Pallas kernels: 17.9 us -> 14.3 us  [vocab_stats(): pl.pallas_call(kernel, grid=(2 * tiles,), in_specs=[pl.BlockSpec(piece.sh...]
  transfers between devices with their start and end apart: 32 -> 31, of which waited for: 18 -> 18; matrix products, arithmetic and copies ran while one was open for 7% -> 8% of each run, Pallas kernels for 15% -> 18%
where the time goes in v6:
time: 214 us; the launch traced here: 213 us
  waiting for transfers between devices  73.4 us (34%)
  starting transfers between devices  52.5 us (25%)
  Pallas kernels  38 us (18%)
  between operations  14.1 us (7%)
  blocking collectives  12.6 us (6%)
  local copies, waits for them, and re-layouts  11.1 us (5%)
  other arithmetic  7.52 us (4%)
  matrix products  4.07 us (2%)
    ppermute x24, waiting for transfers between devices, moved(): return lax.ppermute(value, axis, pairs)  48.5 us
    ppermute x24, starting transfers between devices, moved(): return lax.ppermute(value, axis, pairs)  30.8 us
    pallas_call x2, Pallas kernels, vocab_stats(): pl.pallas_call(kernel, grid=(2 * tiles,), in_specs=[pl.BlockSpec(piece.sh...  14.3 us
    all_to_all x1, blocking collectives, on_device(): state_in = lax.all_to_all(entering, 'ctx', 0, 0, tiled=True)  12.6 us
    pallas_call x1, Pallas kernels, embed_and_project(): pl.pallas_call(kernel, grid=(width // depth,), in_specs=[pl.BlockSpec(mem...  11.1 us
    all_to_all x1, waiting for transfers between devices, on_device(): mine = lax.all_to_all(mine, 'ctx', 0, 0, tiled=True)  10 us
    all_to_all x1, starting transfers between devices, on_device(): packed = lax.all_to_all(packed, 'ctx', 0, 0, tiled=True)  8.34 us
    all_to_all x1, waiting for transfers between devices, on_device(): arrived = lax.all_to_all(message, 'ctx', 0, 0, tiled=True)  7.43 us
  transfers between devices with their start and end apart: 31, of which 18 were waited for; matrix products, arithmetic and copies ran while one was open for 8% of the time, Pallas kernels for 18%

profile of v6, /device:TPU:0, one launch (start us, length us, event | category | flops | bytes accessed | tf_op | source)
XLA Modules:
  0.0 213.4 jit_solution(4941419980104838468)
XLA Ops:
  6.5 0.7 all-gather.3.cloned.1.call-update
  7.3 1.2 copy-done.8
  8.5 0.8 shard_map.154
  9.3 2.9 %collective-permute-start = (bf16[1024,128]{1,0:T(8,128)(2,1)S(1)}, bf16[1024,128]{1,0:T(8,128)(2,1)S(1)}, u32[]{:S(2)}, u32[]{:S(2)}) collective-permute-start(bf16[1024,128]{1,0:T(8,128)(2,1)S(1)} %get-tuple-element.31), channel_id=1, source_target_pairs={{0,3},{1,0},{2,1},{3,2},{4,7},{5,4},{6,5},{7,6},{8,11},{9,8},{10,9... | collective-permute-start | bytes 786440 | tf_op jit(solution)/shard_map/ppermute | solution.py:40
  12.2 0.8 collective-permute-start.1
  13.0 0.9 collective-permute-start.2
  13.9 0.7 pad_add_fusion.3
  14.6 0.6 all_to_all.17
  15.2 8.3 %all-to-all-start = ((s32[32,1,160]{2,1,0:T(1,128)}), s32[32,1,160]{2,1,0:T(1,128)S(1)}, u32[]{:S(2)}, u32[]{:S(2)}) async-start(s32[32,1,160]{2,1,0:T(1,128)} %all_to_all.17), calls=%async_computation | async-start | bytes 65536 | tf_op jit(solution)/shard_map/all_to_all | solution.py:407
  23.5 0.7 constant_dynamic-update-slice_fusion.1
  24.3 6.7 %all-to-all-done = s32[32,1,160]{2,1,0:T(1,128)S(1)} async-done(((s32[32,1,160]{2,1,0:T(1,128)}), s32[32,1,160]{2,1,0:T(1,128)S(1)}, u32[]{:S(2)}, u32[]{:S(2)}) %all-to-all-start) | async-done | bytes 20512 | tf_op jit(solution)/shard_map/all_to_all | solution.py:407
  31.0 0.6 copy-done.10
  31.9 6.9 %shard_map.155 = bf16[1024,128]{1,0:T(8,128)(2,1)} custom-call(s32[2,16,128]{2,1,0:T(8,128)S(1)} %reshape.193.ids_ref, bf16[1024,128]{1,0:T(8,128)(2,1)S(1)} %get-tuple-element.28.refs_0_, bf16[1024,128]{1,0:T(8,128)(2,1)S(1)} %collective-permute-done.refs_1_, bf16[1024,128]{1,0:T(8,128)(2,1)S(1)} %collective-permute-done.1.refs_2_, ...), custom_call_target="tpu_custom_call" | custom-call | flops 4294967296 | bytes 2097152 | tf_op jit(solution)/shard_map/pallas_call | solution.py:146
  38.8 4.0 %all-to-all-start.1 = ((bf16[32,32,128]{2,1,0:T(8,128)(2,1)}), bf16[32,32,128]{2,1,0:T(8,128)(2,1)S(1)}, u32[]{:S(2)}, u32[]{:S(2)}) async-start(bf16[32,32,128]{2,1,0:T(8,128)(2,1)} %bitcast.2), calls=%async_computation.1 | async-start | bytes 524288 | tf_op jit(solution)/shard_map/all_to_all | solution.py:414
  42.9 0.7 slice_reduce_fusion.4
  43.6 10.0 %all-to-all-done.1 = bf16[32,32,128]{2,1,0:T(8,128)(2,1)S(1)} async-done(((bf16[32,32,128]{2,1,0:T(8,128)(2,1)}), bf16[32,32,128]{2,1,0:T(8,128)(2,1)S(1)}, u32[]{:S(2)}, u32[]{:S(2)}) %all-to-all-start.1) | async-done | bytes 262176 | tf_op jit(solution)/shard_map/all_to_all | solution.py:414
  53.6 1.9 collective-permute-start.3
  55.5 1.9 collective-permute-start.4
  57.4 0.6 iota_compare_fusion
  58.5 0.6 pad.16.clone
  59.1 1.2 exponential_negate_fusion
  60.4 2.4 %collective-permute-done.3 = bf16[32,32,128]{2,1,0:T(8,128)(2,1)} collective-permute-done((bf16[32,32,128]{2,1,0:T(8,128)(2,1)S(1)}, bf16[32,32,128]{2,1,0:T(8,128)(2,1)}, u32[]{:S(2)}, u32[]{:S(2)}) %collective-permute-start.3) | collective-permute-done | bytes 262176 | tf_op jit(solution)/shard_map/ppermute | solution.py:40
  62.8 3.5 %collective-permute-done.4 = bf16[32,32,128]{2,1,0:T(8,128)(2,1)} collective-permute-done((bf16[32,32,128]{2,1,0:T(8,128)(2,1)S(1)}, bf16[32,32,128]{2,1,0:T(8,128)(2,1)}, u32[]{:S(2)}, u32[]{:S(2)}) %collective-permute-start.4) | collective-permute-done | bytes 262176 | tf_op jit(solution)/shard_map/ppermute | solution.py:40
  66.3 5.3 %collective-permute-done.5 = bf16[32,32,128]{2,1,0:T(8,128)(2,1)} collective-permute-done((bf16[32,32,128]{2,1,0:T(8,128)(2,1)S(1)}, bf16[32,32,128]{2,1,0:T(8,128)(2,1)}, u32[]{:S(2)}, u32[]{:S(2)}) %collective-permute-start.5) | collective-permute-done | bytes 262176 | tf_op jit(solution)/shard_map/ppermute | solution.py:40
  71.6 11.1 %shard_map.156 = (f32[128,1024]{1,0:T(8,128)S(1)}, f32[128,1024]{1,0:T(8,128)S(1)}, f32[128,256]{1,0:T(8,128)S(1)}, f32[128,16]{1,0:T(8,128)S(1)}, bf16[32,4096]{1,0:T(8,128)(2,1)S(1)}) custom-call(s32[1]{0:T(128)} %bitcast.head_ref.refs_0_, bf16[1024,128]{1,0:T(8,128)(2,1)S(1)} %bitcast.295, bf16[1024,128]{1,0:T(8,128)(2,1)} %bitcast.4.refs_2_, ...), custom_call_target="tpu_custom_call" | custom-call | flops 2432696320 | bytes 19005440 | tf_op jit(solution)/shard_map/pallas_call | solution.py:209
  82.7 0.8 copy-done.1
  83.6 0.8 copy-done.3
  84.3 0.7 copy-done.4
  85.0 0.6 copy-done.6
  86.0 1.1 constant_dynamic-update-slice_fusion.3
  87.1 2.1 collective-permute-start.6
  89.5 0.9 fusion.92
  90.6 1.2 divide_multiply_fusion
  92.8 0.9 maximum_maximum_fusion
  93.6 7.1 %all-to-all-start.2 = ((bf16[32,48,128]{2,1,0:T(8,128)(2,1)}), bf16[32,48,128]{2,1,0:T(8,128)(2,1)S(1)}, u32[]{:S(2)}, u32[]{:S(2)}) async-start(bf16[32,48,128]{2,1,0:T(8,128)(2,1)} %maximum_maximum_fusion), calls=%async_computation.2 | async-start | bytes 786432 | tf_op jit(solution)/shard_map/all_to_all | solution.py:454
  101.0 2.2 %fusion = f32[128,16,64]{0,2,1:T(8,128)S(1)} fusion(f32[128,16,64]{0,2,1:T(8,128)S(1)} %bitcast.299, f32[16,128]{1,0:T(8,128)S(1)} %copy.75, f32[16,128]{1,0:T(8,128)S(1)} %bitcast.309, f32[128,128]{1,0:T(8,128)S(1)} %fusion.38, pred[128,128]{1,0:T(8,128)(4,1)S(1)} %copy-done.13, f32[16]{0:T(128)S(1)} %copy-done.18), kind=kOutput, calls=%fused_computation.2 | convolution fusion | flops 202637312 | bytes 1146944 | tf_op jit(solution)/shard_map/hts,shp->thp/dot_general | solution.py:459
  103.2 7.4 %all-to-all-done.2 = bf16[32,48,128]{2,1,0:T(8,128)(2,1)S(1)} async-done(((bf16[32,48,128]{2,1,0:T(8,128)(2,1)}), bf16[32,48,128]{2,1,0:T(8,128)(2,1)S(1)}, u32[]{:S(2)}, u32[]{:S(2)}) %all-to-all-start.2) | async-done | bytes 393248 | tf_op jit(solution)/shard_map/all_to_all | solution.py:454
  111.6 12.6 %all_to_all.27 = bf16[32,32,128]{2,1,0:T(8,128)(2,1)S(1)} all-to-all(bf16[32,32,128]{2,1,0:T(8,128)(2,1)S(1)} %bitcast.303), channel_id=1, replica_groups=mesh['ctx'=32,'head'=4] {'ctx'}, dimensions={0} | all-to-all | bytes 524288 | tf_op jit(solution)/shard_map/all_to_all | solution.py:471
  125.3 5.0 %shard_map.157 = bf16[4,32,4096]{2,1,0:T(8,128)(2,1)S(1)} custom-call(s32[1]{0:T(128)} %bitcast.head_ref.refs_0_, bf16[128,1024]{1,0:T(8,128)(2,1)S(1)} %multiply_convert_fusion.gated_ref, bf16[1024,4096]{1,0:T(8,128)(2,1)} %all-gather.3.cloned.1.call-done.weights_ref), custom_call_target="tpu_custom_call" | custom-call | flops 1073741824 | bytes 8388608 | tf_op jit(solution)/shard_map/pallas_call | solution.py:248
  130.5 1.7 collective-permute-start.8
  132.2 2.5 %collective-permute-start.9 = (bf16[32,4096]{1,0:T(8,128)(2,1)S(1)}, bf16[32,4096]{1,0:T(8,128)(2,1)S(1)}, u32[]{:S(2)}, u32[]{:S(2)}) collective-permute-start(bf16[32,4096]{1,0:T(8,128)(2,1)S(1)} %get-tuple-element.66), channel_id=1, source_target_pairs={{0,3},{1,0},{2,1},{3,2},{4,7},{5,4},{6,5},{7,6},{8,11},{9,8},{10,9... | collective-permute-start | bytes 786440 | tf_op jit(solution)/shard_map/ppermute | solution.py:40
  134.8 11.0 %collective-permute-done.7 = bf16[32,4096]{1,0:T(8,128)(2,1)S(1)} collective-permute-done((bf16[32,4096]{1,0:T(8,128)(2,1)S(1)}, bf16[32,4096]{1,0:T(8,128)(2,1)S(1)}, u32[]{:S(2)}, u32[]{:S(2)}) %collective-permute-start.7) | collective-permute-done | bytes 262176 | tf_op jit(solution)/shard_map/ppermute | solution.py:40
  145.8 0.6 collective-permute-done.9
  147.1 1.3 collective-permute-start.12
  148.5 1.4 collective-permute-start.13
  149.9 3.7 %collective-permute-done.12 = bf16[32,4096]{1,0:T(8,128)(2,1)S(1)} collective-permute-done((bf16[32,4096]{1,0:T(8,128)(2,1)S(1)}, bf16[32,4096]{1,0:T(8,128)(2,1)S(1)}, u32[]{:S(2)}, u32[]{:S(2)}) %collective-permute-start.12) | collective-permute-done | bytes 262176 | tf_op jit(solution)/shard_map/ppermute | solution.py:40
  153.6 3.0 %collective-permute-done.13 = bf16[32,4096]{1,0:T(8,128)(2,1)S(1)} collective-permute-done((bf16[32,4096]{1,0:T(8,128)(2,1)S(1)}, bf16[32,4096]{1,0:T(8,128)(2,1)S(1)}, u32[]{:S(2)}, u32[]{:S(2)}) %collective-permute-start.13) | collective-permute-done | bytes 262176 | tf_op jit(solution)/shard_map/ppermute | solution.py:40
  156.6 1.2 collective-permute-start.14
  157.8 1.4 collective-permute-done.10
  159.3 0.7 collective-permute-start.11
  160.1 3.2 %collective-permute-start.17 = (bf16[64,4096]{1,0:T(8,128)(2,1)S(1)}, bf16[64,4096]{1,0:T(8,128)(2,1)S(1)}, u32[]{:S(2)}, u32[]{:S(2)}) collective-permute-start(bf16[64,4096]{1,0:T(8,128)(2,1)S(1)} %pad_maximum_fusion.1.refs_0_), channel_id=1, source_target_pairs={{0,96},{4,28},{8,104},{12,4},{16,112},{20,12},{24,120},{28,20},{32... | collective-permute-start | bytes 1572872 | tf_op jit(solution)/shard_map/ppermute | solution.py:40
  163.5 2.3 %collective-permute-done.14.refs_3_ = bf16[64,4096]{1,0:T(8,128)(2,1)S(1)} collective-permute-done((bf16[64,4096]{1,0:T(8,128)(2,1)S(1)}, bf16[64,4096]{1,0:T(8,128)(2,1)S(1)}, u32[]{:S(2)}, u32[]{:S(2)}) %collective-permute-start.14) | collective-permute-done | bytes 524320 | tf_op jit(solution)/shard_map/ppermute | solution.py:40
  165.8 3.9 %collective-permute-done.11.refs_4_ = bf16[64,4096]{1,0:T(8,128)(2,1)S(1)} collective-permute-done((bf16[64,4096]{1,0:T(8,128)(2,1)S(1)}, bf16[64,4096]{1,0:T(8,128)(2,1)S(1)}, u32[]{:S(2)}, u32[]{:S(2)}) %collective-permute-start.11) | collective-permute-done | bytes 524320 | tf_op jit(solution)/shard_map/ppermute | solution.py:40
  169.8 3.2 %collective-permute-start.16 = (bf16[64,4096]{1,0:T(8,128)(2,1)S(1)}, bf16[64,4096]{1,0:T(8,128)(2,1)S(1)}, u32[]{:S(2)}, u32[]{:S(2)}) collective-permute-start(bf16[64,4096]{1,0:T(8,128)(2,1)S(1)} %collective-permute-done.14.refs_3_), channel_id=1, source_target_pairs={{0,96},{4,28},{8,104},{12,4},{16,112},{20,12},{24,120},{28,20},{32... | collective-permute-start | bytes 1572872 | tf_op jit(solution)/shard_map/ppermute | solution.py:40
  173.0 2.4 %collective-permute-done.18.refs_5_ = bf16[64,4096]{1,0:T(8,128)(2,1)S(1)} collective-permute-done((bf16[64,4096]{1,0:T(8,128)(2,1)S(1)}, bf16[64,4096]{1,0:T(8,128)(2,1)S(1)}, u32[]{:S(2)}, u32[]{:S(2)}) %collective-permute-start.18) | collective-permute-done | bytes 524320 | tf_op jit(solution)/shard_map/ppermute | solution.py:40
  175.4 8.4 %shard_map.158 = f32[8,384]{1,0:T(8,128)S(1)} custom-call(bf16[64,4096]{1,0:T(8,128)(2,1)S(1)} %pad_maximum_fusion.1.refs_0_, bf16[64,4096]{1,0:T(8,128)(2,1)S(1)} %constant_dynamic-update-slice_fusion.4.refs_1_, bf16[64,4096]{1,0:T(8,128)(2,1)S(1)} %collective-permute-done.17.refs_2_, bf16[64,4096]{1,0:T(8,128)(2,1)S(1)} %collective-permute-done.14.refs_3_, ...), custom_call_target="tpu_custom_call" | custom-call | flops 3221225472 | bytes 8388608 | tf_op jit(solution)/shard_map/pallas_call | solution.py:345
  184.0 3.2 %collective-permute-start.21 = (f32[8,128]{1,0:T(8,128)S(1)}, f32[8,128]{1,0:T(8,128)S(1)}, u32[]{:S(2)}, u32[]{:S(2)}) collective-permute-start(f32[8,128]{1,0:T(8,128)S(1)} %get-tuple-element.71), channel_id=1, source_target_pairs={{0,96},{4,28},{8,104},{12,4},{16,112},{20,12},{24,120},{28,20},{32... | collective-permute-start | bytes 12296 | tf_op jit(solution)/shard_map/ppermute | solution.py:40
  187.2 5.8 %shard_map.159 = f32[8,128]{1,0:T(8,128)S(1)} custom-call(bf16[64,4096]{1,0:T(8,128)(2,1)S(1)} %collective-permute-done.15.refs_0_, bf16[64,4096]{1,0:T(8,128)(2,1)S(1)} %collective-permute-done.16.refs_1_, s32[2,1,128]{2,1,0:T(1,128)S(1)} %bitcast.297, bf16[4096,512]{1,0:T(8,128)(2,1)} %all-gather.5.cloned.1.call-done.refs_7_.refs_3_, ...), custom_call_target="tpu_custom_call" | custom-call | flops 1073741824 | bytes 8388608 | tf_op jit(solution)/shard_map/pallas_call | solution.py:345
  193.1 5.1 %collective-permute-done.22 = f32[8,128]{1,0:T(8,128)S(1)} collective-permute-done((f32[8,128]{1,0:T(8,128)S(1)}, f32[8,128]{1,0:T(8,128)S(1)}, u32[]{:S(2)}, u32[]{:S(2)}) %collective-permute-start.22) | collective-permute-done | bytes 4128 | tf_op jit(solution)/shard_map/ppermute | solution.py:40
  198.8 1.0 collective-permute-start.23
  199.8 1.1 collective-permute-start.24
  200.9 1.3 collective-permute-start.25
  202.4 2.1 %collective-permute-done.24 = f32[5,32]{1,0:T(8,128)S(1)} collective-permute-done((f32[5,32]{1,0:T(8,128)S(1)}, f32[5,32]{1,0:T(8,128)S(1)}, u32[]{:S(2)}, u32[]{:S(2)}) %collective-permute-start.24) | collective-permute-done | bytes 672 | tf_op jit(solution)/shard_map/ppermute | solution.py:40
  204.6 1.4 collective-permute-done.25
  (135 shorter events, 7.5 us)
Async XLA Ops:
  6.5 104.1 %all-gather.3.cloned.1.call-start = ((), (), s32[]{:S(2)}) async-start(), calls=%async_computation.4 | async-start | bytes 8650752 | tf_op jit(solution)/shard_map/all_gather | solution.py:396
  7.3 1.2 copy-start.8
  9.3 22.6 %collective-permute-start = (bf16[1024,128]{1,0:T(8,128)(2,1)S(1)}, bf16[1024,128]{1,0:T(8,128)(2,1)S(1)}, u32[]{:S(2)}, u32[]{:S(2)}) collective-permute-start(bf16[1024,128]{1,0:T(8,128)(2,1)S(1)} %get-tuple-element.31), channel_id=1, source_target_pairs={{0,3},{1,0},{2,1},{3,2},{4,7},{5,4},{6,5},{7,6},{8,11},{9,8},{10,9... | collective-permute-start | bytes 786440 | tf_op jit(solution)/shard_map/ppermute | solution.py:40
  12.2 19.6 %collective-permute-start.1 = (bf16[1024,128]{1,0:T(8,128)(2,1)S(1)}, bf16[1024,128]{1,0:T(8,128)(2,1)S(1)}, u32[]{:S(2)}, u32[]{:S(2)}) collective-permute-start(bf16[1024,128]{1,0:T(8,128)(2,1)S(1)} %get-tuple-element.30), channel_id=1, source_target_pairs={{0,2},{1,3},{2,0},{3,1},{4,6},{5,7},{6,4},{7,5},{8,10},{9,11},{10,... | collective-permute-start | bytes 786440 | tf_op jit(solution)/shard_map/ppermute | solution.py:40
  13.0 18.9 %collective-permute-start.2 = (bf16[1024,128]{1,0:T(8,128)(2,1)S(1)}, bf16[1024,128]{1,0:T(8,128)(2,1)S(1)}, u32[]{:S(2)}, u32[]{:S(2)}) collective-permute-start(bf16[1024,128]{1,0:T(8,128)(2,1)S(1)} %get-tuple-element.29), channel_id=1, source_target_pairs={{0,1},{1,2},{2,3},{3,0},{4,5},{5,6},{6,7},{7,4},{8,9},{9,10},{10,1... | collective-permute-start | bytes 786440 | tf_op jit(solution)/shard_map/ppermute | solution.py:40
  15.2 15.8 %all-to-all-start = ((s32[32,1,160]{2,1,0:T(1,128)}), s32[32,1,160]{2,1,0:T(1,128)S(1)}, u32[]{:S(2)}, u32[]{:S(2)}) async-start(s32[32,1,160]{2,1,0:T(1,128)} %all_to_all.17), calls=%async_computation | async-start | bytes 65536 | tf_op jit(solution)/shard_map/all_to_all | solution.py:407
  31.0 0.6 copy-start.10
  31.8 11.1 %copy-start.15 = (f32[4,2,128]{2,1,0:T(2,128)S(1)}, f32[4,2,128]{2,1,0:T(2,128)}, u32[]{:S(2)}) copy-start(f32[4,2,128]{2,1,0:T(2,128)} %param.23) | copy-start | bytes 12292
  31.8 26.2 %copy-start.9 = (bf16[4096,16]{0,1:T(8,128)(2,1)S(1)}, bf16[4096,16]{0,1:T(8,128)(2,1)}, u32[]{:S(2)}) copy-start(bf16[4096,16]{0,1:T(8,128)(2,1)} %param.21) | copy-start | bytes 393220
  31.8 39.8 %copy-start.7 = (f32[4096]{0:T(1024)S(1)}, f32[4096]{0:T(1024)}, u32[]{:S(2)}) copy-start(f32[4096]{0:T(1024)} %param.28) | copy-start | bytes 49156
  38.8 32.8 %copy-start = (bf16[4096,2,128]{2,1,0:T(2,128)(2,1)S(1)}, bf16[4096,2,128]{2,1,0:T(2,128)(2,1)}, u32[]{:S(2)}) copy-start(bf16[4096,2,128]{2,1,0:T(2,128)(2,1)} %refs_7_.1) | copy-start | bytes 6291460
  38.8 14.7 %all-to-all-start.1 = ((bf16[32,32,128]{2,1,0:T(8,128)(2,1)}), bf16[32,32,128]{2,1,0:T(8,128)(2,1)S(1)}, u32[]{:S(2)}, u32[]{:S(2)}) async-start(bf16[32,32,128]{2,1,0:T(8,128)(2,1)} %bitcast.2), calls=%async_computation.1 | async-start | bytes 524288 | tf_op jit(solution)/shard_map/all_to_all | solution.py:414
  42.8 103.8 %all-gather.5.cloned.1.call-start = ((), (), s32[]{:S(2)}) async-start(), calls=%async_computation.5 | async-start | bytes 5242880 | tf_op jit(solution)/shard_map/all_gather | solution.py:416
  53.6 9.2 %collective-permute-start.3 = (bf16[32,32,128]{2,1,0:T(8,128)(2,1)S(1)}, bf16[32,32,128]{2,1,0:T(8,128)(2,1)}, u32[]{:S(2)}, u32[]{:S(2)}) collective-permute-start(bf16[32,32,128]{2,1,0:T(8,128)(2,1)S(1)} %all-to-all-done.1), channel_id=1, source_target_pairs={{0,3},{1,0},{2,1},{3,2},{4,7},{5,4},{6,5},{7,6},{8,11},{9,8},{10,9... | collective-permute-start | bytes 786440 | tf_op jit(solution)/shard_map/ppermute | solution.py:40
  55.5 10.8 %collective-permute-start.4 = (bf16[32,32,128]{2,1,0:T(8,128)(2,1)S(1)}, bf16[32,32,128]{2,1,0:T(8,128)(2,1)}, u32[]{:S(2)}, u32[]{:S(2)}) collective-permute-start(bf16[32,32,128]{2,1,0:T(8,128)(2,1)S(1)} %all-to-all-done.1), channel_id=1, source_target_pairs={{0,2},{1,3},{2,0},{3,1},{4,6},{5,7},{6,4},{7,5},{8,10},{9,11},{10,... | collective-permute-start | bytes 786440 | tf_op jit(solution)/shard_map/ppermute | solution.py:40
  57.4 14.2 %collective-permute-start.5 = (bf16[32,32,128]{2,1,0:T(8,128)(2,1)S(1)}, bf16[32,32,128]{2,1,0:T(8,128)(2,1)}, u32[]{:S(2)}, u32[]{:S(2)}) collective-permute-start(bf16[32,32,128]{2,1,0:T(8,128)(2,1)S(1)} %all-to-all-done.1), channel_id=1, source_target_pairs={{0,1},{1,2},{2,3},{3,0},{4,5},{5,6},{6,7},{7,4},{8,9},{9,10},{10,1... | collective-permute-start | bytes 786440 | tf_op jit(solution)/shard_map/ppermute | solution.py:40
  71.6 14.0 %copy-start.16 = (f32[16]{0:T(128)S(1)}, f32[16]{0:T(128)}, u32[]{:S(2)}) copy-start(f32[16]{0:T(128)} %param.24) | copy-start | bytes 196
  71.6 14.0 %copy-start.19 = (f32[16]{0:T(128)S(1)}, f32[16]{0:T(128)}, u32[]{:S(2)}) copy-start(f32[16]{0:T(128)} %exponential_negate_fusion) | copy-start | bytes 196
  82.7 0.8 copy-start.1
  83.6 0.8 copy-start.3
  84.3 0.7 copy-start.4
  85.0 0.6 copy-start.6
  85.0 7.7 %copy-start.17 = (bf16[48]{0:T(256)(128)(2,1)S(1)}, bf16[48]{0:T(256)(128)(2,1)}, u32[]{:S(2)}) copy-start(bf16[48]{0:T(256)(128)(2,1)} %pad.16.clone) | copy-start | bytes 292
  85.0 16.0 %copy-start.13 = (pred[128,128]{1,0:T(8,128)(4,1)S(1)}, pred[128,128]{1,0:T(8,128)(4,1)}, u32[]{:S(2)}) copy-start(pred[128,128]{1,0:T(8,128)(4,1)} %iota_compare_fusion) | copy-start | bytes 49156
  85.0 16.0 %copy-start.18 = (f32[16]{0:T(128)S(1)}, f32[16]{0:T(128)}, u32[]{:S(2)}) copy-start(f32[16]{0:T(128)} %param.26) | copy-start | bytes 196
  87.1 3.5 %collective-permute-start.6 = (f32[3,1280]{1,0:T(4,128)S(1)}, f32[3,1280]{1,0:T(4,128)S(1)}, u32[]{:S(2)}, u32[]{:S(2)}) collective-permute-start(f32[3,1280]{1,0:T(4,128)S(1)} %slice.175), channel_id=1, source_target_pairs={{0,4},{4,8},{8,12},{12,16},{16,20},{20,24},{24,28},{28,32},{32,36}... | collective-permute-start | bytes 46088 | tf_op jit(solution)/shard_map/ppermute | solution.py:46
  92.6 32.2 %copy-start.2 = (f32[128,1024]{1,0:T(8,128)S(1)}, f32[128,1024]{1,0:T(8,128)}, u32[]{:S(2)}) copy-start(f32[128,1024]{1,0:T(8,128)} %copy-done.1) | copy-start | bytes 1572868
  93.6 17.0 %all-to-all-start.2 = ((bf16[32,48,128]{2,1,0:T(8,128)(2,1)}), bf16[32,48,128]{2,1,0:T(8,128)(2,1)S(1)}, u32[]{:S(2)}, u32[]{:S(2)}) async-start(bf16[32,48,128]{2,1,0:T(8,128)(2,1)} %maximum_maximum_fusion), calls=%async_computation.2 | async-start | bytes 786432 | tf_op jit(solution)/shard_map/all_to_all | solution.py:454
  100.7 24.4 %copy-start.14 = (f32[1024]{0:T(1024)S(1)}, f32[1024]{0:T(1024)}, u32[]{:S(2)}) copy-start(f32[1024]{0:T(1024)} %param.27) | copy-start | bytes 12292
  125.2 21.1 %copy-start.5 = (bf16[32,4096]{1,0:T(8,128)(2,1)S(1)}, bf16[32,4096]{1,0:T(8,128)(2,1)}, u32[]{:S(2)}) copy-start(bf16[32,4096]{1,0:T(8,128)(2,1)} %copy-done.4) | copy-start | bytes 786436
  125.3 21.5 %copy-start.11 = (s32[32,1,160]{2,0,1:T(8,128)S(1)}, s32[32,1,160]{2,0,1:T(8,128)}, u32[]{:S(2)}) copy-start(s32[32,1,160]{2,0,1:T(8,128)} %copy-done.10) | copy-start | bytes 61444
  125.3 21.7 %copy-start.12 = (f32[4096]{0:T(1024)S(1)}, f32[4096]{0:T(1024)}, u32[]{:S(2)}) copy-start(f32[4096]{0:T(1024)} %param.29) | copy-start | bytes 49156
  130.3 15.4 %collective-permute-start.7 = (bf16[32,4096]{1,0:T(8,128)(2,1)S(1)}, bf16[32,4096]{1,0:T(8,128)(2,1)S(1)}, u32[]{:S(2)}, u32[]{:S(2)}) collective-permute-start(bf16[32,4096]{1,0:T(8,128)(2,1)S(1)} %get-tuple-element.65), channel_id=1, source_target_pairs={{0,1},{1,2},{2,3},{3,0},{4,5},{5,6},{6,7},{7,4},{8,9},{9,10},{10,1... | collective-permute-start | bytes 786440 | tf_op jit(solution)/shard_map/ppermute | solution.py:40
  130.5 15.3 %collective-permute-start.8 = (bf16[32,4096]{1,0:T(8,128)(2,1)S(1)}, bf16[32,4096]{1,0:T(8,128)(2,1)S(1)}, u32[]{:S(2)}, u32[]{:S(2)}) collective-permute-start(bf16[32,4096]{1,0:T(8,128)(2,1)S(1)} %get-tuple-element.67), channel_id=1, source_target_pairs={{0,2},{1,3},{2,0},{3,1},{4,6},{5,7},{6,4},{7,5},{8,10},{9,11},{10,... | collective-permute-start | bytes 786440 | tf_op jit(solution)/shard_map/ppermute | solution.py:40
  132.2 14.2 %collective-permute-start.9 = (bf16[32,4096]{1,0:T(8,128)(2,1)S(1)}, bf16[32,4096]{1,0:T(8,128)(2,1)S(1)}, u32[]{:S(2)}, u32[]{:S(2)}) collective-permute-start(bf16[32,4096]{1,0:T(8,128)(2,1)S(1)} %get-tuple-element.66), channel_id=1, source_target_pairs={{0,3},{1,0},{2,1},{3,2},{4,7},{5,4},{6,5},{7,6},{8,11},{9,8},{10,9... | collective-permute-start | bytes 786440 | tf_op jit(solution)/shard_map/ppermute | solution.py:40
  146.6 28.8 %collective-permute-start.19 = (bf16[4096,512]{1,0:T(8,128)(2,1)}, bf16[4096,512]{1,0:T(8,128)(2,1)}, u32[]{:S(2)}, u32[]{:S(2)}) collective-permute-start(bf16[4096,512]{1,0:T(8,128)(2,1)} %all-gather.5.cloned.1.call-done.refs_7_.refs_3_), channel_id=1, source_target_pairs={{0,4},{4,0},{8,12},{12,8},{16,20},{20,16},{24,28},{28,24},{32,36},... | collective-permute-start | bytes 12582920 | tf_op jit(solution)/shard_map/ppermute | solution.py:35
  147.1 6.4 %collective-permute-start.12 = (bf16[32,4096]{1,0:T(8,128)(2,1)S(1)}, bf16[32,4096]{1,0:T(8,128)(2,1)S(1)}, u32[]{:S(2)}, u32[]{:S(2)}) collective-permute-start(bf16[32,4096]{1,0:T(8,128)(2,1)S(1)} %fusion.18), channel_id=1, source_target_pairs={{0,24},{4,100},{8,0},{12,108},{16,8},{20,116},{24,16},{28,124},{32... | collective-permute-start | bytes 786440 | tf_op jit(solution)/shard_map/ppermute | solution.py:40
  148.5 8.1 %collective-permute-start.13 = (bf16[32,4096]{1,0:T(8,128)(2,1)S(1)}, bf16[32,4096]{1,0:T(8,128)(2,1)S(1)}, u32[]{:S(2)}, u32[]{:S(2)}) collective-permute-start(bf16[32,4096]{1,0:T(8,128)(2,1)S(1)} %fusion.18), channel_id=1, source_target_pairs={{0,16},{4,68},{8,24},{12,76},{16,0},{20,84},{24,8},{28,92},{32,48}... | collective-permute-start | bytes 786440 | tf_op jit(solution)/shard_map/ppermute | solution.py:40
  149.9 9.4 %collective-permute-start.10 = (bf16[32,4096]{1,0:T(8,128)(2,1)S(1)}, bf16[32,4096]{1,0:T(8,128)(2,1)S(1)}, u32[]{:S(2)}, u32[]{:S(2)}) collective-permute-start(bf16[32,4096]{1,0:T(8,128)(2,1)S(1)} %fusion.18), channel_id=1, source_target_pairs={{0,8},{4,36},{8,16},{12,44},{16,24},{20,52},{24,0},{28,60},{32,40}... | collective-permute-start | bytes 786440 | tf_op jit(solution)/shard_map/ppermute | solution.py:40
  156.6 9.2 %collective-permute-start.14 = (bf16[64,4096]{1,0:T(8,128)(2,1)S(1)}, bf16[64,4096]{1,0:T(8,128)(2,1)S(1)}, u32[]{:S(2)}, u32[]{:S(2)}) collective-permute-start(bf16[64,4096]{1,0:T(8,128)(2,1)S(1)} %constant_dynamic-update-slice_fusion.4.refs_1_), channel_id=1, source_target_pairs={{0,96},{4,28},{8,104},{12,4},{16,112},{20,12},{24,120},{28,20},{32... | collective-permute-start | bytes 1572872 | tf_op jit(solution)/shard_map/ppermute | solution.py:40
  159.3 10.5 %collective-permute-start.11 = (bf16[64,4096]{1,0:T(8,128)(2,1)S(1)}, bf16[64,4096]{1,0:T(8,128)(2,1)S(1)}, u32[]{:S(2)}, u32[]{:S(2)}) collective-permute-start(bf16[64,4096]{1,0:T(8,128)(2,1)S(1)} %pad_maximum_fusion.1.refs_0_), channel_id=1, source_target_pairs={{0,32},{4,12},{8,40},{12,20},{16,48},{20,28},{24,56},{28,4},{32,64... | collective-permute-start | bytes 1572872 | tf_op jit(solution)/shard_map/ppermute | solution.py:40
  160.0 15.4 %collective-permute-start.18 = (bf16[64,4096]{1,0:T(8,128)(2,1)S(1)}, bf16[64,4096]{1,0:T(8,128)(2,1)S(1)}, u32[]{:S(2)}, u32[]{:S(2)}) collective-permute-start(bf16[64,4096]{1,0:T(8,128)(2,1)S(1)} %constant_dynamic-update-slice_fusion.4.refs_1_), channel_id=1, source_target_pairs={{0,32},{4,12},{8,40},{12,20},{16,48},{20,28},{24,56},{28,4},{32,64... | collective-permute-start | bytes 1572872 | tf_op jit(solution)/shard_map/ppermute | solution.py:40
  160.1 15.3 %collective-permute-start.17 = (bf16[64,4096]{1,0:T(8,128)(2,1)S(1)}, bf16[64,4096]{1,0:T(8,128)(2,1)S(1)}, u32[]{:S(2)}, u32[]{:S(2)}) collective-permute-start(bf16[64,4096]{1,0:T(8,128)(2,1)S(1)} %pad_maximum_fusion.1.refs_0_), channel_id=1, source_target_pairs={{0,96},{4,28},{8,104},{12,4},{16,112},{20,12},{24,120},{28,20},{32... | collective-permute-start | bytes 1572872 | tf_op jit(solution)/shard_map/ppermute | solution.py:40
  169.8 14.1 %collective-permute-start.15 = (bf16[64,4096]{1,0:T(8,128)(2,1)S(1)}, bf16[64,4096]{1,0:T(8,128)(2,1)S(1)}, u32[]{:S(2)}, u32[]{:S(2)}) collective-permute-start(bf16[64,4096]{1,0:T(8,128)(2,1)S(1)} %collective-permute-done.11.refs_4_), channel_id=1, source_target_pairs={{0,32},{4,12},{8,40},{12,20},{16,48},{20,28},{24,56},{28,4},{32,64... | collective-permute-start | bytes 1572872 | tf_op jit(solution)/shard_map/ppermute | solution.py:40
  169.8 14.1 %collective-permute-start.16 = (bf16[64,4096]{1,0:T(8,128)(2,1)S(1)}, bf16[64,4096]{1,0:T(8,128)(2,1)S(1)}, u32[]{:S(2)}, u32[]{:S(2)}) collective-permute-start(bf16[64,4096]{1,0:T(8,128)(2,1)S(1)} %collective-permute-done.14.refs_3_), channel_id=1, source_target_pairs={{0,96},{4,28},{8,104},{12,4},{16,112},{20,12},{24,120},{28,20},{32... | collective-permute-start | bytes 1572872 | tf_op jit(solution)/shard_map/ppermute | solution.py:40
  183.9 9.2 %collective-permute-start.20 = (f32[8,128]{1,0:T(8,128)S(1)}, f32[8,128]{1,0:T(8,128)S(1)}, u32[]{:S(2)}, u32[]{:S(2)}) collective-permute-start(f32[8,128]{1,0:T(8,128)S(1)} %get-tuple-element.70), channel_id=1, source_target_pairs={{0,32},{4,12},{8,40},{12,20},{16,48},{20,28},{24,56},{28,4},{32,64... | collective-permute-start | bytes 12296 | tf_op jit(solution)/shard_map/ppermute | solution.py:40
  184.0 9.2 %collective-permute-start.21 = (f32[8,128]{1,0:T(8,128)S(1)}, f32[8,128]{1,0:T(8,128)S(1)}, u32[]{:S(2)}, u32[]{:S(2)}) collective-permute-start(f32[8,128]{1,0:T(8,128)S(1)} %get-tuple-element.71), channel_id=1, source_target_pairs={{0,96},{4,28},{8,104},{12,4},{16,112},{20,12},{24,120},{28,20},{32... | collective-permute-start | bytes 12296 | tf_op jit(solution)/shard_map/ppermute | solution.py:40
  193.0 5.2 %collective-permute-start.22 = (f32[8,128]{1,0:T(8,128)S(1)}, f32[8,128]{1,0:T(8,128)S(1)}, u32[]{:S(2)}, u32[]{:S(2)}) collective-permute-start(f32[8,128]{1,0:T(8,128)S(1)} %shard_map.159), channel_id=1, source_target_pairs={{0,64},{4,20},{8,72},{12,28},{16,80},{20,4},{24,88},{28,12},{32,96... | collective-permute-start | bytes 12296 | tf_op jit(solution)/shard_map/ppermute | solution.py:40
  198.8 3.7 %collective-permute-start.23 = (f32[5,32]{1,0:T(8,128)S(1)}, f32[5,32]{1,0:T(8,128)S(1)}, u32[]{:S(2)}, u32[]{:S(2)}) collective-permute-start(f32[5,32]{1,0:T(8,128)S(1)} %bitcast.313), channel_id=1, source_target_pairs={{0,24},{4,100},{8,0},{12,108},{16,8},{20,116},{24,16},{28,124},{32... | collective-permute-start | bytes 1928 | tf_op jit(solution)/shard_map/ppermute | solution.py:40
  199.8 4.8 %collective-permute-start.24 = (f32[5,32]{1,0:T(8,128)S(1)}, f32[5,32]{1,0:T(8,128)S(1)}, u32[]{:S(2)}, u32[]{:S(2)}) collective-permute-start(f32[5,32]{1,0:T(8,128)S(1)} %bitcast.314), channel_id=1, source_target_pairs={{0,8},{4,36},{8,16},{12,44},{16,24},{20,52},{24,0},{28,60},{32,40}... | collective-permute-start | bytes 1928 | tf_op jit(solution)/shard_map/ppermute | solution.py:40
  200.9 5.1 %collective-permute-start.25 = (f32[5,32]{1,0:T(8,128)S(1)}, f32[5,32]{1,0:T(8,128)S(1)}, u32[]{:S(2)}, u32[]{:S(2)}) collective-permute-start(f32[5,32]{1,0:T(8,128)S(1)} %bitcast.315), channel_id=1, source_target_pairs={{0,16},{4,68},{8,24},{12,76},{16,0},{20,84},{24,8},{28,92},{32,48}... | collective-permute-start | bytes 1928 | tf_op jit(solution)/shard_map/ppermute | solution.py:40
Sparse Core Ops, SparseCore 0:
  9.5 65.1 all-gather.2
  76.4 47.2 all-gather.4

commit v7 on v6

--- a/solution.py
+++ b/solution.py
@@ -235,29 +235,45 @@
 
 
 def project_out(gated, weights, head):
-    count, depth = gated.shape
-    width, tile = weights.shape[1], 1024
-    quarter = count // 4
-
-    def kernel(head_ref, gated_ref, weights_ref, out_ref):
+    count, width = gated.shape[0], weights.shape[1]
+    quarter, depth = count // 4, 256
+    steps = gated.shape[1] // depth
+
+    def kernel(head_ref, gated_ref, weights_ref, out_ref, total_ref):
+        step = pl.program_id(0)
         product = jnp.dot(gated_ref[...], weights_ref[...], preferred_element_type=jnp.float32)
-        for q in range(4):
-            ahead = jnp.bitwise_and(q - head_ref[0], 3)
-            out_ref[ahead] = product[q * quarter : (q + 1) * quarter, :].astype(jnp.bfloat16)
+
+        @pl.when(step == 0)
+        def _():
+            total_ref[...] = product
+
+        @pl.when(jnp.logical_and(step > 0, step < steps - 1))
+        def _():
+            total_ref[...] += product
+
+        @pl.when(step == steps - 1)
+        def _():
+            total = total_ref[...] + product
+            for q in range(4):
+                ahead = jnp.bitwise_and(q - head_ref[0], 3)
+                out_ref[ahead] = total[q * quarter : (q + 1) * quarter, :].astype(jnp.bfloat16)
 
     return pl.pallas_call(
         kernel,
-        grid=(width // tile,),
+        grid=(steps,),
         in_specs=[
             pl.BlockSpec(memory_space=pltpu.SMEM),
-            pl.BlockSpec((count, depth), lambda i: (0, 0)),
-            pl.BlockSpec((depth, tile), lambda i: (0, i)),
+            pl.BlockSpec((count, depth), lambda i: (0, i)),
+            pl.BlockSpec((depth, width), lambda i: (i, 0)),
         ],
-        out_specs=pl.BlockSpec((4, quarter, tile), lambda i: (0, 0, i)),
+        out_specs=pl.BlockSpec((4, quarter, width), lambda i: (0, 0, 0)),
         out_shape=jax.ShapeDtypeStruct((4, quarter, width), jnp.bfloat16),
+        scratch_shapes=[pltpu.VMEM((count, width), jnp.float32)],
         compiler_params=pltpu.CompilerParams(vmem_limit_bytes=48 << 20),
         cost_estimate=pl.CostEstimate(
-            flops=2 * count * depth * width, bytes_accessed=2 * depth * width, transcendentals=0
+            flops=2 * count * steps * depth * width,
+            bytes_accessed=2 * steps * depth * width,
+            transcendentals=0,
         ),
     )(head, gated, weights)
 
@@ -289,8 +305,8 @@
 def vocab_stats(pieces, wanted, tables):
     count = sum(piece.shape[0] for piece in pieces)
     width, columns = tables[0].shape
-    tile = 256
-    tiles = columns // tile
+    depth = 2048
+    blocks = width // depth
     f32 = jnp.float32
 
     def kernel(*refs):
@@ -302,23 +318,26 @@
         def _():
             start = 0
             for ref in piece_refs:
-                rows_ref[start : start + ref.shape[0], :] = ref[...]
+                for k in range(blocks):
+                    rows_ref[k, start : start + ref.shape[0], :] = ref[:, k * depth : (k + 1) * depth]
                 start += ref.shape[0]
 
-        @pl.when(step < tiles)
-        def _():
-            logits_ref[step] = jnp.dot(rows_ref[...], first_ref[...], preferred_element_type=f32)
-
-        @pl.when(step >= tiles)
-        def _():
-            logits_ref[step] = jnp.dot(rows_ref[...], second_ref[...], preferred_element_type=f32)
-
-        @pl.when(step == 2 * tiles - 1)
+        for place, table_ref in enumerate((first_ref, second_ref)):
+            for k in range(blocks):
+
+                @pl.when(step == place * blocks + k)
+                def _(place=place, k=k, table_ref=table_ref):
+                    part = jnp.dot(rows_ref[k], table_ref[...], preferred_element_type=f32)
+                    if k:
+                        part = part + logits_ref[place]
+                    logits_ref[place] = part
+
+        @pl.when(step == 2 * blocks - 1)
         def _():
             lane = lax.broadcasted_iota(jnp.int32, (128, 128), 1)
             column = lax.broadcasted_iota(jnp.int32, (128, columns), 1)
             for r in range(count // 128):
-                logits = [logits_ref[j, r * 128 : (r + 1) * 128, :] for j in range(2 * tiles)]
+                logits = [logits_ref[j, r * 128 : (r + 1) * 128, :] for j in range(2)]
                 logits = jnp.concatenate(logits, axis=1)
                 peak = jnp.max(logits, axis=1, keepdims=True)
                 shifted = logits - peak
@@ -344,20 +363,20 @@
     every = 2 * columns
     return pl.pallas_call(
         kernel,
-        grid=(2 * tiles,),
+        grid=(2 * blocks,),
         in_specs=[pl.BlockSpec(piece.shape, lambda i: (0, 0)) for piece in pieces]
         + [
             pl.BlockSpec(wanted.shape, lambda i: (0, 0, 0)),
-            pl.BlockSpec((width, tile), lambda i: (0, jnp.minimum(i, tiles - 1))),
-            pl.BlockSpec((width, tile), lambda i: (0, jnp.maximum(i - tiles, 0))),
+            pl.BlockSpec((depth, columns), lambda i: (jnp.minimum(i, blocks - 1), 0)),
+            pl.BlockSpec((depth, columns), lambda i: (jnp.maximum(i - blocks, 0), 0)),
         ],
         out_specs=pl.BlockSpec((8, count), lambda i: (0, 0)),
         out_shape=jax.ShapeDtypeStruct((8, count), f32),
         scratch_shapes=[
-            pltpu.VMEM((count, width), jnp.bfloat16),
-            pltpu.VMEM((2 * tiles, count, tile), f32),
+            pltpu.VMEM((blocks, count, depth), jnp.bfloat16),
+            pltpu.VMEM((2, count, columns), f32),
         ],
-        compiler_params=pltpu.CompilerParams(vmem_limit_bytes=50 << 20),
+        compiler_params=pltpu.CompilerParams(vmem_limit_bytes=48 << 20),
         cost_estimate=pl.CostEstimate(
             flops=2 * count * width * every,
             bytes_accessed=2 * width * every,
@@ -480,10 +499,10 @@
     gated_out = rms_scale(gated_raw, norm_gain).astype(bf16)
 
     partial_out = project_out(gated_out, w_out_full, head_at)
+    partial_out, vocab_own = lax.optimization_barrier((partial_out, vocab_own))
+    vocab_other = swap_core(vocab_own)
     summed_out = ring_reduce([partial_out[k] for k in range(4)], shift_head)
     residual = (own_emb.astype(f32) + summed_out).astype(bf16)
-    residual, vocab_own = lax.optimization_barrier((residual, vocab_own))
-    vocab_other = swap_core(vocab_own)
     normed_out = rms_scale(residual.astype(f32), final_gain).astype(bf16)
 
     along_first, along_second = shift_mixed(True), shift_mixed(False)
@@ -507,17 +526,15 @@
     tables = (vocab_own, vocab_other)
     rows = 4 * quarter
     near, near_left, rest_right = lax.optimization_barrier((near, near_left, rest_right))
+    stats = [vocab_stats((near, rest), by_chip[:, 0], tables)]
     near_far = moved(near_left, along_second, 1)
     rest_far = moved(rest_right, along_second, -1)
-    aims = jnp.concatenate([by_chip[:, k] for k in (0, 1, 3)], axis=1)
-    first = (near, rest, near_right, rest_right, near_left, rest_left)
-    first = vocab_stats(first, aims, tables)
-    near_far, rest_far, first = lax.optimization_barrier((near_far, rest_far, first))
-    last = vocab_stats((near_far, rest_far), by_chip[:, 2], tables)
-    stats = [first[:, :rows]]
-    stats.append(moved(first[:, rows : 2 * rows], along_second, 1))
-    stats.append(moved(first[:, 2 * rows :], along_second, 3))
-    stats.append(moved(last, along_second, 2))
+    near_far, rest_far, stats[0] = lax.optimization_barrier((near_far, rest_far, stats[0]))
+    aims = jnp.concatenate([by_chip[:, k] for k in (1, 2, 3)], axis=1)
+    others = (near_right, rest_right, near_far, rest_far, near_left, rest_left)
+    others = vocab_stats(others, aims, tables)
+    for k in range(1, 4):
+        stats.append(moved(others[:, (k - 1) * rows : k * rows], along_second, k))
     merged = tuple(stats[0][:5])
     for other in stats[1:]:
         merged = join_stats(merged, tuple(other[:5]))

time: 214 us -> 205 us (0.958)
  waiting for transfers between devices: 73.4 us -> 57.2 us
  blocking collectives: 12.6 us -> 26 us
  other arithmetic: 7.52 us -> 5.36 us
    all_to_all x0 -> x1, blocking collectives: none -> 13.4 us  [on_device(): mine = lax.all_to_all(mine, 'ctx', 0, 0, tiled=True)]
    all_to_all x1 -> x0, waiting for transfers between devices: 10 us -> none  [on_device(): mine = lax.all_to_all(mine, 'ctx', 0, 0, tiled=True)]
    ppermute x24, waiting for transfers between devices: 48.5 us -> 41.6 us  [moved(): return lax.ppermute(value, axis, pairs)]
    ppermute x24, starting transfers between devices: 30.8 us -> 35 us  [moved(): return lax.ppermute(value, axis, pairs)]
    all_to_all x1 -> x0, starting transfers between devices: 4 us -> none  [on_device(): mine = lax.all_to_all(mine, 'ctx', 0, 0, tiled=True)]
    unnamed x54 -> x48, local copies, waits for them, and re-layouts: 7.29 us -> 6.55 us
  transfers between devices with their start and end apart: 31 -> 30, of which waited for: 18 -> 17; matrix products, arithmetic and copies ran while one was open for 8% -> 6% of each run, Pallas kernels for 18% -> 14%
where the time goes in v7:
time: 205 us; the launch traced here: 204 us
  waiting for transfers between devices  57.2 us (28%)
  starting transfers between devices  52 us (25%)
  Pallas kernels  36 us (18%)
  blocking collectives  26 us (13%)
  between operations  14 us (7%)
  local copies, waits for them, and re-layouts  9.71 us (5%)
  other arithmetic  5.36 us (3%)
  matrix products  4.08 us (2%)
    ppermute x24, waiting for transfers between devices, moved(): return lax.ppermute(value, axis, pairs)  41.6 us
    ppermute x24, starting transfers between devices, moved(): return lax.ppermute(value, axis, pairs)  35 us
    all_to_all x1, blocking collectives, on_device(): mine = lax.all_to_all(mine, 'ctx', 0, 0, tiled=True)  13.4 us
    pallas_call x2, Pallas kernels, vocab_stats(): pl.pallas_call(kernel, grid=(2 * blocks,), in_specs=[pl.BlockSpec(piece.s...  12.7 us
    all_to_all x1, blocking collectives, on_device(): state_in = lax.all_to_all(entering, 'ctx', 0, 0, tiled=True)  12.6 us
    pallas_call x1, Pallas kernels, embed_and_project(): pl.pallas_call(kernel, grid=(width // depth,), in_specs=[pl.BlockSpec(mem...  10.8 us
    all_to_all x1, starting transfers between devices, on_device(): packed = lax.all_to_all(packed, 'ctx', 0, 0, tiled=True)  8.34 us
    all_to_all x1, waiting for transfers between devices, on_device(): arrived = lax.all_to_all(message, 'ctx', 0, 0, tiled=True)  7.43 us
  transfers between devices with their start and end apart: 30, of which 17 were waited for; matrix products, arithmetic and copies ran while one was open for 6% of the time, Pallas kernels for 14%

profile of v7, /device:TPU:0, one launch (start us, length us, event | category | flops | bytes accessed | tf_op | source)
XLA Modules:
  0.0 204.3 jit_solution(6747316301089041354)
XLA Ops:
  6.5 0.7 all-gather.3.cloned.1.call-update
  7.3 1.2 copy-done.7
  8.5 0.8 shard_map.154
  9.3 2.9 %collective-permute-start = (bf16[1024,128]{1,0:T(8,128)(2,1)S(1)}, bf16[1024,128]{1,0:T(8,128)(2,1)S(1)}, u32[]{:S(2)}, u32[]{:S(2)}) collective-permute-start(bf16[1024,128]{1,0:T(8,128)(2,1)S(1)} %get-tuple-element.31), channel_id=1, source_target_pairs={{0,3},{1,0},{2,1},{3,2},{4,7},{5,4},{6,5},{7,6},{8,11},{9,8},{10,9... | collective-permute-start | bytes 786440 | tf_op jit(solution)/shard_map/ppermute | solution.py:40
  12.2 0.8 collective-permute-start.1
  13.0 0.9 collective-permute-start.2
  13.9 0.7 pad_add_fusion.3
  14.6 0.6 all_to_all.17
  15.2 8.3 %all-to-all-start = ((s32[32,1,160]{2,1,0:T(1,128)}), s32[32,1,160]{2,1,0:T(1,128)S(1)}, u32[]{:S(2)}, u32[]{:S(2)}) async-start(s32[32,1,160]{2,1,0:T(1,128)} %all_to_all.17), calls=%async_computation | async-start | bytes 65536 | tf_op jit(solution)/shard_map/all_to_all | solution.py:426
  23.6 7.4 %all-to-all-done = s32[32,1,160]{2,1,0:T(1,128)S(1)} async-done(((s32[32,1,160]{2,1,0:T(1,128)}), s32[32,1,160]{2,1,0:T(1,128)S(1)}, u32[]{:S(2)}, u32[]{:S(2)}) %all-to-all-start) | async-done | bytes 20512 | tf_op jit(solution)/shard_map/all_to_all | solution.py:426
  31.3 6.3 %shard_map.155 = bf16[1024,128]{1,0:T(8,128)(2,1)S(1)} custom-call(s32[2,16,128]{2,1,0:T(8,128)S(1)} %reshape.193.ids_ref, bf16[1024,128]{1,0:T(8,128)(2,1)S(1)} %get-tuple-element.28.refs_0_, bf16[1024,128]{1,0:T(8,128)(2,1)S(1)} %collective-permute-done.refs_1_, bf16[1024,128]{1,0:T(8,128)(2,1)S(1)} %collective-permute-done.1.refs_2_, ...), custom_call_target="tpu_custom_call" | custom-call | flops 4294967296 | bytes 2097152 | tf_op jit(solution)/shard_map/pallas_call | solution.py:146
  37.6 13.4 %all_to_all.27 = bf16[32,32,128]{2,1,0:T(8,128)(2,1)S(1)} all-to-all(bf16[32,32,128]{2,1,0:T(8,128)(2,1)S(1)} %bitcast.298), channel_id=1, replica_groups=mesh['ctx'=32,'head'=4] {'ctx'}, dimensions={0} | all-to-all | bytes 524288 | tf_op jit(solution)/shard_map/all_to_all | solution.py:433
  51.1 1.4 collective-permute-start.3
  52.5 1.5 collective-permute-start.4
  54.1 0.6 iota_compare_fusion
  54.7 1.4 copy.79.refs_8_
  56.1 0.6 pad.16.clone
  56.7 3.8 %collective-permute-done.3 = bf16[32,32,128]{2,1,0:T(8,128)(2,1)} collective-permute-done((bf16[32,32,128]{2,1,0:T(8,128)(2,1)S(1)}, bf16[32,32,128]{2,1,0:T(8,128)(2,1)}, u32[]{:S(2)}, u32[]{:S(2)}) %collective-permute-start.3) | collective-permute-done | bytes 262176 | tf_op jit(solution)/shard_map/ppermute | solution.py:40
  60.4 2.9 %collective-permute-done.4 = bf16[32,32,128]{2,1,0:T(8,128)(2,1)} collective-permute-done((bf16[32,32,128]{2,1,0:T(8,128)(2,1)S(1)}, bf16[32,32,128]{2,1,0:T(8,128)(2,1)}, u32[]{:S(2)}, u32[]{:S(2)}) %collective-permute-start.4) | collective-permute-done | bytes 262176 | tf_op jit(solution)/shard_map/ppermute | solution.py:40
  63.3 4.7 %collective-permute-done.5 = bf16[32,32,128]{2,1,0:T(8,128)(2,1)} collective-permute-done((bf16[32,32,128]{2,1,0:T(8,128)(2,1)S(1)}, bf16[32,32,128]{2,1,0:T(8,128)(2,1)}, u32[]{:S(2)}, u32[]{:S(2)}) %collective-permute-start.5) | collective-permute-done | bytes 262176 | tf_op jit(solution)/shard_map/ppermute | solution.py:40
  68.0 10.8 %shard_map.156 = (f32[128,1024]{1,0:T(8,128)S(1)}, f32[128,1024]{1,0:T(8,128)S(1)}, f32[128,256]{1,0:T(8,128)S(1)}, f32[128,16]{1,0:T(8,128)S(1)}, bf16[32,4096]{1,0:T(8,128)(2,1)S(1)}) custom-call(s32[1]{0:T(128)} %bitcast.head_ref.refs_0_, bf16[1024,128]{1,0:T(8,128)(2,1)S(1)} %bitcast.297, bf16[1024,128]{1,0:T(8,128)(2,1)} %bitcast.4.refs_2_, ...), custom_call_target="tpu_custom_call" | custom-call | flops 2432696320 | bytes 19005440 | tf_op jit(solution)/shard_map/pallas_call | solution.py:209
  78.9 0.8 copy-done.2
  79.8 0.6 copy-done.4
  80.4 2.1 %collective-permute-start.6 = (f32[3,1280]{1,0:T(4,128)S(1)}, f32[3,1280]{1,0:T(4,128)S(1)}, u32[]{:S(2)}, u32[]{:S(2)}) collective-permute-start(f32[3,1280]{1,0:T(4,128)S(1)} %slice.177), channel_id=1, source_target_pairs={{0,4},{4,8},{8,12},{12,16},{16,20},{20,24},{24,28},{28,32},{32,36}... | collective-permute-start | bytes 46088 | tf_op jit(solution)/shard_map/ppermute | solution.py:46
  83.0 0.7 fusion.89
  84.0 0.4 divide_multiply_fusion
  84.7 0.6 convolution_convert_fusion.1
  85.4 0.9 maximum_maximum_fusion
  86.3 6.6 %all-to-all-start.2 = ((bf16[32,48,128]{2,1,0:T(8,128)(2,1)}), bf16[32,48,128]{2,1,0:T(8,128)(2,1)S(1)}, u32[]{:S(2)}, u32[]{:S(2)}) async-start(bf16[32,48,128]{2,1,0:T(8,128)(2,1)} %maximum_maximum_fusion), calls=%async_computation.2 | async-start | bytes 786432 | tf_op jit(solution)/shard_map/all_to_all | solution.py:473
  93.2 2.2 %fusion = f32[128,16,64]{0,2,1:T(8,128)S(1)} fusion(f32[128,16,64]{0,2,1:T(8,128)S(1)} %bitcast.302, f32[16,128]{1,0:T(8,128)S(1)} %copy.85, f32[16,128]{1,0:T(8,128)S(1)} %bitcast.312, f32[128,128]{1,0:T(8,128)S(1)} %fusion.38, pred[128,128]{1,0:T(8,128)(4,1)S(1)} %copy-done.10, f32[16]{0:T(128)S(1)} %copy-done.16), kind=kOutput, calls=%fused_computation.2 | convolution fusion | flops 202637312 | bytes 1146944 | tf_op jit(solution)/shard_map/hts,shp->thp/dot_general | solution.py:478
  95.4 7.4 %all-to-all-done.2 = bf16[32,48,128]{2,1,0:T(8,128)(2,1)S(1)} async-done(((bf16[32,48,128]{2,1,0:T(8,128)(2,1)}), bf16[32,48,128]{2,1,0:T(8,128)(2,1)S(1)}, u32[]{:S(2)}, u32[]{:S(2)}) %all-to-all-start.2) | async-done | bytes 393248 | tf_op jit(solution)/shard_map/all_to_all | solution.py:473
  103.3 0.4 fusion.2
  103.8 12.6 %all_to_all.28 = bf16[32,32,128]{2,1,0:T(8,128)(2,1)S(1)} all-to-all(bf16[32,32,128]{2,1,0:T(8,128)(2,1)S(1)} %bitcast.306), channel_id=1, replica_groups=mesh['ctx'=32,'head'=4] {'ctx'}, dimensions={0} | all-to-all | bytes 524288 | tf_op jit(solution)/shard_map/all_to_all | solution.py:490
  117.4 5.3 %shard_map.157 = bf16[4,32,4096]{2,1,0:T(8,128)(2,1)S(1)} custom-call(s32[1]{0:T(128)} %bitcast.head_ref.refs_0_, bf16[128,1024]{1,0:T(8,128)(2,1)S(1)} %multiply_convert_fusion.gated_ref, bf16[1024,4096]{1,0:T(8,128)(2,1)} %all-gather.3.cloned.1.call-done.weights_ref), custom_call_target="tpu_custom_call" | custom-call | flops 1073741824 | bytes 8388608 | tf_op jit(solution)/shard_map/pallas_call | solution.py:261
  122.9 1.1 collective-permute-start.9
  124.0 2.0 collective-permute-start.8
  126.1 6.0 %collective-permute-done.9 = bf16[32,4096]{1,0:T(8,128)(2,1)S(1)} collective-permute-done((bf16[32,4096]{1,0:T(8,128)(2,1)S(1)}, bf16[32,4096]{1,0:T(8,128)(2,1)S(1)}, u32[]{:S(2)}, u32[]{:S(2)}) %collective-permute-start.9) | collective-permute-done | bytes 262176 | tf_op jit(solution)/shard_map/ppermute | solution.py:40
  132.1 2.6 %collective-permute-done.8 = bf16[32,4096]{1,0:T(8,128)(2,1)S(1)} collective-permute-done((bf16[32,4096]{1,0:T(8,128)(2,1)S(1)}, bf16[32,4096]{1,0:T(8,128)(2,1)S(1)}, u32[]{:S(2)}, u32[]{:S(2)}) %collective-permute-start.8) | collective-permute-done | bytes 262176 | tf_op jit(solution)/shard_map/ppermute | solution.py:40
  134.7 4.7 %collective-permute-done.7 = bf16[32,4096]{1,0:T(8,128)(2,1)S(1)} collective-permute-done((bf16[32,4096]{1,0:T(8,128)(2,1)S(1)}, bf16[32,4096]{1,0:T(8,128)(2,1)S(1)}, u32[]{:S(2)}, u32[]{:S(2)}) %collective-permute-start.7) | collective-permute-done | bytes 262176 | tf_op jit(solution)/shard_map/ppermute | solution.py:40
  139.8 0.7 collective-permute-start.10
  140.5 2.6 %collective-permute-start.12 = (bf16[32,4096]{1,0:T(8,128)(2,1)S(1)}, bf16[32,4096]{1,0:T(8,128)(2,1)S(1)}, u32[]{:S(2)}, u32[]{:S(2)}) collective-permute-start(bf16[32,4096]{1,0:T(8,128)(2,1)S(1)} %fusion.18), channel_id=1, source_target_pairs={{0,24},{4,100},{8,0},{12,108},{16,8},{20,116},{24,16},{28,124},{32... | collective-permute-start | bytes 786440 | tf_op jit(solution)/shard_map/ppermute | solution.py:40
  143.1 0.9 collective-permute-start.13
  144.0 3.4 %collective-permute-done.10 = bf16[32,4096]{1,0:T(8,128)(2,1)S(1)} collective-permute-done((bf16[32,4096]{1,0:T(8,128)(2,1)S(1)}, bf16[32,4096]{1,0:T(8,128)(2,1)S(1)}, u32[]{:S(2)}, u32[]{:S(2)}) %collective-permute-start.10) | collective-permute-done | bytes 262176 | tf_op jit(solution)/shard_map/ppermute | solution.py:40
  147.5 0.6 collective-permute-start.11
  148.1 1.8 collective-permute-done.12
  149.9 1.4 collective-permute-done.13
  151.3 2.8 %collective-permute-start.14 = (bf16[64,4096]{1,0:T(8,128)(2,1)S(1)}, bf16[64,4096]{1,0:T(8,128)(2,1)S(1)}, u32[]{:S(2)}, u32[]{:S(2)}) collective-permute-start(bf16[64,4096]{1,0:T(8,128)(2,1)S(1)} %constant_dynamic-update-slice_fusion.4.refs_1_), channel_id=1, source_target_pairs={{0,96},{4,28},{8,104},{12,4},{16,112},{20,12},{24,120},{28,20},{32... | collective-permute-start | bytes 1572872 | tf_op jit(solution)/shard_map/ppermute | solution.py:40
  154.2 0.9 collective-permute-start.18
  155.1 1.2 collective-permute-start.19
  156.3 1.7 collective-permute-done.11.refs_4_
  158.0 2.8 %collective-permute-done.14.refs_1_ = bf16[64,4096]{1,0:T(8,128)(2,1)S(1)} collective-permute-done((bf16[64,4096]{1,0:T(8,128)(2,1)S(1)}, bf16[64,4096]{1,0:T(8,128)(2,1)S(1)}, u32[]{:S(2)}, u32[]{:S(2)}) %collective-permute-start.14) | collective-permute-done | bytes 524320 | tf_op jit(solution)/shard_map/ppermute | solution.py:40
  160.8 1.2 collective-permute-start.15
  162.0 2.5 %collective-permute-start.16 = (bf16[64,4096]{1,0:T(8,128)(2,1)S(1)}, bf16[64,4096]{1,0:T(8,128)(2,1)}, u32[]{:S(2)}, u32[]{:S(2)}) collective-permute-start(bf16[64,4096]{1,0:T(8,128)(2,1)S(1)} %collective-permute-done.14.refs_1_), channel_id=1, source_target_pairs={{0,96},{4,28},{8,104},{12,4},{16,112},{20,12},{24,120},{28,20},{32... | collective-permute-start | bytes 1572872 | tf_op jit(solution)/shard_map/ppermute | solution.py:40
  164.8 2.2 %copy-done = bf16[4096,512]{1,0:T(8,128)(2,1)S(1)} copy-done((bf16[4096,512]{1,0:T(8,128)(2,1)S(1)}, bf16[4096,512]{1,0:T(8,128)(2,1)}, u32[]{:S(2)}) %copy-start) | copy-done | bytes 4194328
  166.9 4.9 %shard_map.158 = f32[8,128]{1,0:T(8,128)S(1)} custom-call(bf16[64,4096]{1,0:T(8,128)(2,1)S(1)} %pad_maximum_fusion.1.refs_0_, bf16[64,4096]{1,0:T(8,128)(2,1)S(1)} %constant_dynamic-update-slice_fusion.4.refs_1_, s32[2,1,128]{2,1,0:T(1,128)S(1)} %bitcast.300, bf16[4096,512]{1,0:T(8,128)(2,1)S(1)} %copy-done, ...), custom_call_target="tpu_custom_call" | custom-call | flops 1073741824 | bytes 8388608 | tf_op jit(solution)/shard_map/pallas_call | solution.py:364
  172.0 7.8 %shard_map.159 = f32[8,384]{1,0:T(8,128)S(1)} custom-call(bf16[64,4096]{1,0:T(8,128)(2,1)S(1)} %collective-permute-done.18.refs_0_, bf16[64,4096]{1,0:T(8,128)(2,1)S(1)} %collective-permute-done.14.refs_1_, bf16[64,4096]{1,0:T(8,128)(2,1)} %collective-permute-done.15.refs_2_, bf16[64,4096]{1,0:T(8,128)(2,1)} %collective-permute-done.16.refs_3_, ...), custom_call_target="tpu_custom_call" | custom-call | flops 3221225472 | bytes 8388608 | tf_op jit(solution)/shard_map/pallas_call | solution.py:364
  179.8 3.9 %collective-permute-start.22 = (f32[8,128]{1,0:T(8,128)S(1)}, f32[8,128]{1,0:T(8,128)S(1)}, u32[]{:S(2)}, u32[]{:S(2)}) collective-permute-start(f32[8,128]{1,0:T(8,128)S(1)} %get-tuple-element.73), channel_id=1, source_target_pairs={{0,96},{4,28},{8,104},{12,4},{16,112},{20,12},{24,120},{28,20},{32... | collective-permute-start | bytes 12296 | tf_op jit(solution)/shard_map/ppermute | solution.py:40
  183.7 0.9 collective-permute-start.20
  184.6 0.4 collective-permute-done.22
  185.0 3.8 %collective-permute-done.21 = f32[8,128]{1,0:T(8,128)S(1)} collective-permute-done((f32[8,128]{1,0:T(8,128)S(1)}, f32[8,128]{1,0:T(8,128)S(1)}, u32[]{:S(2)}, u32[]{:S(2)}) %collective-permute-start.21) | collective-permute-done | bytes 4128 | tf_op jit(solution)/shard_map/ppermute | solution.py:40
  189.4 2.8 %collective-permute-start.25 = (f32[5,32]{1,0:T(8,128)S(1)}, f32[5,32]{1,0:T(8,128)S(1)}, u32[]{:S(2)}, u32[]{:S(2)}) collective-permute-start(f32[5,32]{1,0:T(8,128)S(1)} %bitcast.316), channel_id=1, source_target_pairs={{0,16},{4,68},{8,24},{12,76},{16,0},{20,84},{24,8},{28,92},{32,48}... | collective-permute-start | bytes 1928 | tf_op jit(solution)/shard_map/ppermute | solution.py:40
  192.1 3.2 %collective-permute-start.23 = (f32[5,32]{1,0:T(8,128)S(1)}, f32[5,32]{1,0:T(8,128)S(1)}, u32[]{:S(2)}, u32[]{:S(2)}) collective-permute-start(f32[5,32]{1,0:T(8,128)S(1)} %bitcast.318), channel_id=1, source_target_pairs={{0,24},{4,100},{8,0},{12,108},{16,8},{20,116},{24,16},{28,124},{32... | collective-permute-start | bytes 1928 | tf_op jit(solution)/shard_map/ppermute | solution.py:40
  195.4 1.6 collective-permute-done.24
  197.0 0.5 fusion.82
  (126 shorter events, 5.0 us)
Async XLA Ops:
  6.5 96.3 %all-gather.3.cloned.1.call-start = ((), (), s32[]{:S(2)}) async-start(), calls=%async_computation.4 | async-start | bytes 8650752 | tf_op jit(solution)/shard_map/all_gather | solution.py:415
  7.3 1.2 copy-start.7
  9.3 22.0 %collective-permute-start = (bf16[1024,128]{1,0:T(8,128)(2,1)S(1)}, bf16[1024,128]{1,0:T(8,128)(2,1)S(1)}, u32[]{:S(2)}, u32[]{:S(2)}) collective-permute-start(bf16[1024,128]{1,0:T(8,128)(2,1)S(1)} %get-tuple-element.31), channel_id=1, source_target_pairs={{0,3},{1,0},{2,1},{3,2},{4,7},{5,4},{6,5},{7,6},{8,11},{9,8},{10,9... | collective-permute-start | bytes 786440 | tf_op jit(solution)/shard_map/ppermute | solution.py:40
  12.2 19.1 %collective-permute-start.1 = (bf16[1024,128]{1,0:T(8,128)(2,1)S(1)}, bf16[1024,128]{1,0:T(8,128)(2,1)S(1)}, u32[]{:S(2)}, u32[]{:S(2)}) collective-permute-start(bf16[1024,128]{1,0:T(8,128)(2,1)S(1)} %get-tuple-element.30), channel_id=1, source_target_pairs={{0,2},{1,3},{2,0},{3,1},{4,6},{5,7},{6,4},{7,5},{8,10},{9,11},{10,... | collective-permute-start | bytes 786440 | tf_op jit(solution)/shard_map/ppermute | solution.py:40
  13.0 18.3 %collective-permute-start.2 = (bf16[1024,128]{1,0:T(8,128)(2,1)S(1)}, bf16[1024,128]{1,0:T(8,128)(2,1)S(1)}, u32[]{:S(2)}, u32[]{:S(2)}) collective-permute-start(bf16[1024,128]{1,0:T(8,128)(2,1)S(1)} %get-tuple-element.29), channel_id=1, source_target_pairs={{0,1},{1,2},{2,3},{3,0},{4,5},{5,6},{6,7},{7,4},{8,9},{9,10},{10,1... | collective-permute-start | bytes 786440 | tf_op jit(solution)/shard_map/ppermute | solution.py:40
  15.2 15.8 %all-to-all-start = ((s32[32,1,160]{2,1,0:T(1,128)}), s32[32,1,160]{2,1,0:T(1,128)S(1)}, u32[]{:S(2)}, u32[]{:S(2)}) async-start(s32[32,1,160]{2,1,0:T(1,128)} %all_to_all.17), calls=%async_computation | async-start | bytes 65536 | tf_op jit(solution)/shard_map/all_to_all | solution.py:426
  23.5 99.2 %all-gather.5.cloned.1.call-start = ((), (), s32[]{:S(2)}) async-start(), calls=%async_computation.5 | async-start | bytes 5242880 | tf_op jit(solution)/shard_map/all_gather | solution.py:435
  31.2 19.8 %copy-start.9 = (f32[4,1024]{1,0:T(4,128)S(1)}, f32[4,1024]{1,0:T(4,128)}, u32[]{:S(2)}) copy-start(f32[4,1024]{1,0:T(4,128)} %param.22) | copy-start | bytes 49156
  31.2 19.8 %copy-start.12 = (f32[4,2,128]{2,1,0:T(2,128)S(1)}, f32[4,2,128]{2,1,0:T(2,128)}, u32[]{:S(2)}) copy-start(f32[4,2,128]{2,1,0:T(2,128)} %param.23) | copy-start | bytes 12292
  31.2 25.4 %copy-start.15 = (f32[16]{0:T(128)S(1)}, f32[16]{0:T(128)}, u32[]{:S(2)}) copy-start(f32[16]{0:T(128)} %param.25) | copy-start | bytes 196
  31.2 36.7 %copy-start.6 = (f32[4096]{0:T(1024)S(1)}, f32[4096]{0:T(1024)}, u32[]{:S(2)}) copy-start(f32[4096]{0:T(1024)} %param.28) | copy-start | bytes 49156
  37.6 30.4 %copy-start.1 = (bf16[4096,2,128]{2,1,0:T(2,128)(2,1)S(1)}, bf16[4096,2,128]{2,1,0:T(2,128)(2,1)}, u32[]{:S(2)}) copy-start(bf16[4096,2,128]{2,1,0:T(2,128)(2,1)} %refs_7_.1) | copy-start | bytes 6291460
  51.1 9.3 %collective-permute-start.3 = (bf16[32,32,128]{2,1,0:T(8,128)(2,1)S(1)}, bf16[32,32,128]{2,1,0:T(8,128)(2,1)}, u32[]{:S(2)}, u32[]{:S(2)}) collective-permute-start(bf16[32,32,128]{2,1,0:T(8,128)(2,1)S(1)} %all_to_all.27), channel_id=1, source_target_pairs={{0,3},{1,0},{2,1},{3,2},{4,7},{5,4},{6,5},{7,6},{8,11},{9,8},{10,9... | collective-permute-start | bytes 786440 | tf_op jit(solution)/shard_map/ppermute | solution.py:40
  52.5 10.8 %collective-permute-start.4 = (bf16[32,32,128]{2,1,0:T(8,128)(2,1)S(1)}, bf16[32,32,128]{2,1,0:T(8,128)(2,1)}, u32[]{:S(2)}, u32[]{:S(2)}) collective-permute-start(bf16[32,32,128]{2,1,0:T(8,128)(2,1)S(1)} %all_to_all.27), channel_id=1, source_target_pairs={{0,2},{1,3},{2,0},{3,1},{4,6},{5,7},{6,4},{7,5},{8,10},{9,11},{10,... | collective-permute-start | bytes 786440 | tf_op jit(solution)/shard_map/ppermute | solution.py:40
  54.0 13.9 %collective-permute-start.5 = (bf16[32,32,128]{2,1,0:T(8,128)(2,1)S(1)}, bf16[32,32,128]{2,1,0:T(8,128)(2,1)}, u32[]{:S(2)}, u32[]{:S(2)}) collective-permute-start(bf16[32,32,128]{2,1,0:T(8,128)(2,1)S(1)} %all_to_all.27), channel_id=1, source_target_pairs={{0,1},{1,2},{2,3},{3,0},{4,5},{5,6},{6,7},{7,4},{8,9},{9,10},{10,1... | collective-permute-start | bytes 786440 | tf_op jit(solution)/shard_map/ppermute | solution.py:40
  68.0 14.5 %copy-start.13 = (f32[16]{0:T(128)S(1)}, f32[16]{0:T(128)}, u32[]{:S(2)}) copy-start(f32[16]{0:T(128)} %param.24) | copy-start | bytes 196
  78.8 0.8 copy-start.2
  79.7 0.7 copy-start.4
  79.7 5.7 %copy-start.14 = (bf16[48]{0:T(256)(128)(2,1)S(1)}, bf16[48]{0:T(256)(128)(2,1)}, u32[]{:S(2)}) copy-start(bf16[48]{0:T(256)(128)(2,1)} %pad.16.clone) | copy-start | bytes 292
  79.7 13.5 %copy-start.10 = (pred[128,128]{1,0:T(8,128)(4,1)S(1)}, pred[128,128]{1,0:T(8,128)(4,1)}, u32[]{:S(2)}) copy-start(pred[128,128]{1,0:T(8,128)(4,1)} %iota_compare_fusion) | copy-start | bytes 49156
  79.7 13.5 %copy-start.16 = (f32[16]{0:T(128)S(1)}, f32[16]{0:T(128)}, u32[]{:S(2)}) copy-start(f32[16]{0:T(128)} %param.26) | copy-start | bytes 196
  80.4 3.6 %collective-permute-start.6 = (f32[3,1280]{1,0:T(4,128)S(1)}, f32[3,1280]{1,0:T(4,128)S(1)}, u32[]{:S(2)}, u32[]{:S(2)}) collective-permute-start(f32[3,1280]{1,0:T(4,128)S(1)} %slice.177), channel_id=1, source_target_pairs={{0,4},{4,8},{8,12},{12,16},{16,20},{20,24},{24,28},{28,32},{32,36}... | collective-permute-start | bytes 46088 | tf_op jit(solution)/shard_map/ppermute | solution.py:46
  85.3 31.7 %copy-start.3 = (f32[128,1024]{1,0:T(8,128)S(1)}, f32[128,1024]{1,0:T(8,128)}, u32[]{:S(2)}) copy-start(f32[128,1024]{1,0:T(8,128)} %copy-done.2) | copy-start | bytes 1572868
  86.3 16.5 %all-to-all-start.2 = ((bf16[32,48,128]{2,1,0:T(8,128)(2,1)}), bf16[32,48,128]{2,1,0:T(8,128)(2,1)S(1)}, u32[]{:S(2)}, u32[]{:S(2)}) async-start(bf16[32,48,128]{2,1,0:T(8,128)(2,1)} %maximum_maximum_fusion), calls=%async_computation.2 | async-start | bytes 786432 | tf_op jit(solution)/shard_map/all_to_all | solution.py:473
  92.9 24.4 %copy-start.11 = (f32[1024]{0:T(1024)S(1)}, f32[1024]{0:T(1024)}, u32[]{:S(2)}) copy-start(f32[1024]{0:T(1024)} %param.27) | copy-start | bytes 12292
  117.4 22.0 %copy-start.5 = (bf16[32,4096]{1,0:T(8,128)(2,1)S(1)}, bf16[32,4096]{1,0:T(8,128)(2,1)}, u32[]{:S(2)}) copy-start(bf16[32,4096]{1,0:T(8,128)(2,1)} %copy-done.4) | copy-start | bytes 786436
  117.4 22.3 %copy-start.8 = (f32[4096]{0:T(1024)S(1)}, f32[4096]{0:T(1024)}, u32[]{:S(2)}) copy-start(f32[4096]{0:T(1024)} %param.29) | copy-start | bytes 49156
  122.9 9.2 %collective-permute-start.9 = (bf16[32,4096]{1,0:T(8,128)(2,1)S(1)}, bf16[32,4096]{1,0:T(8,128)(2,1)S(1)}, u32[]{:S(2)}, u32[]{:S(2)}) collective-permute-start(bf16[32,4096]{1,0:T(8,128)(2,1)S(1)} %get-tuple-element.68), channel_id=1, source_target_pairs={{0,3},{1,0},{2,1},{3,2},{4,7},{5,4},{6,5},{7,6},{8,11},{9,8},{10,9... | collective-permute-start | bytes 786440 | tf_op jit(solution)/shard_map/ppermute | solution.py:40
  124.0 10.7 %collective-permute-start.8 = (bf16[32,4096]{1,0:T(8,128)(2,1)S(1)}, bf16[32,4096]{1,0:T(8,128)(2,1)S(1)}, u32[]{:S(2)}, u32[]{:S(2)}) collective-permute-start(bf16[32,4096]{1,0:T(8,128)(2,1)S(1)} %get-tuple-element.69), channel_id=1, source_target_pairs={{0,2},{1,3},{2,0},{3,1},{4,6},{5,7},{6,4},{7,5},{8,10},{9,11},{10,... | collective-permute-start | bytes 786440 | tf_op jit(solution)/shard_map/ppermute | solution.py:40
  125.9 13.4 %collective-permute-start.7 = (bf16[32,4096]{1,0:T(8,128)(2,1)S(1)}, bf16[32,4096]{1,0:T(8,128)(2,1)S(1)}, u32[]{:S(2)}, u32[]{:S(2)}) collective-permute-start(bf16[32,4096]{1,0:T(8,128)(2,1)S(1)} %get-tuple-element.67), channel_id=1, source_target_pairs={{0,1},{1,2},{2,3},{3,0},{4,5},{5,6},{6,7},{7,4},{8,9},{9,10},{10,1... | collective-permute-start | bytes 786440 | tf_op jit(solution)/shard_map/ppermute | solution.py:40
  126.1 38.7 %collective-permute-start.17 = (bf16[4096,512]{1,0:T(8,128)(2,1)}, bf16[4096,512]{1,0:T(8,128)(2,1)}, u32[]{:S(2)}, u32[]{:S(2)}) collective-permute-start(bf16[4096,512]{1,0:T(8,128)(2,1)} %all-gather.5.cloned.1.call-done.refs_3_.refs_7_), channel_id=1, source_target_pairs={{0,4},{4,0},{8,12},{12,8},{16,20},{20,16},{24,28},{28,24},{32,36},... | collective-permute-start | bytes 12582920 | tf_op jit(solution)/shard_map/ppermute | solution.py:35
  139.8 7.7 %collective-permute-start.10 = (bf16[32,4096]{1,0:T(8,128)(2,1)S(1)}, bf16[32,4096]{1,0:T(8,128)(2,1)S(1)}, u32[]{:S(2)}, u32[]{:S(2)}) collective-permute-start(bf16[32,4096]{1,0:T(8,128)(2,1)S(1)} %fusion.18), channel_id=1, source_target_pairs={{0,8},{4,36},{8,16},{12,44},{16,24},{20,52},{24,0},{28,60},{32,40}... | collective-permute-start | bytes 786440 | tf_op jit(solution)/shard_map/ppermute | solution.py:40
  140.5 9.3 %collective-permute-start.12 = (bf16[32,4096]{1,0:T(8,128)(2,1)S(1)}, bf16[32,4096]{1,0:T(8,128)(2,1)S(1)}, u32[]{:S(2)}, u32[]{:S(2)}) collective-permute-start(bf16[32,4096]{1,0:T(8,128)(2,1)S(1)} %fusion.18), channel_id=1, source_target_pairs={{0,24},{4,100},{8,0},{12,108},{16,8},{20,116},{24,16},{28,124},{32... | collective-permute-start | bytes 786440 | tf_op jit(solution)/shard_map/ppermute | solution.py:40
  143.1 8.1 %collective-permute-start.13 = (bf16[32,4096]{1,0:T(8,128)(2,1)S(1)}, bf16[32,4096]{1,0:T(8,128)(2,1)S(1)}, u32[]{:S(2)}, u32[]{:S(2)}) collective-permute-start(bf16[32,4096]{1,0:T(8,128)(2,1)S(1)} %fusion.18), channel_id=1, source_target_pairs={{0,16},{4,68},{8,24},{12,76},{16,0},{20,84},{24,8},{28,92},{32,48}... | collective-permute-start | bytes 786440 | tf_op jit(solution)/shard_map/ppermute | solution.py:40
  147.5 10.5 %collective-permute-start.11 = (bf16[64,4096]{1,0:T(8,128)(2,1)S(1)}, bf16[64,4096]{1,0:T(8,128)(2,1)S(1)}, u32[]{:S(2)}, u32[]{:S(2)}) collective-permute-start(bf16[64,4096]{1,0:T(8,128)(2,1)S(1)} %pad_maximum_fusion.1.refs_0_), channel_id=1, source_target_pairs={{0,32},{4,12},{8,40},{12,20},{16,48},{20,28},{24,56},{28,4},{32,64... | collective-permute-start | bytes 1572872 | tf_op jit(solution)/shard_map/ppermute | solution.py:40
  151.3 9.5 %collective-permute-start.14 = (bf16[64,4096]{1,0:T(8,128)(2,1)S(1)}, bf16[64,4096]{1,0:T(8,128)(2,1)S(1)}, u32[]{:S(2)}, u32[]{:S(2)}) collective-permute-start(bf16[64,4096]{1,0:T(8,128)(2,1)S(1)} %constant_dynamic-update-slice_fusion.4.refs_1_), channel_id=1, source_target_pairs={{0,96},{4,28},{8,104},{12,4},{16,112},{20,12},{24,120},{28,20},{32... | collective-permute-start | bytes 1572872 | tf_op jit(solution)/shard_map/ppermute | solution.py:40
  154.2 17.8 %collective-permute-start.18 = (bf16[64,4096]{1,0:T(8,128)(2,1)S(1)}, bf16[64,4096]{1,0:T(8,128)(2,1)S(1)}, u32[]{:S(2)}, u32[]{:S(2)}) collective-permute-start(bf16[64,4096]{1,0:T(8,128)(2,1)S(1)} %pad_maximum_fusion.1.refs_0_), channel_id=1, source_target_pairs={{0,96},{4,28},{8,104},{12,4},{16,112},{20,12},{24,120},{28,20},{32... | collective-permute-start | bytes 1572872 | tf_op jit(solution)/shard_map/ppermute | solution.py:40
  155.1 16.9 %collective-permute-start.19 = (bf16[64,4096]{1,0:T(8,128)(2,1)S(1)}, bf16[64,4096]{1,0:T(8,128)(2,1)S(1)}, u32[]{:S(2)}, u32[]{:S(2)}) collective-permute-start(bf16[64,4096]{1,0:T(8,128)(2,1)S(1)} %constant_dynamic-update-slice_fusion.4.refs_1_), channel_id=1, source_target_pairs={{0,32},{4,12},{8,40},{12,20},{16,48},{20,28},{24,56},{28,4},{32,64... | collective-permute-start | bytes 1572872 | tf_op jit(solution)/shard_map/ppermute | solution.py:40
  160.8 11.1 %collective-permute-start.15 = (bf16[64,4096]{1,0:T(8,128)(2,1)S(1)}, bf16[64,4096]{1,0:T(8,128)(2,1)}, u32[]{:S(2)}, u32[]{:S(2)}) collective-permute-start(bf16[64,4096]{1,0:T(8,128)(2,1)S(1)} %collective-permute-done.11.refs_4_), channel_id=1, source_target_pairs={{0,32},{4,12},{8,40},{12,20},{16,48},{20,28},{24,56},{28,4},{32,64... | collective-permute-start | bytes 1572872 | tf_op jit(solution)/shard_map/ppermute | solution.py:40
  162.0 10.0 %collective-permute-start.16 = (bf16[64,4096]{1,0:T(8,128)(2,1)S(1)}, bf16[64,4096]{1,0:T(8,128)(2,1)}, u32[]{:S(2)}, u32[]{:S(2)}) collective-permute-start(bf16[64,4096]{1,0:T(8,128)(2,1)S(1)} %collective-permute-done.14.refs_1_), channel_id=1, source_target_pairs={{0,96},{4,28},{8,104},{12,4},{16,112},{20,12},{24,120},{28,20},{32... | collective-permute-start | bytes 1572872 | tf_op jit(solution)/shard_map/ppermute | solution.py:40
  164.7 2.2 %copy-start = (bf16[4096,512]{1,0:T(8,128)(2,1)S(1)}, bf16[4096,512]{1,0:T(8,128)(2,1)}, u32[]{:S(2)}) copy-start(bf16[4096,512]{1,0:T(8,128)(2,1)} %all-gather.5.cloned.1.call-done.refs_3_.refs_7_) | copy-start | bytes 12582916
  179.8 5.2 %collective-permute-start.22 = (f32[8,128]{1,0:T(8,128)S(1)}, f32[8,128]{1,0:T(8,128)S(1)}, u32[]{:S(2)}, u32[]{:S(2)}) collective-permute-start(f32[8,128]{1,0:T(8,128)S(1)} %get-tuple-element.73), channel_id=1, source_target_pairs={{0,96},{4,28},{8,104},{12,4},{16,112},{20,12},{24,120},{28,20},{32... | collective-permute-start | bytes 12296 | tf_op jit(solution)/shard_map/ppermute | solution.py:40
  183.7 5.1 %collective-permute-start.21 = (f32[8,128]{1,0:T(8,128)S(1)}, f32[8,128]{1,0:T(8,128)S(1)}, u32[]{:S(2)}, u32[]{:S(2)}) collective-permute-start(f32[8,128]{1,0:T(8,128)S(1)} %get-tuple-element.74), channel_id=1, source_target_pairs={{0,64},{4,20},{8,72},{12,28},{16,80},{20,4},{24,88},{28,12},{32,96... | collective-permute-start | bytes 12296 | tf_op jit(solution)/shard_map/ppermute | solution.py:40
  183.7 5.1 %collective-permute-start.20 = (f32[8,128]{1,0:T(8,128)S(1)}, f32[8,128]{1,0:T(8,128)S(1)}, u32[]{:S(2)}, u32[]{:S(2)}) collective-permute-start(f32[8,128]{1,0:T(8,128)S(1)} %get-tuple-element.72), channel_id=1, source_target_pairs={{0,32},{4,12},{8,40},{12,20},{16,48},{20,28},{24,56},{28,4},{32,64... | collective-permute-start | bytes 12296 | tf_op jit(solution)/shard_map/ppermute | solution.py:40
  189.4 6.0 %collective-permute-start.25 = (f32[5,32]{1,0:T(8,128)S(1)}, f32[5,32]{1,0:T(8,128)S(1)}, u32[]{:S(2)}, u32[]{:S(2)}) collective-permute-start(f32[5,32]{1,0:T(8,128)S(1)} %bitcast.316), channel_id=1, source_target_pairs={{0,16},{4,68},{8,24},{12,76},{16,0},{20,84},{24,8},{28,92},{32,48}... | collective-permute-start | bytes 1928 | tf_op jit(solution)/shard_map/ppermute | solution.py:40
  192.1 4.8 %collective-permute-start.24 = (f32[5,32]{1,0:T(8,128)S(1)}, f32[5,32]{1,0:T(8,128)S(1)}, u32[]{:S(2)}, u32[]{:S(2)}) collective-permute-start(f32[5,32]{1,0:T(8,128)S(1)} %bitcast.317), channel_id=1, source_target_pairs={{0,8},{4,36},{8,16},{12,44},{16,24},{20,52},{24,0},{28,60},{32,40}... | collective-permute-start | bytes 1928 | tf_op jit(solution)/shard_map/ppermute | solution.py:40
  192.1 4.8 %collective-permute-start.23 = (f32[5,32]{1,0:T(8,128)S(1)}, f32[5,32]{1,0:T(8,128)S(1)}, u32[]{:S(2)}, u32[]{:S(2)}) collective-permute-start(f32[5,32]{1,0:T(8,128)S(1)} %bitcast.318), channel_id=1, source_target_pairs={{0,24},{4,100},{8,0},{12,108},{16,8},{20,116},{24,16},{28,124},{32... | collective-permute-start | bytes 1928 | tf_op jit(solution)/shard_map/ppermute | solution.py:40
Sparse Core Ops, SparseCore 0:
  9.5 64.0 all-gather.2
  75.3 46.7 all-gather.4
